TPU v7x, 32 devices: a whole 2x2x4 slice. The times are simulated.
32 devices in a mesh: lat: 2 (over x), lon: 16 (over z, y, core).
Axes of the slice: x: 2, y: 2, z: 4, core: 2. Of those that a mesh axis runs over, the one named last changes fastest.
Arguments:
- field: bfloat16 [16, 256, 256], P('lat', 'lon'), may hold values from -6 to 6
- dw_weight: bfloat16 [7, 7, 256], replicated, may hold values from -0.875 to 0.875
- w_expand: bfloat16 [256, 1024], replicated, may hold values from -0.375 to 0.375
- w_reduce: bfloat16 [1024, 256], replicated, may hold values from -0.1875 to 0.1875
- lat_attn: bfloat16 [4, 256, 256], replicated, as said below
- lon_attn: bfloat16 [4, 256, 256], replicated, as said below
Outputs:
- result: bfloat16 [16, 256, 256], P('lat', 'lon')
Inputs may be any that keep to these rules, and one draw needn't show every extreme that they name: `lat_attn`: query, key, value and output projections in this order. `lon_attn`: query, key, value and output projections in this order.
All inputs are finite; a program needn't handle non-finite values.
Results may differ from a plain program's by a relative error of at most 0.03.
Values may be sent and summed in bfloat16 or wider, within the bound.
No kernel may reach another device: no remote copies, remote signals or barrier semaphores. Data moves between devices by JAX's collectives and lax.ppermute only.
A program may use at most 64 MiB of HBM per device.

v0:
```python
import jax
import jax.numpy as jnp
from jax import lax
from jax.sharding import PartitionSpec as P

HEADS = 8


EPSILON = 1e-06


def padded_2(array, sides, width, wrap):
    for axis, dim in sides:
        devices, length = (lax.axis_size(axis), array.shape[dim])
        up = [(i, (i + 1) % devices) for i in range(devices if wrap else devices - 1)]
        down = [(j, i) for i, j in up]
        last = lax.slice_in_dim(array, length - width, length, axis=dim)
        first = lax.slice_in_dim(array, 0, width, axis=dim)
        before = lax.ppermute(last, axis, up)
        after = lax.ppermute(first, axis, down)
        array = jnp.concatenate([before, array, after], axis=dim)
    return array


def layer_norm(values):
    average = jnp.mean(values, axis=-1, keepdims=True)
    centered = values - average
    variance = jnp.mean(centered * centered, axis=-1, keepdims=True)
    return centered * lax.rsqrt(variance + EPSILON)


def project(rows, matrix):
    shape = rows.shape
    flat_rows = rows.reshape(-1, shape[-1])
    product = jnp.dot(flat_rows, matrix, preferred_element_type=jnp.float32)
    return product.reshape(shape[:-1] + (matrix.shape[1],))


def row_attention(sequence, weights):
    count, length, channels = sequence.shape
    head_size = channels // HEADS
    queries = (
        project(sequence, weights[0]).astype(jnp.bfloat16).reshape(count, length, HEADS, head_size)
    )
    key_all = (
        project(sequence, weights[1]).astype(jnp.bfloat16).reshape(count, length, HEADS, head_size)
    )
    value_all = (
        project(sequence, weights[2]).astype(jnp.bfloat16).reshape(count, length, HEADS, head_size)
    )
    scores = jnp.einsum(
        "rqhd,rkhd->rhqk", queries, key_all, preferred_element_type=jnp.float32
    ) * head_size ** (-0.5)
    top = jnp.max(scores, axis=-1, keepdims=True)
    raw_weights = jnp.exp(scores - top)
    totals = jnp.sum(raw_weights, axis=-1)
    mixed = jnp.einsum(
        "rhqk,rkhd->rqhd",
        raw_weights.astype(jnp.bfloat16),
        value_all,
        preferred_element_type=jnp.float32,
    )
    mixed = mixed / jnp.swapaxes(totals, 1, 2)[..., None]
    return mixed.reshape(count, length, channels).astype(jnp.bfloat16)


def absorb(state_now, queries, key_rows, value_rows, score_scale):
    top, totals, partial_value = state_now
    scores = (
        jnp.einsum("lqhd,lkhd->lhqk", queries, key_rows, preferred_element_type=jnp.float32)
        * score_scale
    )
    new_top = jnp.maximum(top, jnp.max(scores, axis=-1))
    probs = jnp.exp(scores - new_top[..., None])
    totals = jnp.sum(probs, axis=-1)
    partial_value = jnp.einsum(
        "lhqk,lkhd->lhqd",
        probs.astype(jnp.bfloat16),
        value_rows,
        preferred_element_type=jnp.float32,
    )
    return (new_top, totals, partial_value)


def shards(field, dw_weight, w_expand, w_reduce, lat_attn, lon_attn):
    lat_rows, lon_cols, channels = field.shape
    head_size = channels // HEADS
    score_scale = head_size ** (-0.5)
    lat_groups = lax.axis_size("lat")
    padded = padded_2(field, (("lat", 0),), 3, False)
    padded = padded_2(padded, (("lon", 1),), 3, True).astype(jnp.float32)
    taps = dw_weight.astype(jnp.float32)
    field_wide = field.astype(jnp.float32)
    convolved = jnp.zeros_like(field_wide)
    for row_off in range(7):
        for col_off in range(7):
            convolved = (
                convolved
                + padded[row_off : row_off + lat_rows, col_off : col_off + lon_cols]
                * taps[row_off, col_off]
            )
    normed = layer_norm(convolved).astype(jnp.bfloat16)
    expanded = jax.nn.gelu(project(normed, w_expand), approximate=False).astype(jnp.bfloat16)
    block_one = (field_wide + project(expanded, w_reduce)).astype(jnp.bfloat16)
    lat_in = layer_norm(block_one.astype(jnp.float32)).astype(jnp.bfloat16)
    grouped = lat_in.reshape(lat_rows, lat_groups, lon_cols // lat_groups, channels)
    flat_columns = lax.all_to_all(grouped, "lat", split_axis=1, concat_axis=0, tiled=True)[:, 0]
    mixed_columns = jnp.swapaxes(row_attention(jnp.swapaxes(flat_columns, 0, 1), lat_attn), 0, 1)
    lat_mix = mixed_columns[:, None]
    lat_back = lax.all_to_all(lat_mix, "lat", split_axis=0, concat_axis=1, tiled=True).reshape(
        lat_rows, lon_cols, channels
    )
    block_two = (block_one.astype(jnp.float32) + project(lat_back, lat_attn[3])).astype(
        jnp.bfloat16
    )
    lon_in = layer_norm(block_two.astype(jnp.float32)).astype(jnp.bfloat16)
    queries = project(lon_in, lon_attn[0]).astype(jnp.bfloat16)
    query_heads = queries.reshape(lat_rows, lon_cols, HEADS, head_size)
    initial = (
        jnp.full((lat_rows, HEADS, lon_cols), -1e30, jnp.float32),
        jnp.zeros((lat_rows, HEADS, lon_cols), jnp.float32),
        jnp.zeros((lat_rows, HEADS, lon_cols, head_size), jnp.float32),
    )
    block_in = lax.all_gather(lon_in, "lon", axis=1, tiled=True)
    key_rows = (
        project(block_in, lon_attn[1]).astype(jnp.bfloat16).reshape(lat_rows, -1, HEADS, head_size)
    )
    value_rows = (
        project(block_in, lon_attn[2]).astype(jnp.bfloat16).reshape(lat_rows, -1, HEADS, head_size)
    )
    state_now = absorb(initial, query_heads, key_rows, value_rows, score_scale)
    partial_value = state_now[2] / state_now[1][..., None]
    mixture = (
        partial_value.transpose(0, 2, 1, 3)
        .reshape(lat_rows, lon_cols, channels)
        .astype(jnp.bfloat16)
    )
    return (block_two.astype(jnp.float32) + project(mixture, lon_attn[3])).astype(jnp.bfloat16)


def solution(mesh):
    return jax.shard_map(
        shards,
        mesh=mesh,
        in_specs=(P("lat", "lon", None), P(), P(), P(), P(), P()),
        out_specs=P("lat", "lon", None),
        check_vma=False,
    )
```

profile of v0, /device:TPU:0, one launch (start us, length us, event | category | flops | bytes accessed | tf_op | source)
XLA Modules:
  0.0 91.0 jit_solution(17774572511314204093)
XLA Ops:
  6.5 0.0 copy-start
  6.5 0.0 all-gather.2.cloned.1.call-start
  6.5 0.8 fusion.178
  7.4 1.3 %collective-permute-start.1 = (bf16[3,16,256]{2,1,0:T(8,128)(2,1)S(1)}, bf16[3,16,256]{2,1,0:T(8,128)(2,1)S(1)}, u32[]{:S(2)}, u32[]{:S(2)}) collective-permute-start(bf16[3,16,256]{2,1,0:T(8,128)(2,1)S(1)} %get-tuple-element.11), channel_id=1, source_target_pairs={{16,0},{17,1},{18,2},{19,3},{20,4},{21,5},{22,6},{23,7},{24,8},{25... | collective-permute-start | bytes 73736 | tf_op jit(solution)/shard_map/ppermute | solution.py:20
  8.6 4.8 %collective-permute-start = (bf16[3,16,256]{2,1,0:T(8,128)(2,1)S(1)}, bf16[3,16,256]{2,1,0:T(8,128)(2,1)S(1)}, u32[]{:S(2)}, u32[]{:S(2)}) collective-permute-start(bf16[3,16,256]{2,1,0:T(8,128)(2,1)S(1)} %get-tuple-element.12), channel_id=1, source_target_pairs={{0,16},{1,17},{2,18},{3,19},{4,20},{5,21},{6,22},{7,23},{8,24},{9,... | collective-permute-start | bytes 73736 | tf_op jit(solution)/shard_map/ppermute | solution.py:19
  13.5 1.0 %fusion.180 = (f32[1,1,256]{2,1,0:T(1,128)S(1)}, f32[1,1,256]{2,1,0:T(1,128)S(1)}, f32[1,1,256]{2,1,0:T(1,128)S(1)}, f32[1,1,256]{2,1,0:T(1,128)S(1)}, f32[1,1,2...) fusion(bf16[7,7,256]{2,1,0:T(8,128)(2,1)} %param.7), kind=kLoop, calls=%fused_computation.270 | loop fusion | bytes 38912 | tf_op jit(solution)/shard_map/slice | solution.py:100
  14.5 1.0 %fusion.179 = (f32[1,1,256]{2,1,0:T(1,128)S(1)}, f32[1,1,256]{2,1,0:T(1,128)S(1)}, f32[1,1,256]{2,1,0:T(1,128)S(1)}, f32[1,1,256]{2,1,0:T(1,128)S(1)}, f32[1,1,2...) fusion(bf16[7,7,256]{2,1,0:T(8,128)(2,1)} %param.7), kind=kLoop, calls=%fused_computation.269 | loop fusion | bytes 38912 | tf_op jit(solution)/shard_map/slice | solution.py:100
  15.5 0.0 collective-permute-done
  15.6 0.8 constant_dynamic-update-slice_fusion.1
  16.4 0.0 collective-permute-done.1
  16.5 0.1 collective-permute-start.2
  16.5 4.6 %collective-permute-start.3 = (bf16[14,3,256]{2,1,0:T(4,128)(2,1)S(1)}, bf16[14,3,256]{2,1,0:T(4,128)(2,1)S(1)}, u32[]{:S(2)}, u32[]{:S(2)}) collective-permute-start(bf16[14,3,256]{2,1,0:T(4,128)(2,1)S(1)} %get-tuple-element.10), channel_id=1, source_target_pairs={{1,0},{2,1},{3,2},{4,3},{5,4},{6,5},{7,6},{8,7},{9,8},{10,9},{11,1... | collective-permute-start | bytes 64520 | tf_op jit(solution)/shard_map/ppermute | solution.py:20
  21.2 1.0 %fusion.181 = (f32[1,1,256]{2,1,0:T(1,128)S(1)}, f32[1,1,256]{2,1,0:T(1,128)S(1)}, f32[1,1,256]{2,1,0:T(1,128)S(1)}, f32[1,1,256]{2,1,0:T(1,128)S(1)}, f32[1,1,2...) fusion(bf16[7,7,256]{2,1,0:T(8,128)(2,1)} %param.7), kind=kLoop, calls=%fused_computation.271 | loop fusion | bytes 22528 | tf_op jit(solution)/shard_map/slice | solution.py:100
  22.1 0.5 collective-permute-done.2
  22.7 0.1 collective-permute-done.3
  22.7 0.1 maximum_convert_fusion
  22.8 0.9 %fusion.175 = (f32[8,16]{1,0:T(8,128)S(1)}, f32[8,16,256]{2,1,0:T(8,128)S(1)}) fusion(f32[256]{0:T(256)S(1)} %bitcast.203, f32[14,22,256]{2,1,0:T(8,128)S(1)} %maximum_convert_fusion, f32[256]{0:T(256)S(1)} %bitcast.202, f32[256]{0:T(256)S(1)} %bitcast.201, f32[256]{0:T(256)S(1)} %bitcast.200, f32[256]{0:T(256)S(1)} %bitcast.199, f32[256]{0:T(256)S(1)} %bitcast.198, ...), kind=kLoop, calls=%fused_computation.266 | loop fusion | flops 3211136 | bytes 6604288 | tf_op jit(solution)/shard_map/reduce_sum | solution.py:26
  23.7 0.0 copy-start.4
  23.7 0.0 copy-start.5
  23.7 0.2 multiply_reduce_fusion.2
  23.9 0.0 copy-done
  23.9 0.4 fusion.130
  24.3 0.2 copy-done.4
  24.6 0.2 copy-done.5
  24.8 0.0 copy-start.3
  24.8 1.4 %fusion.182 = (f32[8,16]{1,0:T(8,128)S(1)}, f32[8,16,256]{2,1,0:T(8,128)S(1)}) fusion(bf16[1024,256]{1,0:T(8,128)(2,1)S(1)} %copy-done.5, f32[8,16,1024]{2,1,0:T(8,128)S(1)} %get-tuple-element.62, u8[16,1024]{1,0:T(8,128)(4,1)S(1)} %get-tuple-element.6, u8[16,1024]{1,0:T(8,128)(4,1)S(1)} %get-tuple-element.5, bf16[8,16,256]{2,1,0:T(8,128)(2,1)S(1)} %copy-done.4), kind=kOutput, calls=%fused_computation.272 | convolution fusion | flops 76447616 | bytes 1278464 | tf_op jit(solution)/shard_map/dot_general | solution.py:35
  26.2 0.2 multiply_reduce_fusion.1
  26.4 0.1 fusion.131
  26.5 6.7 %all_to_all.30 = bf16[8,2,8,256]{3,2,0,1:T(8,128)(2,1)S(1)} all-to-all(bf16[8,2,8,256]{3,2,0,1:T(8,128)(2,1)S(1)} %copy.27), channel_id=1, replica_groups=mesh['lat'=2,'lon'=16] {'lat'}, dimensions={1} | all-to-all | bytes 131072 | tf_op jit(solution)/shard_map/all_to_all | solution.py:107
  33.2 0.0 copy-done.3
  33.2 0.2 convolution_convert_fusion.3
  33.4 0.2 convolution_convert_fusion.4
  33.6 0.2 convolution_convert_fusion.5
  33.7 0.2 reshape.110
  33.9 0.2 reshape.111
  34.1 0.2 reshape.112
  34.3 0.3 fusion.183
  34.5 0.2 fusion.25
  34.7 0.3 fusion.3
  35.0 0.0 copy-start.2
  35.1 0.1 copy.33
  35.1 0.2 convert_element_type.89
  35.3 6.5 %all_to_all.31 = bf16[16,1,8,256]{3,2,1,0:T(8,128)(2,1)S(1)} all-to-all(bf16[16,1,8,256]{3,2,1,0:T(8,128)(2,1)S(1)} %copy.34), channel_id=1, replica_groups=mesh['lat'=2,'lon'=16] {'lat'}, dimensions={0} | all-to-all | bytes 131072 | tf_op jit(solution)/shard_map/all_to_all | solution.py:110
  41.8 0.2 fusion.184
  42.1 0.2 multiply_reduce_fusion
  42.3 0.7 multiply_convert_fusion
  43.0 0.0 all-gather.2.cloned.1.call-update
  43.0 0.0 copy-done.2
  43.1 1.0 %convolution_convert_fusion.2 = bf16[8,16,256]{2,1,0:T(8,128)(2,1)S(1)} fusion(bf16[8,16,256]{2,1,0:T(8,128)(2,1)} %multiply_convert_fusion, bf16[4,256,256]{2,1,0:T(8,128)(2,1)S(1)} %copy-done.2), kind=kOutput, calls=%fused_computation.18 | convolution fusion | flops 16809984 | bytes 262144 | tf_op jit(solution)/shard_map/dot_general | solution.py:35
  44.1 0.2 reshape.113
  44.2 34.5 %all-gather.2.cloned.1.call-done = bf16[8,256,256]{2,1,0:T(8,128)(2,1)} async-done(((bf16[8,16,256]{2,1,0:T(8,128)(2,1)}), bf16[8,256,256]{2,1,0:T(8,128)(2,1)}) %all-gather.2.cloned.1.call-update) | async-done | bytes 1048592 | tf_op jit(solution)/shard_map/all_gather | solution.py:124
  78.8 1.7 %convolution_convert_fusion.1 = bf16[8,256,256]{1,2,0:T(8,128)(2,1)S(1)} fusion(bf16[8,256,256]{2,1,0:T(8,128)(2,1)} %all-gather.2.cloned.1.call-done, bf16[4,256,256]{2,1,0:T(8,128)(2,1)S(1)} %copy-done.2), kind=kOutput, calls=%fused_computation.1 | convolution fusion | flops 268959744 | bytes 2228224 | tf_op jit(solution)/shard_map/dot_general | solution.py:35
  80.5 0.4 fusion.185
  80.9 0.0 copy-start.1
  80.9 0.4 fusion.9
  81.3 0.8 copy-done.1
  82.1 0.5 convolution_convert_fusion
  82.6 0.5 fusion.2
  83.1 0.1 copy.39
  83.2 0.2 convert_element_type.98
  83.3 0.8 fusion.8
  (12 shorter events, 0.1 us)
Async XLA Ops:
  6.5 17.4 %copy-start = (bf16[256,1024]{1,0:T(8,128)(2,1)S(1)}, bf16[256,1024]{1,0:T(8,128)(2,1)}, u32[]{:S(2)}) copy-start(bf16[256,1024]{1,0:T(8,128)(2,1)} %param.8) | copy-start | bytes 1572868
  6.5 72.2 %all-gather.2.cloned.1.call-start = ((), (), s32[]{:S(2)}) async-start(), calls=%async_computation.2 | async-start | bytes 1114112 | tf_op jit(solution)/shard_map/all_gather | solution.py:124
  7.4 9.1 %collective-permute-start.1 = (bf16[3,16,256]{2,1,0:T(8,128)(2,1)S(1)}, bf16[3,16,256]{2,1,0:T(8,128)(2,1)S(1)}, u32[]{:S(2)}, u32[]{:S(2)}) collective-permute-start(bf16[3,16,256]{2,1,0:T(8,128)(2,1)S(1)} %get-tuple-element.11), channel_id=1, source_target_pairs={{16,0},{17,1},{18,2},{19,3},{20,4},{21,5},{22,6},{23,7},{24,8},{25... | collective-permute-start | bytes 73736 | tf_op jit(solution)/shard_map/ppermute | solution.py:20
  8.6 6.9 %collective-permute-start = (bf16[3,16,256]{2,1,0:T(8,128)(2,1)S(1)}, bf16[3,16,256]{2,1,0:T(8,128)(2,1)S(1)}, u32[]{:S(2)}, u32[]{:S(2)}) collective-permute-start(bf16[3,16,256]{2,1,0:T(8,128)(2,1)S(1)} %get-tuple-element.12), channel_id=1, source_target_pairs={{0,16},{1,17},{2,18},{3,19},{4,20},{5,21},{6,22},{7,23},{8,24},{9,... | collective-permute-start | bytes 73736 | tf_op jit(solution)/shard_map/ppermute | solution.py:19
  16.5 6.2 %collective-permute-start.2 = (bf16[14,3,256]{2,1,0:T(4,128)(2,1)S(1)}, bf16[14,3,256]{2,1,0:T(4,128)(2,1)S(1)}, u32[]{:S(2)}, u32[]{:S(2)}) collective-permute-start(bf16[14,3,256]{2,1,0:T(4,128)(2,1)S(1)} %get-tuple-element.9), channel_id=1, source_target_pairs={{0,1},{1,2},{2,3},{3,4},{4,5},{5,6},{6,7},{7,8},{8,9},{9,10},{10,1... | collective-permute-start | bytes 64520 | tf_op jit(solution)/shard_map/ppermute | solution.py:19
  16.5 6.2 %collective-permute-start.3 = (bf16[14,3,256]{2,1,0:T(4,128)(2,1)S(1)}, bf16[14,3,256]{2,1,0:T(4,128)(2,1)S(1)}, u32[]{:S(2)}, u32[]{:S(2)}) collective-permute-start(bf16[14,3,256]{2,1,0:T(4,128)(2,1)S(1)} %get-tuple-element.10), channel_id=1, source_target_pairs={{1,0},{2,1},{3,2},{4,3},{5,4},{6,5},{7,6},{8,7},{9,8},{10,9},{11,1... | collective-permute-start | bytes 64520 | tf_op jit(solution)/shard_map/ppermute | solution.py:20
  23.7 0.9 copy-start.4
  23.7 1.1 %copy-start.5 = (bf16[1024,256]{1,0:T(8,128)(2,1)S(1)}, bf16[1024,256]{1,0:T(8,128)(2,1)}, u32[]{:S(2)}) copy-start(bf16[1024,256]{1,0:T(8,128)(2,1)} %param.9) | copy-start | bytes 1572868
  24.8 8.4 %copy-start.3 = (bf16[4,256,256]{2,1,0:T(8,128)(2,1)S(1)}, bf16[4,256,256]{2,1,0:T(8,128)(2,1)}, u32[]{:S(2)}) copy-start(bf16[4,256,256]{2,1,0:T(8,128)(2,1)} %param.10) | copy-start | bytes 1572868
  35.0 8.0 %copy-start.2 = (bf16[4,256,256]{2,1,0:T(8,128)(2,1)S(1)}, bf16[4,256,256]{2,1,0:T(8,128)(2,1)}, u32[]{:S(2)}) copy-start(bf16[4,256,256]{2,1,0:T(8,128)(2,1)} %param.11) | copy-start | bytes 1572868
  80.9 1.2 %copy-start.1 = (bf16[8,256,256]{2,1,0:T(8,128)(2,1)S(1)}, bf16[8,256,256]{2,1,0:T(8,128)(2,1)}, u32[]{:S(2)}) copy-start(bf16[8,256,256]{2,1,0:T(8,128)(2,1)} %all-gather.2.cloned.1.call-done) | copy-start | bytes 3145732
Sparse Core Ops, SparseCore 0:
  43.2 35.5 all-gather.1
where the time goes:
time: 91.5 us; the launch traced here: 91 us
  waiting for transfers between devices  35.2 us (38%)
  between operations  13.7 us (15%)
  blocking collectives  13.2 us (14%)
  starting transfers between devices  10.8 us (12%)
  matrix products  7.91 us (9%)
  local copies, waits for them, and re-layouts  7.18 us (8%)
  other arithmetic  2.97 us (3%)
    all_gather x1, waiting for transfers between devices, shards(): block_in = lax.all_gather(lon_in, 'lon', axis=1, tiled=True)  34.5 us
    all_to_all x1, blocking collectives, shards(): lax.all_to_all(grouped, 'lat', split_axis=1, concat_axis=0, tiled=True)  6.72 us
    all_to_all x1, blocking collectives, shards(): lax.all_to_all(lat_mix, 'lat', split_axis=0, concat_axis=1, tiled=True)  6.5 us
    dot_general x10, matrix products, project(): product = jnp.dot(flat_rows, matrix, preferred_element_type=jnp.float32)  6.44 us
    ppermute x2, starting transfers between devices, padded_2(): after = lax.ppermute(first, axis, down)  5.92 us
    ppermute x2, starting transfers between devices, padded_2(): before = lax.ppermute(last, axis, up)  4.9 us
    slice x3, local copies, waits for them, and re-layouts, shards(): taps[row_off, col_off]  2.99 us
    unnamed x14, local copies, waits for them, and re-layouts  2.15 us
  transfers between devices with their start and end apart: 5, of which 3 were waited for; matrix products, arithmetic and copies ran while one was open for 6% of the time, Pallas kernels for 0%

commit v1 on v0

v1 whole, which is shorter than its diff:
```python
import jax
import jax.numpy as jnp
from jax import lax
from jax.sharding import PartitionSpec as P

HEADS = 8
HALO = 3
EPSILON = 1e-06


def layer_norm(values):
    average = jnp.mean(values, axis=-1, keepdims=True)
    centered = values - average
    variance = jnp.mean(centered * centered, axis=-1, keepdims=True)
    return centered * lax.rsqrt(variance + EPSILON)


def dot(rows, matrix):
    return jnp.dot(rows, matrix, preferred_element_type=jnp.float32)


def dot_t(rows, matrix):
    return lax.dot_general(
        rows, matrix, (((1,), (1,)), ((), ())), preferred_element_type=jnp.float32
    )


def attend(queries, keys, values, heads, head_size, mask):
    count = queries.shape[0]
    lane_head = lax.broadcasted_iota(jnp.int32, (1, queries.shape[1]), 1) // head_size
    stacked = jnp.concatenate(
        [jnp.where(lane_head == h, queries, jnp.zeros_like(queries)) for h in range(heads)], axis=0
    )
    scores = dot_t(stacked, keys) * head_size ** (-0.5)
    if mask is not None:
        scores = jnp.where(mask, scores, -1e30)
    top = jnp.max(scores, axis=-1, keepdims=True)
    probs = jnp.exp(scores - top)
    totals = jnp.sum(probs, axis=-1, keepdims=True)
    mixed = dot(probs.astype(jnp.bfloat16), values) / totals
    out = mixed[:count]
    for h in range(1, heads):
        out = jnp.where(lane_head == h, mixed[h * count : (h + 1) * count], out)
    return out.astype(jnp.bfloat16)


def gather_windows(field):
    nlat, nlon = lax.axis_size("lat"), lax.axis_size("lon")
    rows, cols, channels = field.shape

    def shift(piece, dlat, dlon):
        pairs = [
            (((i + dlat) % nlat) * nlon + (j + dlon) % nlon, i * nlon + j)
            for i in range(nlat)
            for j in range(nlon)
        ]
        return lax.ppermute(piece, ("lat", "lon"), pairs)

    first, last = field[:, :HALO], field[:, cols - HALO :]
    windows = []
    for s in range(nlat):
        middle = field if s == 0 else shift(field, s, 0)
        windows.append(jnp.concatenate([shift(last, s, -1), middle, shift(first, s, 1)], axis=1))
    return windows


def shards(field, dw_weight, w_expand, w_reduce, lat_attn, lon_attn):
    rows, cols, channels = field.shape
    head_size = channels // HEADS
    nlat, nlon = lax.axis_size("lat"), lax.axis_size("lon")
    my_lat, my_lon = lax.axis_index("lat"), lax.axis_index("lon")
    split = max(1, nlon // rows)
    group = HEADS // split
    group_channels = group * head_size
    my_group = my_lon % split
    lon_qkv = lax.dynamic_slice_in_dim(lon_attn[:3], my_group * group_channels, group_channels, 2)

    windows = gather_windows(field)
    whole = jnp.concatenate(windows, axis=0)
    whole = jnp.roll(whole, my_lat * rows, axis=0)
    all_rows = rows * nlat
    padded = jnp.pad(whole, ((HALO, HALO), (0, 0), (0, 0))).astype(jnp.float32)
    taps = dw_weight.astype(jnp.float32)
    conv = jnp.zeros((all_rows, cols, channels), jnp.float32)
    for a in range(2 * HALO + 1):
        for b in range(2 * HALO + 1):
            conv = conv + padded[a : a + all_rows, b : b + cols] * taps[a, b]
    normed = layer_norm(conv).astype(jnp.bfloat16).reshape(-1, channels)
    expanded = jax.nn.gelu(dot(normed, w_expand), approximate=False).astype(jnp.bfloat16)
    center = whole[:, HALO : HALO + cols].reshape(-1, channels).astype(jnp.float32)
    block_one = (center + dot(expanded, w_reduce)).astype(jnp.bfloat16)
    lat_in = layer_norm(block_one.astype(jnp.float32)).astype(jnp.bfloat16)
    cells = rows * cols
    own_in = lax.dynamic_slice_in_dim(lat_in, my_lat * cells, cells, 0)
    own_one = lax.dynamic_slice_in_dim(block_one, my_lat * cells, cells, 0)
    queries = dot(own_in, lat_attn[0]).astype(jnp.bfloat16)
    keys = dot(lat_in, lat_attn[1]).astype(jnp.bfloat16)
    values = dot(lat_in, lat_attn[2]).astype(jnp.bfloat16)
    row_col = lax.broadcasted_iota(jnp.int32, (HEADS * cells, 1), 0) % cols
    key_col = lax.broadcasted_iota(jnp.int32, (1, all_rows * cols), 1) % cols
    lat_mix = attend(queries, keys, values, HEADS, head_size, row_col == key_col)
    block_two = (own_one.astype(jnp.float32) + dot(lat_mix, lat_attn[3])).astype(jnp.bfloat16)
    lon_in = layer_norm(block_two.astype(jnp.float32)).astype(jnp.bfloat16)

    sent = lon_in.reshape(rows, 1, cols, channels)
    sent = jnp.broadcast_to(sent, (rows, split, cols, channels)).reshape(
        rows * split, cols, channels
    )
    circle = lax.all_to_all(sent, "lon", 0, 0, tiled=True).reshape(nlon * cols, channels)
    lon_q = dot(circle, lon_qkv[0]).astype(jnp.bfloat16)
    lon_k = dot(circle, lon_qkv[1]).astype(jnp.bfloat16)
    lon_v = dot(circle, lon_qkv[2]).astype(jnp.bfloat16)
    lon_mix = attend(lon_q, lon_k, lon_v, group, head_size, None)
    back = lax.all_to_all(lon_mix.reshape(nlon, cols, group_channels), "lon", 0, 0, tiled=True)
    back = back.reshape(rows, split, cols, group_channels)
    back = jnp.concatenate([back[:, s] for s in range(split)], axis=-1).reshape(cells, channels)
    out = block_two.astype(jnp.float32) + dot(back, lon_attn[3])
    return out.astype(jnp.bfloat16).reshape(rows, cols, channels)


def solution(mesh):
    return jax.shard_map(
        shards,
        mesh=mesh,
        in_specs=(P("lat", "lon", None), P(), P(), P(), P(), P()),
        out_specs=P("lat", "lon", None),
        check_vma=False,
    )
```

time: 91.5 us -> 46.3 us (0.51)
  waiting for transfers between devices: 35.2 us -> 9.19 us
  between operations: 13.7 us -> 0.4 us
  local copies, waits for them, and re-layouts: 7.18 us -> 3.31 us
  blocking collectives: 13.2 us -> 9.48 us
  starting transfers between devices: 10.8 us -> 13.2 us
  matrix products: 7.91 us -> 6.06 us
  other arithmetic: 2.97 us -> 4.38 us
    all_gather x1 -> x0, waiting for transfers between devices: 34.5 us -> none  [shards(): block_in = lax.all_gather(lon_in, 'lon', axis=1, tiled=True)]
    all_to_all x0 -> x1, waiting for transfers between devices: none -> 7.85 us  [shards(): lax.all_to_all(sent, 'lon', 0, 0, tiled=True).reshape(nlon * cols, channels)]
    all_to_all x0 -> x1, starting transfers between devices: none -> 4.14 us  [shards(): lax.all_to_all(sent, 'lon', 0, 0, tiled=True).reshape(nlon * cols, channels)]
    all_to_all x2 -> x1, blocking collectives: 13.2 us -> 9.48 us  [shards(): lax.all_to_all(lon_mix.reshape(nlon, cols, group_channels), 'lon', 0, 0,...]
    slice x5 -> x7, local copies, waits for them, and re-layouts: 3.83 us -> 1.97 us  [the longest x3 1.04 us: shards(): conv = conv + padded[a:a + all_rows, b:b + cols] * taps[a, b]]
    dot_general x14 -> x9, matrix products: 7.91 us -> 6.06 us  [the longest x7 5.17 us: dot(): return jnp.dot(rows, matrix, preferred_element_type=jnp.float32)]
    ppermute x4 -> x5, starting transfers between devices: 10.8 us -> 9.01 us  [shift(): return lax.ppermute(piece, ('lat', 'lon'), pairs)]
    unnamed x14 -> x12, local copies, waits for them, and re-layouts: 2.15 us -> 0.7 us
  transfers between devices with their start and end apart: 5 -> 6, of which waited for: 3 -> 2; matrix products, arithmetic and copies ran while one was open for 6% -> 2% of each run, Pallas kernels for 0% -> 0%
where the time goes in v1:
time: 46.3 us; the launch traced here: 46 us
  starting transfers between devices  13.2 us (29%)
  blocking collectives  9.48 us (20%)
  waiting for transfers between devices  9.19 us (20%)
  matrix products  6.06 us (13%)
  other arithmetic  4.38 us (9%)
  local copies, waits for them, and re-layouts  3.31 us (7%)
    all_to_all x1, blocking collectives, shards(): lax.all_to_all(lon_mix.reshape(nlon, cols, group_channels), 'lon', 0, 0,...  9.48 us
    ppermute x5, starting transfers between devices, shift(): return lax.ppermute(piece, ('lat', 'lon'), pairs)  9.01 us
    all_to_all x1, waiting for transfers between devices, shards(): lax.all_to_all(sent, 'lon', 0, 0, tiled=True).reshape(nlon * cols, channels)  7.85 us
    dot_general x7, matrix products, dot(): return jnp.dot(rows, matrix, preferred_element_type=jnp.float32)  5.17 us
    all_to_all x1, starting transfers between devices, shards(): lax.all_to_all(sent, 'lon', 0, 0, tiled=True).reshape(nlon * cols, channels)  4.14 us
    reduce_sum x1, other arithmetic, layer_norm(): average = jnp.mean(values, axis=-1, keepdims=True)  1.75 us
    ppermute x5, waiting for transfers between devices, shift(): return lax.ppermute(piece, ('lat', 'lon'), pairs)  1.34 us
    concatenate x1, other arithmetic, shards(): whole = jnp.roll(whole, my_lat * rows, axis=0)  1.07 us
  transfers between devices with their start and end apart: 6, of which 2 were waited for; matrix products, arithmetic and copies ran while one was open for 2% of the time, Pallas kernels for 0%

profile of v1, /device:TPU:0, one launch (start us, length us, event | category | flops | bytes accessed | tf_op | source)
XLA Modules:
  0.0 46.0 jit_solution(1459194282634450635)
XLA Ops:
  0.0 0.0 copy-start
  0.0 0.0 copy-start.2
  0.0 0.9 %fusion.174 = (bf16[8,3,256]{2,1,0:T(4,128)(2,1)S(1)}, bf16[8,3,256]{2,1,0:T(4,128)(2,1)S(1)}) fusion(bf16[8,16,256]{2,1,0:T(8,128)(2,1)} %param.6), kind=kLoop, calls=%fused_computation.301 | loop fusion | bytes 49152 | tf_op jit(solution)/shard_map/slice | solution.py:59
  0.9 0.0 copy-start.3
  0.9 0.5 %collective-permute-start = (bf16[8,3,256]{2,1,0:T(4,128)(2,1)S(1)}, bf16[8,3,256]{2,1,0:T(4,128)(2,1)S(1)}, u32[]{:S(2)}, u32[]{:S(2)}) collective-permute-start(bf16[8,3,256]{2,1,0:T(4,128)(2,1)S(1)} %get-tuple-element.14), channel_id=1, source_target_pairs={{15,0},{0,1},{1,2},{2,3},{3,4},{4,5},{5,6},{6,7},{7,8},{8,9},{9,10... | collective-permute-start | bytes 36872 | tf_op jit(solution)/shard_map/ppermute | solution.py:57
  1.4 3.7 %collective-permute-start.2 = (bf16[8,3,256]{2,1,0:T(4,128)(2,1)S(1)}, bf16[8,3,256]{2,1,0:T(4,128)(2,1)S(1)}, u32[]{:S(2)}, u32[]{:S(2)}) collective-permute-start(bf16[8,3,256]{2,1,0:T(4,128)(2,1)S(1)} %get-tuple-element.14), channel_id=1, source_target_pairs={{31,0},{16,1},{17,2},{18,3},{19,4},{20,5},{21,6},{22,7},{23,8},{24... | collective-permute-start | bytes 36872 | tf_op jit(solution)/shard_map/ppermute | solution.py:57
  5.1 2.7 %collective-permute-start.1 = (bf16[8,3,256]{2,1,0:T(4,128)(2,1)S(1)}, bf16[8,3,256]{2,1,0:T(4,128)(2,1)S(1)}, u32[]{:S(2)}, u32[]{:S(2)}) collective-permute-start(bf16[8,3,256]{2,1,0:T(4,128)(2,1)S(1)} %get-tuple-element.13), channel_id=1, source_target_pairs={{1,0},{2,1},{3,2},{4,3},{5,4},{6,5},{7,6},{8,7},{9,8},{10,9},{11,1... | collective-permute-start | bytes 36872 | tf_op jit(solution)/shard_map/ppermute | solution.py:57
  7.8 0.3 collective-permute-start.4
  8.1 0.0 copy-done.2
  8.1 1.8 %collective-permute-start.3 = (bf16[8,16,256]{2,1,0:T(8,128)(2,1)S(1)}, bf16[8,16,256]{2,1,0:T(8,128)(2,1)S(1)}, u32[]{:S(2)}, u32[]{:S(2)}) collective-permute-start(bf16[8,16,256]{2,1,0:T(8,128)(2,1)S(1)} %copy-done.2), channel_id=1, source_target_pairs={{16,0},{17,1},{18,2},{19,3},{20,4},{21,5},{22,6},{23,7},{24,8},{25... | collective-permute-start | bytes 196616 | tf_op jit(solution)/shard_map/ppermute | solution.py:57
  9.9 1.0 %fusion.175 = (f32[1,1,256]{2,1,0:T(1,128)S(1)}, f32[1,1,256]{2,1,0:T(1,128)S(1)}, f32[1,1,256]{2,1,0:T(1,128)S(1)}, f32[1,1,256]{2,1,0:T(1,128)S(1)}, f32[1,1,2...) fusion(bf16[7,7,256]{2,1,0:T(8,128)(2,1)} %param.7), kind=kLoop, calls=%fused_computation.302 | loop fusion | bytes 38912 | tf_op jit(solution)/shard_map/slice | solution.py:87
  10.9 0.0 copy-done.3
  11.1 0.0 collective-permute-done
  11.1 0.0 collective-permute-done.1
  11.1 0.0 collective-permute-done.2
  11.1 0.0 collective-permute-done.4
  11.1 1.3 %collective-permute-done.3 = bf16[8,16,256]{2,1,0:T(8,128)(2,1)S(1)} collective-permute-done((bf16[8,16,256]{2,1,0:T(8,128)(2,1)S(1)}, bf16[8,16,256]{2,1,0:T(8,128)(2,1)S(1)}, u32[]{:S(2)}, u32[]{:S(2)}) %collective-permute-start.3) | collective-permute-done | bytes 65568 | tf_op jit(solution)/shard_map/ppermute | solution.py:57
  12.4 1.1 %fusion.87 = bf16[16,22,256]{2,1,0:T(8,128)(2,1)S(1)} fusion(s32[]{:T(128)S(6)} %select_n.213, bf16[8,3,256]{2,1,0:T(4,128)(2,1)S(1)} %collective-permute-done, bf16[8,16,256]{2,1,0:T(8,128)(2,1)S(1)} %copy-done.2, bf16[8,3,256]{2,1,0:T(4,128)(2,1)S(1)} %collective-permute-done.1, bf16[8,3,256]{2,1,0:T(4,128)(2,1)S(1)} %collective-permute-done.2, ...), kind=kLoop, calls=%fused_computation.174 | loop fusion | flops 2162688 | bytes 360452 | tf_op jit(solution)/shard_map/jit(_roll_dynamic)/concatenate | solution.py:80
  13.6 1.8 %fusion.171 = (f32[16,16]{1,0:T(8,128)S(1)}, f32[16,16,256]{2,1,0:T(8,128)S(1)}) fusion(f32[256]{0:T(256)S(1)} %bitcast.165, f32[22,22,256]{2,1,0:T(8,128)S(1)} %pad_convert_fusion, f32[256]{0:T(256)S(1)} %bitcast.164, f32[256]{0:T(256)S(1)} %bitcast.163, f32[256]{0:T(256)S(1)} %bitcast.162, f32[256]{0:T(256)S(1)} %bitcast.161, f32[256]{0:T(256)S(1)} %bitcast.160, ...), kind=kLoop, calls=%fused_computation.299 | loop fusion | flops 6422272 | bytes 13158400 | tf_op jit(solution)/shard_map/reduce_sum | solution.py:12
  15.3 0.0 copy-start.4
  15.4 0.2 multiply_reduce_fusion
  15.6 0.1 multiply_convert_fusion
  15.7 0.0 copy-done
  15.7 0.7 %copy-done.4 = bf16[256,1024]{1,0:T(8,128)(2,1)S(1)} copy-done((bf16[256,1024]{1,0:T(8,128)(2,1)S(1)}, bf16[256,1024]{1,0:T(8,128)(2,1)}, u32[]{:S(2)}) %copy-start.4) | copy-done | bytes 524312
  16.4 0.0 copy-start.5
  16.4 2.7 %convert_reduce_fusion = (f32[256]{0:T(256)S(1)}, bf16[256,256]{1,0:T(8,128)(2,1)S(1)}) fusion(bf16[1024,256]{1,0:T(8,128)(2,1)S(1)} %copy-done, bf16[256,256]{1,0:T(8,128)(2,1)S(1)} %bitcast.114, bf16[256,256]{1,0:T(8,128)(2,1)S(1)} %bitcast.110, bf16[256,1024]{1,0:T(8,128)(2,1)S(1)} %copy-done.4), kind=kOutput, calls=%fused_computation.58 | convolution fusion | flops 285802240 | bytes 1442816 | tf_op jit(solution)/shard_map/dot_general | solution.py:19
  19.1 0.2 fusion.26
  19.3 0.1 fusion.27
  19.5 0.0 copy-done.5
  19.5 0.2 select_dynamic-update-slice_fusion.7
  19.9 0.5 fusion.178
  20.3 0.2 fusion.15
  20.5 0.5 %convolution_divide_fusion = bf16[1024,256]{1,0:T(8,128)(2,1)S(1)} fusion(bf16[256,256]{1,0:T(8,128)(2,1)S(1)} %fusion.27, f32[1024,256]{0,1:T(8,128)S(1)} %get-tuple-element.69, f32[1024]{0:T(1024)S(1)} %fusion.15, f32[1024]{0:T(1024)S(1)} %get-tuple-element.68, bf16[4,256,256]{2,1,0:T(8,128)(2,1)S(1)} %copy-done.5), kind=kOutput, calls=%fused_computation.1 | convolution fusion | flops 168886272 | bytes 1843200 | tf_op jit(solution)/shard_map/dot_general | solution.py:19
  21.0 0.3 fusion.181
  21.3 0.0 copy-start.1
  21.3 0.2 multiply_reduce_fusion.1
  21.5 0.1 multiply_convert_fusion.1
  21.6 0.6 %broadcast_in_dim.155 = bf16[8,2,16,256]{3,2,1,0:T(8,128)(2,1)} broadcast(bf16[8,16,256]{2,1,0:T(8,128)(2,1)S(1)} %bitcast.107), dimensions={0,2,3} | broadcast | bytes 196608 | tf_op jit(solution)/shard_map/broadcast_in_dim | solution.py:106
  22.3 4.1 %all-to-all-start = ((bf16[16,16,256]{2,1,0:T(8,128)(2,1)}), bf16[16,16,256]{2,1,0:T(8,128)(2,1)S(1)}, u32[]{:S(2)}, u32[]{:S(2)}) async-start(bf16[16,16,256]{2,1,0:T(8,128)(2,1)} %bitcast.56), calls=%async_computation | async-start | bytes 262144 | tf_op jit(solution)/shard_map/all_to_all | solution.py:109
  26.4 0.0 copy-done.1
  26.5 7.8 %all-to-all-done = bf16[16,16,256]{2,1,0:T(8,128)(2,1)S(1)} async-done(((bf16[16,16,256]{2,1,0:T(8,128)(2,1)}), bf16[16,16,256]{2,1,0:T(8,128)(2,1)S(1)}, u32[]{:S(2)}, u32[]{:S(2)}) %all-to-all-start) | async-done | bytes 131104 | tf_op jit(solution)/shard_map/all_to_all | solution.py:109
  34.4 0.2 broadcast_select_fusion.2
  34.5 0.4 fusion.182
  35.0 0.2 fusion.17
  35.1 0.5 %convolution_divide_fusion.1 = bf16[1024,128]{1,0:T(8,128)(2,1)S(1)} fusion(bf16[256,256]{1,0:T(8,128)(2,1)S(1)} %bitcast.113, f32[1024,256]{0,1:T(8,128)S(1)} %get-tuple-element.73, f32[1024]{0:T(1024)S(1)} %get-tuple-element.72, f32[1024]{0:T(1024)S(1)} %fusion.17, bf16[3,256,256]{2,1,0:T(8,128)(2,1)S(1)} %slice.485, s32[]{:T(128)S(6)} %add.338, ...), kind=kOutput, calls=%fused_computation.5 | convolution fusion | flops 84705280 | bytes 1515528 | tf_op jit(solution)/shard_map/dot_general | solution.py:19
  35.7 9.5 %all_to_all.10 = bf16[16,16,128]{2,1,0:T(8,128)(2,1)S(1)} all-to-all(bf16[16,16,128]{2,1,0:T(8,128)(2,1)S(1)} %bitcast.108), channel_id=1, replica_groups=mesh['lat'=2,'lon'=16] {'lon'}, dimensions={0} | all-to-all | bytes 131072 | tf_op jit(solution)/shard_map/all_to_all | solution.py:114
  45.2 0.8 %fusion.4 = bf16[128,256]{1,0:T(8,128)(2,1)} fusion(f32[128,256]{1,0:T(8,128)S(1)} %get-tuple-element.71, bf16[4,256,256]{2,1,0:T(8,128)(2,1)S(1)} %copy-done.1, bf16[128,128]{1,0:T(8,128)(2,1)S(1)} %bitcast.116, bf16[128,128]{1,0:T(8,128)(2,1)S(1)} %bitcast.115), kind=kOutput, calls=%fused_computation.14 | convolution fusion | flops 16973824 | bytes 393216 | tf_op jit(solution)/shard_map/dot_general | solution.py:19
  (28 shorter events, 0.4 us)
Async XLA Ops:
  0.0 15.7 %copy-start = (bf16[1024,256]{1,0:T(8,128)(2,1)S(1)}, bf16[1024,256]{1,0:T(8,128)(2,1)}, u32[]{:S(2)}) copy-start(bf16[1024,256]{1,0:T(8,128)(2,1)} %param.9) | copy-start | bytes 1572868
  0.0 8.1 %copy-start.2 = (bf16[8,16,256]{2,1,0:T(8,128)(2,1)S(1)}, bf16[8,16,256]{2,1,0:T(8,128)(2,1)}, u32[]{:S(2)}) copy-start(bf16[8,16,256]{2,1,0:T(8,128)(2,1)} %param.6) | copy-start | bytes 196612
  0.9 10.0 %copy-start.3 = (bf16[7,7,256]{2,1,0:T(8,128)(2,1)S(1)}, bf16[7,7,256]{2,1,0:T(8,128)(2,1)}, u32[]{:S(2)}) copy-start(bf16[7,7,256]{2,1,0:T(8,128)(2,1)} %param.7) | copy-start | bytes 75268
  0.9 10.2 %collective-permute-start = (bf16[8,3,256]{2,1,0:T(4,128)(2,1)S(1)}, bf16[8,3,256]{2,1,0:T(4,128)(2,1)S(1)}, u32[]{:S(2)}, u32[]{:S(2)}) collective-permute-start(bf16[8,3,256]{2,1,0:T(4,128)(2,1)S(1)} %get-tuple-element.14), channel_id=1, source_target_pairs={{15,0},{0,1},{1,2},{2,3},{3,4},{4,5},{5,6},{6,7},{7,8},{8,9},{9,10... | collective-permute-start | bytes 36872 | tf_op jit(solution)/shard_map/ppermute | solution.py:57
  1.4 9.7 %collective-permute-start.2 = (bf16[8,3,256]{2,1,0:T(4,128)(2,1)S(1)}, bf16[8,3,256]{2,1,0:T(4,128)(2,1)S(1)}, u32[]{:S(2)}, u32[]{:S(2)}) collective-permute-start(bf16[8,3,256]{2,1,0:T(4,128)(2,1)S(1)} %get-tuple-element.14), channel_id=1, source_target_pairs={{31,0},{16,1},{17,2},{18,3},{19,4},{20,5},{21,6},{22,7},{23,8},{24... | collective-permute-start | bytes 36872 | tf_op jit(solution)/shard_map/ppermute | solution.py:57
  5.1 6.0 %collective-permute-start.1 = (bf16[8,3,256]{2,1,0:T(4,128)(2,1)S(1)}, bf16[8,3,256]{2,1,0:T(4,128)(2,1)S(1)}, u32[]{:S(2)}, u32[]{:S(2)}) collective-permute-start(bf16[8,3,256]{2,1,0:T(4,128)(2,1)S(1)} %get-tuple-element.13), channel_id=1, source_target_pairs={{1,0},{2,1},{3,2},{4,3},{5,4},{6,5},{7,6},{8,7},{9,8},{10,9},{11,1... | collective-permute-start | bytes 36872 | tf_op jit(solution)/shard_map/ppermute | solution.py:57
  7.8 3.3 %collective-permute-start.4 = (bf16[8,3,256]{2,1,0:T(4,128)(2,1)S(1)}, bf16[8,3,256]{2,1,0:T(4,128)(2,1)S(1)}, u32[]{:S(2)}, u32[]{:S(2)}) collective-permute-start(bf16[8,3,256]{2,1,0:T(4,128)(2,1)S(1)} %get-tuple-element.13), channel_id=1, source_target_pairs={{17,0},{18,1},{19,2},{20,3},{21,4},{22,5},{23,6},{24,7},{25,8},{26... | collective-permute-start | bytes 36872 | tf_op jit(solution)/shard_map/ppermute | solution.py:57
  8.1 4.3 %collective-permute-start.3 = (bf16[8,16,256]{2,1,0:T(8,128)(2,1)S(1)}, bf16[8,16,256]{2,1,0:T(8,128)(2,1)S(1)}, u32[]{:S(2)}, u32[]{:S(2)}) collective-permute-start(bf16[8,16,256]{2,1,0:T(8,128)(2,1)S(1)} %copy-done.2), channel_id=1, source_target_pairs={{16,0},{17,1},{18,2},{19,3},{20,4},{21,5},{22,6},{23,7},{24,8},{25... | collective-permute-start | bytes 196616 | tf_op jit(solution)/shard_map/ppermute | solution.py:57
  15.3 1.1 %copy-start.4 = (bf16[256,1024]{1,0:T(8,128)(2,1)S(1)}, bf16[256,1024]{1,0:T(8,128)(2,1)}, u32[]{:S(2)}) copy-start(bf16[256,1024]{1,0:T(8,128)(2,1)} %param.8) | copy-start | bytes 1572868
  16.4 3.1 %copy-start.5 = (bf16[4,256,256]{2,1,0:T(8,128)(2,1)S(1)}, bf16[4,256,256]{2,1,0:T(8,128)(2,1)}, u32[]{:S(2)}) copy-start(bf16[4,256,256]{2,1,0:T(8,128)(2,1)} %param.10) | copy-start | bytes 1572868
  21.3 5.1 %copy-start.1 = (bf16[4,256,256]{2,1,0:T(8,128)(2,1)S(1)}, bf16[4,256,256]{2,1,0:T(8,128)(2,1)}, u32[]{:S(2)}) copy-start(bf16[4,256,256]{2,1,0:T(8,128)(2,1)} %param.11) | copy-start | bytes 1572868
  22.3 12.1 %all-to-all-start = ((bf16[16,16,256]{2,1,0:T(8,128)(2,1)}), bf16[16,16,256]{2,1,0:T(8,128)(2,1)S(1)}, u32[]{:S(2)}, u32[]{:S(2)}) async-start(bf16[16,16,256]{2,1,0:T(8,128)(2,1)} %bitcast.56), calls=%async_computation | async-start | bytes 262144 | tf_op jit(solution)/shard_map/all_to_all | solution.py:109

commit v2 on v1

v2 whole, which is shorter than its diff:
```python
import functools

import jax
import jax.numpy as jnp
from jax import lax
from jax.experimental import pallas as pl
from jax.experimental.pallas import tpu as pltpu
from jax.sharding import PartitionSpec as P

HEADS = 8
HALO = 3
STRIP = 8
EPSILON = 1e-06
VMEM_BYTES = 24 * 1024 * 1024


def layer_norm(values):
    average = jnp.mean(values, axis=-1, keepdims=True)
    centered = values - average
    variance = jnp.mean(centered * centered, axis=-1, keepdims=True)
    return centered * lax.rsqrt(variance + EPSILON)


def dot(rows, matrix):
    return jnp.dot(rows, matrix, preferred_element_type=jnp.float32)


def dot_t(rows, matrix):
    return lax.dot_general(
        rows, matrix, (((1,), (1,)), ((), ())), preferred_element_type=jnp.float32
    )


def gelu(values):
    return 0.5 * values * (1.0 + lax.erf(values * 0.5**0.5))


def attend(queries, keys, values, heads, head_size, mask):
    scale = head_size ** (-0.5)
    lane_head = lax.broadcasted_iota(jnp.int32, (1, queries.shape[1]), 1) // head_size
    out = jnp.zeros(queries.shape, jnp.float32)
    for h in range(heads):
        mine = lane_head == h
        scores = dot_t(jnp.where(mine, queries, jnp.zeros_like(queries)), keys) * scale
        if mask is not None:
            scores = jnp.where(mask, scores, -1e30)
        top = jnp.max(scores, axis=-1, keepdims=True)
        probs = jnp.exp(scores - top)
        totals = jnp.sum(probs, axis=-1, keepdims=True)
        mixed = dot(probs.astype(jnp.bfloat16), values) / totals
        out = jnp.where(mine, mixed, out)
    return out.astype(jnp.bfloat16)


def cell_kernel(
    nlat,
    split,
    lat_ref,
    *refs,
):
    pieces = refs[: 3 * nlat]
    dw_ref, expand_ref, reduce_ref, attn_ref = refs[3 * nlat : 3 * nlat + 4]
    two_ref, sent_ref, padded, taps, normed, one, lat_in = refs[3 * nlat + 4 :]
    rows, cols, channels = pieces[1].shape
    cells = rows * cols
    all_rows = rows * nlat
    my_lat = lat_ref[0]
    lanes = 128

    padded[:HALO] = jnp.zeros((HALO,) + padded.shape[1:], jnp.float32)
    padded[HALO + all_rows :] = jnp.zeros((HALO,) + padded.shape[1:], jnp.float32)
    for s in range(nlat):
        source = lax.rem(my_lat + s, nlat)
        place = pl.ds(HALO + source * rows, rows)
        left, middle, right = pieces[3 * s : 3 * s + 3]
        padded[place, :STRIP] = left[...].astype(jnp.float32)
        padded[place, STRIP : STRIP + cols] = middle[...].astype(jnp.float32)
        padded[place, STRIP + cols :] = right[...].astype(jnp.float32)
    taps[...] = dw_ref[...].astype(jnp.float32)

    def conv_block(block, carry):
        start = block * rows
        parts = []
        for c in range(0, channels, lanes):
            acc = jnp.zeros((rows, cols, lanes), jnp.float32)
            for b in range(2 * HALO + 1):
                first = STRIP - HALO + b
                slab = padded[
                    pl.ds(start, rows + 2 * HALO), first : first + cols, c : c + lanes
                ]
                for a in range(2 * HALO + 1):
                    tap = taps[a, b : b + 1, c : c + lanes].reshape(1, 1, lanes)
                    acc = acc + slab[a : a + rows] * tap
            parts.append(acc.reshape(cells, lanes))
        conv = jnp.concatenate(parts, axis=-1)
        normed[pl.ds(pl.multiple_of(block * cells, cells), cells)] = layer_norm(conv).astype(
            jnp.bfloat16
        )
        return carry

    def mlp_block(block, size):
        place = pl.ds(pl.multiple_of(block * size, size), size)
        inputs = normed[place]
        hidden = expand_ref.shape[1]
        total = jnp.zeros((size, channels), jnp.float32)
        for k in range(0, hidden, channels):
            wide = gelu(dot(inputs, expand_ref[:, k : k + channels])).astype(jnp.bfloat16)
            total = total + dot(wide, reduce_ref[k : k + channels])
        lats = size // cols
        center = padded[
            pl.ds(HALO + block * lats, lats), STRIP : STRIP + cols, :
        ].reshape(size, channels)
        block_one = (center + total).astype(jnp.bfloat16)
        one[place] = block_one
        lat_in[place] = layer_norm(block_one.astype(jnp.float32)).astype(jnp.bfloat16)

    if nlat <= 2:
        for block in range(nlat):
            conv_block(block, 0)
        mlp_block(0, nlat * cells)
    else:
        lax.fori_loop(0, nlat, conv_block, 0)

        def mlp_step(block, carry):
            mlp_block(block, cells)
            return carry

        lax.fori_loop(0, nlat, mlp_step, 0)

    own = pl.ds(pl.multiple_of(my_lat * cells, cells), cells)
    every = lat_in[...]
    queries = dot(lat_in[own], attn_ref[0]).astype(jnp.bfloat16)
    keys = dot(every, attn_ref[1]).astype(jnp.bfloat16)
    values = dot(every, attn_ref[2]).astype(jnp.bfloat16)
    row_col = lax.broadcasted_iota(jnp.int32, (cells, 1), 0) % cols
    key_col = lax.broadcasted_iota(jnp.int32, (1, all_rows * cols), 1) % cols
    mix = attend(queries, keys, values, HEADS, channels // HEADS, row_col == key_col)
    block_two = (one[own].astype(jnp.float32) + dot(mix, attn_ref[3])).astype(jnp.bfloat16)
    two_ref[...] = block_two
    lon_in = layer_norm(block_two.astype(jnp.float32)).astype(jnp.bfloat16)
    lon_in = lon_in.reshape(rows, cols, channels)
    for s in range(split):
        for r in range(rows):
            sent_ref[r * split + s] = lon_in[r]


def circle_kernel(group, head_size, circle_ref, weights_ref, mix_ref):
    circle = circle_ref[...]
    queries = dot(circle, weights_ref[0]).astype(jnp.bfloat16)
    keys = dot(circle, weights_ref[1]).astype(jnp.bfloat16)
    values = dot(circle, weights_ref[2]).astype(jnp.bfloat16)
    mix_ref[...] = attend(queries, keys, values, group, head_size, None)


def last_kernel(split, back_ref, two_ref, weight_ref, out_ref):
    rows, cols = out_ref.shape[:2]
    width = back_ref.shape[-1]
    total = two_ref[...].astype(jnp.float32)
    for s in range(split):
        part = jnp.concatenate([back_ref[r * split + s] for r in range(rows)], axis=0)
        total = total + dot(part, weight_ref[s * width : (s + 1) * width])
    out_ref[...] = total.astype(jnp.bfloat16).reshape(out_ref.shape)


def call(kernel, out_shape, count, scratch=(), prefetch=0):
    smem = [pl.BlockSpec(memory_space=pltpu.SMEM)] * prefetch
    vmem = pl.BlockSpec(memory_space=pltpu.VMEM)
    return pl.pallas_call(
        kernel,
        out_shape=out_shape,
        in_specs=smem + [vmem] * count,
        out_specs=jax.tree.map(lambda _: vmem, out_shape),
        scratch_shapes=list(scratch),
        compiler_params=pltpu.CompilerParams(vmem_limit_bytes=VMEM_BYTES),
    )


def gather_windows(field):
    nlat, nlon = lax.axis_size("lat"), lax.axis_size("lon")
    cols = field.shape[1]

    def shift(piece, dlat, dlon):
        pairs = [
            (((i + dlat) % nlat) * nlon + (j + dlon) % nlon, i * nlon + j)
            for i in range(nlat)
            for j in range(nlon)
        ]
        return lax.ppermute(piece, ("lat", "lon"), pairs)

    first, last = field[:, :STRIP], field[:, cols - STRIP :]
    pieces = []
    for s in range(nlat):
        middle = field if s == 0 else shift(field, s, 0)
        pieces += [shift(last, s, -1), middle, shift(first, s, 1)]
    return pieces


def shards(field, dw_weight, w_expand, w_reduce, lat_attn, lon_attn):
    rows, cols, channels = field.shape
    head_size = channels // HEADS
    nlat, nlon = lax.axis_size("lat"), lax.axis_size("lon")
    my_lat, my_lon = lax.axis_index("lat"), lax.axis_index("lon")
    split = nlon // rows
    group = HEADS // split
    width = group * head_size
    cells = rows * cols
    all_rows = rows * nlat
    lon_qkv = lax.dynamic_slice_in_dim(lon_attn[:3], (my_lon % split) * width, width, 2)

    pieces = gather_windows(field)
    bf16, f32 = jnp.bfloat16, jnp.float32
    block_two, sent = call(
        functools.partial(cell_kernel, nlat, split),
        (
            jax.ShapeDtypeStruct((cells, channels), bf16),
            jax.ShapeDtypeStruct((rows * split, cols, channels), bf16),
        ),
        len(pieces) + 4,
        [
            pltpu.VMEM((all_rows + 2 * HALO, cols + 2 * STRIP, channels), f32),
            pltpu.VMEM(dw_weight.shape, f32),
            pltpu.VMEM((all_rows * cols, channels), bf16),
            pltpu.VMEM((all_rows * cols, channels), bf16),
            pltpu.VMEM((all_rows * cols, channels), bf16),
        ],
        prefetch=1,
    )(my_lat.astype(jnp.int32).reshape(1), *pieces, dw_weight, w_expand, w_reduce, lat_attn)

    circle = lax.all_to_all(sent, "lon", 0, 0, tiled=True).reshape(nlon * cols, channels)
    lon_mix = call(
        functools.partial(circle_kernel, group, head_size),
        jax.ShapeDtypeStruct((nlon * cols, width), bf16),
        2,
    )(circle, lon_qkv)
    back = lax.all_to_all(lon_mix.reshape(nlon, cols, width), "lon", 0, 0, tiled=True)
    return call(
        functools.partial(last_kernel, split),
        jax.ShapeDtypeStruct((rows, cols, channels), bf16),
        3,
    )(back, block_two, lon_attn[3])


def solution(mesh):
    return jax.shard_map(
        shards,
        mesh=mesh,
        in_specs=(P("lat", "lon", None), P(), P(), P(), P(), P()),
        out_specs=P("lat", "lon", None),
        check_vma=False,
    )
```

time: 46.3 us -> 50.8 us (1.097)
  blocking collectives: 9.48 us -> 0 us
  Pallas kernels: 0 us -> 8.41 us
  starting transfers between devices: 13.2 us -> 21.5 us
  waiting for transfers between devices: 9.19 us -> 15.3 us
  matrix products: 6.06 us -> 0 us
  other arithmetic: 4.38 us -> 0 us
  local copies, waits for them, and re-layouts: 3.31 us -> 4.95 us
    all_to_all x1 -> x0, blocking collectives: 9.48 us -> none  [shards(): lax.all_to_all(lon_mix.reshape(nlon, cols, group_channels), 'lon', 0, 0,...]
    pallas_call x0 -> x3, Pallas kernels: none -> 8.41 us  [the longest x1 6.12 us: shards(): call(functools.partial(cell_kernel, nlat, split), (jax.ShapeDtypeStruct((...]
    all_to_all x0 -> x1, waiting for transfers between devices: none -> 6.83 us  [shards(): lax.all_to_all(lon_mix.reshape(nlon, cols, width), 'lon', 0, 0, tiled=True)]
    dot_general x9 -> x0, matrix products: 6.06 us -> none  [the longest x7 5.17 us: dot(): return jnp.dot(rows, matrix, preferred_element_type=jnp.float32)]
    ppermute x5, starting transfers between devices: 9.01 us -> 12.7 us  [shift(): return lax.ppermute(piece, ('lat', 'lon'), pairs)]
    all_to_all x0 -> x1, starting transfers between devices: none -> 3.5 us  [shards(): lax.all_to_all(lon_mix.reshape(nlon, cols, width), 'lon', 0, 0, tiled=True)]
    reduce_sum x6 -> x0, other arithmetic: 2.67 us -> none  [the longest x1 1.75 us: layer_norm(): average = jnp.mean(values, axis=-1, keepdims=True)]
    unnamed x12, local copies, waits for them, and re-layouts: 0.7 us -> 3.13 us
  transfers between devices with their start and end apart: 6 -> 7, of which waited for: 2 -> 3; matrix products, arithmetic and copies ran while one was open for 2% -> 2% of each run, Pallas kernels for 0% -> 0%
where the time goes in v2:
time: 50.8 us; the launch traced here: 50.3 us
  starting transfers between devices  21.5 us (42%)
  waiting for transfers between devices  15.3 us (30%)
  Pallas kernels  8.41 us (17%)
  local copies, waits for them, and re-layouts  4.95 us (10%)
    ppermute x5, starting transfers between devices, shift(): return lax.ppermute(piece, ('lat', 'lon'), pairs)  12.7 us
    all_to_all x1, waiting for transfers between devices, shards(): lax.all_to_all(sent, 'lon', 0, 0, tiled=True).reshape(nlon * cols, channels)  6.88 us
    all_to_all x1, waiting for transfers between devices, shards(): lax.all_to_all(lon_mix.reshape(nlon, cols, width), 'lon', 0, 0, tiled=True)  6.83 us
    pallas_call x1, Pallas kernels, shards(): call(functools.partial(cell_kernel, nlat, split), (jax.ShapeDtypeStruct((...  6.12 us
    all_to_all x1, starting transfers between devices, shards(): lax.all_to_all(sent, 'lon', 0, 0, tiled=True).reshape(nlon * cols, channels)  5.33 us
    all_to_all x1, starting transfers between devices, shards(): lax.all_to_all(lon_mix.reshape(nlon, cols, width), 'lon', 0, 0, tiled=True)  3.5 us
    unnamed x12, local copies, waits for them, and re-layouts  3.13 us
    ppermute x5, waiting for transfers between devices, shift(): return lax.ppermute(piece, ('lat', 'lon'), pairs)  1.6 us
  transfers between devices with their start and end apart: 7, of which 3 were waited for; matrix products, arithmetic and copies ran while one was open for 2% of the time, Pallas kernels for 0%

profile of v2, /device:TPU:0, one launch (start us, length us, event | category | flops | bytes accessed | tf_op | source)
XLA Modules:
  0.0 50.3 jit_solution(15203192576434883968)
XLA Ops:
  0.0 0.0 copy-start.3
  0.0 2.9 %collective-permute-start.3 = (bf16[8,16,256]{2,1,0:T(8,128)(2,1)}, bf16[8,16,256]{2,1,0:T(8,128)(2,1)S(1)}, u32[]{:S(2)}, u32[]{:S(2)}) collective-permute-start(bf16[8,16,256]{2,1,0:T(8,128)(2,1)} %refs_1_.1), channel_id=1, source_target_pairs={{16,0},{17,1},{18,2},{19,3},{20,4},{21,5},{22,6},{23,7},{24,8},{25... | collective-permute-start | bytes 196616 | tf_op jit(solution)/shard_map/ppermute | solution.py:188
  2.9 0.0 copy-start.4
  2.9 0.8 %fusion = (bf16[8,8,256]{2,1,0:T(8,128)(2,1)S(1)}, bf16[8,8,256]{2,1,0:T(8,128)(2,1)S(1)}) fusion(bf16[8,16,256]{2,1,0:T(8,128)(2,1)} %refs_1_.1), kind=kLoop, calls=%fused_computation.2 | loop fusion | bytes 131072 | tf_op jit(solution)/shard_map/slice | solution.py:190
  3.7 0.0 collective-permute-start
  3.7 4.4 %collective-permute-start.1 = (bf16[8,8,256]{2,1,0:T(8,128)(2,1)S(1)}, bf16[8,8,256]{2,1,0:T(8,128)(2,1)S(1)}, u32[]{:S(2)}, u32[]{:S(2)}) collective-permute-start(bf16[8,8,256]{2,1,0:T(8,128)(2,1)S(1)} %get-tuple-element.9), channel_id=1, source_target_pairs={{1,0},{2,1},{3,2},{4,3},{5,4},{6,5},{7,6},{8,7},{9,8},{10,9},{11,1... | collective-permute-start | bytes 98312 | tf_op jit(solution)/shard_map/ppermute | solution.py:188
  8.2 0.0 collective-permute-start.2
  8.2 5.3 %collective-permute-start.4 = (bf16[8,8,256]{2,1,0:T(8,128)(2,1)S(1)}, bf16[8,8,256]{2,1,0:T(8,128)(2,1)S(1)}, u32[]{:S(2)}, u32[]{:S(2)}) collective-permute-start(bf16[8,8,256]{2,1,0:T(8,128)(2,1)S(1)} %get-tuple-element.9), channel_id=1, source_target_pairs={{17,0},{18,1},{19,2},{20,3},{21,4},{22,5},{23,6},{24,7},{25,8},{26... | collective-permute-start | bytes 98312 | tf_op jit(solution)/shard_map/ppermute | solution.py:188
  13.5 0.0 collective-permute-done.refs_0_
  13.5 0.0 collective-permute-done.1.refs_2_
  13.5 1.6 %collective-permute-done.2.refs_3_ = bf16[8,8,256]{2,1,0:T(8,128)(2,1)S(1)} collective-permute-done((bf16[8,8,256]{2,1,0:T(8,128)(2,1)S(1)}, bf16[8,8,256]{2,1,0:T(8,128)(2,1)S(1)}, u32[]{:S(2)}, u32[]{:S(2)}) %collective-permute-start.2) | collective-permute-done | bytes 32800 | tf_op jit(solution)/shard_map/ppermute | solution.py:188
  15.1 0.0 collective-permute-done.4.refs_5_
  15.1 0.0 collective-permute-done.3.refs_4_
  15.1 0.0 copy-done.3
  15.1 0.0 copy-done.4
  15.1 0.0 copy-start
  15.2 1.0 %copy-done = bf16[256,1024]{1,0:T(8,128)(2,1)S(1)} copy-done((bf16[256,1024]{1,0:T(8,128)(2,1)S(1)}, bf16[256,1024]{1,0:T(8,128)(2,1)}, u32[]{:S(2)}) %copy-start) | copy-done | bytes 524312
  16.2 0.0 copy-start.1
  16.2 1.0 %copy-done.1 = bf16[1024,256]{1,0:T(8,128)(2,1)S(1)} copy-done((bf16[1024,256]{1,0:T(8,128)(2,1)S(1)}, bf16[1024,256]{1,0:T(8,128)(2,1)}, u32[]{:S(2)}) %copy-start.1) | copy-done | bytes 524312
  17.2 0.0 copy-start.2
  17.2 1.0 %copy-done.2 = bf16[4,256,256]{2,1,0:T(8,128)(2,1)S(1)} copy-done((bf16[4,256,256]{2,1,0:T(8,128)(2,1)S(1)}, bf16[4,256,256]{2,1,0:T(8,128)(2,1)}, u32[]{:S(2)}) %copy-start.2) | copy-done | bytes 524312
  18.3 6.1 %shard_map.64 = (bf16[128,256]{1,0:T(8,128)(2,1)S(1)}, bf16[16,16,256]{2,1,0:T(8,128)(2,1)}) custom-call(s32[1]{0:T(128)} %bitcast.lat_ref, bf16[8,8,256]{2,1,0:T(8,128)(2,1)S(1)} %collective-permute-done.refs_0_, bf16[8,16,256]{2,1,0:T(8,128)(2,1)S(1)} %copy-done.3, bf16[8,8,256]{2,1,0:T(8,128)(2,1)S(1)} %collective-permute-done.1.refs_2_, ...), custom_call_target="tpu_custom_call" | custom-call | tf_op jit(solution)/shard_map/pallas_call | solution.py:212
  24.4 5.3 %all-to-all-start = ((bf16[16,16,256]{2,1,0:T(8,128)(2,1)}), bf16[16,16,256]{2,1,0:T(8,128)(2,1)S(1)}, u32[]{:S(2)}, u32[]{:S(2)}) async-start(bf16[16,16,256]{2,1,0:T(8,128)(2,1)} %get-tuple-element.7), calls=%async_computation | async-start | bytes 262144 | tf_op jit(solution)/shard_map/all_to_all | solution.py:229
  29.7 0.0 slice-start
  29.8 0.0 copy-start.5
  29.8 1.0 %slice-done = bf16[3,256,256]{2,1,0:T(8,128)(2,1)S(1)} async-done(((bf16[4,256,256]{2,1,0:T(8,128)(2,1)}), bf16[3,256,256]{2,1,0:T(8,128)(2,1)S(1)}, s32[]{:S(2)}) %slice-start) | async-done | bytes 393240 | tf_op jit(solution)/shard_map/slice | solution.py:208
  30.8 6.9 %all-to-all-done = bf16[16,16,256]{2,1,0:T(8,128)(2,1)S(1)} async-done(((bf16[16,16,256]{2,1,0:T(8,128)(2,1)}), bf16[16,16,256]{2,1,0:T(8,128)(2,1)S(1)}, u32[]{:S(2)}, u32[]{:S(2)}) %all-to-all-start) | async-done | bytes 131104 | tf_op jit(solution)/shard_map/all_to_all | solution.py:229
  37.7 1.5 %shard_map.65 = bf16[256,128]{1,0:T(8,128)(2,1)} custom-call(bf16[256,256]{1,0:T(8,128)(2,1)S(1)} %bitcast.5, bf16[3,256,128]{2,1,0:T(8,128)(2,1)S(1)} %constant_dynamic-slice_fusion.weights_ref), custom_call_target="tpu_custom_call" | custom-call | tf_op jit(solution)/shard_map/pallas_call | solution.py:230
  39.1 3.5 %all-to-all-start.1 = ((bf16[16,16,128]{2,1,0:T(8,128)(2,1)}), bf16[16,16,128]{2,1,0:T(8,128)(2,1)S(1)}, u32[]{:S(2)}, u32[]{:S(2)}) async-start(bf16[16,16,128]{2,1,0:T(8,128)(2,1)} %bitcast.2), calls=%async_computation.1 | async-start | bytes 131072 | tf_op jit(solution)/shard_map/all_to_all | solution.py:235
  42.7 0.0 copy-done.5
  42.7 6.8 %all-to-all-done.1.back_ref = bf16[16,16,128]{2,1,0:T(8,128)(2,1)S(1)} async-done(((bf16[16,16,128]{2,1,0:T(8,128)(2,1)}), bf16[16,16,128]{2,1,0:T(8,128)(2,1)S(1)}, u32[]{:S(2)}, u32[]{:S(2)}) %all-to-all-start.1) | async-done | bytes 65568 | tf_op jit(solution)/shard_map/all_to_all | solution.py:235
  49.5 0.8 %shard_map.66 = bf16[8,16,256]{2,1,0:T(8,128)(2,1)} custom-call(bf16[16,16,128]{2,1,0:T(8,128)(2,1)S(1)} %all-to-all-done.1.back_ref, bf16[128,256]{1,0:T(8,128)(2,1)S(1)} %get-tuple-element.8.two_ref, bf16[256,256]{1,0:T(8,128)(2,1)S(1)} %slice_bitcast_fusion.weight_ref), custom_call_target="tpu_custom_call" | custom-call | tf_op jit(solution)/shard_map/pallas_call | solution.py:236
  (2 shorter events, 0.0 us)
Async XLA Ops:
  0.0 15.1 %copy-start.3 = (bf16[8,16,256]{2,1,0:T(8,128)(2,1)S(1)}, bf16[8,16,256]{2,1,0:T(8,128)(2,1)}, u32[]{:S(2)}) copy-start(bf16[8,16,256]{2,1,0:T(8,128)(2,1)} %refs_1_.1) | copy-start | bytes 196612
  0.0 15.1 %collective-permute-start.3 = (bf16[8,16,256]{2,1,0:T(8,128)(2,1)}, bf16[8,16,256]{2,1,0:T(8,128)(2,1)S(1)}, u32[]{:S(2)}, u32[]{:S(2)}) collective-permute-start(bf16[8,16,256]{2,1,0:T(8,128)(2,1)} %refs_1_.1), channel_id=1, source_target_pairs={{16,0},{17,1},{18,2},{19,3},{20,4},{21,5},{22,6},{23,7},{24,8},{25... | collective-permute-start | bytes 196616 | tf_op jit(solution)/shard_map/ppermute | solution.py:188
  2.9 12.2 %copy-start.4 = (bf16[7,7,256]{2,1,0:T(8,128)(2,1)S(1)}, bf16[7,7,256]{2,1,0:T(8,128)(2,1)}, u32[]{:S(2)}) copy-start(bf16[7,7,256]{2,1,0:T(8,128)(2,1)} %refs_6_.1) | copy-start | bytes 75268
  3.7 9.8 %collective-permute-start = (bf16[8,8,256]{2,1,0:T(8,128)(2,1)S(1)}, bf16[8,8,256]{2,1,0:T(8,128)(2,1)S(1)}, u32[]{:S(2)}, u32[]{:S(2)}) collective-permute-start(bf16[8,8,256]{2,1,0:T(8,128)(2,1)S(1)} %get-tuple-element.10), channel_id=1, source_target_pairs={{15,0},{0,1},{1,2},{2,3},{3,4},{4,5},{5,6},{6,7},{7,8},{8,9},{9,10... | collective-permute-start | bytes 98312 | tf_op jit(solution)/shard_map/ppermute | solution.py:188
  3.7 9.8 %collective-permute-start.1 = (bf16[8,8,256]{2,1,0:T(8,128)(2,1)S(1)}, bf16[8,8,256]{2,1,0:T(8,128)(2,1)S(1)}, u32[]{:S(2)}, u32[]{:S(2)}) collective-permute-start(bf16[8,8,256]{2,1,0:T(8,128)(2,1)S(1)} %get-tuple-element.9), channel_id=1, source_target_pairs={{1,0},{2,1},{3,2},{4,3},{5,4},{6,5},{7,6},{8,7},{9,8},{10,9},{11,1... | collective-permute-start | bytes 98312 | tf_op jit(solution)/shard_map/ppermute | solution.py:188
  8.2 6.9 %collective-permute-start.2 = (bf16[8,8,256]{2,1,0:T(8,128)(2,1)S(1)}, bf16[8,8,256]{2,1,0:T(8,128)(2,1)S(1)}, u32[]{:S(2)}, u32[]{:S(2)}) collective-permute-start(bf16[8,8,256]{2,1,0:T(8,128)(2,1)S(1)} %get-tuple-element.10), channel_id=1, source_target_pairs={{31,0},{16,1},{17,2},{18,3},{19,4},{20,5},{21,6},{22,7},{23,8},{24... | collective-permute-start | bytes 98312 | tf_op jit(solution)/shard_map/ppermute | solution.py:188
  8.2 6.9 %collective-permute-start.4 = (bf16[8,8,256]{2,1,0:T(8,128)(2,1)S(1)}, bf16[8,8,256]{2,1,0:T(8,128)(2,1)S(1)}, u32[]{:S(2)}, u32[]{:S(2)}) collective-permute-start(bf16[8,8,256]{2,1,0:T(8,128)(2,1)S(1)} %get-tuple-element.9), channel_id=1, source_target_pairs={{17,0},{18,1},{19,2},{20,3},{21,4},{22,5},{23,6},{24,7},{25,8},{26... | collective-permute-start | bytes 98312 | tf_op jit(solution)/shard_map/ppermute | solution.py:188
  15.1 1.0 %copy-start = (bf16[256,1024]{1,0:T(8,128)(2,1)S(1)}, bf16[256,1024]{1,0:T(8,128)(2,1)}, u32[]{:S(2)}) copy-start(bf16[256,1024]{1,0:T(8,128)(2,1)} %refs_7_.1) | copy-start | bytes 1572868
  16.2 1.0 %copy-start.1 = (bf16[1024,256]{1,0:T(8,128)(2,1)S(1)}, bf16[1024,256]{1,0:T(8,128)(2,1)}, u32[]{:S(2)}) copy-start(bf16[1024,256]{1,0:T(8,128)(2,1)} %refs_8_.1) | copy-start | bytes 1572868
  17.2 1.0 %copy-start.2 = (bf16[4,256,256]{2,1,0:T(8,128)(2,1)S(1)}, bf16[4,256,256]{2,1,0:T(8,128)(2,1)}, u32[]{:S(2)}) copy-start(bf16[4,256,256]{2,1,0:T(8,128)(2,1)} %refs_9_.1) | copy-start | bytes 1572868
  24.4 13.3 %all-to-all-start = ((bf16[16,16,256]{2,1,0:T(8,128)(2,1)}), bf16[16,16,256]{2,1,0:T(8,128)(2,1)S(1)}, u32[]{:S(2)}, u32[]{:S(2)}) async-start(bf16[16,16,256]{2,1,0:T(8,128)(2,1)} %get-tuple-element.7), calls=%async_computation | async-start | bytes 262144 | tf_op jit(solution)/shard_map/all_to_all | solution.py:229
  29.7 1.0 %slice-start = ((bf16[4,256,256]{2,1,0:T(8,128)(2,1)}), bf16[3,256,256]{2,1,0:T(8,128)(2,1)S(1)}, s32[]{:S(2)}) async-start(bf16[4,256,256]{2,1,0:T(8,128)(2,1)} %param.11), calls=%async_computation.2 | async-start | bytes 786432 | tf_op jit(solution)/shard_map/slice | solution.py:208
  29.8 12.9 %copy-start.5 = (bf16[4,256,256]{2,1,0:T(8,128)(2,1)S(1)}, bf16[4,256,256]{2,1,0:T(8,128)(2,1)}, u32[]{:S(2)}) copy-start(bf16[4,256,256]{2,1,0:T(8,128)(2,1)} %param.11) | copy-start | bytes 1572868
  39.1 10.4 %all-to-all-start.1 = ((bf16[16,16,128]{2,1,0:T(8,128)(2,1)}), bf16[16,16,128]{2,1,0:T(8,128)(2,1)S(1)}, u32[]{:S(2)}, u32[]{:S(2)}) async-start(bf16[16,16,128]{2,1,0:T(8,128)(2,1)} %bitcast.2), calls=%async_computation.1 | async-start | bytes 131072 | tf_op jit(solution)/shard_map/all_to_all | solution.py:235

commit v3 on v1

v3 whole, which is shorter than its diff:
```python
import functools

import jax
import jax.numpy as jnp
from jax import lax
from jax.experimental import pallas as pl
from jax.experimental.pallas import tpu as pltpu
from jax.sharding import PartitionSpec as P

HEADS = 8
HALO = 3
TAPS = 2 * HALO + 1
STRIP = 8
SIDE = 4
LANES = 128
EPSILON = 1e-06
VMEM_BYTES = 24 * 1024 * 1024
STAGE_BYTES = 103 * 512 * 1024
bf16, f32 = jnp.bfloat16, jnp.float32


def layer_norm(values):
    average = jnp.mean(values, axis=-1, keepdims=True)
    centered = values - average
    variance = jnp.mean(centered * centered, axis=-1, keepdims=True)
    return centered * lax.rsqrt(variance + EPSILON)


def dot(rows, matrix):
    return jnp.dot(rows, matrix, preferred_element_type=f32)


def dot_t(rows, matrix):
    return lax.dot_general(rows, matrix, (((1,), (1,)), ((), ())), preferred_element_type=f32)


def gelu(values):
    return 0.5 * values * (1.0 + lax.erf(values * 0.5**0.5))


def attend(queries, keys, values, mask):
    head_size = queries.shape[1] // HEADS
    scale = head_size ** (-0.5)
    lane_head = lax.broadcasted_iota(jnp.int32, (1, queries.shape[1]), 1) // head_size
    out = jnp.zeros(queries.shape, f32)
    for h in range(HEADS):
        mine = lane_head == h
        scores = dot_t(jnp.where(mine, queries, jnp.zeros_like(queries)), keys) * scale
        if mask is not None:
            scores = jnp.where(mask, scores, -1e30)
        top = jnp.max(scores, axis=-1, keepdims=True)
        probs = jnp.exp(scores - top)
        totals = jnp.sum(probs, axis=-1, keepdims=True)
        mixed = dot(probs.astype(bf16), values) / totals
        out = jnp.where(mine, mixed, out)
    return out.astype(bf16)


def stage_kernel(*refs):
    count = (len(refs) - 1) // 2
    sems = refs[-1]
    copies = []
    for i in range(count):
        source, target = refs[i], refs[count + i]
        pieces = sems.shape[1]
        size = source.shape[0] // pieces
        for k in range(pieces):
            part = pl.ds(k * size, size)
            copies.append(pltpu.make_async_copy(source.at[part], target.at[part], sems.at[i, k]))
    for copy in copies:
        copy.start()
    for copy in copies:
        copy.wait()


def strip_kernel(nlat, place_ref, *refs):
    tiles = refs[:nlat]
    whole_ref, near_ref, far_ref, whole = refs[nlat + 1 :]
    rows, cols, channels = tiles[0].shape
    for s in range(nlat):
        source = lax.rem(place_ref[0] + s, nlat)
        whole[pl.ds(source * rows, rows)] = tiles[s][...].astype(f32)
    values = whole[...]
    whole_ref[...] = values.astype(bf16)
    first, last = values[:, :STRIP], values[:, cols - STRIP :]
    even = place_ref[1] == 0
    near_ref[...] = jnp.where(even, last, first).reshape(near_ref.shape).astype(bf16)
    far_ref[...] = jnp.where(even, first, last).reshape(far_ref.shape).astype(bf16)


def chain(my_lat, slab, shape, dw_ref, expand_ref, reduce_ref, attn_ref, center, scratch):
    taps, one, lat_in = scratch
    rows, all_rows, columns, channels = shape
    cells = all_rows * columns
    taps[...] = dw_ref[...].astype(f32)
    parts = []
    for c in range(0, channels, LANES):
        acc = jnp.zeros((all_rows, columns, LANES), f32)
        for b in range(TAPS):
            block = slab(b, c)
            for a in range(TAPS):
                tap = taps[a, b : b + 1, c : c + LANES].reshape(1, 1, LANES)
                acc = acc + block[a : a + all_rows] * tap
        parts.append(acc.reshape(cells, LANES))
    normed = layer_norm(jnp.concatenate(parts, axis=-1)).astype(bf16)
    total = center.reshape(cells, channels)
    for k in range(0, expand_ref.shape[1], channels):
        wide = gelu(dot(normed, expand_ref[:, k : k + channels])).astype(bf16)
        total = total + dot(wide, reduce_ref[k : k + channels])
    block_one = total.astype(bf16)
    one[...] = block_one
    every = layer_norm(block_one.astype(f32)).astype(bf16)
    lat_in[...] = every
    count = rows * columns
    own = pl.ds(pl.multiple_of(my_lat * count, count), count)
    queries = dot(lat_in[own], attn_ref[0]).astype(bf16)
    keys = dot(every, attn_ref[1]).astype(bf16)
    values = dot(every, attn_ref[2]).astype(bf16)
    row_col = lax.broadcasted_iota(jnp.int32, (count, 1), 0) % columns
    key_col = lax.broadcasted_iota(jnp.int32, (1, cells), 1) % columns
    mix = attend(queries, keys, values, row_col == key_col)
    block_two = (one[own].astype(f32) + dot(mix, attn_ref[3])).astype(bf16)
    return block_two, layer_norm(block_two.astype(f32))


def fill(padded, all_rows, first, values):
    width = values.shape[1]
    padded[HALO : HALO + all_rows, first : first + width] = values


def clear(padded, all_rows):
    edge = jnp.zeros((HALO,) + padded.shape[1:], f32)
    padded[:HALO] = edge
    padded[HALO + all_rows :] = edge


def inner_kernel(
    rows, place_ref, whole_ref, dw_ref, expand_ref, reduce_ref, attn_ref,
    two_ref, in_ref, padded, *scratch
):
    all_rows, cols, channels = whole_ref.shape
    columns = cols - 2 * SIDE
    clear(padded, all_rows)
    fill(padded, all_rows, 0, whole_ref[...].astype(f32))

    def slab(b, c):
        first = SIDE - HALO + b
        return padded[:, first : first + columns, c : c + LANES]

    center = padded[HALO : HALO + all_rows, SIDE : SIDE + columns]
    shape = (rows, all_rows, columns, channels)
    block_two, lon_in = chain(
        place_ref[0], slab, shape, dw_ref, expand_ref, reduce_ref, attn_ref, center, scratch
    )
    two_ref[...] = block_two
    in_ref[...] = lon_in.astype(bf16)


def outer_kernel(
    rows, place_ref, whole_ref, near_ref, far_ref, inner_in_ref,
    dw_ref, expand_ref, reduce_ref, attn_ref,
    two_ref, sent_ref, padded, *scratch
):
    all_rows, cols, channels = whole_ref.shape
    columns = 2 * SIDE
    strip_shape = (all_rows, STRIP, channels)
    near = near_ref[...].astype(f32).reshape(strip_shape)
    far = far_ref[...].astype(f32).reshape(strip_shape)
    even = place_ref[1] == 0
    clear(padded, all_rows)
    fill(padded, all_rows, 0, jnp.where(even, far, near))
    fill(padded, all_rows, STRIP, whole_ref[...].astype(f32))
    fill(padded, all_rows, STRIP + cols, jnp.where(even, near, far))
    sublane = lax.broadcasted_iota(jnp.int32, (1, columns, 1), 1)

    def halves(shift, rows_of, c, width):
        right = STRIP + cols - SIDE + shift
        left = STRIP - SIDE + shift
        return jnp.where(
            sublane < SIDE,
            padded[rows_of, right : right + columns, c : c + width],
            padded[rows_of, left : left + columns, c : c + width],
        )

    def slab(b, c):
        return halves(b - HALO, slice(None), c, LANES)

    center = halves(0, slice(HALO, HALO + all_rows), 0, channels)
    shape = (rows, all_rows, columns, channels)
    block_two, lon_in = chain(
        place_ref[0], slab, shape, dw_ref, expand_ref, reduce_ref, attn_ref, center, scratch
    )
    two_ref[...] = block_two
    inner = inner_in_ref[...].astype(f32).reshape(rows, cols - columns, channels)
    outer = lon_in.reshape(rows, columns, channels)
    sent_ref[...] = jnp.concatenate([inner, outer], axis=1).astype(bf16)


def circle_kernel(count, *refs):
    parts = refs[:count]
    attn_ref, mix_ref = refs[count:]
    circle = jnp.concatenate([part[...] for part in parts], axis=0)
    queries = dot(parts[0][...], attn_ref[0]).astype(bf16)
    keys = dot(circle, attn_ref[1]).astype(bf16)
    values = dot(circle, attn_ref[2]).astype(bf16)
    mix_ref[...] = attend(queries, keys, values, None)


def last_kernel(back_ref, inner_ref, outer_ref, attn_ref, out_ref):
    rows, cols, channels = out_ref.shape
    columns = 2 * SIDE
    change = dot(back_ref[...], attn_ref[3]).reshape(rows, cols, channels)
    inner = inner_ref[...].astype(f32).reshape(rows, cols - columns, channels)
    outer = outer_ref[...].astype(f32).reshape(rows, columns, channels)
    inner = inner + change[:, : cols - columns]
    outer = outer + change[:, cols - columns :]
    total = jnp.concatenate([outer[:, SIDE:], inner, outer[:, :SIDE]], axis=1)
    out_ref[...] = total.astype(bf16)


def call(
    kernel, outs, operands, scratch=(), any_space=False, prefetch=0, flops=0, grant=VMEM_BYTES
):
    vmem = pl.BlockSpec(memory_space=pltpu.VMEM)
    given = pl.BlockSpec(memory_space=pl.ANY) if any_space else vmem
    smem = pl.BlockSpec(memory_space=pltpu.SMEM)
    shapes = [jax.ShapeDtypeStruct(shape, bf16) for shape in outs]
    moved = sum(x.size * x.dtype.itemsize for x in operands)
    result = pl.pallas_call(
        kernel,
        out_shape=shapes,
        in_specs=[smem] * prefetch + [given] * (len(operands) - prefetch),
        out_specs=[vmem] * len(outs),
        scratch_shapes=list(scratch),
        compiler_params=pltpu.CompilerParams(vmem_limit_bytes=grant),
        cost_estimate=pl.CostEstimate(flops=flops, bytes_accessed=moved, transcendentals=0),
    )(*operands)
    return result


def shards(field, dw_weight, w_expand, w_reduce, lat_attn, lon_attn):
    rows, cols, channels = field.shape
    nlat, nlon = lax.axis_size("lat"), lax.axis_size("lon")
    my_lat, my_lon = lax.axis_index("lat"), lax.axis_index("lon")
    split = nlon // rows
    all_rows = rows * nlat
    columns = 2 * SIDE
    place = jnp.stack([my_lat, my_lon % 2]).astype(jnp.int32)

    tiles = [field]
    for s in range(1, nlat):
        tiles.append(lax.ppermute(field, "lat", [((i + s) % nlat, i) for i in range(nlat)]))
    weights = (w_expand, w_reduce, lat_attn, lon_attn)
    staged = call(
        stage_kernel,
        [w.shape for w in weights],
        weights,
        [pltpu.SemaphoreType.DMA((len(weights), 4))],
        any_space=True,
        grant=STAGE_BYTES,
    )
    expand, reduce, lat_proj, lon_proj = staged

    strip = (all_rows * STRIP, channels)
    whole, near, far = call(
        functools.partial(strip_kernel, nlat),
        [(all_rows, cols, channels), strip, strip],
        [place, *tiles, reduce],
        [pltpu.VMEM((all_rows, cols, channels), f32)],
        prefetch=1,
    )
    near = lax.ppermute(near, "lon", [(j, j ^ 1) for j in range(nlon)])
    far = lax.ppermute(
        far, "lon", [(j, (j - 1) % nlon if j % 2 == 0 else (j + 1) % nlon) for j in range(nlon)]
    )

    def scratch(width, count):
        return [
            pltpu.VMEM((all_rows + 2 * HALO, width, channels), f32),
            pltpu.VMEM(dw_weight.shape, f32),
            pltpu.VMEM((all_rows * count, channels), bf16),
            pltpu.VMEM((all_rows * count, channels), bf16),
        ]

    work = 4 * all_rows * columns * channels * w_expand.shape[1]
    inner_two, inner_in = call(
        functools.partial(inner_kernel, rows),
        [(rows * (cols - columns), channels)] * 2,
        [place, whole, dw_weight, expand, reduce, lat_proj],
        scratch(cols, cols - columns),
        prefetch=1,
        flops=work,
    )
    outer_two, sent = call(
        functools.partial(outer_kernel, rows),
        [(rows * columns, channels), (rows, cols, channels)],
        [place, whole, near, far, inner_in, dw_weight, expand, reduce, lat_proj],
        scratch(cols + 2 * STRIP, columns),
        prefetch=1,
        flops=work,
    )

    groups = [[r * split + s for r in range(rows)] for s in range(split)]
    part = lax.all_to_all(sent, "lon", 0, 0, tiled=True, axis_index_groups=groups)
    part = part.reshape(rows * cols, channels)
    parts = [part]
    for s in range(1, split):
        pairs = [(j - j % split + (j + s) % split, j) for j in range(nlon)]
        parts.append(lax.ppermute(part, "lon", pairs))
    (mix,) = call(
        functools.partial(circle_kernel, split), [(rows * cols, channels)], [*parts, lon_proj]
    )
    mix = mix.reshape(rows, cols, channels)
    back = lax.all_to_all(mix, "lon", 0, 0, tiled=True, axis_index_groups=groups)
    (out,) = call(
        last_kernel,
        [(rows, cols, channels)],
        [back.reshape(rows * cols, channels), inner_two, outer_two, lon_proj],
    )
    return out


def solution(mesh):
    return jax.shard_map(
        shards,
        mesh=mesh,
        in_specs=(P("lat", "lon", None), P(), P(), P(), P(), P()),
        out_specs=P("lat", "lon", None),
        check_vma=False,
    )
```

time: 46.3 us -> 43 us (0.929)
  Pallas kernels: 0 us -> 13.7 us
  blocking collectives: 9.48 us -> 18.9 us
  waiting for transfers between devices: 9.19 us -> 1.86 us
  matrix products: 6.06 us -> 0 us
  starting transfers between devices: 13.2 us -> 8.2 us
  other arithmetic: 4.38 us -> 0.08 us
  local copies, waits for them, and re-layouts: 3.31 us -> 0.01 us
    pallas_call x0 -> x6, Pallas kernels: none -> 13.7 us  [call(): pl.pallas_call(kernel, out_shape=shapes, in_specs=[smem] * prefetch + [gi...]
    all_to_all x1 -> x2, blocking collectives: 9.48 us -> 18.9 us  [the longest x1 9.58 us: shards(): lax.all_to_all(sent, 'lon', 0, 0, tiled=True, axis_index_groups=groups)]
    all_to_all x1 -> x0, waiting for transfers between devices: 7.85 us -> none  [shards(): lax.all_to_all(sent, 'lon', 0, 0, tiled=True).reshape(nlon * cols, channels)]
    dot_general x9 -> x0, matrix products: 6.06 us -> none  [the longest x7 5.17 us: dot(): return jnp.dot(rows, matrix, preferred_element_type=jnp.float32)]
    all_to_all x1 -> x0, starting transfers between devices: 4.14 us -> none  [shards(): lax.all_to_all(sent, 'lon', 0, 0, tiled=True).reshape(nlon * cols, channels)]
    reduce_sum x6 -> x0, other arithmetic: 2.67 us -> none  [the longest x1 1.75 us: layer_norm(): average = jnp.mean(values, axis=-1, keepdims=True)]
    slice x7 -> x0, local copies, waits for them, and re-layouts: 1.97 us -> none  [the longest x3 1.04 us: shards(): conv = conv + padded[a:a + all_rows, b:b + cols] * taps[a, b]]
    concatenate x2 -> x0, other arithmetic: 1.08 us -> none  [the longest x1 1.07 us: shards(): whole = jnp.roll(whole, my_lat * rows, axis=0)]
  transfers between devices with their start and end apart: 6 -> 4, of which waited for: 2 -> 2; matrix products, arithmetic and copies ran while one was open for 2% -> 0% of each run, Pallas kernels for 0% -> 14%
where the time goes in v3:
time: 43 us; the launch traced here: 42.8 us
  blocking collectives  18.9 us (44%)
  Pallas kernels  13.7 us (32%)
  starting transfers between devices  8.2 us (19%)
  waiting for transfers between devices  1.86 us (4%)
    pallas_call x6, Pallas kernels, call(): pl.pallas_call(kernel, out_shape=shapes, in_specs=[smem] * prefetch + [gi...  13.7 us
    all_to_all x1, blocking collectives, shards(): lax.all_to_all(sent, 'lon', 0, 0, tiled=True, axis_index_groups=groups)  9.58 us
    all_to_all x1, blocking collectives, shards(): lax.all_to_all(mix, 'lon', 0, 0, tiled=True, axis_index_groups=groups)  9.29 us
    ppermute x1, starting transfers between devices, shards(): lax.ppermute(far, 'lon', [(j, (j - 1) % nlon if j % 2 == 0 else (j + 1) %...  5.19 us
    ppermute x1, starting transfers between devices, shards(): lax.ppermute(field, 'lat', [((i + s) % nlat, i) for i in range(nlat)])  2.94 us
    ppermute x1, waiting for transfers between devices, shards(): parts.append(lax.ppermute(part, 'lon', pairs))  1.25 us
  transfers between devices with their start and end apart: 4, of which 2 were waited for; matrix products, arithmetic and copies ran while one was open for 0% of the time, Pallas kernels for 14%

profile of v3, /device:TPU:0, one launch (start us, length us, event | category | flops | bytes accessed | tf_op | source)
XLA Modules:
  0.0 42.8 jit_solution(10957128274391196588)
XLA Ops:
  0.0 2.9 %collective-permute-start = (bf16[8,16,256]{2,1,0:T(8,128)(2,1)}, bf16[8,16,256]{2,1,0:T(8,128)(2,1)S(1)}, u32[]{:S(2)}, u32[]{:S(2)}) collective-permute-start(bf16[8,16,256]{2,1,0:T(8,128)(2,1)} %refs_0_.3), channel_id=1, source_target_pairs={{16,0},{0,16},{17,1},{1,17},{18,2},{2,18},{19,3},{3,19},{20,4},{4,... | collective-permute-start | bytes 196616 | tf_op jit(solution)/shard_map/ppermute | solution.py:252
  2.9 0.0 copy-start.1
  2.9 1.8 %shard_map.64 = (bf16[256,1024]{1,0:T(8,128)(2,1)S(1)}, bf16[1024,256]{1,0:T(8,128)(2,1)S(1)}, bf16[4,256,256]{2,1,0:T(8,128)(2,1)S(1)}, bf16[4,256,256]{2,1,0:T(8,128)(2,1)S(1)}) custom-call(bf16[256,1024]{1,0:T(8,128)(2,1)} %refs_0_.2, bf16[1024,256]{1,0:T(8,128)(2,1)} %refs_1_.1, bf16[4,256,256]{2,1,0:T(8,128)(2,1)} %refs_2_.1, bf16[4,256,256]{2,1,0:T(8,128)(2,1)} %refs_3_.1), custom_call_target="tpu_custom_call" | custom-call | bytes 2097152 | tf_op jit(solution)/shard_map/pallas_call | solution.py:229
  4.7 0.1 pad_add_fusion.place_ref
  4.8 0.6 %collective-permute-done.refs_1_ = bf16[8,16,256]{2,1,0:T(8,128)(2,1)S(1)} collective-permute-done((bf16[8,16,256]{2,1,0:T(8,128)(2,1)}, bf16[8,16,256]{2,1,0:T(8,128)(2,1)S(1)}, u32[]{:S(2)}, u32[]{:S(2)}) %collective-permute-start) | collective-permute-done | bytes 65568 | tf_op jit(solution)/shard_map/ppermute | solution.py:252
  5.4 0.0 copy-done.1
  5.4 0.0 copy-start
  5.4 0.6 %shard_map.65 = (bf16[16,16,256]{2,1,0:T(8,128)(2,1)S(1)}, bf16[128,256]{1,0:T(8,128)(2,1)S(1)}, bf16[128,256]{1,0:T(8,128)(2,1)S(1)}) custom-call(s32[2]{0:T(128)S(1)} %pad_add_fusion.place_ref, bf16[8,16,256]{2,1,0:T(8,128)(2,1)S(1)} %copy-done.1, bf16[8,16,256]{2,1,0:T(8,128)(2,1)S(1)} %collective-permute-done.refs_1_, ...), custom_call_target="tpu_custom_call" | custom-call | bytes 655368 | tf_op jit(solution)/shard_map/pallas_call | solution.py:229
  6.0 0.1 collective-permute-start.1
  6.1 5.2 %collective-permute-start.2 = (bf16[128,256]{1,0:T(8,128)(2,1)S(1)}, bf16[128,256]{1,0:T(8,128)(2,1)S(1)}, u32[]{:S(2)}, u32[]{:S(2)}) collective-permute-start(bf16[128,256]{1,0:T(8,128)(2,1)S(1)} %get-tuple-element.19), channel_id=1, source_target_pairs={{0,15},{1,2},{2,1},{3,4},{4,3},{5,6},{6,5},{7,8},{8,7},{9,10},{10,... | collective-permute-start | bytes 196616 | tf_op jit(solution)/shard_map/ppermute | solution.py:273
  11.3 0.0 copy-done
  11.3 4.4 %shard_map.66 = (bf16[64,256]{1,0:T(8,128)(2,1)S(1)}, bf16[64,256]{1,0:T(8,128)(2,1)S(1)}) custom-call(s32[2]{0:T(128)S(1)} %pad_add_fusion.place_ref, bf16[16,16,256]{2,1,0:T(8,128)(2,1)S(1)} %get-tuple-element.17.whole_ref, bf16[7,7,256]{2,1,0:T(8,128)(2,1)S(1)} %copy-done, bf16[256,1024]{1,0:T(8,128)(2,1)S(1)} %get-tuple-element.20.expand_ref, ...), custom_call_target="tpu_custom_call" | custom-call | flops 134217728 | bytes 1729032 | tf_op jit(solution)/shard_map/pallas_call | solution.py:229
  15.7 0.0 collective-permute-done.1.near_ref
  15.7 0.0 collective-permute-done.2.far_ref
  15.7 3.8 %shard_map.67 = (bf16[64,256]{1,0:T(8,128)(2,1)S(1)}, bf16[8,16,256]{2,1,0:T(8,128)(2,1)S(1)}) custom-call(s32[2]{0:T(128)S(1)} %pad_add_fusion.place_ref, bf16[16,16,256]{2,1,0:T(8,128)(2,1)S(1)} %get-tuple-element.17.whole_ref, bf16[128,256]{1,0:T(8,128)(2,1)S(1)} %collective-permute-done.1.near_ref, bf16[128,256]{1,0:T(8,128)(2,1)S(1)} %collective-permute-done.2.far_ref, ...), custom_call_target="tpu_custom_call" | custom-call | flops 134217728 | bytes 1892872 | tf_op jit(solution)/shard_map/pallas_call | solution.py:229
  19.6 9.6 %all_to_all.10 = bf16[8,16,256]{2,1,0:T(8,128)(2,1)S(1)} all-to-all(bf16[8,16,256]{2,1,0:T(8,128)(2,1)S(1)} %get-tuple-element.23), channel_id=1, replica_groups={{0,2,4,6,8,10,12,14},{1,3,5,7,9,11,13,15},{16,18,20,22,24,26,28,30},{17..., dimensions={0} | all-to-all | bytes 131072 | tf_op jit(solution)/shard_map/all_to_all | solution.py:304
  29.2 0.0 collective-permute-start.3
  29.2 1.3 %collective-permute-done.3.refs_1_ = bf16[128,256]{1,0:T(8,128)(2,1)S(1)} collective-permute-done((bf16[128,256]{1,0:T(8,128)(2,1)S(1)}, bf16[128,256]{1,0:T(8,128)(2,1)S(1)}, u32[]{:S(2)}, u32[]{:S(2)}) %collective-permute-start.3) | collective-permute-done | bytes 65568 | tf_op jit(solution)/shard_map/ppermute | solution.py:309
  30.4 2.3 %shard_map.68 = bf16[128,256]{1,0:T(8,128)(2,1)S(1)} custom-call(bf16[128,256]{1,0:T(8,128)(2,1)S(1)} %bitcast.6, bf16[128,256]{1,0:T(8,128)(2,1)S(1)} %collective-permute-done.3.refs_1_, bf16[4,256,256]{2,1,0:T(8,128)(2,1)S(1)} %get-tuple-element.24.refs_2_.attn_ref), custom_call_target="tpu_custom_call" | custom-call | bytes 655360 | tf_op jit(solution)/shard_map/pallas_call | solution.py:229
  32.7 9.3 %all_to_all.11 = bf16[8,16,256]{2,1,0:T(8,128)(2,1)S(1)} all-to-all(bf16[8,16,256]{2,1,0:T(8,128)(2,1)S(1)} %bitcast.8), channel_id=1, replica_groups={{0,2,4,6,8,10,12,14},{1,3,5,7,9,11,13,15},{16,18,20,22,24,26,28,30},{17..., dimensions={0} | all-to-all | bytes 131072 | tf_op jit(solution)/shard_map/all_to_all | solution.py:314
  42.0 0.8 %shard_map.69 = bf16[8,16,256]{2,1,0:T(8,128)(2,1)} custom-call(bf16[128,256]{1,0:T(8,128)(2,1)S(1)} %bitcast.7, bf16[64,256]{1,0:T(8,128)(2,1)S(1)} %get-tuple-element.25.inner_ref, bf16[64,256]{1,0:T(8,128)(2,1)S(1)} %get-tuple-element.26.outer_ref, bf16[4,256,256]{2,1,0:T(8,128)(2,1)S(1)} %get-tuple-element.24.refs_2_.attn_ref), custom_call_target="tpu_custom_call" | custom-call | bytes 655360 | tf_op jit(solution)/shard_map/pallas_call | solution.py:229
Async XLA Ops:
  0.0 5.4 %collective-permute-start = (bf16[8,16,256]{2,1,0:T(8,128)(2,1)}, bf16[8,16,256]{2,1,0:T(8,128)(2,1)S(1)}, u32[]{:S(2)}, u32[]{:S(2)}) collective-permute-start(bf16[8,16,256]{2,1,0:T(8,128)(2,1)} %refs_0_.3), channel_id=1, source_target_pairs={{16,0},{0,16},{17,1},{1,17},{18,2},{2,18},{19,3},{3,19},{20,4},{4,... | collective-permute-start | bytes 196616 | tf_op jit(solution)/shard_map/ppermute | solution.py:252
  2.9 2.5 %copy-start.1 = (bf16[8,16,256]{2,1,0:T(8,128)(2,1)S(1)}, bf16[8,16,256]{2,1,0:T(8,128)(2,1)}, u32[]{:S(2)}) copy-start(bf16[8,16,256]{2,1,0:T(8,128)(2,1)} %refs_0_.3) | copy-start | bytes 196612
  5.4 5.9 %copy-start = (bf16[7,7,256]{2,1,0:T(8,128)(2,1)S(1)}, bf16[7,7,256]{2,1,0:T(8,128)(2,1)}, u32[]{:S(2)}) copy-start(bf16[7,7,256]{2,1,0:T(8,128)(2,1)} %dw_ref.3) | copy-start | bytes 75268
  6.0 9.7 %collective-permute-start.1 = (bf16[128,256]{1,0:T(8,128)(2,1)S(1)}, bf16[128,256]{1,0:T(8,128)(2,1)S(1)}, u32[]{:S(2)}, u32[]{:S(2)}) collective-permute-start(bf16[128,256]{1,0:T(8,128)(2,1)S(1)} %get-tuple-element.18), channel_id=1, source_target_pairs={{0,1},{1,0},{2,3},{3,2},{4,5},{5,4},{6,7},{7,6},{8,9},{9,8},{10,11... | collective-permute-start | bytes 196616 | tf_op jit(solution)/shard_map/ppermute | solution.py:272
  6.1 9.6 %collective-permute-start.2 = (bf16[128,256]{1,0:T(8,128)(2,1)S(1)}, bf16[128,256]{1,0:T(8,128)(2,1)S(1)}, u32[]{:S(2)}, u32[]{:S(2)}) collective-permute-start(bf16[128,256]{1,0:T(8,128)(2,1)S(1)} %get-tuple-element.19), channel_id=1, source_target_pairs={{0,15},{1,2},{2,1},{3,4},{4,3},{5,6},{6,5},{7,8},{8,7},{9,10},{10,... | collective-permute-start | bytes 196616 | tf_op jit(solution)/shard_map/ppermute | solution.py:273
  29.2 1.3 %collective-permute-start.3 = (bf16[128,256]{1,0:T(8,128)(2,1)S(1)}, bf16[128,256]{1,0:T(8,128)(2,1)S(1)}, u32[]{:S(2)}, u32[]{:S(2)}) collective-permute-start(bf16[128,256]{1,0:T(8,128)(2,1)S(1)} %bitcast.5), channel_id=1, source_target_pairs={{1,0},{0,1},{3,2},{2,3},{5,4},{4,5},{7,6},{6,7},{9,8},{8,9},{11,10... | collective-permute-start | bytes 196616 | tf_op jit(solution)/shard_map/ppermute | solution.py:309

commit v4 on v3

--- a/solution.py
+++ b/solution.py
@@ -13,6 +13,7 @@
 STRIP = 8
 SIDE = 4
 LANES = 128
+LEVELS = 4
 EPSILON = 1e-06
 VMEM_BYTES = 24 * 1024 * 1024
 STAGE_BYTES = 103 * 512 * 1024
@@ -39,20 +40,23 @@
 
 
 def attend(queries, keys, values, mask):
-    head_size = queries.shape[1] // HEADS
-    scale = head_size ** (-0.5)
-    lane_head = lax.broadcasted_iota(jnp.int32, (1, queries.shape[1]), 1) // head_size
-    out = jnp.zeros(queries.shape, f32)
-    for h in range(HEADS):
-        mine = lane_head == h
-        scores = dot_t(jnp.where(mine, queries, jnp.zeros_like(queries)), keys) * scale
-        if mask is not None:
-            scores = jnp.where(mask, scores, -1e30)
-        top = jnp.max(scores, axis=-1, keepdims=True)
-        probs = jnp.exp(scores - top)
-        totals = jnp.sum(probs, axis=-1, keepdims=True)
-        mixed = dot(probs.astype(bf16), values) / totals
-        out = jnp.where(mine, mixed, out)
+    count, channels = queries.shape
+    head_size = channels // HEADS
+    lane_head = lax.broadcasted_iota(jnp.int32, (1, channels), 1) // head_size
+    picks = [lane_head == h for h in range(HEADS)]
+    none = jnp.zeros_like(queries)
+    stacked = jnp.concatenate([jnp.where(pick, queries, none) for pick in picks], axis=0)
+    scores = dot_t(stacked, keys) * head_size ** (-0.5)
+    if mask is not None:
+        scores = scores.reshape(HEADS, count, keys.shape[0])
+        scores = jnp.where(mask[None], scores, -1e30).reshape(HEADS * count, keys.shape[0])
+    top = jnp.max(scores, axis=-1, keepdims=True)
+    probs = jnp.exp(scores - top)
+    totals = jnp.sum(probs, axis=-1, keepdims=True)
+    mixed = dot(probs.astype(bf16), values) * (1.0 / totals)
+    out = mixed[:count]
+    for h in range(1, HEADS):
+        out = jnp.where(picks[h], mixed[h * count : (h + 1) * count], out)
     return out.astype(bf16)
 
 
@@ -75,17 +79,17 @@
 
 def strip_kernel(nlat, place_ref, *refs):
     tiles = refs[:nlat]
-    whole_ref, near_ref, far_ref, whole = refs[nlat + 1 :]
+    near_ref, far_ref, near, far = refs[nlat + 1 :]
     rows, cols, channels = tiles[0].shape
+    even = place_ref[1] == 0
     for s in range(nlat):
-        source = lax.rem(place_ref[0] + s, nlat)
-        whole[pl.ds(source * rows, rows)] = tiles[s][...].astype(f32)
-    values = whole[...]
-    whole_ref[...] = values.astype(bf16)
-    first, last = values[:, :STRIP], values[:, cols - STRIP :]
-    even = place_ref[1] == 0
-    near_ref[...] = jnp.where(even, last, first).reshape(near_ref.shape).astype(bf16)
-    far_ref[...] = jnp.where(even, first, last).reshape(far_ref.shape).astype(bf16)
+        values = tiles[s][...].astype(f32)
+        first, last = values[:, :STRIP], values[:, cols - STRIP :]
+        where = pl.ds(lax.rem(place_ref[0] + s, nlat) * rows, rows)
+        near[where] = jnp.where(even, last, first)
+        far[where] = jnp.where(even, first, last)
+    near_ref[...] = near[...].reshape(near_ref.shape).astype(bf16)
+    far_ref[...] = far[...].reshape(far_ref.shape).astype(bf16)
 
 
 def chain(my_lat, slab, shape, dw_ref, expand_ref, reduce_ref, attn_ref, center, scratch):
@@ -128,20 +132,27 @@
     padded[HALO : HALO + all_rows, first : first + width] = values
 
 
+def fill_tiles(padded, my_lat, first, tiles):
+    rows, cols = tiles[0].shape[:2]
+    for s in range(len(tiles)):
+        place = HALO + lax.rem(my_lat + s, len(tiles)) * rows
+        padded[pl.ds(place, rows), first : first + cols] = tiles[s][...].astype(f32)
+
+
 def clear(padded, all_rows):
     edge = jnp.zeros((HALO,) + padded.shape[1:], f32)
     padded[:HALO] = edge
     padded[HALO + all_rows :] = edge
 
 
-def inner_kernel(
-    rows, place_ref, whole_ref, dw_ref, expand_ref, reduce_ref, attn_ref,
-    two_ref, in_ref, padded, *scratch
-):
-    all_rows, cols, channels = whole_ref.shape
+def inner_kernel(nlat, place_ref, *refs):
+    tiles, refs = refs[:nlat], refs[nlat:]
+    dw_ref, expand_ref, reduce_ref, attn_ref, two_ref, in_ref, padded, *scratch = refs
+    rows, cols, channels = tiles[0].shape
+    all_rows = rows * nlat
     columns = cols - 2 * SIDE
     clear(padded, all_rows)
-    fill(padded, all_rows, 0, whole_ref[...].astype(f32))
+    fill_tiles(padded, place_ref[0], 0, tiles)
 
     def slab(b, c):
         first = SIDE - HALO + b
@@ -156,12 +167,13 @@
     in_ref[...] = lon_in.astype(bf16)
 
 
-def outer_kernel(
-    rows, place_ref, whole_ref, near_ref, far_ref, inner_in_ref,
-    dw_ref, expand_ref, reduce_ref, attn_ref,
-    two_ref, sent_ref, padded, *scratch
-):
-    all_rows, cols, channels = whole_ref.shape
+def outer_kernel(nlat, levels, place_ref, *refs):
+    tiles, refs = refs[:nlat], refs[nlat:]
+    near_ref, far_ref, inner_in_ref, dw_ref, expand_ref, reduce_ref, attn_ref = refs[:7]
+    two_ref, *refs = refs[7:]
+    sent_refs, (sent, padded, *scratch) = refs[:levels], refs[levels:]
+    rows, cols, channels = tiles[0].shape
+    all_rows = rows * nlat
     columns = 2 * SIDE
     strip_shape = (all_rows, STRIP, channels)
     near = near_ref[...].astype(f32).reshape(strip_shape)
@@ -169,7 +181,7 @@
     even = place_ref[1] == 0
     clear(padded, all_rows)
     fill(padded, all_rows, 0, jnp.where(even, far, near))
-    fill(padded, all_rows, STRIP, whole_ref[...].astype(f32))
+    fill_tiles(padded, place_ref[0], STRIP, tiles)
     fill(padded, all_rows, STRIP + cols, jnp.where(even, near, far))
     sublane = lax.broadcasted_iota(jnp.int32, (1, columns, 1), 1)
 
@@ -193,23 +205,43 @@
     two_ref[...] = block_two
     inner = inner_in_ref[...].astype(f32).reshape(rows, cols - columns, channels)
     outer = lon_in.reshape(rows, columns, channels)
-    sent_ref[...] = jnp.concatenate([inner, outer], axis=1).astype(bf16)
-
-
-def circle_kernel(count, *refs):
-    parts = refs[:count]
-    attn_ref, mix_ref = refs[count:]
-    circle = jnp.concatenate([part[...] for part in parts], axis=0)
-    queries = dot(parts[0][...], attn_ref[0]).astype(bf16)
-    keys = dot(circle, attn_ref[1]).astype(bf16)
-    values = dot(circle, attn_ref[2]).astype(bf16)
-    mix_ref[...] = attend(queries, keys, values, None)
-
-
-def last_kernel(back_ref, inner_ref, outer_ref, attn_ref, out_ref):
+    sent[...] = jnp.concatenate([inner, outer], axis=1).astype(bf16)
+    some = rows // levels
+    for k in range(levels):
+        part = sent[pl.ds((place_ref[2] ^ k) * some, some)]
+        sent_refs[k][...] = part.reshape(sent_refs[k].shape)
+
+
+def circle_kernel(levels, some, *refs):
+    attn_ref, mix_refs = refs[-levels - 1], refs[-levels:]
+    parts = refs[: -levels - 1]
+    count = parts[0].shape[0] // (some * levels)
+
+    def latitude(part, r):
+        starts = [(k * some + r) * count for k in range(levels)]
+        return jnp.concatenate([part[start : start + count] for start in starts], axis=0)
+
+    for r in range(some):
+        own = latitude(parts[0], r)
+        every = jnp.concatenate([own] + [latitude(part, r) for part in parts[1:]], axis=0)
+        queries = dot(own, attn_ref[0]).astype(bf16)
+        keys = dot(every, attn_ref[1]).astype(bf16)
+        values = dot(every, attn_ref[2]).astype(bf16)
+        mix = attend(queries, keys, values, None)
+        for k in range(levels):
+            mix_refs[k][r * count : (r + 1) * count] = mix[k * count : (k + 1) * count]
+
+
+def last_kernel(levels, place_ref, *refs):
+    parts = refs[:levels]
+    inner_ref, outer_ref, attn_ref, out_ref, back = refs[levels:]
     rows, cols, channels = out_ref.shape
     columns = 2 * SIDE
-    change = dot(back_ref[...], attn_ref[3]).reshape(rows, cols, channels)
+    some = parts[0].shape[0]
+    for k in range(levels):
+        start = (place_ref[2] ^ k) * some
+        back[pl.ds(pl.multiple_of(start, some), some)] = parts[k][...]
+    change = dot(back[...], attn_ref[3]).reshape(rows, cols, channels)
     inner = inner_ref[...].astype(f32).reshape(rows, cols - columns, channels)
     outer = outer_ref[...].astype(f32).reshape(rows, columns, channels)
     inner = inner + change[:, : cols - columns]
@@ -242,10 +274,15 @@
     rows, cols, channels = field.shape
     nlat, nlon = lax.axis_size("lat"), lax.axis_size("lon")
     my_lat, my_lon = lax.axis_index("lat"), lax.axis_index("lon")
-    split = nlon // rows
+    levels = min(LEVELS, nlon)
+    column = nlon // levels
+    some = rows // levels
     all_rows = rows * nlat
     columns = 2 * SIDE
-    place = jnp.stack([my_lat, my_lon % 2]).astype(jnp.int32)
+    place = jnp.stack([my_lat, my_lon % 2, my_lon // column]).astype(jnp.int32)
+
+    def swap(piece, mask):
+        return lax.ppermute(piece, "lon", [(j, j ^ mask) for j in range(nlon)])
 
     tiles = [field]
     for s in range(1, nlat):
@@ -262,14 +299,15 @@
     expand, reduce, lat_proj, lon_proj = staged
 
     strip = (all_rows * STRIP, channels)
-    whole, near, far = call(
+    strip_scratch = pltpu.VMEM((all_rows, STRIP, channels), f32)
+    near, far = call(
         functools.partial(strip_kernel, nlat),
-        [(all_rows, cols, channels), strip, strip],
+        [strip, strip],
         [place, *tiles, reduce],
-        [pltpu.VMEM((all_rows, cols, channels), f32)],
+        [strip_scratch, strip_scratch],
         prefetch=1,
     )
-    near = lax.ppermute(near, "lon", [(j, j ^ 1) for j in range(nlon)])
+    near = swap(near, 1)
     far = lax.ppermute(
         far, "lon", [(j, (j - 1) % nlon if j % 2 == 0 else (j + 1) % nlon) for j in range(nlon)]
     )
@@ -284,38 +322,39 @@
 
     work = 4 * all_rows * columns * channels * w_expand.shape[1]
     inner_two, inner_in = call(
-        functools.partial(inner_kernel, rows),
+        functools.partial(inner_kernel, nlat),
         [(rows * (cols - columns), channels)] * 2,
-        [place, whole, dw_weight, expand, reduce, lat_proj],
+        [place, *tiles, dw_weight, expand, reduce, lat_proj],
         scratch(cols, cols - columns),
         prefetch=1,
         flops=work,
     )
-    outer_two, sent = call(
-        functools.partial(outer_kernel, rows),
-        [(rows * columns, channels), (rows, cols, channels)],
-        [place, whole, near, far, inner_in, dw_weight, expand, reduce, lat_proj],
-        scratch(cols + 2 * STRIP, columns),
+    piece = (some * cols, channels)
+    outer_two, *parts = call(
+        functools.partial(outer_kernel, nlat, levels),
+        [(rows * columns, channels)] + [piece] * levels,
+        [place, *tiles, near, far, inner_in, dw_weight, expand, reduce, lat_proj],
+        [pltpu.VMEM((rows, cols, channels), bf16)] + scratch(cols + 2 * STRIP, columns),
         prefetch=1,
         flops=work,
     )
 
-    groups = [[r * split + s for r in range(rows)] for s in range(split)]
-    part = lax.all_to_all(sent, "lon", 0, 0, tiled=True, axis_index_groups=groups)
-    part = part.reshape(rows * cols, channels)
-    parts = [part]
-    for s in range(1, split):
-        pairs = [(j - j % split + (j + s) % split, j) for j in range(nlon)]
-        parts.append(lax.ppermute(part, "lon", pairs))
-    (mix,) = call(
-        functools.partial(circle_kernel, split), [(rows * cols, channels)], [*parts, lon_proj]
-    )
-    mix = mix.reshape(rows, cols, channels)
-    back = lax.all_to_all(mix, "lon", 0, 0, tiled=True, axis_index_groups=groups)
+    parts = [parts[0]] + [swap(parts[k], k * column) for k in range(1, levels)]
+    circle = [jnp.concatenate(parts, axis=0)]
+    mask = column // 2
+    while mask:
+        circle = circle + [swap(part, mask) for part in circle]
+        mask //= 2
+    mixes = call(
+        functools.partial(circle_kernel, levels, some), [piece] * levels, [*circle, lon_proj]
+    )
+    mixes = [mixes[0]] + [swap(mixes[k], k * column) for k in range(1, levels)]
     (out,) = call(
-        last_kernel,
+        functools.partial(last_kernel, levels),
         [(rows, cols, channels)],
-        [back.reshape(rows * cols, channels), inner_two, outer_two, lon_proj],
+        [place, *mixes, inner_two, outer_two, lon_proj],
+        [pltpu.VMEM((rows * cols, channels), bf16)],
+        prefetch=1,
     )
     return out
 

time: 43 us -> 42.2 us (0.981)
  blocking collectives: 18.9 us -> 0 us
  starting transfers between devices: 8.2 us -> 18.5 us
  waiting for transfers between devices: 1.86 us -> 12 us
  Pallas kernels: 13.7 us -> 11.4 us
    all_to_all x2 -> x0, blocking collectives: 18.9 us -> none  [the longest x1 9.58 us: shards(): lax.all_to_all(sent, 'lon', 0, 0, tiled=True, axis_index_groups=groups)]
    ppermute x2 -> x10, starting transfers between devices: 0.07 us -> 10.3 us  [swap(): return lax.ppermute(piece, 'lon', [(j, j ^ mask) for j in range(nlon)])]
    ppermute x2 -> x10, waiting for transfers between devices: 1.25 us -> 11.4 us  [swap(): return lax.ppermute(piece, 'lon', [(j, j ^ mask) for j in range(nlon)])]
    pallas_call x6, Pallas kernels: 13.7 us -> 11.4 us  [call(): pl.pallas_call(kernel, out_shape=shapes, in_specs=[smem] * prefetch + [gi...]
  transfers between devices with their start and end apart: 4 -> 12, of which waited for: 2 -> 7; matrix products, arithmetic and copies ran while one was open for 0% -> 0% of each run, Pallas kernels for 14% -> 13%
where the time goes in v4:
time: 42.2 us; the launch traced here: 42 us
  starting transfers between devices  18.5 us (44%)
  waiting for transfers between devices  12 us (28%)
  Pallas kernels  11.4 us (27%)
    ppermute x10, waiting for transfers between devices, swap(): return lax.ppermute(piece, 'lon', [(j, j ^ mask) for j in range(nlon)])  11.4 us
    pallas_call x6, Pallas kernels, call(): pl.pallas_call(kernel, out_shape=shapes, in_specs=[smem] * prefetch + [gi...  11.4 us
    ppermute x10, starting transfers between devices, swap(): return lax.ppermute(piece, 'lon', [(j, j ^ mask) for j in range(nlon)])  10.3 us
    ppermute x1, starting transfers between devices, shards(): lax.ppermute(far, 'lon', [(j, (j - 1) % nlon if j % 2 == 0 else (j + 1) %...  5.19 us
    ppermute x1, starting transfers between devices, shards(): lax.ppermute(field, 'lat', [((i + s) % nlat, i) for i in range(nlat)])  2.94 us
  transfers between devices with their start and end apart: 12, of which 7 were waited for; matrix products, arithmetic and copies ran while one was open for 0% of the time, Pallas kernels for 13%

profile of v4, /device:TPU:0, one launch (start us, length us, event | category | flops | bytes accessed | tf_op | source)
XLA Modules:
  0.0 42.0 jit_solution(16254064046853403677)
XLA Ops:
  0.0 2.9 %collective-permute-start = (bf16[8,16,256]{2,1,0:T(8,128)(2,1)}, bf16[8,16,256]{2,1,0:T(8,128)(2,1)S(1)}, u32[]{:S(2)}, u32[]{:S(2)}) collective-permute-start(bf16[8,16,256]{2,1,0:T(8,128)(2,1)} %refs_0_.7), channel_id=1, source_target_pairs={{16,0},{0,16},{17,1},{1,17},{18,2},{2,18},{19,3},{3,19},{20,4},{4,... | collective-permute-start | bytes 196616 | tf_op jit(solution)/shard_map/ppermute | solution.py:289
  2.9 0.0 copy-start
  2.9 1.8 %shard_map.64 = (bf16[256,1024]{1,0:T(8,128)(2,1)S(1)}, bf16[1024,256]{1,0:T(8,128)(2,1)S(1)}, bf16[4,256,256]{2,1,0:T(8,128)(2,1)S(1)}, bf16[4,256,256]{2,1,0:T(8,128)(2,1)S(1)}) custom-call(bf16[256,1024]{1,0:T(8,128)(2,1)} %refs_0_.4, bf16[1024,256]{1,0:T(8,128)(2,1)} %refs_1_.1, bf16[4,256,256]{2,1,0:T(8,128)(2,1)} %refs_2_.2, bf16[4,256,256]{2,1,0:T(8,128)(2,1)} %refs_3_.1), custom_call_target="tpu_custom_call" | custom-call | bytes 2097152 | tf_op jit(solution)/shard_map/pallas_call | solution.py:261
  4.7 0.1 pad_add_fusion.place_ref
  4.8 0.6 %collective-permute-done.refs_1_ = bf16[8,16,256]{2,1,0:T(8,128)(2,1)S(1)} collective-permute-done((bf16[8,16,256]{2,1,0:T(8,128)(2,1)}, bf16[8,16,256]{2,1,0:T(8,128)(2,1)S(1)}, u32[]{:S(2)}, u32[]{:S(2)}) %collective-permute-start) | collective-permute-done | bytes 65568 | tf_op jit(solution)/shard_map/ppermute | solution.py:289
  5.4 0.0 copy-done
  5.4 0.0 copy-start.1
  5.4 0.6 %shard_map.65 = (bf16[128,256]{1,0:T(8,128)(2,1)S(1)}, bf16[128,256]{1,0:T(8,128)(2,1)S(1)}) custom-call(s32[3]{0:T(128)S(1)} %pad_add_fusion.place_ref, bf16[8,16,256]{2,1,0:T(8,128)(2,1)S(1)} %copy-done, bf16[8,16,256]{2,1,0:T(8,128)(2,1)S(1)} %collective-permute-done.refs_1_, bf16[1024,256]{1,0:T(8,128)(2,1)S(1)} %get-tuple-element.22.refs_2_.refs_4_.refs_7_), custom_call_target="tpu_custom_call" | custom-call | bytes 655372 | tf_op jit(solution)/shard_map/pallas_call | solution.py:261
  6.0 0.1 collective-permute-start.1
  6.1 5.2 %collective-permute-start.2 = (bf16[128,256]{1,0:T(8,128)(2,1)S(1)}, bf16[128,256]{1,0:T(8,128)(2,1)S(1)}, u32[]{:S(2)}, u32[]{:S(2)}) collective-permute-start(bf16[128,256]{1,0:T(8,128)(2,1)S(1)} %get-tuple-element.24), channel_id=1, source_target_pairs={{0,15},{1,2},{2,1},{3,4},{4,3},{5,6},{6,5},{7,8},{8,7},{9,10},{10,... | collective-permute-start | bytes 196616 | tf_op jit(solution)/shard_map/ppermute | solution.py:311
  11.3 0.0 copy-done.1
  11.3 3.5 %shard_map.66 = (bf16[64,256]{1,0:T(8,128)(2,1)S(1)}, bf16[64,256]{1,0:T(8,128)(2,1)S(1)}) custom-call(s32[3]{0:T(128)S(1)} %pad_add_fusion.place_ref, bf16[8,16,256]{2,1,0:T(8,128)(2,1)S(1)} %copy-done, bf16[8,16,256]{2,1,0:T(8,128)(2,1)S(1)} %collective-permute-done.refs_1_, bf16[7,7,256]{2,1,0:T(8,128)(2,1)S(1)} %copy-done.1, ...), custom_call_target="tpu_custom_call" | custom-call | flops 134217728 | bytes 1729036 | tf_op jit(solution)/shard_map/pallas_call | solution.py:261
  14.8 0.0 collective-permute-done.1.refs_2_
  14.8 0.0 collective-permute-done.2.refs_3_
  14.8 3.0 %shard_map.67 = (bf16[64,256]{1,0:T(8,128)(2,1)S(1)}, bf16[32,256]{1,0:T(8,128)(2,1)S(1)}, bf16[32,256]{1,0:T(8,128)(2,1)S(1)}, bf16[32,256]{1,0:T(8,128)(2,1)S(1)}, bf16[32,256]{1,0:T(8,128)(2,1)S(1)}) custom-call(s32[3]{0:T(128)S(1)} %pad_add_fusion.place_ref, bf16[8,16,256]{2,1,0:T(8,128)(2,1)S(1)} %copy-done, ...), custom_call_target="tpu_custom_call" | custom-call | flops 134217728 | bytes 1892876 | tf_op jit(solution)/shard_map/pallas_call | solution.py:261
  17.8 0.1 collective-permute-start.3
  17.9 1.0 %collective-permute-start.4 = (bf16[32,256]{1,0:T(8,128)(2,1)S(1)}, bf16[32,256]{1,0:T(8,128)(2,1)S(1)}, u32[]{:S(2)}, u32[]{:S(2)}) collective-permute-start(bf16[32,256]{1,0:T(8,128)(2,1)S(1)} %get-tuple-element.30), channel_id=1, source_target_pairs={{0,8},{1,9},{2,10},{3,11},{4,12},{5,13},{6,14},{7,15},{8,0},{9,1},... | collective-permute-start | bytes 49160 | tf_op jit(solution)/shard_map/ppermute | solution.py:285
  18.9 3.4 %collective-permute-start.5 = (bf16[32,256]{1,0:T(8,128)(2,1)S(1)}, bf16[32,256]{1,0:T(8,128)(2,1)S(1)}, u32[]{:S(2)}, u32[]{:S(2)}) collective-permute-start(bf16[32,256]{1,0:T(8,128)(2,1)S(1)} %get-tuple-element.31), channel_id=1, source_target_pairs={{0,12},{1,13},{2,14},{3,15},{4,8},{5,9},{6,10},{7,11},{8,4},{9,5},... | collective-permute-start | bytes 49160 | tf_op jit(solution)/shard_map/ppermute | solution.py:285
  22.2 0.0 collective-permute-done.3
  22.2 0.3 collective-permute-done.4
  22.6 1.8 %collective-permute-done.5 = bf16[32,256]{1,0:T(8,128)(2,1)S(1)} collective-permute-done((bf16[32,256]{1,0:T(8,128)(2,1)S(1)}, bf16[32,256]{1,0:T(8,128)(2,1)S(1)}, u32[]{:S(2)}, u32[]{:S(2)}) %collective-permute-start.5) | collective-permute-done | bytes 16416 | tf_op jit(solution)/shard_map/ppermute | solution.py:285
  24.4 0.6 %collective-permute-start.6 = (bf16[128,256]{1,0:T(8,128)(2,1)S(1)}, bf16[128,256]{1,0:T(8,128)(2,1)S(1)}, u32[]{:S(2)}, u32[]{:S(2)}) collective-permute-start(bf16[128,256]{1,0:T(8,128)(2,1)S(1)} %constant_dynamic-update-slice_fusion.refs_0_), channel_id=1, source_target_pairs={{0,2},{1,3},{2,0},{3,1},{4,6},{5,7},{6,4},{7,5},{8,10},{9,11},{10,... | collective-permute-start | bytes 196616 | tf_op jit(solution)/shard_map/ppermute | solution.py:285
  25.0 0.7 %collective-permute-start.7 = (bf16[128,256]{1,0:T(8,128)(2,1)S(1)}, bf16[128,256]{1,0:T(8,128)(2,1)S(1)}, u32[]{:S(2)}, u32[]{:S(2)}) collective-permute-start(bf16[128,256]{1,0:T(8,128)(2,1)S(1)} %constant_dynamic-update-slice_fusion.refs_0_), channel_id=1, source_target_pairs={{0,1},{1,0},{2,3},{3,2},{4,5},{5,4},{6,7},{7,6},{8,9},{9,8},{10,11... | collective-permute-start | bytes 196616 | tf_op jit(solution)/shard_map/ppermute | solution.py:285
  25.8 2.9 %collective-permute-done.6.refs_1_ = bf16[128,256]{1,0:T(8,128)(2,1)S(1)} collective-permute-done((bf16[128,256]{1,0:T(8,128)(2,1)S(1)}, bf16[128,256]{1,0:T(8,128)(2,1)S(1)}, u32[]{:S(2)}, u32[]{:S(2)}) %collective-permute-start.6) | collective-permute-done | bytes 65568 | tf_op jit(solution)/shard_map/ppermute | solution.py:285
  28.7 0.0 collective-permute-start.8
  28.7 0.0 collective-permute-done.7.refs_2_
  28.7 1.2 %collective-permute-done.8.refs_3_ = bf16[128,256]{1,0:T(8,128)(2,1)S(1)} collective-permute-done((bf16[128,256]{1,0:T(8,128)(2,1)S(1)}, bf16[128,256]{1,0:T(8,128)(2,1)S(1)}, u32[]{:S(2)}, u32[]{:S(2)}) %collective-permute-start.8) | collective-permute-done | bytes 65568 | tf_op jit(solution)/shard_map/ppermute | solution.py:285
  29.9 1.2 %shard_map.68 = (bf16[32,256]{1,0:T(8,128)(2,1)S(1)}, bf16[32,256]{1,0:T(8,128)(2,1)S(1)}, bf16[32,256]{1,0:T(8,128)(2,1)S(1)}, bf16[32,256]{1,0:T(8,128)(2,1)S(1)}) custom-call(bf16[128,256]{1,0:T(8,128)(2,1)S(1)} %constant_dynamic-update-slice_fusion.refs_0_, bf16[128,256]{1,0:T(8,128)(2,1)S(1)} %collective-permute-done.6.refs_1_, ...), custom_call_target="tpu_custom_call" | custom-call | bytes 786432 | tf_op jit(solution)/shard_map/pallas_call | solution.py:261
  31.1 0.3 collective-permute-start.9
  31.4 3.8 %collective-permute-start.10 = (bf16[32,256]{1,0:T(8,128)(2,1)S(1)}, bf16[32,256]{1,0:T(8,128)(2,1)S(1)}, u32[]{:S(2)}, u32[]{:S(2)}) collective-permute-start(bf16[32,256]{1,0:T(8,128)(2,1)S(1)} %get-tuple-element.35), channel_id=1, source_target_pairs={{0,8},{1,9},{2,10},{3,11},{4,12},{5,13},{6,14},{7,15},{8,0},{9,1},... | collective-permute-start | bytes 49160 | tf_op jit(solution)/shard_map/ppermute | solution.py:285
  35.1 0.4 %collective-permute-start.11 = (bf16[32,256]{1,0:T(8,128)(2,1)S(1)}, bf16[32,256]{1,0:T(8,128)(2,1)S(1)}, u32[]{:S(2)}, u32[]{:S(2)}) collective-permute-start(bf16[32,256]{1,0:T(8,128)(2,1)S(1)} %get-tuple-element.36), channel_id=1, source_target_pairs={{0,12},{1,13},{2,14},{3,15},{4,8},{5,9},{6,10},{7,11},{8,4},{9,5},... | collective-permute-start | bytes 49160 | tf_op jit(solution)/shard_map/ppermute | solution.py:285
  35.6 0.0 collective-permute-done.9.refs_1_
  35.6 1.3 %collective-permute-done.10.refs_2_ = bf16[32,256]{1,0:T(8,128)(2,1)S(1)} collective-permute-done((bf16[32,256]{1,0:T(8,128)(2,1)S(1)}, bf16[32,256]{1,0:T(8,128)(2,1)S(1)}, u32[]{:S(2)}, u32[]{:S(2)}) %collective-permute-start.10) | collective-permute-done | bytes 16416 | tf_op jit(solution)/shard_map/ppermute | solution.py:285
  36.9 3.8 %collective-permute-done.11.refs_3_ = bf16[32,256]{1,0:T(8,128)(2,1)S(1)} collective-permute-done((bf16[32,256]{1,0:T(8,128)(2,1)S(1)}, bf16[32,256]{1,0:T(8,128)(2,1)S(1)}, u32[]{:S(2)}, u32[]{:S(2)}) %collective-permute-start.11) | collective-permute-done | bytes 16416 | tf_op jit(solution)/shard_map/ppermute | solution.py:285
  40.7 1.3 %shard_map.69 = bf16[8,16,256]{2,1,0:T(8,128)(2,1)} custom-call(s32[3]{0:T(128)S(1)} %pad_add_fusion.place_ref, bf16[32,256]{1,0:T(8,128)(2,1)S(1)} %get-tuple-element.33.refs_0_, bf16[32,256]{1,0:T(8,128)(2,1)S(1)} %collective-permute-done.9.refs_1_, bf16[32,256]{1,0:T(8,128)(2,1)S(1)} %collective-permute-done.10.refs_2_, ...), custom_call_target="tpu_custom_call" | custom-call | bytes 655372 | tf_op jit(solution)/shard_map/pallas_call | solution.py:261
  (4 shorter events, 0.0 us)
Async XLA Ops:
  0.0 5.4 %collective-permute-start = (bf16[8,16,256]{2,1,0:T(8,128)(2,1)}, bf16[8,16,256]{2,1,0:T(8,128)(2,1)S(1)}, u32[]{:S(2)}, u32[]{:S(2)}) collective-permute-start(bf16[8,16,256]{2,1,0:T(8,128)(2,1)} %refs_0_.7), channel_id=1, source_target_pairs={{16,0},{0,16},{17,1},{1,17},{18,2},{2,18},{19,3},{3,19},{20,4},{4,... | collective-permute-start | bytes 196616 | tf_op jit(solution)/shard_map/ppermute | solution.py:289
  2.9 2.5 %copy-start = (bf16[8,16,256]{2,1,0:T(8,128)(2,1)S(1)}, bf16[8,16,256]{2,1,0:T(8,128)(2,1)}, u32[]{:S(2)}) copy-start(bf16[8,16,256]{2,1,0:T(8,128)(2,1)} %refs_0_.7) | copy-start | bytes 196612
  5.4 5.9 %copy-start.1 = (bf16[7,7,256]{2,1,0:T(8,128)(2,1)S(1)}, bf16[7,7,256]{2,1,0:T(8,128)(2,1)}, u32[]{:S(2)}) copy-start(bf16[7,7,256]{2,1,0:T(8,128)(2,1)} %refs_5_.1) | copy-start | bytes 75268
  6.0 8.8 %collective-permute-start.1 = (bf16[128,256]{1,0:T(8,128)(2,1)S(1)}, bf16[128,256]{1,0:T(8,128)(2,1)S(1)}, u32[]{:S(2)}, u32[]{:S(2)}) collective-permute-start(bf16[128,256]{1,0:T(8,128)(2,1)S(1)} %get-tuple-element.23), channel_id=1, source_target_pairs={{0,1},{1,0},{2,3},{3,2},{4,5},{5,4},{6,7},{7,6},{8,9},{9,8},{10,11... | collective-permute-start | bytes 196616 | tf_op jit(solution)/shard_map/ppermute | solution.py:285
  6.1 8.7 %collective-permute-start.2 = (bf16[128,256]{1,0:T(8,128)(2,1)S(1)}, bf16[128,256]{1,0:T(8,128)(2,1)S(1)}, u32[]{:S(2)}, u32[]{:S(2)}) collective-permute-start(bf16[128,256]{1,0:T(8,128)(2,1)S(1)} %get-tuple-element.24), channel_id=1, source_target_pairs={{0,15},{1,2},{2,1},{3,4},{4,3},{5,6},{6,5},{7,8},{8,7},{9,10},{10,... | collective-permute-start | bytes 196616 | tf_op jit(solution)/shard_map/ppermute | solution.py:311
  17.8 4.5 %collective-permute-start.3 = (bf16[32,256]{1,0:T(8,128)(2,1)S(1)}, bf16[32,256]{1,0:T(8,128)(2,1)S(1)}, u32[]{:S(2)}, u32[]{:S(2)}) collective-permute-start(bf16[32,256]{1,0:T(8,128)(2,1)S(1)} %get-tuple-element.29), channel_id=1, source_target_pairs={{0,4},{1,5},{2,6},{3,7},{4,0},{5,1},{6,2},{7,3},{8,12},{9,13},{10,... | collective-permute-start | bytes 49160 | tf_op jit(solution)/shard_map/ppermute | solution.py:285
  17.9 4.7 %collective-permute-start.4 = (bf16[32,256]{1,0:T(8,128)(2,1)S(1)}, bf16[32,256]{1,0:T(8,128)(2,1)S(1)}, u32[]{:S(2)}, u32[]{:S(2)}) collective-permute-start(bf16[32,256]{1,0:T(8,128)(2,1)S(1)} %get-tuple-element.30), channel_id=1, source_target_pairs={{0,8},{1,9},{2,10},{3,11},{4,12},{5,13},{6,14},{7,15},{8,0},{9,1},... | collective-permute-start | bytes 49160 | tf_op jit(solution)/shard_map/ppermute | solution.py:285
  18.9 5.5 %collective-permute-start.5 = (bf16[32,256]{1,0:T(8,128)(2,1)S(1)}, bf16[32,256]{1,0:T(8,128)(2,1)S(1)}, u32[]{:S(2)}, u32[]{:S(2)}) collective-permute-start(bf16[32,256]{1,0:T(8,128)(2,1)S(1)} %get-tuple-element.31), channel_id=1, source_target_pairs={{0,12},{1,13},{2,14},{3,15},{4,8},{5,9},{6,10},{7,11},{8,4},{9,5},... | collective-permute-start | bytes 49160 | tf_op jit(solution)/shard_map/ppermute | solution.py:285
  24.4 4.3 %collective-permute-start.6 = (bf16[128,256]{1,0:T(8,128)(2,1)S(1)}, bf16[128,256]{1,0:T(8,128)(2,1)S(1)}, u32[]{:S(2)}, u32[]{:S(2)}) collective-permute-start(bf16[128,256]{1,0:T(8,128)(2,1)S(1)} %constant_dynamic-update-slice_fusion.refs_0_), channel_id=1, source_target_pairs={{0,2},{1,3},{2,0},{3,1},{4,6},{5,7},{6,4},{7,5},{8,10},{9,11},{10,... | collective-permute-start | bytes 196616 | tf_op jit(solution)/shard_map/ppermute | solution.py:285
  25.0 3.7 %collective-permute-start.7 = (bf16[128,256]{1,0:T(8,128)(2,1)S(1)}, bf16[128,256]{1,0:T(8,128)(2,1)S(1)}, u32[]{:S(2)}, u32[]{:S(2)}) collective-permute-start(bf16[128,256]{1,0:T(8,128)(2,1)S(1)} %constant_dynamic-update-slice_fusion.refs_0_), channel_id=1, source_target_pairs={{0,1},{1,0},{2,3},{3,2},{4,5},{5,4},{6,7},{7,6},{8,9},{9,8},{10,11... | collective-permute-start | bytes 196616 | tf_op jit(solution)/shard_map/ppermute | solution.py:285
  28.7 1.3 %collective-permute-start.8 = (bf16[128,256]{1,0:T(8,128)(2,1)S(1)}, bf16[128,256]{1,0:T(8,128)(2,1)S(1)}, u32[]{:S(2)}, u32[]{:S(2)}) collective-permute-start(bf16[128,256]{1,0:T(8,128)(2,1)S(1)} %collective-permute-done.6.refs_1_), channel_id=1, source_target_pairs={{0,1},{1,0},{2,3},{3,2},{4,5},{5,4},{6,7},{7,6},{8,9},{9,8},{10,11... | collective-permute-start | bytes 196616 | tf_op jit(solution)/shard_map/ppermute | solution.py:285
  31.1 4.5 %collective-permute-start.9 = (bf16[32,256]{1,0:T(8,128)(2,1)S(1)}, bf16[32,256]{1,0:T(8,128)(2,1)S(1)}, u32[]{:S(2)}, u32[]{:S(2)}) collective-permute-start(bf16[32,256]{1,0:T(8,128)(2,1)S(1)} %get-tuple-element.34), channel_id=1, source_target_pairs={{0,4},{1,5},{2,6},{3,7},{4,0},{5,1},{6,2},{7,3},{8,12},{9,13},{10,... | collective-permute-start | bytes 49160 | tf_op jit(solution)/shard_map/ppermute | solution.py:285
  31.4 5.5 %collective-permute-start.10 = (bf16[32,256]{1,0:T(8,128)(2,1)S(1)}, bf16[32,256]{1,0:T(8,128)(2,1)S(1)}, u32[]{:S(2)}, u32[]{:S(2)}) collective-permute-start(bf16[32,256]{1,0:T(8,128)(2,1)S(1)} %get-tuple-element.35), channel_id=1, source_target_pairs={{0,8},{1,9},{2,10},{3,11},{4,12},{5,13},{6,14},{7,15},{8,0},{9,1},... | collective-permute-start | bytes 49160 | tf_op jit(solution)/shard_map/ppermute | solution.py:285
  35.1 5.5 %collective-permute-start.11 = (bf16[32,256]{1,0:T(8,128)(2,1)S(1)}, bf16[32,256]{1,0:T(8,128)(2,1)S(1)}, u32[]{:S(2)}, u32[]{:S(2)}) collective-permute-start(bf16[32,256]{1,0:T(8,128)(2,1)S(1)} %get-tuple-element.36), channel_id=1, source_target_pairs={{0,12},{1,13},{2,14},{3,15},{4,8},{5,9},{6,10},{7,11},{8,4},{9,5},... | collective-permute-start | bytes 49160 | tf_op jit(solution)/shard_map/ppermute | solution.py:285

commit v5 on v4

--- a/solution.py
+++ b/solution.py
@@ -36,7 +36,13 @@
 
 
 def gelu(values):
-    return 0.5 * values * (1.0 + lax.erf(values * 0.5**0.5))
+    size = jnp.abs(values)
+    t = 1.0 / (1.0 + (0.3275911 * 0.5**0.5) * size)
+    tail = 1.061405429 * t - 1.453152027
+    for coefficient in (1.421413741, -0.284496736, 0.254829592):
+        tail = tail * t + coefficient
+    tail = (0.5 * size * t) * tail * jnp.exp(-0.5 * values * values)
+    return jnp.maximum(values, 0.0) - tail
 
 
 def attend(queries, keys, values, mask):
@@ -107,10 +113,15 @@
                 acc = acc + block[a : a + all_rows] * tap
         parts.append(acc.reshape(cells, LANES))
     normed = layer_norm(jnp.concatenate(parts, axis=-1)).astype(bf16)
-    total = center.reshape(cells, channels)
-    for k in range(0, expand_ref.shape[1], channels):
-        wide = gelu(dot(normed, expand_ref[:, k : k + channels])).astype(bf16)
-        total = total + dot(wide, reduce_ref[k : k + channels])
+
+    def widen(k, total):
+        part = pl.ds(pl.multiple_of(k * channels, channels), channels)
+        wide = gelu(dot(normed, expand_ref[:, part])).astype(bf16)
+        return total + dot(wide, reduce_ref[part])
+
+    total = lax.fori_loop(
+        0, expand_ref.shape[1] // channels, widen, center.reshape(cells, channels)
+    )
     block_one = total.astype(bf16)
     one[...] = block_one
     every = layer_norm(block_one.astype(f32)).astype(bf16)
@@ -234,20 +245,24 @@
 
 def last_kernel(levels, place_ref, *refs):
     parts = refs[:levels]
-    inner_ref, outer_ref, attn_ref, out_ref, back = refs[levels:]
+    inner_ref, outer_ref, attn_ref, out_ref = refs[levels:]
     rows, cols, channels = out_ref.shape
     columns = 2 * SIDE
-    some = parts[0].shape[0]
+    some = rows // levels
+    every = jnp.concatenate([part[...] for part in parts], axis=0)
+    change = dot(every, attn_ref[3]).reshape(levels, some, cols, channels)
     for k in range(levels):
         start = (place_ref[2] ^ k) * some
-        back[pl.ds(pl.multiple_of(start, some), some)] = parts[k][...]
-    change = dot(back[...], attn_ref[3]).reshape(rows, cols, channels)
-    inner = inner_ref[...].astype(f32).reshape(rows, cols - columns, channels)
-    outer = outer_ref[...].astype(f32).reshape(rows, columns, channels)
-    inner = inner + change[:, : cols - columns]
-    outer = outer + change[:, cols - columns :]
-    total = jnp.concatenate([outer[:, SIDE:], inner, outer[:, :SIDE]], axis=1)
-    out_ref[...] = total.astype(bf16)
+
+        def state(ref, width):
+            count = some * width
+            place = pl.ds(pl.multiple_of(start * width, count), count)
+            return ref[place].astype(f32).reshape(some, width, channels)
+
+        inner = state(inner_ref, cols - columns) + change[k, :, : cols - columns]
+        outer = state(outer_ref, columns) + change[k, :, cols - columns :]
+        total = jnp.concatenate([outer[:, SIDE:], inner, outer[:, :SIDE]], axis=1)
+        out_ref[pl.ds(start, some)] = total.astype(bf16)
 
 
 def call(
@@ -284,6 +299,10 @@
     def swap(piece, mask):
         return lax.ppermute(piece, "lon", [(j, j ^ mask) for j in range(nlon)])
 
+    def exchange(pieces):
+        moved = [swap(pieces[k], k * column) for k in range(levels - 1, 0, -1)]
+        return [pieces[0]] + moved[::-1]
+
     tiles = [field]
     for s in range(1, nlat):
         tiles.append(lax.ppermute(field, "lat", [((i + s) % nlat, i) for i in range(nlat)]))
@@ -339,7 +358,7 @@
         flops=work,
     )
 
-    parts = [parts[0]] + [swap(parts[k], k * column) for k in range(1, levels)]
+    parts = exchange(parts)
     circle = [jnp.concatenate(parts, axis=0)]
     mask = column // 2
     while mask:
@@ -348,12 +367,11 @@
     mixes = call(
         functools.partial(circle_kernel, levels, some), [piece] * levels, [*circle, lon_proj]
     )
-    mixes = [mixes[0]] + [swap(mixes[k], k * column) for k in range(1, levels)]
+    mixes = exchange(mixes)
     (out,) = call(
         functools.partial(last_kernel, levels),
         [(rows, cols, channels)],
         [place, *mixes, inner_two, outer_two, lon_proj],
-        [pltpu.VMEM((rows * cols, channels), bf16)],
         prefetch=1,
     )
     return out

time: 42.2 us -> 44.5 us (1.055)
  Pallas kernels: 11.4 us -> 13.7 us
  starting transfers between devices: 18.5 us -> 17.9 us
  waiting for transfers between devices: 12 us -> 12.6 us
    pallas_call x6, Pallas kernels: 11.4 us -> 13.7 us  [call(): pl.pallas_call(kernel, out_shape=shapes, in_specs=[smem] * prefetch + [gi...]
    ppermute x10, starting transfers between devices: 10.3 us -> 9.73 us  [swap(): return lax.ppermute(piece, 'lon', [(j, j ^ mask) for j in range(nlon)])]
    ppermute x10, waiting for transfers between devices: 11.4 us -> 12 us  [swap(): return lax.ppermute(piece, 'lon', [(j, j ^ mask) for j in range(nlon)])]
  transfers between devices with their start and end apart: 12 -> 12, of which waited for: 7 -> 7; matrix products, arithmetic and copies ran while one was open for 0% -> 0% of each run, Pallas kernels for 13% -> 14%
where the time goes in v5:
time: 44.5 us; the launch traced here: 44.4 us
  starting transfers between devices  17.9 us (40%)
  Pallas kernels  13.7 us (31%)
  waiting for transfers between devices  12.6 us (28%)
    pallas_call x6, Pallas kernels, call(): pl.pallas_call(kernel, out_shape=shapes, in_specs=[smem] * prefetch + [gi...  13.7 us
    ppermute x10, waiting for transfers between devices, swap(): return lax.ppermute(piece, 'lon', [(j, j ^ mask) for j in range(nlon)])  12 us
    ppermute x10, starting transfers between devices, swap(): return lax.ppermute(piece, 'lon', [(j, j ^ mask) for j in range(nlon)])  9.73 us
    ppermute x1, starting transfers between devices, shards(): lax.ppermute(far, 'lon', [(j, (j - 1) % nlon if j % 2 == 0 else (j + 1) %...  5.19 us
    ppermute x1, starting transfers between devices, shards(): lax.ppermute(field, 'lat', [((i + s) % nlat, i) for i in range(nlat)])  2.94 us
  transfers between devices with their start and end apart: 12, of which 7 were waited for; matrix products, arithmetic and copies ran while one was open for 0% of the time, Pallas kernels for 14%

profile of v5, /device:TPU:0, one launch (start us, length us, event | category | flops | bytes accessed | tf_op | source)
XLA Modules:
  0.0 44.4 jit_solution(5184207253846512497)
XLA Ops:
  0.0 2.9 %collective-permute-start = (bf16[8,16,256]{2,1,0:T(8,128)(2,1)}, bf16[8,16,256]{2,1,0:T(8,128)(2,1)S(1)}, u32[]{:S(2)}, u32[]{:S(2)}) collective-permute-start(bf16[8,16,256]{2,1,0:T(8,128)(2,1)} %refs_0_.7), channel_id=1, source_target_pairs={{16,0},{0,16},{17,1},{1,17},{18,2},{2,18},{19,3},{3,19},{20,4},{4,... | collective-permute-start | bytes 196616 | tf_op jit(solution)/shard_map/ppermute | solution.py:308
  2.9 0.0 copy-start
  2.9 1.8 %shard_map.64 = (bf16[256,1024]{1,0:T(8,128)(2,1)S(1)}, bf16[1024,256]{1,0:T(8,128)(2,1)S(1)}, bf16[4,256,256]{2,1,0:T(8,128)(2,1)S(1)}, bf16[4,256,256]{2,1,0:T(8,128)(2,1)S(1)}) custom-call(bf16[256,1024]{1,0:T(8,128)(2,1)} %refs_0_.4, bf16[1024,256]{1,0:T(8,128)(2,1)} %refs_1_.1, bf16[4,256,256]{2,1,0:T(8,128)(2,1)} %refs_2_.2, bf16[4,256,256]{2,1,0:T(8,128)(2,1)} %refs_3_.1), custom_call_target="tpu_custom_call" | custom-call | bytes 2097152 | tf_op jit(solution)/shard_map/pallas_call | solution.py:276
  4.7 0.1 pad_add_fusion.place_ref
  4.8 0.6 %collective-permute-done.refs_1_ = bf16[8,16,256]{2,1,0:T(8,128)(2,1)S(1)} collective-permute-done((bf16[8,16,256]{2,1,0:T(8,128)(2,1)}, bf16[8,16,256]{2,1,0:T(8,128)(2,1)S(1)}, u32[]{:S(2)}, u32[]{:S(2)}) %collective-permute-start) | collective-permute-done | bytes 65568 | tf_op jit(solution)/shard_map/ppermute | solution.py:308
  5.4 0.0 copy-done
  5.4 0.0 copy-start.1
  5.4 0.6 %shard_map.65 = (bf16[128,256]{1,0:T(8,128)(2,1)S(1)}, bf16[128,256]{1,0:T(8,128)(2,1)S(1)}) custom-call(s32[3]{0:T(128)S(1)} %pad_add_fusion.place_ref, bf16[8,16,256]{2,1,0:T(8,128)(2,1)S(1)} %copy-done, bf16[8,16,256]{2,1,0:T(8,128)(2,1)S(1)} %collective-permute-done.refs_1_, bf16[1024,256]{1,0:T(8,128)(2,1)S(1)} %get-tuple-element.22.refs_2_.refs_4_.refs_7_), custom_call_target="tpu_custom_call" | custom-call | bytes 655372 | tf_op jit(solution)/shard_map/pallas_call | solution.py:276
  6.0 0.1 collective-permute-start.1
  6.1 5.2 %collective-permute-start.2 = (bf16[128,256]{1,0:T(8,128)(2,1)S(1)}, bf16[128,256]{1,0:T(8,128)(2,1)S(1)}, u32[]{:S(2)}, u32[]{:S(2)}) collective-permute-start(bf16[128,256]{1,0:T(8,128)(2,1)S(1)} %get-tuple-element.24), channel_id=1, source_target_pairs={{0,15},{1,2},{2,1},{3,4},{4,3},{5,6},{6,5},{7,8},{8,7},{9,10},{10,... | collective-permute-start | bytes 196616 | tf_op jit(solution)/shard_map/ppermute | solution.py:330
  11.3 0.0 copy-done.1
  11.3 4.7 %shard_map.66 = (bf16[64,256]{1,0:T(8,128)(2,1)S(1)}, bf16[64,256]{1,0:T(8,128)(2,1)S(1)}) custom-call(s32[3]{0:T(128)S(1)} %pad_add_fusion.place_ref, bf16[8,16,256]{2,1,0:T(8,128)(2,1)S(1)} %copy-done, bf16[8,16,256]{2,1,0:T(8,128)(2,1)S(1)} %collective-permute-done.refs_1_, bf16[7,7,256]{2,1,0:T(8,128)(2,1)S(1)} %copy-done.1, ...), custom_call_target="tpu_custom_call" | custom-call | flops 134217728 | bytes 1729036 | tf_op jit(solution)/shard_map/pallas_call | solution.py:276
  15.9 0.0 collective-permute-done.1.refs_2_
  16.0 0.0 collective-permute-done.2.refs_3_
  16.0 4.1 %shard_map.67 = (bf16[64,256]{1,0:T(8,128)(2,1)S(1)}, bf16[32,256]{1,0:T(8,128)(2,1)S(1)}, bf16[32,256]{1,0:T(8,128)(2,1)S(1)}, bf16[32,256]{1,0:T(8,128)(2,1)S(1)}, bf16[32,256]{1,0:T(8,128)(2,1)S(1)}) custom-call(s32[3]{0:T(128)S(1)} %pad_add_fusion.place_ref, bf16[8,16,256]{2,1,0:T(8,128)(2,1)S(1)} %copy-done, ...), custom_call_target="tpu_custom_call" | custom-call | flops 134217728 | bytes 1892876 | tf_op jit(solution)/shard_map/pallas_call | solution.py:276
  20.1 0.1 collective-permute-start.3
  20.2 1.0 %collective-permute-start.4 = (bf16[32,256]{1,0:T(8,128)(2,1)S(1)}, bf16[32,256]{1,0:T(8,128)(2,1)S(1)}, u32[]{:S(2)}, u32[]{:S(2)}) collective-permute-start(bf16[32,256]{1,0:T(8,128)(2,1)S(1)} %get-tuple-element.30), channel_id=1, source_target_pairs={{0,8},{1,9},{2,10},{3,11},{4,12},{5,13},{6,14},{7,15},{8,0},{9,1},... | collective-permute-start | bytes 49160 | tf_op jit(solution)/shard_map/ppermute | solution.py:300
  21.2 3.4 %collective-permute-start.5 = (bf16[32,256]{1,0:T(8,128)(2,1)S(1)}, bf16[32,256]{1,0:T(8,128)(2,1)S(1)}, u32[]{:S(2)}, u32[]{:S(2)}) collective-permute-start(bf16[32,256]{1,0:T(8,128)(2,1)S(1)} %get-tuple-element.31), channel_id=1, source_target_pairs={{0,12},{1,13},{2,14},{3,15},{4,8},{5,9},{6,10},{7,11},{8,4},{9,5},... | collective-permute-start | bytes 49160 | tf_op jit(solution)/shard_map/ppermute | solution.py:300
  24.6 0.0 collective-permute-done.3
  24.6 0.3 collective-permute-done.4
  24.9 1.8 %collective-permute-done.5 = bf16[32,256]{1,0:T(8,128)(2,1)S(1)} collective-permute-done((bf16[32,256]{1,0:T(8,128)(2,1)S(1)}, bf16[32,256]{1,0:T(8,128)(2,1)S(1)}, u32[]{:S(2)}, u32[]{:S(2)}) %collective-permute-start.5) | collective-permute-done | bytes 16416 | tf_op jit(solution)/shard_map/ppermute | solution.py:300
  26.7 0.8 %collective-permute-start.6 = (bf16[128,256]{1,0:T(8,128)(2,1)S(1)}, bf16[128,256]{1,0:T(8,128)(2,1)S(1)}, u32[]{:S(2)}, u32[]{:S(2)}) collective-permute-start(bf16[128,256]{1,0:T(8,128)(2,1)S(1)} %constant_dynamic-update-slice_fusion.refs_0_), channel_id=1, source_target_pairs={{0,2},{1,3},{2,0},{3,1},{4,6},{5,7},{6,4},{7,5},{8,10},{9,11},{10,... | collective-permute-start | bytes 196616 | tf_op jit(solution)/shard_map/ppermute | solution.py:300
  27.5 0.0 collective-permute-start.7
  27.5 3.5 %collective-permute-done.6.refs_1_ = bf16[128,256]{1,0:T(8,128)(2,1)S(1)} collective-permute-done((bf16[128,256]{1,0:T(8,128)(2,1)S(1)}, bf16[128,256]{1,0:T(8,128)(2,1)S(1)}, u32[]{:S(2)}, u32[]{:S(2)}) %collective-permute-start.6) | collective-permute-done | bytes 65568 | tf_op jit(solution)/shard_map/ppermute | solution.py:300
  31.0 0.0 collective-permute-start.8
  31.0 0.0 collective-permute-done.7.refs_2_
  31.0 1.2 %collective-permute-done.8.refs_3_ = bf16[128,256]{1,0:T(8,128)(2,1)S(1)} collective-permute-done((bf16[128,256]{1,0:T(8,128)(2,1)S(1)}, bf16[128,256]{1,0:T(8,128)(2,1)S(1)}, u32[]{:S(2)}, u32[]{:S(2)}) %collective-permute-start.8) | collective-permute-done | bytes 65568 | tf_op jit(solution)/shard_map/ppermute | solution.py:300
  32.3 1.2 %shard_map.68 = (bf16[32,256]{1,0:T(8,128)(2,1)S(1)}, bf16[32,256]{1,0:T(8,128)(2,1)S(1)}, bf16[32,256]{1,0:T(8,128)(2,1)S(1)}, bf16[32,256]{1,0:T(8,128)(2,1)S(1)}) custom-call(bf16[128,256]{1,0:T(8,128)(2,1)S(1)} %constant_dynamic-update-slice_fusion.refs_0_, bf16[128,256]{1,0:T(8,128)(2,1)S(1)} %collective-permute-done.6.refs_1_, ...), custom_call_target="tpu_custom_call" | custom-call | bytes 786432 | tf_op jit(solution)/shard_map/pallas_call | solution.py:276
  33.5 0.3 collective-permute-start.9
  33.7 3.8 %collective-permute-start.10 = (bf16[32,256]{1,0:T(8,128)(2,1)S(1)}, bf16[32,256]{1,0:T(8,128)(2,1)S(1)}, u32[]{:S(2)}, u32[]{:S(2)}) collective-permute-start(bf16[32,256]{1,0:T(8,128)(2,1)S(1)} %get-tuple-element.35), channel_id=1, source_target_pairs={{0,8},{1,9},{2,10},{3,11},{4,12},{5,13},{6,14},{7,15},{8,0},{9,1},... | collective-permute-start | bytes 49160 | tf_op jit(solution)/shard_map/ppermute | solution.py:300
  37.5 0.4 %collective-permute-start.11 = (bf16[32,256]{1,0:T(8,128)(2,1)S(1)}, bf16[32,256]{1,0:T(8,128)(2,1)S(1)}, u32[]{:S(2)}, u32[]{:S(2)}) collective-permute-start(bf16[32,256]{1,0:T(8,128)(2,1)S(1)} %get-tuple-element.36), channel_id=1, source_target_pairs={{0,12},{1,13},{2,14},{3,15},{4,8},{5,9},{6,10},{7,11},{8,4},{9,5},... | collective-permute-start | bytes 49160 | tf_op jit(solution)/shard_map/ppermute | solution.py:300
  37.9 0.0 collective-permute-done.9.refs_1_
  37.9 1.3 %collective-permute-done.10.refs_2_ = bf16[32,256]{1,0:T(8,128)(2,1)S(1)} collective-permute-done((bf16[32,256]{1,0:T(8,128)(2,1)S(1)}, bf16[32,256]{1,0:T(8,128)(2,1)S(1)}, u32[]{:S(2)}, u32[]{:S(2)}) %collective-permute-start.10) | collective-permute-done | bytes 16416 | tf_op jit(solution)/shard_map/ppermute | solution.py:300
  39.2 3.8 %collective-permute-done.11.refs_3_ = bf16[32,256]{1,0:T(8,128)(2,1)S(1)} collective-permute-done((bf16[32,256]{1,0:T(8,128)(2,1)S(1)}, bf16[32,256]{1,0:T(8,128)(2,1)S(1)}, u32[]{:S(2)}, u32[]{:S(2)}) %collective-permute-start.11) | collective-permute-done | bytes 16416 | tf_op jit(solution)/shard_map/ppermute | solution.py:300
  43.0 1.3 %shard_map.69 = bf16[8,16,256]{2,1,0:T(8,128)(2,1)} custom-call(s32[3]{0:T(128)S(1)} %pad_add_fusion.place_ref, bf16[32,256]{1,0:T(8,128)(2,1)S(1)} %get-tuple-element.33.refs_0_, bf16[32,256]{1,0:T(8,128)(2,1)S(1)} %collective-permute-done.9.refs_1_, bf16[32,256]{1,0:T(8,128)(2,1)S(1)} %collective-permute-done.10.refs_2_, ...), custom_call_target="tpu_custom_call" | custom-call | bytes 655372 | tf_op jit(solution)/shard_map/pallas_call | solution.py:276
  (4 shorter events, 0.0 us)
Async XLA Ops:
  0.0 5.4 %collective-permute-start = (bf16[8,16,256]{2,1,0:T(8,128)(2,1)}, bf16[8,16,256]{2,1,0:T(8,128)(2,1)S(1)}, u32[]{:S(2)}, u32[]{:S(2)}) collective-permute-start(bf16[8,16,256]{2,1,0:T(8,128)(2,1)} %refs_0_.7), channel_id=1, source_target_pairs={{16,0},{0,16},{17,1},{1,17},{18,2},{2,18},{19,3},{3,19},{20,4},{4,... | collective-permute-start | bytes 196616 | tf_op jit(solution)/shard_map/ppermute | solution.py:308
  2.9 2.5 %copy-start = (bf16[8,16,256]{2,1,0:T(8,128)(2,1)S(1)}, bf16[8,16,256]{2,1,0:T(8,128)(2,1)}, u32[]{:S(2)}) copy-start(bf16[8,16,256]{2,1,0:T(8,128)(2,1)} %refs_0_.7) | copy-start | bytes 196612
  5.4 5.9 %copy-start.1 = (bf16[7,7,256]{2,1,0:T(8,128)(2,1)S(1)}, bf16[7,7,256]{2,1,0:T(8,128)(2,1)}, u32[]{:S(2)}) copy-start(bf16[7,7,256]{2,1,0:T(8,128)(2,1)} %refs_5_.1) | copy-start | bytes 75268
  6.0 10.0 %collective-permute-start.1 = (bf16[128,256]{1,0:T(8,128)(2,1)S(1)}, bf16[128,256]{1,0:T(8,128)(2,1)S(1)}, u32[]{:S(2)}, u32[]{:S(2)}) collective-permute-start(bf16[128,256]{1,0:T(8,128)(2,1)S(1)} %get-tuple-element.23), channel_id=1, source_target_pairs={{0,1},{1,0},{2,3},{3,2},{4,5},{5,4},{6,7},{7,6},{8,9},{9,8},{10,11... | collective-permute-start | bytes 196616 | tf_op jit(solution)/shard_map/ppermute | solution.py:300
  6.1 9.9 %collective-permute-start.2 = (bf16[128,256]{1,0:T(8,128)(2,1)S(1)}, bf16[128,256]{1,0:T(8,128)(2,1)S(1)}, u32[]{:S(2)}, u32[]{:S(2)}) collective-permute-start(bf16[128,256]{1,0:T(8,128)(2,1)S(1)} %get-tuple-element.24), channel_id=1, source_target_pairs={{0,15},{1,2},{2,1},{3,4},{4,3},{5,6},{6,5},{7,8},{8,7},{9,10},{10,... | collective-permute-start | bytes 196616 | tf_op jit(solution)/shard_map/ppermute | solution.py:330
  20.1 4.5 %collective-permute-start.3 = (bf16[32,256]{1,0:T(8,128)(2,1)S(1)}, bf16[32,256]{1,0:T(8,128)(2,1)S(1)}, u32[]{:S(2)}, u32[]{:S(2)}) collective-permute-start(bf16[32,256]{1,0:T(8,128)(2,1)S(1)} %get-tuple-element.29), channel_id=1, source_target_pairs={{0,4},{1,5},{2,6},{3,7},{4,0},{5,1},{6,2},{7,3},{8,12},{9,13},{10,... | collective-permute-start | bytes 49160 | tf_op jit(solution)/shard_map/ppermute | solution.py:300
  20.2 4.7 %collective-permute-start.4 = (bf16[32,256]{1,0:T(8,128)(2,1)S(1)}, bf16[32,256]{1,0:T(8,128)(2,1)S(1)}, u32[]{:S(2)}, u32[]{:S(2)}) collective-permute-start(bf16[32,256]{1,0:T(8,128)(2,1)S(1)} %get-tuple-element.30), channel_id=1, source_target_pairs={{0,8},{1,9},{2,10},{3,11},{4,12},{5,13},{6,14},{7,15},{8,0},{9,1},... | collective-permute-start | bytes 49160 | tf_op jit(solution)/shard_map/ppermute | solution.py:300
  21.2 5.5 %collective-permute-start.5 = (bf16[32,256]{1,0:T(8,128)(2,1)S(1)}, bf16[32,256]{1,0:T(8,128)(2,1)S(1)}, u32[]{:S(2)}, u32[]{:S(2)}) collective-permute-start(bf16[32,256]{1,0:T(8,128)(2,1)S(1)} %get-tuple-element.31), channel_id=1, source_target_pairs={{0,12},{1,13},{2,14},{3,15},{4,8},{5,9},{6,10},{7,11},{8,4},{9,5},... | collective-permute-start | bytes 49160 | tf_op jit(solution)/shard_map/ppermute | solution.py:300
  26.7 4.3 %collective-permute-start.6 = (bf16[128,256]{1,0:T(8,128)(2,1)S(1)}, bf16[128,256]{1,0:T(8,128)(2,1)S(1)}, u32[]{:S(2)}, u32[]{:S(2)}) collective-permute-start(bf16[128,256]{1,0:T(8,128)(2,1)S(1)} %constant_dynamic-update-slice_fusion.refs_0_), channel_id=1, source_target_pairs={{0,2},{1,3},{2,0},{3,1},{4,6},{5,7},{6,4},{7,5},{8,10},{9,11},{10,... | collective-permute-start | bytes 196616 | tf_op jit(solution)/shard_map/ppermute | solution.py:300
  27.5 3.5 %collective-permute-start.7 = (bf16[128,256]{1,0:T(8,128)(2,1)S(1)}, bf16[128,256]{1,0:T(8,128)(2,1)S(1)}, u32[]{:S(2)}, u32[]{:S(2)}) collective-permute-start(bf16[128,256]{1,0:T(8,128)(2,1)S(1)} %constant_dynamic-update-slice_fusion.refs_0_), channel_id=1, source_target_pairs={{0,1},{1,0},{2,3},{3,2},{4,5},{5,4},{6,7},{7,6},{8,9},{9,8},{10,11... | collective-permute-start | bytes 196616 | tf_op jit(solution)/shard_map/ppermute | solution.py:300
  31.0 1.3 %collective-permute-start.8 = (bf16[128,256]{1,0:T(8,128)(2,1)S(1)}, bf16[128,256]{1,0:T(8,128)(2,1)S(1)}, u32[]{:S(2)}, u32[]{:S(2)}) collective-permute-start(bf16[128,256]{1,0:T(8,128)(2,1)S(1)} %collective-permute-done.6.refs_1_), channel_id=1, source_target_pairs={{0,1},{1,0},{2,3},{3,2},{4,5},{5,4},{6,7},{7,6},{8,9},{9,8},{10,11... | collective-permute-start | bytes 196616 | tf_op jit(solution)/shard_map/ppermute | solution.py:300
  33.5 4.5 %collective-permute-start.9 = (bf16[32,256]{1,0:T(8,128)(2,1)S(1)}, bf16[32,256]{1,0:T(8,128)(2,1)S(1)}, u32[]{:S(2)}, u32[]{:S(2)}) collective-permute-start(bf16[32,256]{1,0:T(8,128)(2,1)S(1)} %get-tuple-element.34), channel_id=1, source_target_pairs={{0,4},{1,5},{2,6},{3,7},{4,0},{5,1},{6,2},{7,3},{8,12},{9,13},{10,... | collective-permute-start | bytes 49160 | tf_op jit(solution)/shard_map/ppermute | solution.py:300
  33.7 5.5 %collective-permute-start.10 = (bf16[32,256]{1,0:T(8,128)(2,1)S(1)}, bf16[32,256]{1,0:T(8,128)(2,1)S(1)}, u32[]{:S(2)}, u32[]{:S(2)}) collective-permute-start(bf16[32,256]{1,0:T(8,128)(2,1)S(1)} %get-tuple-element.35), channel_id=1, source_target_pairs={{0,8},{1,9},{2,10},{3,11},{4,12},{5,13},{6,14},{7,15},{8,0},{9,1},... | collective-permute-start | bytes 49160 | tf_op jit(solution)/shard_map/ppermute | solution.py:300
  37.5 5.5 %collective-permute-start.11 = (bf16[32,256]{1,0:T(8,128)(2,1)S(1)}, bf16[32,256]{1,0:T(8,128)(2,1)S(1)}, u32[]{:S(2)}, u32[]{:S(2)}) collective-permute-start(bf16[32,256]{1,0:T(8,128)(2,1)S(1)} %get-tuple-element.36), channel_id=1, source_target_pairs={{0,12},{1,13},{2,14},{3,15},{4,8},{5,9},{6,10},{7,11},{8,4},{9,5},... | collective-permute-start | bytes 49160 | tf_op jit(solution)/shard_map/ppermute | solution.py:300

commit v6 on v5

--- a/solution.py
+++ b/solution.py
@@ -83,15 +83,19 @@
         copy.wait()
 
 
-def strip_kernel(nlat, place_ref, *refs):
+def level_of(levels):
+    return lax.axis_index("lon") // (lax.axis_size("lon") // levels)
+
+
+def strip_kernel(nlat, *refs):
     tiles = refs[:nlat]
     near_ref, far_ref, near, far = refs[nlat + 1 :]
     rows, cols, channels = tiles[0].shape
-    even = place_ref[1] == 0
+    even = lax.axis_index("lon") % 2 == 0
     for s in range(nlat):
         values = tiles[s][...].astype(f32)
         first, last = values[:, :STRIP], values[:, cols - STRIP :]
-        where = pl.ds(lax.rem(place_ref[0] + s, nlat) * rows, rows)
+        where = pl.ds(lax.rem(lax.axis_index("lat") + s, nlat) * rows, rows)
         near[where] = jnp.where(even, last, first)
         far[where] = jnp.where(even, first, last)
     near_ref[...] = near[...].reshape(near_ref.shape).astype(bf16)
@@ -115,13 +119,13 @@
     normed = layer_norm(jnp.concatenate(parts, axis=-1)).astype(bf16)
 
     def widen(k, total):
-        part = pl.ds(pl.multiple_of(k * channels, channels), channels)
+        part = slice(k * channels, (k + 1) * channels)
         wide = gelu(dot(normed, expand_ref[:, part])).astype(bf16)
         return total + dot(wide, reduce_ref[part])
 
-    total = lax.fori_loop(
-        0, expand_ref.shape[1] // channels, widen, center.reshape(cells, channels)
-    )
+    total = center.reshape(cells, channels)
+    for k in range(expand_ref.shape[1] // channels):
+        total = widen(k, total)
     block_one = total.astype(bf16)
     one[...] = block_one
     every = layer_norm(block_one.astype(f32)).astype(bf16)
@@ -156,14 +160,15 @@
     padded[HALO + all_rows :] = edge
 
 
-def inner_kernel(nlat, place_ref, *refs):
+def inner_kernel(nlat, *refs):
     tiles, refs = refs[:nlat], refs[nlat:]
     dw_ref, expand_ref, reduce_ref, attn_ref, two_ref, in_ref, padded, *scratch = refs
     rows, cols, channels = tiles[0].shape
     all_rows = rows * nlat
     columns = cols - 2 * SIDE
     clear(padded, all_rows)
-    fill_tiles(padded, place_ref[0], 0, tiles)
+    my_lat = lax.axis_index("lat")
+    fill_tiles(padded, my_lat, 0, tiles)
 
     def slab(b, c):
         first = SIDE - HALO + b
@@ -172,13 +177,13 @@
     center = padded[HALO : HALO + all_rows, SIDE : SIDE + columns]
     shape = (rows, all_rows, columns, channels)
     block_two, lon_in = chain(
-        place_ref[0], slab, shape, dw_ref, expand_ref, reduce_ref, attn_ref, center, scratch
+        my_lat, slab, shape, dw_ref, expand_ref, reduce_ref, attn_ref, center, scratch
     )
     two_ref[...] = block_two
     in_ref[...] = lon_in.astype(bf16)
 
 
-def outer_kernel(nlat, levels, place_ref, *refs):
+def outer_kernel(nlat, levels, *refs):
     tiles, refs = refs[:nlat], refs[nlat:]
     near_ref, far_ref, inner_in_ref, dw_ref, expand_ref, reduce_ref, attn_ref = refs[:7]
     two_ref, *refs = refs[7:]
@@ -189,10 +194,11 @@
     strip_shape = (all_rows, STRIP, channels)
     near = near_ref[...].astype(f32).reshape(strip_shape)
     far = far_ref[...].astype(f32).reshape(strip_shape)
-    even = place_ref[1] == 0
+    even = lax.axis_index("lon") % 2 == 0
     clear(padded, all_rows)
     fill(padded, all_rows, 0, jnp.where(even, far, near))
-    fill_tiles(padded, place_ref[0], STRIP, tiles)
+    my_lat = lax.axis_index("lat")
+    fill_tiles(padded, my_lat, STRIP, tiles)
     fill(padded, all_rows, STRIP + cols, jnp.where(even, near, far))
     sublane = lax.broadcasted_iota(jnp.int32, (1, columns, 1), 1)
 
@@ -211,7 +217,7 @@
     center = halves(0, slice(HALO, HALO + all_rows), 0, channels)
     shape = (rows, all_rows, columns, channels)
     block_two, lon_in = chain(
-        place_ref[0], slab, shape, dw_ref, expand_ref, reduce_ref, attn_ref, center, scratch
+        my_lat, slab, shape, dw_ref, expand_ref, reduce_ref, attn_ref, center, scratch
     )
     two_ref[...] = block_two
     inner = inner_in_ref[...].astype(f32).reshape(rows, cols - columns, channels)
@@ -219,7 +225,7 @@
     sent[...] = jnp.concatenate([inner, outer], axis=1).astype(bf16)
     some = rows // levels
     for k in range(levels):
-        part = sent[pl.ds((place_ref[2] ^ k) * some, some)]
+        part = sent[pl.ds((level_of(levels) ^ k) * some, some)]
         sent_refs[k][...] = part.reshape(sent_refs[k].shape)
 
 
@@ -243,7 +249,7 @@
             mix_refs[k][r * count : (r + 1) * count] = mix[k * count : (k + 1) * count]
 
 
-def last_kernel(levels, place_ref, *refs):
+def last_kernel(levels, *refs):
     parts = refs[:levels]
     inner_ref, outer_ref, attn_ref, out_ref = refs[levels:]
     rows, cols, channels = out_ref.shape
@@ -252,7 +258,7 @@
     every = jnp.concatenate([part[...] for part in parts], axis=0)
     change = dot(every, attn_ref[3]).reshape(levels, some, cols, channels)
     for k in range(levels):
-        start = (place_ref[2] ^ k) * some
+        start = (level_of(levels) ^ k) * some
 
         def state(ref, width):
             count = some * width
@@ -266,17 +272,16 @@
 
 
 def call(
-    kernel, outs, operands, scratch=(), any_space=False, prefetch=0, flops=0, grant=VMEM_BYTES
+    kernel, outs, operands, scratch=(), any_space=False, flops=0, grant=VMEM_BYTES
 ):
     vmem = pl.BlockSpec(memory_space=pltpu.VMEM)
     given = pl.BlockSpec(memory_space=pl.ANY) if any_space else vmem
-    smem = pl.BlockSpec(memory_space=pltpu.SMEM)
     shapes = [jax.ShapeDtypeStruct(shape, bf16) for shape in outs]
     moved = sum(x.size * x.dtype.itemsize for x in operands)
     result = pl.pallas_call(
         kernel,
         out_shape=shapes,
-        in_specs=[smem] * prefetch + [given] * (len(operands) - prefetch),
+        in_specs=[given] * len(operands),
         out_specs=[vmem] * len(outs),
         scratch_shapes=list(scratch),
         compiler_params=pltpu.CompilerParams(vmem_limit_bytes=grant),
@@ -288,13 +293,11 @@
 def shards(field, dw_weight, w_expand, w_reduce, lat_attn, lon_attn):
     rows, cols, channels = field.shape
     nlat, nlon = lax.axis_size("lat"), lax.axis_size("lon")
-    my_lat, my_lon = lax.axis_index("lat"), lax.axis_index("lon")
     levels = min(LEVELS, nlon)
     column = nlon // levels
     some = rows // levels
     all_rows = rows * nlat
     columns = 2 * SIDE
-    place = jnp.stack([my_lat, my_lon % 2, my_lon // column]).astype(jnp.int32)
 
     def swap(piece, mask):
         return lax.ppermute(piece, "lon", [(j, j ^ mask) for j in range(nlon)])
@@ -322,9 +325,8 @@
     near, far = call(
         functools.partial(strip_kernel, nlat),
         [strip, strip],
-        [place, *tiles, reduce],
+        [*tiles, reduce],
         [strip_scratch, strip_scratch],
-        prefetch=1,
     )
     near = swap(near, 1)
     far = lax.ppermute(
@@ -343,18 +345,16 @@
     inner_two, inner_in = call(
         functools.partial(inner_kernel, nlat),
         [(rows * (cols - columns), channels)] * 2,
-        [place, *tiles, dw_weight, expand, reduce, lat_proj],
+        [*tiles, dw_weight, expand, reduce, lat_proj],
         scratch(cols, cols - columns),
-        prefetch=1,
         flops=work,
     )
     piece = (some * cols, channels)
     outer_two, *parts = call(
         functools.partial(outer_kernel, nlat, levels),
         [(rows * columns, channels)] + [piece] * levels,
-        [place, *tiles, near, far, inner_in, dw_weight, expand, reduce, lat_proj],
+        [*tiles, near, far, inner_in, dw_weight, expand, reduce, lat_proj],
         [pltpu.VMEM((rows, cols, channels), bf16)] + scratch(cols + 2 * STRIP, columns),
-        prefetch=1,
         flops=work,
     )
 
@@ -371,8 +371,7 @@
     (out,) = call(
         functools.partial(last_kernel, levels),
         [(rows, cols, channels)],
-        [place, *mixes, inner_two, outer_two, lon_proj],
-        prefetch=1,
+        [*mixes, inner_two, outer_two, lon_proj],
     )
     return out
 

time: 44.5 us -> 40.4 us (0.908)
  Pallas kernels: 13.7 us -> 9.61 us
  starting transfers between devices: 17.9 us -> 18.7 us
  waiting for transfers between devices: 12.6 us -> 11.9 us
    pallas_call x6, Pallas kernels: 13.7 us -> 9.61 us  [call(): pl.pallas_call(kernel, out_shape=shapes, in_specs=[given] * len(operands)...]
    ppermute x10, starting transfers between devices: 9.73 us -> 10.6 us  [swap(): return lax.ppermute(piece, 'lon', [(j, j ^ mask) for j in range(nlon)])]
    ppermute x10, waiting for transfers between devices: 12 us -> 11.1 us  [swap(): return lax.ppermute(piece, 'lon', [(j, j ^ mask) for j in range(nlon)])]
  transfers between devices with their start and end apart: 12 -> 12, of which waited for: 7 -> 7; matrix products, arithmetic and copies ran while one was open for 0% -> 0% of each run, Pallas kernels for 14% -> 12%
where the time goes in v6:
time: 40.4 us; the launch traced here: 40.3 us
  starting transfers between devices  18.7 us (46%)
  waiting for transfers between devices  11.9 us (29%)
  Pallas kernels  9.61 us (24%)
    ppermute x10, waiting for transfers between devices, swap(): return lax.ppermute(piece, 'lon', [(j, j ^ mask) for j in range(nlon)])  11.1 us
    ppermute x10, starting transfers between devices, swap(): return lax.ppermute(piece, 'lon', [(j, j ^ mask) for j in range(nlon)])  10.6 us
    pallas_call x6, Pallas kernels, call(): pl.pallas_call(kernel, out_shape=shapes, in_specs=[given] * len(operands)...  9.61 us
    ppermute x1, starting transfers between devices, shards(): lax.ppermute(far, 'lon', [(j, (j - 1) % nlon if j % 2 == 0 else (j + 1) %...  5.12 us
    ppermute x1, starting transfers between devices, shards(): lax.ppermute(field, 'lat', [((i + s) % nlat, i) for i in range(nlat)])  2.94 us
  transfers between devices with their start and end apart: 12, of which 7 were waited for; matrix products, arithmetic and copies ran while one was open for 0% of the time, Pallas kernels for 12%

profile of v6, /device:TPU:0, one launch (start us, length us, event | category | flops | bytes accessed | tf_op | source)
XLA Modules:
  0.0 40.3 jit_solution(95837051065789950)
XLA Ops:
  0.0 0.0 copy-start
  0.0 2.9 %collective-permute-start = (bf16[8,16,256]{2,1,0:T(8,128)(2,1)}, bf16[8,16,256]{2,1,0:T(8,128)(2,1)S(1)}, u32[]{:S(2)}, u32[]{:S(2)}) collective-permute-start(bf16[8,16,256]{2,1,0:T(8,128)(2,1)} %refs_0_.7), channel_id=1, source_target_pairs={{16,0},{0,16},{17,1},{1,17},{18,2},{2,18},{19,3},{3,19},{20,4},{4,... | collective-permute-start | bytes 196616 | tf_op jit(solution)/shard_map/ppermute | solution.py:311
  2.9 1.7 %shard_map.64 = (bf16[256,1024]{1,0:T(8,128)(2,1)S(1)}, bf16[1024,256]{1,0:T(8,128)(2,1)S(1)}, bf16[4,256,256]{2,1,0:T(8,128)(2,1)S(1)}, bf16[4,256,256]{2,1,0:T(8,128)(2,1)S(1)}) custom-call(bf16[256,1024]{1,0:T(8,128)(2,1)} %refs_0_.4, bf16[1024,256]{1,0:T(8,128)(2,1)} %refs_1_.1, bf16[4,256,256]{2,1,0:T(8,128)(2,1)} %refs_2_.2, bf16[4,256,256]{2,1,0:T(8,128)(2,1)} %refs_3_.1), custom_call_target="tpu_custom_call" | custom-call | bytes 2097152 | tf_op jit(solution)/shard_map/pallas_call | solution.py:281
  4.7 0.8 %collective-permute-done.refs_1_ = bf16[8,16,256]{2,1,0:T(8,128)(2,1)S(1)} collective-permute-done((bf16[8,16,256]{2,1,0:T(8,128)(2,1)}, bf16[8,16,256]{2,1,0:T(8,128)(2,1)S(1)}, u32[]{:S(2)}, u32[]{:S(2)}) %collective-permute-start) | collective-permute-done | bytes 65568 | tf_op jit(solution)/shard_map/ppermute | solution.py:311
  5.5 0.0 copy-done
  5.5 0.0 copy-start.1
  5.5 0.1 collective-permute-start.1
  5.6 5.1 %collective-permute-start.2 = (bf16[128,256]{1,0:T(8,128)(2,1)S(1)}, bf16[128,256]{1,0:T(8,128)(2,1)S(1)}, u32[]{:S(2)}, u32[]{:S(2)}) collective-permute-start(bf16[128,256]{1,0:T(8,128)(2,1)S(1)} %get-tuple-element.24), channel_id=1, source_target_pairs={{0,15},{1,2},{2,1},{3,4},{4,3},{5,6},{6,5},{7,8},{8,7},{9,10},{10,... | collective-permute-start | bytes 196616 | tf_op jit(solution)/shard_map/ppermute | solution.py:332
  10.7 0.0 copy-done.1
  10.7 3.2 %shard_map.66 = (bf16[64,256]{1,0:T(8,128)(2,1)S(1)}, bf16[64,256]{1,0:T(8,128)(2,1)S(1)}) custom-call(bf16[8,16,256]{2,1,0:T(8,128)(2,1)S(1)} %copy-done, bf16[8,16,256]{2,1,0:T(8,128)(2,1)S(1)} %collective-permute-done.refs_1_, bf16[7,7,256]{2,1,0:T(8,128)(2,1)S(1)} %copy-done.1, bf16[256,1024]{1,0:T(8,128)(2,1)S(1)} %get-tuple-element.25.refs_3_.refs_6_, ...), custom_call_target="tpu_custom_call" | custom-call | flops 134217728 | bytes 1729024 | tf_op jit(solution)/shard_map/pallas_call | solution.py:281
  13.9 0.0 collective-permute-done.1.refs_2_
  13.9 0.0 collective-permute-done.2.refs_3_
  13.9 2.6 %shard_map.67 = (bf16[64,256]{1,0:T(8,128)(2,1)S(1)}, bf16[32,256]{1,0:T(8,128)(2,1)S(1)}, bf16[32,256]{1,0:T(8,128)(2,1)S(1)}, bf16[32,256]{1,0:T(8,128)(2,1)S(1)}, bf16[32,256]{1,0:T(8,128)(2,1)S(1)}) custom-call(bf16[8,16,256]{2,1,0:T(8,128)(2,1)S(1)} %copy-done, bf16[8,16,256]{2,1,0:T(8,128)(2,1)S(1)} %collective-permute-done.refs_1_, ...), custom_call_target="tpu_custom_call" | custom-call | flops 134217728 | bytes 1892864 | tf_op jit(solution)/shard_map/pallas_call | solution.py:281
  16.6 0.1 collective-permute-start.3
  16.7 1.0 %collective-permute-start.4 = (bf16[32,256]{1,0:T(8,128)(2,1)S(1)}, bf16[32,256]{1,0:T(8,128)(2,1)S(1)}, u32[]{:S(2)}, u32[]{:S(2)}) collective-permute-start(bf16[32,256]{1,0:T(8,128)(2,1)S(1)} %get-tuple-element.30), channel_id=1, source_target_pairs={{0,8},{1,9},{2,10},{3,11},{4,12},{5,13},{6,14},{7,15},{8,0},{9,1},... | collective-permute-start | bytes 49160 | tf_op jit(solution)/shard_map/ppermute | solution.py:303
  17.7 3.3 %collective-permute-start.5 = (bf16[32,256]{1,0:T(8,128)(2,1)S(1)}, bf16[32,256]{1,0:T(8,128)(2,1)S(1)}, u32[]{:S(2)}, u32[]{:S(2)}) collective-permute-start(bf16[32,256]{1,0:T(8,128)(2,1)S(1)} %get-tuple-element.31), channel_id=1, source_target_pairs={{0,12},{1,13},{2,14},{3,15},{4,8},{5,9},{6,10},{7,11},{8,4},{9,5},... | collective-permute-start | bytes 49160 | tf_op jit(solution)/shard_map/ppermute | solution.py:303
  21.0 0.0 collective-permute-done.3
  21.0 0.3 collective-permute-done.4
  21.4 1.9 %collective-permute-done.5 = bf16[32,256]{1,0:T(8,128)(2,1)S(1)} collective-permute-done((bf16[32,256]{1,0:T(8,128)(2,1)S(1)}, bf16[32,256]{1,0:T(8,128)(2,1)S(1)}, u32[]{:S(2)}, u32[]{:S(2)}) %collective-permute-start.5) | collective-permute-done | bytes 16416 | tf_op jit(solution)/shard_map/ppermute | solution.py:303
  23.2 0.6 %collective-permute-start.6 = (bf16[128,256]{1,0:T(8,128)(2,1)S(1)}, bf16[128,256]{1,0:T(8,128)(2,1)S(1)}, u32[]{:S(2)}, u32[]{:S(2)}) collective-permute-start(bf16[128,256]{1,0:T(8,128)(2,1)S(1)} %constant_dynamic-update-slice_fusion.refs_0_), channel_id=1, source_target_pairs={{0,2},{1,3},{2,0},{3,1},{4,6},{5,7},{6,4},{7,5},{8,10},{9,11},{10,... | collective-permute-start | bytes 196616 | tf_op jit(solution)/shard_map/ppermute | solution.py:303
  23.8 1.1 %collective-permute-start.7 = (bf16[128,256]{1,0:T(8,128)(2,1)S(1)}, bf16[128,256]{1,0:T(8,128)(2,1)S(1)}, u32[]{:S(2)}, u32[]{:S(2)}) collective-permute-start(bf16[128,256]{1,0:T(8,128)(2,1)S(1)} %constant_dynamic-update-slice_fusion.refs_0_), channel_id=1, source_target_pairs={{0,1},{1,0},{2,3},{3,2},{4,5},{5,4},{6,7},{7,6},{8,9},{9,8},{10,11... | collective-permute-start | bytes 196616 | tf_op jit(solution)/shard_map/ppermute | solution.py:303
  24.9 2.6 %collective-permute-done.6.refs_1_ = bf16[128,256]{1,0:T(8,128)(2,1)S(1)} collective-permute-done((bf16[128,256]{1,0:T(8,128)(2,1)S(1)}, bf16[128,256]{1,0:T(8,128)(2,1)S(1)}, u32[]{:S(2)}, u32[]{:S(2)}) %collective-permute-start.6) | collective-permute-done | bytes 65568 | tf_op jit(solution)/shard_map/ppermute | solution.py:303
  27.5 0.0 collective-permute-start.8
  27.5 0.0 collective-permute-done.7.refs_2_
  27.5 1.2 %collective-permute-done.8.refs_3_ = bf16[128,256]{1,0:T(8,128)(2,1)S(1)} collective-permute-done((bf16[128,256]{1,0:T(8,128)(2,1)S(1)}, bf16[128,256]{1,0:T(8,128)(2,1)S(1)}, u32[]{:S(2)}, u32[]{:S(2)}) %collective-permute-start.8) | collective-permute-done | bytes 65568 | tf_op jit(solution)/shard_map/ppermute | solution.py:303
  28.8 1.2 %shard_map.68 = (bf16[32,256]{1,0:T(8,128)(2,1)S(1)}, bf16[32,256]{1,0:T(8,128)(2,1)S(1)}, bf16[32,256]{1,0:T(8,128)(2,1)S(1)}, bf16[32,256]{1,0:T(8,128)(2,1)S(1)}) custom-call(bf16[128,256]{1,0:T(8,128)(2,1)S(1)} %constant_dynamic-update-slice_fusion.refs_0_, bf16[128,256]{1,0:T(8,128)(2,1)S(1)} %collective-permute-done.6.refs_1_, ...), custom_call_target="tpu_custom_call" | custom-call | bytes 786432 | tf_op jit(solution)/shard_map/pallas_call | solution.py:281
  30.0 0.2 collective-permute-start.9
  30.2 3.8 %collective-permute-start.10 = (bf16[32,256]{1,0:T(8,128)(2,1)S(1)}, bf16[32,256]{1,0:T(8,128)(2,1)S(1)}, u32[]{:S(2)}, u32[]{:S(2)}) collective-permute-start(bf16[32,256]{1,0:T(8,128)(2,1)S(1)} %get-tuple-element.35), channel_id=1, source_target_pairs={{0,8},{1,9},{2,10},{3,11},{4,12},{5,13},{6,14},{7,15},{8,0},{9,1},... | collective-permute-start | bytes 49160 | tf_op jit(solution)/shard_map/ppermute | solution.py:303
  33.9 0.5 %collective-permute-start.11 = (bf16[32,256]{1,0:T(8,128)(2,1)S(1)}, bf16[32,256]{1,0:T(8,128)(2,1)S(1)}, u32[]{:S(2)}, u32[]{:S(2)}) collective-permute-start(bf16[32,256]{1,0:T(8,128)(2,1)S(1)} %get-tuple-element.36), channel_id=1, source_target_pairs={{0,12},{1,13},{2,14},{3,15},{4,8},{5,9},{6,10},{7,11},{8,4},{9,5},... | collective-permute-start | bytes 49160 | tf_op jit(solution)/shard_map/ppermute | solution.py:303
  34.4 0.0 collective-permute-done.9.refs_1_
  34.4 1.2 %collective-permute-done.10.refs_2_ = bf16[32,256]{1,0:T(8,128)(2,1)S(1)} collective-permute-done((bf16[32,256]{1,0:T(8,128)(2,1)S(1)}, bf16[32,256]{1,0:T(8,128)(2,1)S(1)}, u32[]{:S(2)}, u32[]{:S(2)}) %collective-permute-start.10) | collective-permute-done | bytes 16416 | tf_op jit(solution)/shard_map/ppermute | solution.py:303
  35.7 3.8 %collective-permute-done.11.refs_3_ = bf16[32,256]{1,0:T(8,128)(2,1)S(1)} collective-permute-done((bf16[32,256]{1,0:T(8,128)(2,1)S(1)}, bf16[32,256]{1,0:T(8,128)(2,1)S(1)}, u32[]{:S(2)}, u32[]{:S(2)}) %collective-permute-start.11) | collective-permute-done | bytes 16416 | tf_op jit(solution)/shard_map/ppermute | solution.py:303
  39.5 0.8 %shard_map.69 = bf16[8,16,256]{2,1,0:T(8,128)(2,1)} custom-call(bf16[32,256]{1,0:T(8,128)(2,1)S(1)} %get-tuple-element.33.refs_0_, bf16[32,256]{1,0:T(8,128)(2,1)S(1)} %collective-permute-done.9.refs_1_, bf16[32,256]{1,0:T(8,128)(2,1)S(1)} %collective-permute-done.10.refs_2_, bf16[32,256]{1,0:T(8,128)(2,1)S(1)} %collective-permute-done.11.refs_3_, ...), custom_call_target="tpu_custom_call" | custom-call | bytes 655360 | tf_op jit(solution)/shard_map/pallas_call | solution.py:281
  (5 shorter events, 0.1 us)
Async XLA Ops:
  0.0 5.5 %copy-start = (bf16[8,16,256]{2,1,0:T(8,128)(2,1)S(1)}, bf16[8,16,256]{2,1,0:T(8,128)(2,1)}, u32[]{:S(2)}) copy-start(bf16[8,16,256]{2,1,0:T(8,128)(2,1)} %refs_0_.7) | copy-start | bytes 196612
  0.0 5.5 %collective-permute-start = (bf16[8,16,256]{2,1,0:T(8,128)(2,1)}, bf16[8,16,256]{2,1,0:T(8,128)(2,1)S(1)}, u32[]{:S(2)}, u32[]{:S(2)}) collective-permute-start(bf16[8,16,256]{2,1,0:T(8,128)(2,1)} %refs_0_.7), channel_id=1, source_target_pairs={{16,0},{0,16},{17,1},{1,17},{18,2},{2,18},{19,3},{3,19},{20,4},{4,... | collective-permute-start | bytes 196616 | tf_op jit(solution)/shard_map/ppermute | solution.py:311
  5.5 5.3 %copy-start.1 = (bf16[7,7,256]{2,1,0:T(8,128)(2,1)S(1)}, bf16[7,7,256]{2,1,0:T(8,128)(2,1)}, u32[]{:S(2)}) copy-start(bf16[7,7,256]{2,1,0:T(8,128)(2,1)} %refs_5_.1) | copy-start | bytes 75268
  5.5 8.4 %collective-permute-start.1 = (bf16[128,256]{1,0:T(8,128)(2,1)S(1)}, bf16[128,256]{1,0:T(8,128)(2,1)S(1)}, u32[]{:S(2)}, u32[]{:S(2)}) collective-permute-start(bf16[128,256]{1,0:T(8,128)(2,1)S(1)} %get-tuple-element.23), channel_id=1, source_target_pairs={{0,1},{1,0},{2,3},{3,2},{4,5},{5,4},{6,7},{7,6},{8,9},{9,8},{10,11... | collective-permute-start | bytes 196616 | tf_op jit(solution)/shard_map/ppermute | solution.py:303
  5.6 8.3 %collective-permute-start.2 = (bf16[128,256]{1,0:T(8,128)(2,1)S(1)}, bf16[128,256]{1,0:T(8,128)(2,1)S(1)}, u32[]{:S(2)}, u32[]{:S(2)}) collective-permute-start(bf16[128,256]{1,0:T(8,128)(2,1)S(1)} %get-tuple-element.24), channel_id=1, source_target_pairs={{0,15},{1,2},{2,1},{3,4},{4,3},{5,6},{6,5},{7,8},{8,7},{9,10},{10,... | collective-permute-start | bytes 196616 | tf_op jit(solution)/shard_map/ppermute | solution.py:332
  16.6 4.5 %collective-permute-start.3 = (bf16[32,256]{1,0:T(8,128)(2,1)S(1)}, bf16[32,256]{1,0:T(8,128)(2,1)S(1)}, u32[]{:S(2)}, u32[]{:S(2)}) collective-permute-start(bf16[32,256]{1,0:T(8,128)(2,1)S(1)} %get-tuple-element.29), channel_id=1, source_target_pairs={{0,4},{1,5},{2,6},{3,7},{4,0},{5,1},{6,2},{7,3},{8,12},{9,13},{10,... | collective-permute-start | bytes 49160 | tf_op jit(solution)/shard_map/ppermute | solution.py:303
  16.7 4.7 %collective-permute-start.4 = (bf16[32,256]{1,0:T(8,128)(2,1)S(1)}, bf16[32,256]{1,0:T(8,128)(2,1)S(1)}, u32[]{:S(2)}, u32[]{:S(2)}) collective-permute-start(bf16[32,256]{1,0:T(8,128)(2,1)S(1)} %get-tuple-element.30), channel_id=1, source_target_pairs={{0,8},{1,9},{2,10},{3,11},{4,12},{5,13},{6,14},{7,15},{8,0},{9,1},... | collective-permute-start | bytes 49160 | tf_op jit(solution)/shard_map/ppermute | solution.py:303
  17.7 5.5 %collective-permute-start.5 = (bf16[32,256]{1,0:T(8,128)(2,1)S(1)}, bf16[32,256]{1,0:T(8,128)(2,1)S(1)}, u32[]{:S(2)}, u32[]{:S(2)}) collective-permute-start(bf16[32,256]{1,0:T(8,128)(2,1)S(1)} %get-tuple-element.31), channel_id=1, source_target_pairs={{0,12},{1,13},{2,14},{3,15},{4,8},{5,9},{6,10},{7,11},{8,4},{9,5},... | collective-permute-start | bytes 49160 | tf_op jit(solution)/shard_map/ppermute | solution.py:303
  23.2 4.3 %collective-permute-start.6 = (bf16[128,256]{1,0:T(8,128)(2,1)S(1)}, bf16[128,256]{1,0:T(8,128)(2,1)S(1)}, u32[]{:S(2)}, u32[]{:S(2)}) collective-permute-start(bf16[128,256]{1,0:T(8,128)(2,1)S(1)} %constant_dynamic-update-slice_fusion.refs_0_), channel_id=1, source_target_pairs={{0,2},{1,3},{2,0},{3,1},{4,6},{5,7},{6,4},{7,5},{8,10},{9,11},{10,... | collective-permute-start | bytes 196616 | tf_op jit(solution)/shard_map/ppermute | solution.py:303
  23.8 3.7 %collective-permute-start.7 = (bf16[128,256]{1,0:T(8,128)(2,1)S(1)}, bf16[128,256]{1,0:T(8,128)(2,1)S(1)}, u32[]{:S(2)}, u32[]{:S(2)}) collective-permute-start(bf16[128,256]{1,0:T(8,128)(2,1)S(1)} %constant_dynamic-update-slice_fusion.refs_0_), channel_id=1, source_target_pairs={{0,1},{1,0},{2,3},{3,2},{4,5},{5,4},{6,7},{7,6},{8,9},{9,8},{10,11... | collective-permute-start | bytes 196616 | tf_op jit(solution)/shard_map/ppermute | solution.py:303
  27.5 1.3 %collective-permute-start.8 = (bf16[128,256]{1,0:T(8,128)(2,1)S(1)}, bf16[128,256]{1,0:T(8,128)(2,1)S(1)}, u32[]{:S(2)}, u32[]{:S(2)}) collective-permute-start(bf16[128,256]{1,0:T(8,128)(2,1)S(1)} %collective-permute-done.6.refs_1_), channel_id=1, source_target_pairs={{0,1},{1,0},{2,3},{3,2},{4,5},{5,4},{6,7},{7,6},{8,9},{9,8},{10,11... | collective-permute-start | bytes 196616 | tf_op jit(solution)/shard_map/ppermute | solution.py:303
  30.0 4.5 %collective-permute-start.9 = (bf16[32,256]{1,0:T(8,128)(2,1)S(1)}, bf16[32,256]{1,0:T(8,128)(2,1)S(1)}, u32[]{:S(2)}, u32[]{:S(2)}) collective-permute-start(bf16[32,256]{1,0:T(8,128)(2,1)S(1)} %get-tuple-element.34), channel_id=1, source_target_pairs={{0,4},{1,5},{2,6},{3,7},{4,0},{5,1},{6,2},{7,3},{8,12},{9,13},{10,... | collective-permute-start | bytes 49160 | tf_op jit(solution)/shard_map/ppermute | solution.py:303
  30.2 5.5 %collective-permute-start.10 = (bf16[32,256]{1,0:T(8,128)(2,1)S(1)}, bf16[32,256]{1,0:T(8,128)(2,1)S(1)}, u32[]{:S(2)}, u32[]{:S(2)}) collective-permute-start(bf16[32,256]{1,0:T(8,128)(2,1)S(1)} %get-tuple-element.35), channel_id=1, source_target_pairs={{0,8},{1,9},{2,10},{3,11},{4,12},{5,13},{6,14},{7,15},{8,0},{9,1},... | collective-permute-start | bytes 49160 | tf_op jit(solution)/shard_map/ppermute | solution.py:303
  33.9 5.5 %collective-permute-start.11 = (bf16[32,256]{1,0:T(8,128)(2,1)S(1)}, bf16[32,256]{1,0:T(8,128)(2,1)S(1)}, u32[]{:S(2)}, u32[]{:S(2)}) collective-permute-start(bf16[32,256]{1,0:T(8,128)(2,1)S(1)} %get-tuple-element.36), channel_id=1, source_target_pairs={{0,12},{1,13},{2,14},{3,15},{4,8},{5,9},{6,10},{7,11},{8,4},{9,5},... | collective-permute-start | bytes 49160 | tf_op jit(solution)/shard_map/ppermute | solution.py:303

commit v7 on v6

--- a/solution.py
+++ b/solution.py
@@ -83,23 +83,26 @@
         copy.wait()
 
 
-def level_of(levels):
-    return lax.axis_index("lon") // (lax.axis_size("lon") // levels)
-
-
-def strip_kernel(nlat, *refs):
-    tiles = refs[:nlat]
-    near_ref, far_ref, near, far = refs[nlat + 1 :]
-    rows, cols, channels = tiles[0].shape
+def peer(levels, k):
+    level = lax.axis_index("lon") // (lax.axis_size("lon") // levels)
+    return level ^ ((levels - k) % levels)
+
+
+def strip_kernel(tile_ref, near_ref, far_ref):
+    cols = tile_ref.shape[1]
+    values = tile_ref[...].astype(f32)
+    first, last = values[:, :STRIP], values[:, cols - STRIP :]
     even = lax.axis_index("lon") % 2 == 0
-    for s in range(nlat):
-        values = tiles[s][...].astype(f32)
-        first, last = values[:, :STRIP], values[:, cols - STRIP :]
-        where = pl.ds(lax.rem(lax.axis_index("lat") + s, nlat) * rows, rows)
-        near[where] = jnp.where(even, last, first)
-        far[where] = jnp.where(even, first, last)
-    near_ref[...] = near[...].reshape(near_ref.shape).astype(bf16)
-    far_ref[...] = far[...].reshape(far_ref.shape).astype(bf16)
+    near_ref[...] = jnp.where(even, last, first).reshape(near_ref.shape).astype(bf16)
+    far_ref[...] = jnp.where(even, first, last).reshape(far_ref.shape).astype(bf16)
+
+
+def merge_kernel(near_ref, far_ref, after_ref, sides_ref):
+    near, far = near_ref[...].astype(f32), far_ref[...].astype(f32)
+    even = lax.axis_index("lon") % 2 == 0
+    left, right = jnp.where(even, far, near), jnp.where(even, near, far)
+    place = lax.broadcasted_iota(jnp.int32, (near.shape[0], 1), 0) % STRIP
+    sides_ref[...] = jnp.where(place < SIDE, right, left).astype(bf16)
 
 
 def chain(my_lat, slab, shape, dw_ref, expand_ref, reduce_ref, attn_ref, center, scratch):
@@ -142,16 +145,11 @@
     return block_two, layer_norm(block_two.astype(f32))
 
 
-def fill(padded, all_rows, first, values):
-    width = values.shape[1]
-    padded[HALO : HALO + all_rows, first : first + width] = values
-
-
 def fill_tiles(padded, my_lat, first, tiles):
     rows, cols = tiles[0].shape[:2]
     for s in range(len(tiles)):
         place = HALO + lax.rem(my_lat + s, len(tiles)) * rows
-        padded[pl.ds(place, rows), first : first + cols] = tiles[s][...].astype(f32)
+        padded[pl.ds(place, rows), first : first + cols] = tiles[s].astype(f32)
 
 
 def clear(padded, all_rows):
@@ -168,7 +166,7 @@
     columns = cols - 2 * SIDE
     clear(padded, all_rows)
     my_lat = lax.axis_index("lat")
-    fill_tiles(padded, my_lat, 0, tiles)
+    fill_tiles(padded, my_lat, 0, [tile[...] for tile in tiles])
 
     def slab(b, c):
         first = SIDE - HALO + b
@@ -184,22 +182,20 @@
 
 
 def outer_kernel(nlat, levels, *refs):
-    tiles, refs = refs[:nlat], refs[nlat:]
-    near_ref, far_ref, inner_in_ref, dw_ref, expand_ref, reduce_ref, attn_ref = refs[:7]
-    two_ref, *refs = refs[7:]
+    tiles, sides, refs = refs[:nlat], refs[nlat : 2 * nlat], refs[2 * nlat :]
+    inner_in_ref, dw_ref, expand_ref, reduce_ref, attn_ref = refs[:5]
+    two_ref, *refs = refs[5:]
     sent_refs, (sent, padded, *scratch) = refs[:levels], refs[levels:]
     rows, cols, channels = tiles[0].shape
     all_rows = rows * nlat
     columns = 2 * SIDE
-    strip_shape = (all_rows, STRIP, channels)
-    near = near_ref[...].astype(f32).reshape(strip_shape)
-    far = far_ref[...].astype(f32).reshape(strip_shape)
-    even = lax.axis_index("lon") % 2 == 0
+    my_lat = lax.axis_index("lat")
+    tiles = [tile[...] for tile in tiles]
+    sides = [side[...].astype(f32).reshape(rows, STRIP, channels) for side in sides]
     clear(padded, all_rows)
-    fill(padded, all_rows, 0, jnp.where(even, far, near))
-    my_lat = lax.axis_index("lat")
+    fill_tiles(padded, my_lat, 0, sides)
     fill_tiles(padded, my_lat, STRIP, tiles)
-    fill(padded, all_rows, STRIP + cols, jnp.where(even, near, far))
+    fill_tiles(padded, my_lat, STRIP + cols, sides)
     sublane = lax.broadcasted_iota(jnp.int32, (1, columns, 1), 1)
 
     def halves(shift, rows_of, c, width):
@@ -225,7 +221,7 @@
     sent[...] = jnp.concatenate([inner, outer], axis=1).astype(bf16)
     some = rows // levels
     for k in range(levels):
-        part = sent[pl.ds((level_of(levels) ^ k) * some, some)]
+        part = sent[pl.ds(peer(levels, k) * some, some)]
         sent_refs[k][...] = part.reshape(sent_refs[k].shape)
 
 
@@ -258,7 +254,7 @@
     every = jnp.concatenate([part[...] for part in parts], axis=0)
     change = dot(every, attn_ref[3]).reshape(levels, some, cols, channels)
     for k in range(levels):
-        start = (level_of(levels) ^ k) * some
+        start = peer(levels, k) * some
 
         def state(ref, width):
             count = some * width
@@ -303,12 +299,20 @@
         return lax.ppermute(piece, "lon", [(j, j ^ mask) for j in range(nlon)])
 
     def exchange(pieces):
-        moved = [swap(pieces[k], k * column) for k in range(levels - 1, 0, -1)]
-        return [pieces[0]] + moved[::-1]
-
-    tiles = [field]
-    for s in range(1, nlat):
-        tiles.append(lax.ppermute(field, "lat", [((i + s) % nlat, i) for i in range(nlat)]))
+        moved = [swap(pieces[k], (levels - k) * column) for k in range(1, levels)]
+        return [pieces[0]] + moved
+
+    def gather(tile):
+        pairs = [[((i + s) % nlat, i) for i in range(nlat)] for s in range(1, nlat)]
+        return [tile] + [lax.ppermute(tile, "lat", pair) for pair in pairs]
+
+    tiles = gather(field)
+    strip = (rows * STRIP, channels)
+    near, far = call(strip_kernel, [strip, strip], [field])
+    near = swap(near, 1)
+    far = lax.ppermute(
+        far, "lon", [(j, (j - 1) % nlon if j % 2 == 0 else (j + 1) % nlon) for j in range(nlon)]
+    )
     weights = (w_expand, w_reduce, lat_attn, lon_attn)
     staged = call(
         stage_kernel,
@@ -320,19 +324,6 @@
     )
     expand, reduce, lat_proj, lon_proj = staged
 
-    strip = (all_rows * STRIP, channels)
-    strip_scratch = pltpu.VMEM((all_rows, STRIP, channels), f32)
-    near, far = call(
-        functools.partial(strip_kernel, nlat),
-        [strip, strip],
-        [*tiles, reduce],
-        [strip_scratch, strip_scratch],
-    )
-    near = swap(near, 1)
-    far = lax.ppermute(
-        far, "lon", [(j, (j - 1) % nlon if j % 2 == 0 else (j + 1) % nlon) for j in range(nlon)]
-    )
-
     def scratch(width, count):
         return [
             pltpu.VMEM((all_rows + 2 * HALO, width, channels), f32),
@@ -349,11 +340,13 @@
         scratch(cols, cols - columns),
         flops=work,
     )
+    (sides,) = call(merge_kernel, [strip], [near, far, inner_in])
+    sides = gather(sides)
     piece = (some * cols, channels)
     outer_two, *parts = call(
         functools.partial(outer_kernel, nlat, levels),
         [(rows * columns, channels)] + [piece] * levels,
-        [*tiles, near, far, inner_in, dw_weight, expand, reduce, lat_proj],
+        [*tiles, *sides, inner_in, dw_weight, expand, reduce, lat_proj],
         [pltpu.VMEM((rows, cols, channels), bf16)] + scratch(cols + 2 * STRIP, columns),
         flops=work,
     )

time: 40.4 us -> 41.4 us (1.025)
  starting transfers between devices: 18.7 us -> 17.2 us
  waiting for transfers between devices: 11.9 us -> 13.4 us
  local copies, waits for them, and re-layouts: 0.02 us -> 0.89 us
    ppermute x1 -> x2, waiting for transfers between devices: 0.78 us -> 3.38 us  [gather(): return [tile] + [lax.ppermute(tile, 'lat', pair) for pair in pairs]]
    ppermute x10, starting transfers between devices: 10.6 us -> 8.98 us  [swap(): return lax.ppermute(piece, 'lon', [(j, j ^ mask) for j in range(nlon)])]
    ppermute x10, waiting for transfers between devices: 11.1 us -> 10.1 us  [swap(): return lax.ppermute(piece, 'lon', [(j, j ^ mask) for j in range(nlon)])]
    unnamed x7 -> x9, local copies, waits for them, and re-layouts: 0.01 us -> 0.89 us
    ppermute x1 -> x2, starting transfers between devices: 2.94 us -> 3.54 us  [gather(): return [tile] + [lax.ppermute(tile, 'lat', pair) for pair in pairs]]
    ppermute x1, starting transfers between devices: 5.12 us -> 4.64 us  [shards(): lax.ppermute(far, 'lon', [(j, (j - 1) % nlon if j % 2 == 0 else (j + 1) %...]
    pallas_call x6 -> x7, Pallas kernels: 9.61 us -> 9.59 us  [call(): pl.pallas_call(kernel, out_shape=shapes, in_specs=[given] * len(operands)...]
  transfers between devices with their start and end apart: 12 -> 13, of which waited for: 7 -> 8; matrix products, arithmetic and copies ran while one was open for 0% -> 0% of each run, Pallas kernels for 12% -> 12%
where the time goes in v7:
time: 41.4 us; the launch traced here: 41.2 us
  starting transfers between devices  17.2 us (42%)
  waiting for transfers between devices  13.4 us (32%)
  Pallas kernels  9.59 us (23%)
  local copies, waits for them, and re-layouts  0.89 us (2%)
    ppermute x10, waiting for transfers between devices, swap(): return lax.ppermute(piece, 'lon', [(j, j ^ mask) for j in range(nlon)])  10.1 us
    pallas_call x7, Pallas kernels, call(): pl.pallas_call(kernel, out_shape=shapes, in_specs=[given] * len(operands)...  9.59 us
    ppermute x10, starting transfers between devices, swap(): return lax.ppermute(piece, 'lon', [(j, j ^ mask) for j in range(nlon)])  8.98 us
    ppermute x1, starting transfers between devices, shards(): lax.ppermute(far, 'lon', [(j, (j - 1) % nlon if j % 2 == 0 else (j + 1) %...  4.64 us
    ppermute x2, starting transfers between devices, gather(): return [tile] + [lax.ppermute(tile, 'lat', pair) for pair in pairs]  3.54 us
    ppermute x2, waiting for transfers between devices, gather(): return [tile] + [lax.ppermute(tile, 'lat', pair) for pair in pairs]  3.38 us
    unnamed x9, local copies, waits for them, and re-layouts  0.89 us
  transfers between devices with their start and end apart: 13, of which 8 were waited for; matrix products, arithmetic and copies ran while one was open for 0% of the time, Pallas kernels for 12%

profile of v7, /device:TPU:0, one launch (start us, length us, event | category | flops | bytes accessed | tf_op | source)
XLA Modules:
  0.0 41.2 jit_solution(730575814495797683)
XLA Ops:
  0.0 2.9 %collective-permute-start = (bf16[8,16,256]{2,1,0:T(8,128)(2,1)}, bf16[8,16,256]{2,1,0:T(8,128)(2,1)S(1)}, u32[]{:S(2)}, u32[]{:S(2)}) collective-permute-start(bf16[8,16,256]{2,1,0:T(8,128)(2,1)} %refs_0_.5), channel_id=1, source_target_pairs={{16,0},{0,16},{17,1},{1,17},{18,2},{2,18},{19,3},{3,19},{20,4},{4,... | collective-permute-start | bytes 196616 | tf_op jit(solution)/shard_map/ppermute | solution.py:307
  2.9 0.0 copy-start
  2.9 0.9 %copy-done = bf16[8,16,256]{2,1,0:T(8,128)(2,1)S(1)} copy-done((bf16[8,16,256]{2,1,0:T(8,128)(2,1)S(1)}, bf16[8,16,256]{2,1,0:T(8,128)(2,1)}, u32[]{:S(2)}) %copy-start) | copy-done | bytes 65560
  3.8 0.1 collective-permute-start.1
  3.9 0.0 copy-start.1
  3.9 0.0 copy-start.2
  3.9 4.6 %collective-permute-start.2 = (bf16[64,256]{1,0:T(8,128)(2,1)S(1)}, bf16[64,256]{1,0:T(8,128)(2,1)S(1)}, u32[]{:S(2)}, u32[]{:S(2)}) collective-permute-start(bf16[64,256]{1,0:T(8,128)(2,1)S(1)} %get-tuple-element.23), channel_id=1, source_target_pairs={{0,15},{1,2},{2,1},{3,4},{4,3},{5,6},{6,5},{7,8},{8,7},{9,10},{10,... | collective-permute-start | bytes 98312 | tf_op jit(solution)/shard_map/ppermute | solution.py:313
  8.6 1.7 %shard_map.65 = (bf16[256,1024]{1,0:T(8,128)(2,1)S(1)}, bf16[1024,256]{1,0:T(8,128)(2,1)S(1)}, bf16[4,256,256]{2,1,0:T(8,128)(2,1)S(1)}, bf16[4,256,256]{2,1,0:T(8,128)(2,1)S(1)}) custom-call(bf16[256,1024]{1,0:T(8,128)(2,1)} %refs_0_.3, bf16[1024,256]{1,0:T(8,128)(2,1)} %refs_1_.1, bf16[4,256,256]{2,1,0:T(8,128)(2,1)} %refs_2_.2, bf16[4,256,256]{2,1,0:T(8,128)(2,1)} %refs_3_.1), custom_call_target="tpu_custom_call" | custom-call | bytes 2097152 | tf_op jit(solution)/shard_map/pallas_call | solution.py:277
  10.3 0.0 collective-permute-done.refs_1_
  10.3 0.0 copy-done.1
  10.3 0.0 copy-done.2
  10.3 3.2 %shard_map.66 = (bf16[64,256]{1,0:T(8,128)(2,1)S(1)}, bf16[64,256]{1,0:T(8,128)(2,1)S(1)}) custom-call(bf16[8,16,256]{2,1,0:T(8,128)(2,1)S(1)} %copy-done.1, bf16[8,16,256]{2,1,0:T(8,128)(2,1)S(1)} %collective-permute-done.refs_1_, bf16[7,7,256]{2,1,0:T(8,128)(2,1)S(1)} %copy-done.2, bf16[256,1024]{1,0:T(8,128)(2,1)S(1)} %get-tuple-element.24.refs_3_.refs_6_, ...), custom_call_target="tpu_custom_call" | custom-call | flops 134217728 | bytes 1729024 | tf_op jit(solution)/shard_map/pallas_call | solution.py:277
  13.5 0.0 collective-permute-done.1.near_ref
  13.5 0.0 collective-permute-done.2.far_ref
  13.6 0.6 %collective-permute-start.3 = (bf16[64,256]{1,0:T(8,128)(2,1)S(1)}, bf16[64,256]{1,0:T(8,128)(2,1)S(1)}, u32[]{:S(2)}, u32[]{:S(2)}) collective-permute-start(bf16[64,256]{1,0:T(8,128)(2,1)S(1)} %shard_map.67.refs_2_), channel_id=1, source_target_pairs={{16,0},{0,16},{17,1},{1,17},{18,2},{2,18},{19,3},{3,19},{20,4},{4,... | collective-permute-start | bytes 98312 | tf_op jit(solution)/shard_map/ppermute | solution.py:307
  14.2 3.4 %collective-permute-done.3.refs_3_ = bf16[64,256]{1,0:T(8,128)(2,1)S(1)} collective-permute-done((bf16[64,256]{1,0:T(8,128)(2,1)S(1)}, bf16[64,256]{1,0:T(8,128)(2,1)S(1)}, u32[]{:S(2)}, u32[]{:S(2)}) %collective-permute-start.3) | collective-permute-done | bytes 32800 | tf_op jit(solution)/shard_map/ppermute | solution.py:307
  17.6 2.6 %shard_map.68 = (bf16[64,256]{1,0:T(8,128)(2,1)S(1)}, bf16[32,256]{1,0:T(8,128)(2,1)S(1)}, bf16[32,256]{1,0:T(8,128)(2,1)S(1)}, bf16[32,256]{1,0:T(8,128)(2,1)S(1)}, bf16[32,256]{1,0:T(8,128)(2,1)S(1)}) custom-call(bf16[8,16,256]{2,1,0:T(8,128)(2,1)S(1)} %copy-done.1, bf16[8,16,256]{2,1,0:T(8,128)(2,1)S(1)} %collective-permute-done.refs_1_, ...), custom_call_target="tpu_custom_call" | custom-call | flops 134217728 | bytes 1827328 | tf_op jit(solution)/shard_map/pallas_call | solution.py:277
  20.2 0.5 %collective-permute-start.4 = (bf16[32,256]{1,0:T(8,128)(2,1)S(1)}, bf16[32,256]{1,0:T(8,128)(2,1)S(1)}, u32[]{:S(2)}, u32[]{:S(2)}) collective-permute-start(bf16[32,256]{1,0:T(8,128)(2,1)S(1)} %get-tuple-element.29), channel_id=1, source_target_pairs={{0,12},{1,13},{2,14},{3,15},{4,8},{5,9},{6,10},{7,11},{8,4},{9,5},... | collective-permute-start | bytes 49160 | tf_op jit(solution)/shard_map/ppermute | solution.py:299
  20.7 0.0 collective-permute-start.5
  20.7 3.9 %collective-permute-start.6 = (bf16[32,256]{1,0:T(8,128)(2,1)S(1)}, bf16[32,256]{1,0:T(8,128)(2,1)S(1)}, u32[]{:S(2)}, u32[]{:S(2)}) collective-permute-start(bf16[32,256]{1,0:T(8,128)(2,1)S(1)} %get-tuple-element.31), channel_id=1, source_target_pairs={{0,4},{1,5},{2,6},{3,7},{4,0},{5,1},{6,2},{7,3},{8,12},{9,13},{10,... | collective-permute-start | bytes 49160 | tf_op jit(solution)/shard_map/ppermute | solution.py:299
  24.7 1.1 %collective-permute-done.4 = bf16[32,256]{1,0:T(8,128)(2,1)S(1)} collective-permute-done((bf16[32,256]{1,0:T(8,128)(2,1)S(1)}, bf16[32,256]{1,0:T(8,128)(2,1)S(1)}, u32[]{:S(2)}, u32[]{:S(2)}) %collective-permute-start.4) | collective-permute-done | bytes 16416 | tf_op jit(solution)/shard_map/ppermute | solution.py:299
  25.8 0.0 collective-permute-done.5
  25.8 0.6 %collective-permute-done.6 = bf16[32,256]{1,0:T(8,128)(2,1)S(1)} collective-permute-done((bf16[32,256]{1,0:T(8,128)(2,1)S(1)}, bf16[32,256]{1,0:T(8,128)(2,1)S(1)}, u32[]{:S(2)}, u32[]{:S(2)}) %collective-permute-start.6) | collective-permute-done | bytes 16416 | tf_op jit(solution)/shard_map/ppermute | solution.py:299
  26.4 0.0 collective-permute-start.7
  26.4 0.0 collective-permute-start.8
  26.4 4.3 %collective-permute-done.7.refs_1_ = bf16[128,256]{1,0:T(8,128)(2,1)S(1)} collective-permute-done((bf16[128,256]{1,0:T(8,128)(2,1)S(1)}, bf16[128,256]{1,0:T(8,128)(2,1)S(1)}, u32[]{:S(2)}, u32[]{:S(2)}) %collective-permute-start.7) | collective-permute-done | bytes 65568 | tf_op jit(solution)/shard_map/ppermute | solution.py:299
  30.6 0.0 collective-permute-start.9
  30.6 0.0 collective-permute-done.8.refs_2_
  30.6 1.2 %collective-permute-done.9.refs_3_ = bf16[128,256]{1,0:T(8,128)(2,1)S(1)} collective-permute-done((bf16[128,256]{1,0:T(8,128)(2,1)S(1)}, bf16[128,256]{1,0:T(8,128)(2,1)S(1)}, u32[]{:S(2)}, u32[]{:S(2)}) %collective-permute-start.9) | collective-permute-done | bytes 65568 | tf_op jit(solution)/shard_map/ppermute | solution.py:299
  31.9 1.2 %shard_map.69 = (bf16[32,256]{1,0:T(8,128)(2,1)S(1)}, bf16[32,256]{1,0:T(8,128)(2,1)S(1)}, bf16[32,256]{1,0:T(8,128)(2,1)S(1)}, bf16[32,256]{1,0:T(8,128)(2,1)S(1)}) custom-call(bf16[128,256]{1,0:T(8,128)(2,1)S(1)} %constant_dynamic-update-slice_fusion.refs_0_, bf16[128,256]{1,0:T(8,128)(2,1)S(1)} %collective-permute-done.7.refs_1_, ...), custom_call_target="tpu_custom_call" | custom-call | bytes 786432 | tf_op jit(solution)/shard_map/pallas_call | solution.py:277
  33.1 2.5 %collective-permute-start.10 = (bf16[32,256]{1,0:T(8,128)(2,1)S(1)}, bf16[32,256]{1,0:T(8,128)(2,1)S(1)}, u32[]{:S(2)}, u32[]{:S(2)}) collective-permute-start(bf16[32,256]{1,0:T(8,128)(2,1)S(1)} %get-tuple-element.34), channel_id=1, source_target_pairs={{0,12},{1,13},{2,14},{3,15},{4,8},{5,9},{6,10},{7,11},{8,4},{9,5},... | collective-permute-start | bytes 49160 | tf_op jit(solution)/shard_map/ppermute | solution.py:299
  35.6 1.1 %collective-permute-start.11 = (bf16[32,256]{1,0:T(8,128)(2,1)S(1)}, bf16[32,256]{1,0:T(8,128)(2,1)S(1)}, u32[]{:S(2)}, u32[]{:S(2)}) collective-permute-start(bf16[32,256]{1,0:T(8,128)(2,1)S(1)} %get-tuple-element.35), channel_id=1, source_target_pairs={{0,8},{1,9},{2,10},{3,11},{4,12},{5,13},{6,14},{7,15},{8,0},{9,1},... | collective-permute-start | bytes 49160 | tf_op jit(solution)/shard_map/ppermute | solution.py:299
  36.7 0.9 %collective-permute-start.12 = (bf16[32,256]{1,0:T(8,128)(2,1)S(1)}, bf16[32,256]{1,0:T(8,128)(2,1)S(1)}, u32[]{:S(2)}, u32[]{:S(2)}) collective-permute-start(bf16[32,256]{1,0:T(8,128)(2,1)S(1)} %get-tuple-element.36), channel_id=1, source_target_pairs={{0,4},{1,5},{2,6},{3,7},{4,0},{5,1},{6,2},{7,3},{8,12},{9,13},{10,... | collective-permute-start | bytes 49160 | tf_op jit(solution)/shard_map/ppermute | solution.py:299
  37.6 1.2 %collective-permute-done.10.refs_1_ = bf16[32,256]{1,0:T(8,128)(2,1)S(1)} collective-permute-done((bf16[32,256]{1,0:T(8,128)(2,1)S(1)}, bf16[32,256]{1,0:T(8,128)(2,1)S(1)}, u32[]{:S(2)}, u32[]{:S(2)}) %collective-permute-start.10) | collective-permute-done | bytes 16416 | tf_op jit(solution)/shard_map/ppermute | solution.py:299
  38.7 1.5 %collective-permute-done.11.refs_2_ = bf16[32,256]{1,0:T(8,128)(2,1)S(1)} collective-permute-done((bf16[32,256]{1,0:T(8,128)(2,1)S(1)}, bf16[32,256]{1,0:T(8,128)(2,1)S(1)}, u32[]{:S(2)}, u32[]{:S(2)}) %collective-permute-start.11) | collective-permute-done | bytes 16416 | tf_op jit(solution)/shard_map/ppermute | solution.py:299
  40.2 0.2 collective-permute-done.12.refs_3_
  40.4 0.8 %shard_map.70 = bf16[8,16,256]{2,1,0:T(8,128)(2,1)} custom-call(bf16[32,256]{1,0:T(8,128)(2,1)S(1)} %get-tuple-element.33.refs_0_, bf16[32,256]{1,0:T(8,128)(2,1)S(1)} %collective-permute-done.10.refs_1_, bf16[32,256]{1,0:T(8,128)(2,1)S(1)} %collective-permute-done.11.refs_2_, bf16[32,256]{1,0:T(8,128)(2,1)S(1)} %collective-permute-done.12.refs_3_, ...), custom_call_target="tpu_custom_call" | custom-call | bytes 655360 | tf_op jit(solution)/shard_map/pallas_call | solution.py:277
  (6 shorter events, 0.0 us)
Async XLA Ops:
  0.0 10.3 %collective-permute-start = (bf16[8,16,256]{2,1,0:T(8,128)(2,1)}, bf16[8,16,256]{2,1,0:T(8,128)(2,1)S(1)}, u32[]{:S(2)}, u32[]{:S(2)}) collective-permute-start(bf16[8,16,256]{2,1,0:T(8,128)(2,1)} %refs_0_.5), channel_id=1, source_target_pairs={{16,0},{0,16},{17,1},{1,17},{18,2},{2,18},{19,3},{3,19},{20,4},{4,... | collective-permute-start | bytes 196616 | tf_op jit(solution)/shard_map/ppermute | solution.py:307
  2.9 0.9 %copy-start = (bf16[8,16,256]{2,1,0:T(8,128)(2,1)S(1)}, bf16[8,16,256]{2,1,0:T(8,128)(2,1)}, u32[]{:S(2)}) copy-start(bf16[8,16,256]{2,1,0:T(8,128)(2,1)} %refs_0_.5) | copy-start | bytes 196612
  3.8 9.7 %collective-permute-start.1 = (bf16[64,256]{1,0:T(8,128)(2,1)S(1)}, bf16[64,256]{1,0:T(8,128)(2,1)S(1)}, u32[]{:S(2)}, u32[]{:S(2)}) collective-permute-start(bf16[64,256]{1,0:T(8,128)(2,1)S(1)} %get-tuple-element.22), channel_id=1, source_target_pairs={{0,1},{1,0},{2,3},{3,2},{4,5},{5,4},{6,7},{7,6},{8,9},{9,8},{10,11... | collective-permute-start | bytes 98312 | tf_op jit(solution)/shard_map/ppermute | solution.py:299
  3.9 6.4 %copy-start.1 = (bf16[8,16,256]{2,1,0:T(8,128)(2,1)S(1)}, bf16[8,16,256]{2,1,0:T(8,128)(2,1)}, u32[]{:S(2)}) copy-start(bf16[8,16,256]{2,1,0:T(8,128)(2,1)} %refs_0_.5) | copy-start | bytes 196612
  3.9 6.4 %copy-start.2 = (bf16[7,7,256]{2,1,0:T(8,128)(2,1)S(1)}, bf16[7,7,256]{2,1,0:T(8,128)(2,1)}, u32[]{:S(2)}) copy-start(bf16[7,7,256]{2,1,0:T(8,128)(2,1)} %refs_5_.1) | copy-start | bytes 75268
  3.9 9.6 %collective-permute-start.2 = (bf16[64,256]{1,0:T(8,128)(2,1)S(1)}, bf16[64,256]{1,0:T(8,128)(2,1)S(1)}, u32[]{:S(2)}, u32[]{:S(2)}) collective-permute-start(bf16[64,256]{1,0:T(8,128)(2,1)S(1)} %get-tuple-element.23), channel_id=1, source_target_pairs={{0,15},{1,2},{2,1},{3,4},{4,3},{5,6},{6,5},{7,8},{8,7},{9,10},{10,... | collective-permute-start | bytes 98312 | tf_op jit(solution)/shard_map/ppermute | solution.py:313
  13.6 4.0 %collective-permute-start.3 = (bf16[64,256]{1,0:T(8,128)(2,1)S(1)}, bf16[64,256]{1,0:T(8,128)(2,1)S(1)}, u32[]{:S(2)}, u32[]{:S(2)}) collective-permute-start(bf16[64,256]{1,0:T(8,128)(2,1)S(1)} %shard_map.67.refs_2_), channel_id=1, source_target_pairs={{16,0},{0,16},{17,1},{1,17},{18,2},{2,18},{19,3},{3,19},{20,4},{4,... | collective-permute-start | bytes 98312 | tf_op jit(solution)/shard_map/ppermute | solution.py:307
  20.2 5.6 %collective-permute-start.4 = (bf16[32,256]{1,0:T(8,128)(2,1)S(1)}, bf16[32,256]{1,0:T(8,128)(2,1)S(1)}, u32[]{:S(2)}, u32[]{:S(2)}) collective-permute-start(bf16[32,256]{1,0:T(8,128)(2,1)S(1)} %get-tuple-element.29), channel_id=1, source_target_pairs={{0,12},{1,13},{2,14},{3,15},{4,8},{5,9},{6,10},{7,11},{8,4},{9,5},... | collective-permute-start | bytes 49160 | tf_op jit(solution)/shard_map/ppermute | solution.py:299
  20.7 5.1 %collective-permute-start.5 = (bf16[32,256]{1,0:T(8,128)(2,1)S(1)}, bf16[32,256]{1,0:T(8,128)(2,1)S(1)}, u32[]{:S(2)}, u32[]{:S(2)}) collective-permute-start(bf16[32,256]{1,0:T(8,128)(2,1)S(1)} %get-tuple-element.30), channel_id=1, source_target_pairs={{0,8},{1,9},{2,10},{3,11},{4,12},{5,13},{6,14},{7,15},{8,0},{9,1},... | collective-permute-start | bytes 49160 | tf_op jit(solution)/shard_map/ppermute | solution.py:299
  20.7 5.6 %collective-permute-start.6 = (bf16[32,256]{1,0:T(8,128)(2,1)S(1)}, bf16[32,256]{1,0:T(8,128)(2,1)S(1)}, u32[]{:S(2)}, u32[]{:S(2)}) collective-permute-start(bf16[32,256]{1,0:T(8,128)(2,1)S(1)} %get-tuple-element.31), channel_id=1, source_target_pairs={{0,4},{1,5},{2,6},{3,7},{4,0},{5,1},{6,2},{7,3},{8,12},{9,13},{10,... | collective-permute-start | bytes 49160 | tf_op jit(solution)/shard_map/ppermute | solution.py:299
  26.4 4.3 %collective-permute-start.7 = (bf16[128,256]{1,0:T(8,128)(2,1)S(1)}, bf16[128,256]{1,0:T(8,128)(2,1)S(1)}, u32[]{:S(2)}, u32[]{:S(2)}) collective-permute-start(bf16[128,256]{1,0:T(8,128)(2,1)S(1)} %constant_dynamic-update-slice_fusion.refs_0_), channel_id=1, source_target_pairs={{0,2},{1,3},{2,0},{3,1},{4,6},{5,7},{6,4},{7,5},{8,10},{9,11},{10,... | collective-permute-start | bytes 196616 | tf_op jit(solution)/shard_map/ppermute | solution.py:299
  26.4 4.3 %collective-permute-start.8 = (bf16[128,256]{1,0:T(8,128)(2,1)S(1)}, bf16[128,256]{1,0:T(8,128)(2,1)S(1)}, u32[]{:S(2)}, u32[]{:S(2)}) collective-permute-start(bf16[128,256]{1,0:T(8,128)(2,1)S(1)} %constant_dynamic-update-slice_fusion.refs_0_), channel_id=1, source_target_pairs={{0,1},{1,0},{2,3},{3,2},{4,5},{5,4},{6,7},{7,6},{8,9},{9,8},{10,11... | collective-permute-start | bytes 196616 | tf_op jit(solution)/shard_map/ppermute | solution.py:299
  30.6 1.3 %collective-permute-start.9 = (bf16[128,256]{1,0:T(8,128)(2,1)S(1)}, bf16[128,256]{1,0:T(8,128)(2,1)S(1)}, u32[]{:S(2)}, u32[]{:S(2)}) collective-permute-start(bf16[128,256]{1,0:T(8,128)(2,1)S(1)} %collective-permute-done.7.refs_1_), channel_id=1, source_target_pairs={{0,1},{1,0},{2,3},{3,2},{4,5},{5,4},{6,7},{7,6},{8,9},{9,8},{10,11... | collective-permute-start | bytes 196616 | tf_op jit(solution)/shard_map/ppermute | solution.py:299
  33.1 5.6 %collective-permute-start.10 = (bf16[32,256]{1,0:T(8,128)(2,1)S(1)}, bf16[32,256]{1,0:T(8,128)(2,1)S(1)}, u32[]{:S(2)}, u32[]{:S(2)}) collective-permute-start(bf16[32,256]{1,0:T(8,128)(2,1)S(1)} %get-tuple-element.34), channel_id=1, source_target_pairs={{0,12},{1,13},{2,14},{3,15},{4,8},{5,9},{6,10},{7,11},{8,4},{9,5},... | collective-permute-start | bytes 49160 | tf_op jit(solution)/shard_map/ppermute | solution.py:299
  35.6 4.6 %collective-permute-start.11 = (bf16[32,256]{1,0:T(8,128)(2,1)S(1)}, bf16[32,256]{1,0:T(8,128)(2,1)S(1)}, u32[]{:S(2)}, u32[]{:S(2)}) collective-permute-start(bf16[32,256]{1,0:T(8,128)(2,1)S(1)} %get-tuple-element.35), channel_id=1, source_target_pairs={{0,8},{1,9},{2,10},{3,11},{4,12},{5,13},{6,14},{7,15},{8,0},{9,1},... | collective-permute-start | bytes 49160 | tf_op jit(solution)/shard_map/ppermute | solution.py:299
  36.7 3.8 %collective-permute-start.12 = (bf16[32,256]{1,0:T(8,128)(2,1)S(1)}, bf16[32,256]{1,0:T(8,128)(2,1)S(1)}, u32[]{:S(2)}, u32[]{:S(2)}) collective-permute-start(bf16[32,256]{1,0:T(8,128)(2,1)S(1)} %get-tuple-element.36), channel_id=1, source_target_pairs={{0,4},{1,5},{2,6},{3,7},{4,0},{5,1},{6,2},{7,3},{8,12},{9,13},{10,... | collective-permute-start | bytes 49160 | tf_op jit(solution)/shard_map/ppermute | solution.py:299

commit v8 on v6

--- a/solution.py
+++ b/solution.py
@@ -83,8 +83,9 @@
         copy.wait()
 
 
-def level_of(levels):
-    return lax.axis_index("lon") // (lax.axis_size("lon") // levels)
+def peer(levels, k):
+    level = lax.axis_index("lon") // (lax.axis_size("lon") // levels)
+    return level ^ ((levels - k) % levels)
 
 
 def strip_kernel(nlat, *refs):
@@ -225,7 +226,7 @@
     sent[...] = jnp.concatenate([inner, outer], axis=1).astype(bf16)
     some = rows // levels
     for k in range(levels):
-        part = sent[pl.ds((level_of(levels) ^ k) * some, some)]
+        part = sent[pl.ds(peer(levels, k) * some, some)]
         sent_refs[k][...] = part.reshape(sent_refs[k].shape)
 
 
@@ -258,7 +259,7 @@
     every = jnp.concatenate([part[...] for part in parts], axis=0)
     change = dot(every, attn_ref[3]).reshape(levels, some, cols, channels)
     for k in range(levels):
-        start = (level_of(levels) ^ k) * some
+        start = peer(levels, k) * some
 
         def state(ref, width):
             count = some * width
@@ -303,8 +304,11 @@
         return lax.ppermute(piece, "lon", [(j, j ^ mask) for j in range(nlon)])
 
     def exchange(pieces):
-        moved = [swap(pieces[k], k * column) for k in range(levels - 1, 0, -1)]
-        return [pieces[0]] + moved[::-1]
+        moved = []
+        for k in range(1, levels):
+            level = levels - k
+            moved.append(swap(pieces[k], level * column + level * 2 // levels))
+        return [pieces[0]] + moved
 
     tiles = [field]
     for s in range(1, nlat):
@@ -362,7 +366,7 @@
     circle = [jnp.concatenate(parts, axis=0)]
     mask = column // 2
     while mask:
-        circle = circle + [swap(part, mask) for part in circle]
+        circle = circle + [swap(part, mask + mask // 2) for part in circle]
         mask //= 2
     mixes = call(
         functools.partial(circle_kernel, levels, some), [piece] * levels, [*circle, lon_proj]

time: 40.4 us -> 36.6 us (0.906)
  waiting for transfers between devices: 11.9 us -> 7.73 us
    ppermute x10, waiting for transfers between devices: 11.1 us -> 6.94 us  [swap(): return lax.ppermute(piece, 'lon', [(j, j ^ mask) for j in range(nlon)])]
  transfers between devices with their start and end apart: 12 -> 12, of which waited for: 7 -> 8; matrix products, arithmetic and copies ran while one was open for 0% -> 0% of each run, Pallas kernels for 12% -> 13%
where the time goes in v8:
time: 36.6 us; the launch traced here: 36.4 us
  starting transfers between devices  19 us (52%)
  Pallas kernels  9.61 us (26%)
  waiting for transfers between devices  7.73 us (21%)
    ppermute x10, starting transfers between devices, swap(): return lax.ppermute(piece, 'lon', [(j, j ^ mask) for j in range(nlon)])  11 us
    pallas_call x6, Pallas kernels, call(): pl.pallas_call(kernel, out_shape=shapes, in_specs=[given] * len(operands)...  9.61 us
    ppermute x10, waiting for transfers between devices, swap(): return lax.ppermute(piece, 'lon', [(j, j ^ mask) for j in range(nlon)])  6.94 us
    ppermute x1, starting transfers between devices, shards(): lax.ppermute(far, 'lon', [(j, (j - 1) % nlon if j % 2 == 0 else (j + 1) %...  5.12 us
    ppermute x1, starting transfers between devices, shards(): lax.ppermute(field, 'lat', [((i + s) % nlat, i) for i in range(nlat)])  2.94 us
    ppermute x1, waiting for transfers between devices, shards(): lax.ppermute(field, 'lat', [((i + s) % nlat, i) for i in range(nlat)])  0.78 us
  transfers between devices with their start and end apart: 12, of which 8 were waited for; matrix products, arithmetic and copies ran while one was open for 0% of the time, Pallas kernels for 13%

profile of v8, /device:TPU:0, one launch (start us, length us, event | category | flops | bytes accessed | tf_op | source)
XLA Modules:
  0.0 36.4 jit_solution(2644110522499068702)
XLA Ops:
  0.0 0.0 copy-start
  0.0 2.9 %collective-permute-start = (bf16[8,16,256]{2,1,0:T(8,128)(2,1)}, bf16[8,16,256]{2,1,0:T(8,128)(2,1)S(1)}, u32[]{:S(2)}, u32[]{:S(2)}) collective-permute-start(bf16[8,16,256]{2,1,0:T(8,128)(2,1)} %refs_0_.7), channel_id=1, source_target_pairs={{16,0},{0,16},{17,1},{1,17},{18,2},{2,18},{19,3},{3,19},{20,4},{4,... | collective-permute-start | bytes 196616 | tf_op jit(solution)/shard_map/ppermute | solution.py:315
  2.9 1.7 %shard_map.64 = (bf16[256,1024]{1,0:T(8,128)(2,1)S(1)}, bf16[1024,256]{1,0:T(8,128)(2,1)S(1)}, bf16[4,256,256]{2,1,0:T(8,128)(2,1)S(1)}, bf16[4,256,256]{2,1,0:T(8,128)(2,1)S(1)}) custom-call(bf16[256,1024]{1,0:T(8,128)(2,1)} %refs_0_.4, bf16[1024,256]{1,0:T(8,128)(2,1)} %refs_1_.1, bf16[4,256,256]{2,1,0:T(8,128)(2,1)} %refs_2_.2, bf16[4,256,256]{2,1,0:T(8,128)(2,1)} %refs_3_.1), custom_call_target="tpu_custom_call" | custom-call | bytes 2097152 | tf_op jit(solution)/shard_map/pallas_call | solution.py:282
  4.7 0.8 %collective-permute-done.refs_1_ = bf16[8,16,256]{2,1,0:T(8,128)(2,1)S(1)} collective-permute-done((bf16[8,16,256]{2,1,0:T(8,128)(2,1)}, bf16[8,16,256]{2,1,0:T(8,128)(2,1)S(1)}, u32[]{:S(2)}, u32[]{:S(2)}) %collective-permute-start) | collective-permute-done | bytes 65568 | tf_op jit(solution)/shard_map/ppermute | solution.py:315
  5.5 0.0 copy-done
  5.5 0.0 copy-start.1
  5.5 0.1 collective-permute-start.1
  5.6 5.1 %collective-permute-start.2 = (bf16[128,256]{1,0:T(8,128)(2,1)S(1)}, bf16[128,256]{1,0:T(8,128)(2,1)S(1)}, u32[]{:S(2)}, u32[]{:S(2)}) collective-permute-start(bf16[128,256]{1,0:T(8,128)(2,1)S(1)} %get-tuple-element.24), channel_id=1, source_target_pairs={{0,15},{1,2},{2,1},{3,4},{4,3},{5,6},{6,5},{7,8},{8,7},{9,10},{10,... | collective-permute-start | bytes 196616 | tf_op jit(solution)/shard_map/ppermute | solution.py:336
  10.7 0.0 copy-done.1
  10.7 3.2 %shard_map.66 = (bf16[64,256]{1,0:T(8,128)(2,1)S(1)}, bf16[64,256]{1,0:T(8,128)(2,1)S(1)}) custom-call(bf16[8,16,256]{2,1,0:T(8,128)(2,1)S(1)} %copy-done, bf16[8,16,256]{2,1,0:T(8,128)(2,1)S(1)} %collective-permute-done.refs_1_, bf16[7,7,256]{2,1,0:T(8,128)(2,1)S(1)} %copy-done.1, bf16[256,1024]{1,0:T(8,128)(2,1)S(1)} %get-tuple-element.25.refs_3_.refs_6_, ...), custom_call_target="tpu_custom_call" | custom-call | flops 134217728 | bytes 1729024 | tf_op jit(solution)/shard_map/pallas_call | solution.py:282
  13.9 0.0 collective-permute-done.1.refs_2_
  13.9 0.0 collective-permute-done.2.refs_3_
  13.9 2.6 %shard_map.67 = (bf16[64,256]{1,0:T(8,128)(2,1)S(1)}, bf16[32,256]{1,0:T(8,128)(2,1)S(1)}, bf16[32,256]{1,0:T(8,128)(2,1)S(1)}, bf16[32,256]{1,0:T(8,128)(2,1)S(1)}, bf16[32,256]{1,0:T(8,128)(2,1)S(1)}) custom-call(bf16[8,16,256]{2,1,0:T(8,128)(2,1)S(1)} %copy-done, bf16[8,16,256]{2,1,0:T(8,128)(2,1)S(1)} %collective-permute-done.refs_1_, ...), custom_call_target="tpu_custom_call" | custom-call | flops 134217728 | bytes 1892864 | tf_op jit(solution)/shard_map/pallas_call | solution.py:282
  16.6 0.3 collective-permute-start.3
  16.9 0.0 collective-permute-start.4
  16.9 3.9 %collective-permute-start.5 = (bf16[32,256]{1,0:T(8,128)(2,1)S(1)}, bf16[32,256]{1,0:T(8,128)(2,1)S(1)}, u32[]{:S(2)}, u32[]{:S(2)}) collective-permute-start(bf16[32,256]{1,0:T(8,128)(2,1)S(1)} %get-tuple-element.31), channel_id=1, source_target_pairs={{0,4},{1,5},{2,6},{3,7},{4,0},{5,1},{6,2},{7,3},{8,12},{9,13},{10,... | collective-permute-start | bytes 49160 | tf_op jit(solution)/shard_map/ppermute | solution.py:304
  20.8 0.9 %collective-permute-done.3 = bf16[32,256]{1,0:T(8,128)(2,1)S(1)} collective-permute-done((bf16[32,256]{1,0:T(8,128)(2,1)S(1)}, bf16[32,256]{1,0:T(8,128)(2,1)S(1)}, u32[]{:S(2)}, u32[]{:S(2)}) %collective-permute-start.3) | collective-permute-done | bytes 16416 | tf_op jit(solution)/shard_map/ppermute | solution.py:304
  21.7 0.0 collective-permute-done.4
  21.7 0.8 %collective-permute-done.5 = bf16[32,256]{1,0:T(8,128)(2,1)S(1)} collective-permute-done((bf16[32,256]{1,0:T(8,128)(2,1)S(1)}, bf16[32,256]{1,0:T(8,128)(2,1)S(1)}, u32[]{:S(2)}, u32[]{:S(2)}) %collective-permute-start.5) | collective-permute-done | bytes 16416 | tf_op jit(solution)/shard_map/ppermute | solution.py:304
  22.5 0.0 collective-permute-start.6
  22.5 2.2 %collective-permute-start.7 = (bf16[128,256]{1,0:T(8,128)(2,1)S(1)}, bf16[128,256]{1,0:T(8,128)(2,1)S(1)}, u32[]{:S(2)}, u32[]{:S(2)}) collective-permute-start(bf16[128,256]{1,0:T(8,128)(2,1)S(1)} %constant_dynamic-update-slice_fusion.refs_0_), channel_id=1, source_target_pairs={{0,1},{1,0},{2,3},{3,2},{4,5},{5,4},{6,7},{7,6},{8,9},{9,8},{10,11... | collective-permute-start | bytes 196616 | tf_op jit(solution)/shard_map/ppermute | solution.py:304
  24.6 1.7 %collective-permute-done.6.refs_1_ = bf16[128,256]{1,0:T(8,128)(2,1)S(1)} collective-permute-done((bf16[128,256]{1,0:T(8,128)(2,1)S(1)}, bf16[128,256]{1,0:T(8,128)(2,1)S(1)}, u32[]{:S(2)}, u32[]{:S(2)}) %collective-permute-start.6) | collective-permute-done | bytes 65568 | tf_op jit(solution)/shard_map/ppermute | solution.py:304
  26.3 0.4 %collective-permute-start.8 = (bf16[128,256]{1,0:T(8,128)(2,1)S(1)}, bf16[128,256]{1,0:T(8,128)(2,1)S(1)}, u32[]{:S(2)}, u32[]{:S(2)}) collective-permute-start(bf16[128,256]{1,0:T(8,128)(2,1)S(1)} %collective-permute-done.6.refs_1_), channel_id=1, source_target_pairs={{0,1},{1,0},{2,3},{3,2},{4,5},{5,4},{6,7},{7,6},{8,9},{9,8},{10,11... | collective-permute-start | bytes 196616 | tf_op jit(solution)/shard_map/ppermute | solution.py:304
  26.7 0.0 collective-permute-done.7.refs_2_
  26.7 0.9 %collective-permute-done.8.refs_3_ = bf16[128,256]{1,0:T(8,128)(2,1)S(1)} collective-permute-done((bf16[128,256]{1,0:T(8,128)(2,1)S(1)}, bf16[128,256]{1,0:T(8,128)(2,1)S(1)}, u32[]{:S(2)}, u32[]{:S(2)}) %collective-permute-start.8) | collective-permute-done | bytes 65568 | tf_op jit(solution)/shard_map/ppermute | solution.py:304
  27.6 1.2 %shard_map.68 = (bf16[32,256]{1,0:T(8,128)(2,1)S(1)}, bf16[32,256]{1,0:T(8,128)(2,1)S(1)}, bf16[32,256]{1,0:T(8,128)(2,1)S(1)}, bf16[32,256]{1,0:T(8,128)(2,1)S(1)}) custom-call(bf16[128,256]{1,0:T(8,128)(2,1)S(1)} %constant_dynamic-update-slice_fusion.refs_0_, bf16[128,256]{1,0:T(8,128)(2,1)S(1)} %collective-permute-done.6.refs_1_, ...), custom_call_target="tpu_custom_call" | custom-call | bytes 786432 | tf_op jit(solution)/shard_map/pallas_call | solution.py:282
  28.8 1.8 %collective-permute-start.9 = (bf16[32,256]{1,0:T(8,128)(2,1)S(1)}, bf16[32,256]{1,0:T(8,128)(2,1)S(1)}, u32[]{:S(2)}, u32[]{:S(2)}) collective-permute-start(bf16[32,256]{1,0:T(8,128)(2,1)S(1)} %get-tuple-element.34), channel_id=1, source_target_pairs={{0,13},{1,12},{2,15},{3,14},{4,9},{5,8},{6,11},{7,10},{8,5},{9,4},... | collective-permute-start | bytes 49160 | tf_op jit(solution)/shard_map/ppermute | solution.py:304
  30.6 1.4 %collective-permute-start.10 = (bf16[32,256]{1,0:T(8,128)(2,1)S(1)}, bf16[32,256]{1,0:T(8,128)(2,1)S(1)}, u32[]{:S(2)}, u32[]{:S(2)}) collective-permute-start(bf16[32,256]{1,0:T(8,128)(2,1)S(1)} %get-tuple-element.35), channel_id=1, source_target_pairs={{0,9},{1,8},{2,11},{3,10},{4,13},{5,12},{6,15},{7,14},{8,1},{9,0},... | collective-permute-start | bytes 49160 | tf_op jit(solution)/shard_map/ppermute | solution.py:304
  31.9 1.1 %collective-permute-start.11 = (bf16[32,256]{1,0:T(8,128)(2,1)S(1)}, bf16[32,256]{1,0:T(8,128)(2,1)S(1)}, u32[]{:S(2)}, u32[]{:S(2)}) collective-permute-start(bf16[32,256]{1,0:T(8,128)(2,1)S(1)} %get-tuple-element.36), channel_id=1, source_target_pairs={{0,4},{1,5},{2,6},{3,7},{4,0},{5,1},{6,2},{7,3},{8,12},{9,13},{10,... | collective-permute-start | bytes 49160 | tf_op jit(solution)/shard_map/ppermute | solution.py:304
  33.0 0.9 %collective-permute-done.9.refs_1_ = bf16[32,256]{1,0:T(8,128)(2,1)S(1)} collective-permute-done((bf16[32,256]{1,0:T(8,128)(2,1)S(1)}, bf16[32,256]{1,0:T(8,128)(2,1)S(1)}, u32[]{:S(2)}, u32[]{:S(2)}) %collective-permute-start.9) | collective-permute-done | bytes 16416 | tf_op jit(solution)/shard_map/ppermute | solution.py:304
  33.8 1.1 %collective-permute-done.10.refs_2_ = bf16[32,256]{1,0:T(8,128)(2,1)S(1)} collective-permute-done((bf16[32,256]{1,0:T(8,128)(2,1)S(1)}, bf16[32,256]{1,0:T(8,128)(2,1)S(1)}, u32[]{:S(2)}, u32[]{:S(2)}) %collective-permute-start.10) | collective-permute-done | bytes 16416 | tf_op jit(solution)/shard_map/ppermute | solution.py:304
  35.0 0.7 %collective-permute-done.11.refs_3_ = bf16[32,256]{1,0:T(8,128)(2,1)S(1)} collective-permute-done((bf16[32,256]{1,0:T(8,128)(2,1)S(1)}, bf16[32,256]{1,0:T(8,128)(2,1)S(1)}, u32[]{:S(2)}, u32[]{:S(2)}) %collective-permute-start.11) | collective-permute-done | bytes 16416 | tf_op jit(solution)/shard_map/ppermute | solution.py:304
  35.6 0.8 %shard_map.69 = bf16[8,16,256]{2,1,0:T(8,128)(2,1)} custom-call(bf16[32,256]{1,0:T(8,128)(2,1)S(1)} %get-tuple-element.33.refs_0_, bf16[32,256]{1,0:T(8,128)(2,1)S(1)} %collective-permute-done.9.refs_1_, bf16[32,256]{1,0:T(8,128)(2,1)S(1)} %collective-permute-done.10.refs_2_, bf16[32,256]{1,0:T(8,128)(2,1)S(1)} %collective-permute-done.11.refs_3_, ...), custom_call_target="tpu_custom_call" | custom-call | bytes 655360 | tf_op jit(solution)/shard_map/pallas_call | solution.py:282
  (5 shorter events, 0.1 us)
Async XLA Ops:
  0.0 5.5 %copy-start = (bf16[8,16,256]{2,1,0:T(8,128)(2,1)S(1)}, bf16[8,16,256]{2,1,0:T(8,128)(2,1)}, u32[]{:S(2)}) copy-start(bf16[8,16,256]{2,1,0:T(8,128)(2,1)} %refs_0_.7) | copy-start | bytes 196612
  0.0 5.5 %collective-permute-start = (bf16[8,16,256]{2,1,0:T(8,128)(2,1)}, bf16[8,16,256]{2,1,0:T(8,128)(2,1)S(1)}, u32[]{:S(2)}, u32[]{:S(2)}) collective-permute-start(bf16[8,16,256]{2,1,0:T(8,128)(2,1)} %refs_0_.7), channel_id=1, source_target_pairs={{16,0},{0,16},{17,1},{1,17},{18,2},{2,18},{19,3},{3,19},{20,4},{4,... | collective-permute-start | bytes 196616 | tf_op jit(solution)/shard_map/ppermute | solution.py:315
  5.5 5.3 %copy-start.1 = (bf16[7,7,256]{2,1,0:T(8,128)(2,1)S(1)}, bf16[7,7,256]{2,1,0:T(8,128)(2,1)}, u32[]{:S(2)}) copy-start(bf16[7,7,256]{2,1,0:T(8,128)(2,1)} %refs_5_.1) | copy-start | bytes 75268
  5.5 8.4 %collective-permute-start.1 = (bf16[128,256]{1,0:T(8,128)(2,1)S(1)}, bf16[128,256]{1,0:T(8,128)(2,1)S(1)}, u32[]{:S(2)}, u32[]{:S(2)}) collective-permute-start(bf16[128,256]{1,0:T(8,128)(2,1)S(1)} %get-tuple-element.23), channel_id=1, source_target_pairs={{0,1},{1,0},{2,3},{3,2},{4,5},{5,4},{6,7},{7,6},{8,9},{9,8},{10,11... | collective-permute-start | bytes 196616 | tf_op jit(solution)/shard_map/ppermute | solution.py:304
  5.6 8.3 %collective-permute-start.2 = (bf16[128,256]{1,0:T(8,128)(2,1)S(1)}, bf16[128,256]{1,0:T(8,128)(2,1)S(1)}, u32[]{:S(2)}, u32[]{:S(2)}) collective-permute-start(bf16[128,256]{1,0:T(8,128)(2,1)S(1)} %get-tuple-element.24), channel_id=1, source_target_pairs={{0,15},{1,2},{2,1},{3,4},{4,3},{5,6},{6,5},{7,8},{8,7},{9,10},{10,... | collective-permute-start | bytes 196616 | tf_op jit(solution)/shard_map/ppermute | solution.py:336
  16.6 5.1 %collective-permute-start.3 = (bf16[32,256]{1,0:T(8,128)(2,1)S(1)}, bf16[32,256]{1,0:T(8,128)(2,1)S(1)}, u32[]{:S(2)}, u32[]{:S(2)}) collective-permute-start(bf16[32,256]{1,0:T(8,128)(2,1)S(1)} %get-tuple-element.29), channel_id=1, source_target_pairs={{0,13},{1,12},{2,15},{3,14},{4,9},{5,8},{6,11},{7,10},{8,5},{9,4},... | collective-permute-start | bytes 49160 | tf_op jit(solution)/shard_map/ppermute | solution.py:304
  16.9 4.8 %collective-permute-start.4 = (bf16[32,256]{1,0:T(8,128)(2,1)S(1)}, bf16[32,256]{1,0:T(8,128)(2,1)S(1)}, u32[]{:S(2)}, u32[]{:S(2)}) collective-permute-start(bf16[32,256]{1,0:T(8,128)(2,1)S(1)} %get-tuple-element.30), channel_id=1, source_target_pairs={{0,9},{1,8},{2,11},{3,10},{4,13},{5,12},{6,15},{7,14},{8,1},{9,0},... | collective-permute-start | bytes 49160 | tf_op jit(solution)/shard_map/ppermute | solution.py:304
  16.9 5.6 %collective-permute-start.5 = (bf16[32,256]{1,0:T(8,128)(2,1)S(1)}, bf16[32,256]{1,0:T(8,128)(2,1)S(1)}, u32[]{:S(2)}, u32[]{:S(2)}) collective-permute-start(bf16[32,256]{1,0:T(8,128)(2,1)S(1)} %get-tuple-element.31), channel_id=1, source_target_pairs={{0,4},{1,5},{2,6},{3,7},{4,0},{5,1},{6,2},{7,3},{8,12},{9,13},{10,... | collective-permute-start | bytes 49160 | tf_op jit(solution)/shard_map/ppermute | solution.py:304
  22.5 3.8 %collective-permute-start.6 = (bf16[128,256]{1,0:T(8,128)(2,1)S(1)}, bf16[128,256]{1,0:T(8,128)(2,1)S(1)}, u32[]{:S(2)}, u32[]{:S(2)}) collective-permute-start(bf16[128,256]{1,0:T(8,128)(2,1)S(1)} %constant_dynamic-update-slice_fusion.refs_0_), channel_id=1, source_target_pairs={{0,3},{1,2},{2,1},{3,0},{4,7},{5,6},{6,5},{7,4},{8,11},{9,10},{10,... | collective-permute-start | bytes 196616 | tf_op jit(solution)/shard_map/ppermute | solution.py:304
  22.5 4.2 %collective-permute-start.7 = (bf16[128,256]{1,0:T(8,128)(2,1)S(1)}, bf16[128,256]{1,0:T(8,128)(2,1)S(1)}, u32[]{:S(2)}, u32[]{:S(2)}) collective-permute-start(bf16[128,256]{1,0:T(8,128)(2,1)S(1)} %constant_dynamic-update-slice_fusion.refs_0_), channel_id=1, source_target_pairs={{0,1},{1,0},{2,3},{3,2},{4,5},{5,4},{6,7},{7,6},{8,9},{9,8},{10,11... | collective-permute-start | bytes 196616 | tf_op jit(solution)/shard_map/ppermute | solution.py:304
  26.3 1.3 %collective-permute-start.8 = (bf16[128,256]{1,0:T(8,128)(2,1)S(1)}, bf16[128,256]{1,0:T(8,128)(2,1)S(1)}, u32[]{:S(2)}, u32[]{:S(2)}) collective-permute-start(bf16[128,256]{1,0:T(8,128)(2,1)S(1)} %collective-permute-done.6.refs_1_), channel_id=1, source_target_pairs={{0,1},{1,0},{2,3},{3,2},{4,5},{5,4},{6,7},{7,6},{8,9},{9,8},{10,11... | collective-permute-start | bytes 196616 | tf_op jit(solution)/shard_map/ppermute | solution.py:304
  28.8 5.0 %collective-permute-start.9 = (bf16[32,256]{1,0:T(8,128)(2,1)S(1)}, bf16[32,256]{1,0:T(8,128)(2,1)S(1)}, u32[]{:S(2)}, u32[]{:S(2)}) collective-permute-start(bf16[32,256]{1,0:T(8,128)(2,1)S(1)} %get-tuple-element.34), channel_id=1, source_target_pairs={{0,13},{1,12},{2,15},{3,14},{4,9},{5,8},{6,11},{7,10},{8,5},{9,4},... | collective-permute-start | bytes 49160 | tf_op jit(solution)/shard_map/ppermute | solution.py:304
  30.6 4.4 %collective-permute-start.10 = (bf16[32,256]{1,0:T(8,128)(2,1)S(1)}, bf16[32,256]{1,0:T(8,128)(2,1)S(1)}, u32[]{:S(2)}, u32[]{:S(2)}) collective-permute-start(bf16[32,256]{1,0:T(8,128)(2,1)S(1)} %get-tuple-element.35), channel_id=1, source_target_pairs={{0,9},{1,8},{2,11},{3,10},{4,13},{5,12},{6,15},{7,14},{8,1},{9,0},... | collective-permute-start | bytes 49160 | tf_op jit(solution)/shard_map/ppermute | solution.py:304
  31.9 3.7 %collective-permute-start.11 = (bf16[32,256]{1,0:T(8,128)(2,1)S(1)}, bf16[32,256]{1,0:T(8,128)(2,1)S(1)}, u32[]{:S(2)}, u32[]{:S(2)}) collective-permute-start(bf16[32,256]{1,0:T(8,128)(2,1)S(1)} %get-tuple-element.36), channel_id=1, source_target_pairs={{0,4},{1,5},{2,6},{3,7},{4,0},{5,1},{6,2},{7,3},{8,12},{9,13},{10,... | collective-permute-start | bytes 49160 | tf_op jit(solution)/shard_map/ppermute | solution.py:304

commit v9 on v8

--- a/solution.py
+++ b/solution.py
@@ -14,6 +14,7 @@
 SIDE = 4
 LANES = 128
 LEVELS = 4
+STAGES = 4
 EPSILON = 1e-06
 VMEM_BYTES = 24 * 1024 * 1024
 STAGE_BYTES = 103 * 512 * 1024
@@ -66,21 +67,24 @@
     return out.astype(bf16)
 
 
-def stage_kernel(*refs):
-    count = (len(refs) - 1) // 2
-    sems = refs[-1]
+def stage(sources, targets, sems):
     copies = []
-    for i in range(count):
-        source, target = refs[i], refs[count + i]
-        pieces = sems.shape[1]
-        size = source.shape[0] // pieces
-        for k in range(pieces):
+    for i, (source, target) in enumerate(zip(sources, targets)):
+        size = source.shape[0] // STAGES
+        pieces = []
+        for k in range(STAGES):
             part = pl.ds(k * size, size)
-            copies.append(pltpu.make_async_copy(source.at[part], target.at[part], sems.at[i, k]))
-    for copy in copies:
-        copy.start()
-    for copy in copies:
-        copy.wait()
+            pieces.append(pltpu.make_async_copy(source.at[part], target.at[part], sems.at[i, k]))
+        copies.append(pieces)
+    for pieces in copies:
+        for piece in pieces:
+            piece.start()
+
+    def ready(i):
+        for piece in copies[i]:
+            piece.wait()
+
+    return ready
 
 
 def peer(levels, k):
@@ -88,9 +92,13 @@
     return level ^ ((levels - k) % levels)
 
 
+def copy_kernel(source_ref, target_ref):
+    target_ref[...] = source_ref[...]
+
+
 def strip_kernel(nlat, *refs):
     tiles = refs[:nlat]
-    near_ref, far_ref, near, far = refs[nlat + 1 :]
+    near_ref, far_ref, near, far = refs[nlat:]
     rows, cols, channels = tiles[0].shape
     even = lax.axis_index("lon") % 2 == 0
     for s in range(nlat):
@@ -99,11 +107,35 @@
         where = pl.ds(lax.rem(lax.axis_index("lat") + s, nlat) * rows, rows)
         near[where] = jnp.where(even, last, first)
         far[where] = jnp.where(even, first, last)
-    near_ref[...] = near[...].reshape(near_ref.shape).astype(bf16)
-    far_ref[...] = far[...].reshape(far_ref.shape).astype(bf16)
-
-
-def chain(my_lat, slab, shape, dw_ref, expand_ref, reduce_ref, attn_ref, center, scratch):
+    for strip, strip_ref, is_last in ((near, near_ref, even), (far, far_ref, ~even)):
+        strip_ref[...] = pack(strip[...], is_last).reshape(strip_ref.shape).astype(bf16)
+
+
+def lower_half():
+    return lax.broadcasted_iota(jnp.int32, (1, STRIP, 1), 1) < SIDE
+
+
+def turn(values):
+    return jnp.concatenate([values[:, SIDE:], values[:, :SIDE]], axis=1)
+
+
+def pack(strip, is_last):
+    half = strip.shape[0] // 2
+    turned = turn(strip)
+    low = jnp.where(is_last, turned, strip)
+    high = jnp.where(is_last, strip, turned)
+    return jnp.where(lower_half(), low[:half], high[half:])
+
+
+def unpack(packed, is_left):
+    turned = turn(packed)
+    low = jnp.where(is_left, turned, packed)
+    high = jnp.where(is_left, packed, turned)
+    return jnp.concatenate([low, high], axis=0)
+
+
+def chain(my_lat, slab, shape, weights, center, scratch, ready=lambda i: None):
+    dw_ref, expand_ref, reduce_ref, attn_ref = weights
     taps, one, lat_in = scratch
     rows, all_rows, columns, channels = shape
     cells = all_rows * columns
@@ -119,6 +151,9 @@
         parts.append(acc.reshape(cells, LANES))
     normed = layer_norm(jnp.concatenate(parts, axis=-1)).astype(bf16)
 
+    ready(0)
+    ready(1)
+
     def widen(k, total):
         part = slice(k * channels, (k + 1) * channels)
         wide = gelu(dot(normed, expand_ref[:, part])).astype(bf16)
@@ -131,6 +166,7 @@
     one[...] = block_one
     every = layer_norm(block_one.astype(f32)).astype(bf16)
     lat_in[...] = every
+    ready(2)
     count = rows * columns
     own = pl.ds(pl.multiple_of(my_lat * count, count), count)
     queries = dot(lat_in[own], attn_ref[0]).astype(bf16)
@@ -162,13 +198,15 @@
 
 
 def inner_kernel(nlat, *refs):
-    tiles, refs = refs[:nlat], refs[nlat:]
-    dw_ref, expand_ref, reduce_ref, attn_ref, two_ref, in_ref, padded, *scratch = refs
+    tiles, dw_ref, sources, refs = refs[:nlat], refs[nlat], refs[nlat + 1 : nlat + 5], refs[nlat + 5 :]
+    two_ref, in_ref, *targets = refs[:6]
+    padded, sems, *scratch = refs[6:]
+    ready = stage(sources, targets, sems)
     rows, cols, channels = tiles[0].shape
     all_rows = rows * nlat
     columns = cols - 2 * SIDE
+    my_lat = lax.axis_index("lat")
     clear(padded, all_rows)
-    my_lat = lax.axis_index("lat")
     fill_tiles(padded, my_lat, 0, tiles)
 
     def slab(b, c):
@@ -177,30 +215,40 @@
 
     center = padded[HALO : HALO + all_rows, SIDE : SIDE + columns]
     shape = (rows, all_rows, columns, channels)
-    block_two, lon_in = chain(
-        my_lat, slab, shape, dw_ref, expand_ref, reduce_ref, attn_ref, center, scratch
-    )
+    weights = (dw_ref, *targets[:3])
+    block_two, lon_in = chain(my_lat, slab, shape, weights, center, scratch, ready)
     two_ref[...] = block_two
     in_ref[...] = lon_in.astype(bf16)
+    ready(3)
 
 
 def outer_kernel(nlat, levels, *refs):
     tiles, refs = refs[:nlat], refs[nlat:]
-    near_ref, far_ref, inner_in_ref, dw_ref, expand_ref, reduce_ref, attn_ref = refs[:7]
-    two_ref, *refs = refs[7:]
+    near_ref, far_ref, inner_in_ref = refs[:3]
+    ends, weights = refs[3 : nlat + 3], refs[nlat + 3 : nlat + 7]
+    two_ref, *refs = refs[nlat + 7 :]
     sent_refs, (sent, padded, *scratch) = refs[:levels], refs[levels:]
     rows, cols, channels = tiles[0].shape
     all_rows = rows * nlat
     columns = 2 * SIDE
-    strip_shape = (all_rows, STRIP, channels)
-    near = near_ref[...].astype(f32).reshape(strip_shape)
-    far = far_ref[...].astype(f32).reshape(strip_shape)
+    packed = (all_rows // 2, STRIP, channels)
+    near = near_ref[...].astype(f32).reshape(packed)
+    far = far_ref[...].astype(f32).reshape(packed)
     even = lax.axis_index("lon") % 2 == 0
+    my_lat = lax.axis_index("lat")
     clear(padded, all_rows)
-    fill(padded, all_rows, 0, jnp.where(even, far, near))
-    my_lat = lax.axis_index("lat")
+    fill(padded, all_rows, 0, unpack(jnp.where(even, far, near), True))
     fill_tiles(padded, my_lat, STRIP, tiles)
-    fill(padded, all_rows, STRIP + cols, jnp.where(even, near, far))
+    fill(padded, all_rows, STRIP + cols, unpack(jnp.where(even, near, far), False))
+
+    @pl.when(lax.axis_index("lon") == 0)
+    def _():
+        fill_tiles(padded, my_lat, 0, [end[...].astype(f32)[:, cols - STRIP :] for end in ends])
+
+    @pl.when(lax.axis_index("lon") == lax.axis_size("lon") - 1)
+    def _():
+        fill_tiles(padded, my_lat, STRIP + cols, [end[...].astype(f32)[:, :STRIP] for end in ends])
+
     sublane = lax.broadcasted_iota(jnp.int32, (1, columns, 1), 1)
 
     def halves(shift, rows_of, c, width):
@@ -217,9 +265,7 @@
 
     center = halves(0, slice(HALO, HALO + all_rows), 0, channels)
     shape = (rows, all_rows, columns, channels)
-    block_two, lon_in = chain(
-        my_lat, slab, shape, dw_ref, expand_ref, reduce_ref, attn_ref, center, scratch
-    )
+    block_two, lon_in = chain(my_lat, slab, shape, weights, center, scratch)
     two_ref[...] = block_two
     inner = inner_in_ref[...].astype(f32).reshape(rows, cols - columns, channels)
     outer = lon_in.reshape(rows, columns, channels)
@@ -272,17 +318,15 @@
         out_ref[pl.ds(start, some)] = total.astype(bf16)
 
 
-def call(
-    kernel, outs, operands, scratch=(), any_space=False, flops=0, grant=VMEM_BYTES
-):
+def call(kernel, outs, operands, scratch=(), kept=0, flops=0, grant=VMEM_BYTES):
     vmem = pl.BlockSpec(memory_space=pltpu.VMEM)
-    given = pl.BlockSpec(memory_space=pl.ANY) if any_space else vmem
+    given = [vmem] * (len(operands) - kept) + [pl.BlockSpec(memory_space=pl.ANY)] * kept
     shapes = [jax.ShapeDtypeStruct(shape, bf16) for shape in outs]
     moved = sum(x.size * x.dtype.itemsize for x in operands)
     result = pl.pallas_call(
         kernel,
         out_shape=shapes,
-        in_specs=[given] * len(operands),
+        in_specs=given,
         out_specs=[vmem] * len(outs),
         scratch_shapes=list(scratch),
         compiler_params=pltpu.CompilerParams(vmem_limit_bytes=grant),
@@ -313,52 +357,53 @@
     tiles = [field]
     for s in range(1, nlat):
         tiles.append(lax.ppermute(field, "lat", [((i + s) % nlat, i) for i in range(nlat)]))
-    weights = (w_expand, w_reduce, lat_attn, lon_attn)
-    staged = call(
-        stage_kernel,
-        [w.shape for w in weights],
-        weights,
-        [pltpu.SemaphoreType.DMA((len(weights), 4))],
-        any_space=True,
-        grant=STAGE_BYTES,
-    )
-    expand, reduce, lat_proj, lon_proj = staged
-
-    strip = (all_rows * STRIP, channels)
+    tiles[0] = call(copy_kernel, [field.shape], [field])[0]
+    last = nlon - 1
+    ends = []
+    for s in range(nlat):
+        pairs = []
+        for i in range(nlat):
+            here, there = i * nlon, (i + s) % nlat * nlon
+            pairs += [(there + last, here), (there, here + last)]
+        ends.append(lax.ppermute(field, ("lat", "lon"), pairs))
+
+    strip = (all_rows * SIDE, channels)
     strip_scratch = pltpu.VMEM((all_rows, STRIP, channels), f32)
     near, far = call(
         functools.partial(strip_kernel, nlat),
         [strip, strip],
-        [*tiles, reduce],
+        tiles,
         [strip_scratch, strip_scratch],
     )
     near = swap(near, 1)
-    far = lax.ppermute(
-        far, "lon", [(j, (j - 1) % nlon if j % 2 == 0 else (j + 1) % nlon) for j in range(nlon)]
-    )
-
-    def scratch(width, count):
-        return [
-            pltpu.VMEM((all_rows + 2 * HALO, width, channels), f32),
-            pltpu.VMEM(dw_weight.shape, f32),
-            pltpu.VMEM((all_rows * count, channels), bf16),
-            pltpu.VMEM((all_rows * count, channels), bf16),
-        ]
+    odd = range(1, nlon - 1, 2)
+    far = lax.ppermute(far, "lon", [p for j in odd for p in ((j, j + 1), (j + 1, j))])
+
+    def padded(width):
+        return pltpu.VMEM((all_rows + 2 * HALO, width, channels), f32)
+
+    def scratch(count):
+        kept = pltpu.VMEM((all_rows * count, channels), bf16)
+        return [pltpu.VMEM(dw_weight.shape, f32), kept, kept]
 
     work = 4 * all_rows * columns * channels * w_expand.shape[1]
-    inner_two, inner_in = call(
+    weights = (w_expand, w_reduce, lat_attn, lon_attn)
+    inner = (rows * (cols - columns), channels)
+    inner_two, inner_in, expand, reduce, lat_proj, lon_proj = call(
         functools.partial(inner_kernel, nlat),
-        [(rows * (cols - columns), channels)] * 2,
-        [*tiles, dw_weight, expand, reduce, lat_proj],
-        scratch(cols, cols - columns),
+        [inner, inner] + [w.shape for w in weights],
+        [*tiles, dw_weight, *weights],
+        [padded(cols), pltpu.SemaphoreType.DMA((len(weights), STAGES)), *scratch(cols - columns)],
+        kept=len(weights),
         flops=work,
+        grant=STAGE_BYTES,
     )
     piece = (some * cols, channels)
     outer_two, *parts = call(
         functools.partial(outer_kernel, nlat, levels),
         [(rows * columns, channels)] + [piece] * levels,
-        [*tiles, near, far, inner_in, dw_weight, expand, reduce, lat_proj],
-        [pltpu.VMEM((rows, cols, channels), bf16)] + scratch(cols + 2 * STRIP, columns),
+        [*tiles, near, far, inner_in, *ends, dw_weight, expand, reduce, lat_proj],
+        [pltpu.VMEM((rows, cols, channels), bf16), padded(cols + 2 * STRIP), *scratch(columns)],
         flops=work,
     )
 

time: 36.6 us -> 42.1 us (1.15)
  waiting for transfers between devices: 7.73 us -> 11.2 us
  starting transfers between devices: 19 us -> 21.4 us
  Pallas kernels: 9.61 us -> 8.24 us
  local copies, waits for them, and re-layouts: 0.02 us -> 0.86 us
    ppermute x1 -> x3, starting transfers between devices: 5.12 us -> 8.35 us  [the longest x2 7.69 us: shards(): ends.append(lax.ppermute(field, ('lat', 'lon'), pairs))]
    ppermute x10, waiting for transfers between devices: 6.94 us -> 10 us  [swap(): return lax.ppermute(piece, 'lon', [(j, j ^ mask) for j in range(nlon)])]
    pallas_call x6, Pallas kernels: 9.61 us -> 8.24 us  [call(): pl.pallas_call(kernel, out_shape=shapes, in_specs=given, out_specs=[vmem]...]
    ppermute x1 -> x3, waiting for transfers between devices: 0.01 us -> 1.15 us  [the longest x2 1.14 us: shards(): ends.append(lax.ppermute(field, ('lat', 'lon'), pairs))]
    unnamed x7, local copies, waits for them, and re-layouts: 0.01 us -> 0.85 us
    ppermute x10, starting transfers between devices: 11 us -> 10.1 us  [swap(): return lax.ppermute(piece, 'lon', [(j, j ^ mask) for j in range(nlon)])]
    ppermute x1, waiting for transfers between devices: 0.78 us -> 0.01 us  [shards(): lax.ppermute(field, 'lat', [((i + s) % nlat, i) for i in range(nlat)])]
  transfers between devices with their start and end apart: 12 -> 14, of which waited for: 8 -> 8; matrix products, arithmetic and copies ran while one was open for 0% -> 0% of each run, Pallas kernels for 13% -> 9%
where the time goes in v9:
time: 42.1 us; the launch traced here: 41.8 us
  starting transfers between devices  21.4 us (51%)
  waiting for transfers between devices  11.2 us (27%)
  Pallas kernels  8.24 us (20%)
  local copies, waits for them, and re-layouts  0.86 us (2%)
    ppermute x10, starting transfers between devices, swap(): return lax.ppermute(piece, 'lon', [(j, j ^ mask) for j in range(nlon)])  10.1 us
    ppermute x10, waiting for transfers between devices, swap(): return lax.ppermute(piece, 'lon', [(j, j ^ mask) for j in range(nlon)])  10 us
    pallas_call x6, Pallas kernels, call(): pl.pallas_call(kernel, out_shape=shapes, in_specs=given, out_specs=[vmem]...  8.24 us
    ppermute x2, starting transfers between devices, shards(): ends.append(lax.ppermute(field, ('lat', 'lon'), pairs))  7.69 us
    ppermute x1, starting transfers between devices, shards(): lax.ppermute(field, 'lat', [((i + s) % nlat, i) for i in range(nlat)])  2.94 us
    ppermute x2, waiting for transfers between devices, shards(): ends.append(lax.ppermute(field, ('lat', 'lon'), pairs))  1.14 us
    unnamed x7, local copies, waits for them, and re-layouts  0.85 us
  transfers between devices with their start and end apart: 14, of which 8 were waited for; matrix products, arithmetic and copies ran while one was open for 0% of the time, Pallas kernels for 9%

profile of v9, /device:TPU:0, one launch (start us, length us, event | category | flops | bytes accessed | tf_op | source)
XLA Modules:
  0.0 41.8 jit_solution(311909832749094479)
XLA Ops:
  0.0 2.9 %collective-permute-start = (bf16[8,16,256]{2,1,0:T(8,128)(2,1)}, bf16[8,16,256]{2,1,0:T(8,128)(2,1)S(1)}, u32[]{:S(2)}, u32[]{:S(2)}) collective-permute-start(bf16[8,16,256]{2,1,0:T(8,128)(2,1)} %source_ref.1), channel_id=1, source_target_pairs={{16,0},{0,16},{17,1},{1,17},{18,2},{2,18},{19,3},{3,19},{20,4},{4,... | collective-permute-start | bytes 196616 | tf_op jit(solution)/shard_map/ppermute | solution.py:359
  2.9 5.6 %collective-permute-start.4 = (bf16[8,16,256]{2,1,0:T(8,128)(2,1)}, bf16[8,16,256]{2,1,0:T(8,128)(2,1)S(1)}, u32[]{:S(2)}, u32[]{:S(2)}) collective-permute-start(bf16[8,16,256]{2,1,0:T(8,128)(2,1)} %source_ref.1), channel_id=1, source_target_pairs={{31,0},{16,15},{15,16},{0,31}} | collective-permute-start | bytes 196616 | tf_op jit(solution)/shard_map/ppermute | solution.py:368
  8.5 2.1 %collective-permute-start.3 = (bf16[8,16,256]{2,1,0:T(8,128)(2,1)}, bf16[8,16,256]{2,1,0:T(8,128)(2,1)S(1)}, u32[]{:S(2)}, u32[]{:S(2)}) collective-permute-start(bf16[8,16,256]{2,1,0:T(8,128)(2,1)} %source_ref.1), channel_id=1, source_target_pairs={{15,0},{0,15},{31,16},{16,31}} | collective-permute-start | bytes 196616 | tf_op jit(solution)/shard_map/ppermute | solution.py:368
  10.6 0.0 copy-start.1
  10.7 0.8 %copy-done.1 = bf16[8,16,256]{2,1,0:T(8,128)(2,1)S(1)} copy-done((bf16[8,16,256]{2,1,0:T(8,128)(2,1)S(1)}, bf16[8,16,256]{2,1,0:T(8,128)(2,1)}, u32[]{:S(2)}) %copy-start.1) | copy-done | bytes 65560
  11.5 0.0 copy-start
  11.5 0.0 collective-permute-done.refs_1_
  11.5 0.1 shard_map.65
  11.6 0.1 collective-permute-start.1
  11.7 0.7 %collective-permute-start.2 = (bf16[64,256]{1,0:T(8,128)(2,1)S(1)}, bf16[64,256]{1,0:T(8,128)(2,1)S(1)}, u32[]{:S(2)}, u32[]{:S(2)}) collective-permute-start(bf16[64,256]{1,0:T(8,128)(2,1)S(1)} %get-tuple-element.23), channel_id=1, source_target_pairs={{1,2},{2,1},{3,4},{4,3},{5,6},{6,5},{7,8},{8,7},{9,10},{10,9},{11,... | collective-permute-start | bytes 98312 | tf_op jit(solution)/shard_map/ppermute | solution.py:380
  12.3 0.0 copy-done
  12.3 3.5 %shard_map.66 = (bf16[64,256]{1,0:T(8,128)(2,1)S(1)}, bf16[64,256]{1,0:T(8,128)(2,1)S(1)}, bf16[256,1024]{1,0:T(8,128)(2,1)S(1)}, bf16[1024,256]{1,0:T(8,128)(2,...) custom-call(bf16[8,16,256]{2,1,0:T(8,128)(2,1)S(1)} %shard_map.64.refs_0_, ...), custom_call_target="tpu_custom_call" | custom-call | flops 134217728 | bytes 2253312 | tf_op jit(solution)/shard_map/pallas_call | solution.py:326
  15.9 0.0 collective-permute-done.4.refs_6_
  15.9 1.1 %collective-permute-done.3.refs_5_ = bf16[8,16,256]{2,1,0:T(8,128)(2,1)S(1)} collective-permute-done((bf16[8,16,256]{2,1,0:T(8,128)(2,1)}, bf16[8,16,256]{2,1,0:T(8,128)(2,1)S(1)}, u32[]{:S(2)}, u32[]{:S(2)}) %collective-permute-start.3) | collective-permute-done | bytes 65568 | tf_op jit(solution)/shard_map/ppermute | solution.py:368
  17.0 0.0 collective-permute-done.1.refs_2_
  17.0 0.0 collective-permute-done.2.refs_3_
  17.0 2.6 %shard_map.67 = (bf16[64,256]{1,0:T(8,128)(2,1)S(1)}, bf16[32,256]{1,0:T(8,128)(2,1)S(1)}, bf16[32,256]{1,0:T(8,128)(2,1)S(1)}, bf16[32,256]{1,0:T(8,128)(2,1)S(1)}, bf16[32,256]{1,0:T(8,128)(2,1)S(1)}) custom-call(bf16[8,16,256]{2,1,0:T(8,128)(2,1)S(1)} %shard_map.64.refs_0_, bf16[8,16,256]{2,1,0:T(8,128)(2,1)S(1)} %collective-permute-done.refs_1_, ...), custom_call_target="tpu_custom_call" | custom-call | flops 134217728 | bytes 1958400 | tf_op jit(solution)/shard_map/pallas_call | solution.py:326
  19.6 5.1 %collective-permute-start.5 = (bf16[32,256]{1,0:T(8,128)(2,1)S(1)}, bf16[32,256]{1,0:T(8,128)(2,1)S(1)}, u32[]{:S(2)}, u32[]{:S(2)}) collective-permute-start(bf16[32,256]{1,0:T(8,128)(2,1)S(1)} %get-tuple-element.29), channel_id=1, source_target_pairs={{0,13},{1,12},{2,15},{3,14},{4,9},{5,8},{6,11},{7,10},{8,5},{9,4},... | collective-permute-start | bytes 49160 | tf_op jit(solution)/shard_map/ppermute | solution.py:348
  24.7 0.0 collective-permute-start.6
  24.7 0.6 %collective-permute-start.7 = (bf16[32,256]{1,0:T(8,128)(2,1)S(1)}, bf16[32,256]{1,0:T(8,128)(2,1)S(1)}, u32[]{:S(2)}, u32[]{:S(2)}) collective-permute-start(bf16[32,256]{1,0:T(8,128)(2,1)S(1)} %get-tuple-element.31), channel_id=1, source_target_pairs={{0,4},{1,5},{2,6},{3,7},{4,0},{5,1},{6,2},{7,3},{8,12},{9,13},{10,... | collective-permute-start | bytes 49160 | tf_op jit(solution)/shard_map/ppermute | solution.py:348
  25.4 0.9 %collective-permute-done.5 = bf16[32,256]{1,0:T(8,128)(2,1)S(1)} collective-permute-done((bf16[32,256]{1,0:T(8,128)(2,1)S(1)}, bf16[32,256]{1,0:T(8,128)(2,1)S(1)}, u32[]{:S(2)}, u32[]{:S(2)}) %collective-permute-start.5) | collective-permute-done | bytes 16416 | tf_op jit(solution)/shard_map/ppermute | solution.py:348
  26.3 2.5 %collective-permute-done.6 = bf16[32,256]{1,0:T(8,128)(2,1)S(1)} collective-permute-done((bf16[32,256]{1,0:T(8,128)(2,1)S(1)}, bf16[32,256]{1,0:T(8,128)(2,1)S(1)}, u32[]{:S(2)}, u32[]{:S(2)}) %collective-permute-start.6) | collective-permute-done | bytes 16416 | tf_op jit(solution)/shard_map/ppermute | solution.py:348
  28.8 0.0 collective-permute-done.7
  28.8 0.1 collective-permute-start.8
  28.9 0.1 collective-permute-start.9
  29.0 3.6 %collective-permute-done.8.refs_1_ = bf16[128,256]{1,0:T(8,128)(2,1)S(1)} collective-permute-done((bf16[128,256]{1,0:T(8,128)(2,1)S(1)}, bf16[128,256]{1,0:T(8,128)(2,1)S(1)}, u32[]{:S(2)}, u32[]{:S(2)}) %collective-permute-start.8) | collective-permute-done | bytes 65568 | tf_op jit(solution)/shard_map/ppermute | solution.py:348
  32.6 0.0 collective-permute-start.10
  32.6 0.0 collective-permute-done.9.refs_2_
  32.6 1.2 %collective-permute-done.10.refs_3_ = bf16[128,256]{1,0:T(8,128)(2,1)S(1)} collective-permute-done((bf16[128,256]{1,0:T(8,128)(2,1)S(1)}, bf16[128,256]{1,0:T(8,128)(2,1)S(1)}, u32[]{:S(2)}, u32[]{:S(2)}) %collective-permute-start.10) | collective-permute-done | bytes 65568 | tf_op jit(solution)/shard_map/ppermute | solution.py:348
  33.8 1.2 %shard_map.68 = (bf16[32,256]{1,0:T(8,128)(2,1)S(1)}, bf16[32,256]{1,0:T(8,128)(2,1)S(1)}, bf16[32,256]{1,0:T(8,128)(2,1)S(1)}, bf16[32,256]{1,0:T(8,128)(2,1)S(1)}) custom-call(bf16[128,256]{1,0:T(8,128)(2,1)S(1)} %constant_dynamic-update-slice_fusion.refs_0_, bf16[128,256]{1,0:T(8,128)(2,1)S(1)} %collective-permute-done.8.refs_1_, ...), custom_call_target="tpu_custom_call" | custom-call | bytes 786432 | tf_op jit(solution)/shard_map/pallas_call | solution.py:326
  35.1 1.1 %collective-permute-start.11 = (bf16[32,256]{1,0:T(8,128)(2,1)S(1)}, bf16[32,256]{1,0:T(8,128)(2,1)S(1)}, u32[]{:S(2)}, u32[]{:S(2)}) collective-permute-start(bf16[32,256]{1,0:T(8,128)(2,1)S(1)} %get-tuple-element.34), channel_id=1, source_target_pairs={{0,13},{1,12},{2,15},{3,14},{4,9},{5,8},{6,11},{7,10},{8,5},{9,4},... | collective-permute-start | bytes 49160 | tf_op jit(solution)/shard_map/ppermute | solution.py:348
  36.2 0.4 %collective-permute-start.12 = (bf16[32,256]{1,0:T(8,128)(2,1)S(1)}, bf16[32,256]{1,0:T(8,128)(2,1)S(1)}, u32[]{:S(2)}, u32[]{:S(2)}) collective-permute-start(bf16[32,256]{1,0:T(8,128)(2,1)S(1)} %get-tuple-element.35), channel_id=1, source_target_pairs={{0,9},{1,8},{2,11},{3,10},{4,13},{5,12},{6,15},{7,14},{8,1},{9,0},... | collective-permute-start | bytes 49160 | tf_op jit(solution)/shard_map/ppermute | solution.py:348
  36.6 2.6 %collective-permute-start.13 = (bf16[32,256]{1,0:T(8,128)(2,1)S(1)}, bf16[32,256]{1,0:T(8,128)(2,1)S(1)}, u32[]{:S(2)}, u32[]{:S(2)}) collective-permute-start(bf16[32,256]{1,0:T(8,128)(2,1)S(1)} %get-tuple-element.36), channel_id=1, source_target_pairs={{0,4},{1,5},{2,6},{3,7},{4,0},{5,1},{6,2},{7,3},{8,12},{9,13},{10,... | collective-permute-start | bytes 49160 | tf_op jit(solution)/shard_map/ppermute | solution.py:348
  39.2 0.9 %collective-permute-done.11.refs_1_ = bf16[32,256]{1,0:T(8,128)(2,1)S(1)} collective-permute-done((bf16[32,256]{1,0:T(8,128)(2,1)S(1)}, bf16[32,256]{1,0:T(8,128)(2,1)S(1)}, u32[]{:S(2)}, u32[]{:S(2)}) %collective-permute-start.11) | collective-permute-done | bytes 16416 | tf_op jit(solution)/shard_map/ppermute | solution.py:348
  40.1 0.5 %collective-permute-done.12.refs_2_ = bf16[32,256]{1,0:T(8,128)(2,1)S(1)} collective-permute-done((bf16[32,256]{1,0:T(8,128)(2,1)S(1)}, bf16[32,256]{1,0:T(8,128)(2,1)S(1)}, u32[]{:S(2)}, u32[]{:S(2)}) %collective-permute-start.12) | collective-permute-done | bytes 16416 | tf_op jit(solution)/shard_map/ppermute | solution.py:348
  40.6 0.4 collective-permute-done.13.refs_3_
  41.0 0.8 %shard_map.69 = bf16[8,16,256]{2,1,0:T(8,128)(2,1)} custom-call(bf16[32,256]{1,0:T(8,128)(2,1)S(1)} %get-tuple-element.33.refs_0_, bf16[32,256]{1,0:T(8,128)(2,1)S(1)} %collective-permute-done.11.refs_1_, bf16[32,256]{1,0:T(8,128)(2,1)S(1)} %collective-permute-done.12.refs_2_, bf16[32,256]{1,0:T(8,128)(2,1)S(1)} %collective-permute-done.13.refs_3_, ...), custom_call_target="tpu_custom_call" | custom-call | bytes 655360 | tf_op jit(solution)/shard_map/pallas_call | solution.py:326
  (5 shorter events, 0.0 us)
Async XLA Ops:
  0.0 11.5 %collective-permute-start = (bf16[8,16,256]{2,1,0:T(8,128)(2,1)}, bf16[8,16,256]{2,1,0:T(8,128)(2,1)S(1)}, u32[]{:S(2)}, u32[]{:S(2)}) collective-permute-start(bf16[8,16,256]{2,1,0:T(8,128)(2,1)} %source_ref.1), channel_id=1, source_target_pairs={{16,0},{0,16},{17,1},{1,17},{18,2},{2,18},{19,3},{3,19},{20,4},{4,... | collective-permute-start | bytes 196616 | tf_op jit(solution)/shard_map/ppermute | solution.py:359
  2.9 12.9 %collective-permute-start.4 = (bf16[8,16,256]{2,1,0:T(8,128)(2,1)}, bf16[8,16,256]{2,1,0:T(8,128)(2,1)S(1)}, u32[]{:S(2)}, u32[]{:S(2)}) collective-permute-start(bf16[8,16,256]{2,1,0:T(8,128)(2,1)} %source_ref.1), channel_id=1, source_target_pairs={{31,0},{16,15},{15,16},{0,31}} | collective-permute-start | bytes 196616 | tf_op jit(solution)/shard_map/ppermute | solution.py:368
  8.5 8.5 %collective-permute-start.3 = (bf16[8,16,256]{2,1,0:T(8,128)(2,1)}, bf16[8,16,256]{2,1,0:T(8,128)(2,1)S(1)}, u32[]{:S(2)}, u32[]{:S(2)}) collective-permute-start(bf16[8,16,256]{2,1,0:T(8,128)(2,1)} %source_ref.1), channel_id=1, source_target_pairs={{15,0},{0,15},{31,16},{16,31}} | collective-permute-start | bytes 196616 | tf_op jit(solution)/shard_map/ppermute | solution.py:368
  10.6 0.9 %copy-start.1 = (bf16[8,16,256]{2,1,0:T(8,128)(2,1)S(1)}, bf16[8,16,256]{2,1,0:T(8,128)(2,1)}, u32[]{:S(2)}) copy-start(bf16[8,16,256]{2,1,0:T(8,128)(2,1)} %source_ref.1) | copy-start | bytes 196612
  11.5 0.8 %copy-start = (bf16[7,7,256]{2,1,0:T(8,128)(2,1)S(1)}, bf16[7,7,256]{2,1,0:T(8,128)(2,1)}, u32[]{:S(2)}) copy-start(bf16[7,7,256]{2,1,0:T(8,128)(2,1)} %refs_7_.1) | copy-start | bytes 75268
  11.6 5.4 %collective-permute-start.1 = (bf16[64,256]{1,0:T(8,128)(2,1)S(1)}, bf16[64,256]{1,0:T(8,128)(2,1)S(1)}, u32[]{:S(2)}, u32[]{:S(2)}) collective-permute-start(bf16[64,256]{1,0:T(8,128)(2,1)S(1)} %get-tuple-element.22), channel_id=1, source_target_pairs={{0,1},{1,0},{2,3},{3,2},{4,5},{5,4},{6,7},{7,6},{8,9},{9,8},{10,11... | collective-permute-start | bytes 98312 | tf_op jit(solution)/shard_map/ppermute | solution.py:348
  11.7 5.4 %collective-permute-start.2 = (bf16[64,256]{1,0:T(8,128)(2,1)S(1)}, bf16[64,256]{1,0:T(8,128)(2,1)S(1)}, u32[]{:S(2)}, u32[]{:S(2)}) collective-permute-start(bf16[64,256]{1,0:T(8,128)(2,1)S(1)} %get-tuple-element.23), channel_id=1, source_target_pairs={{1,2},{2,1},{3,4},{4,3},{5,6},{6,5},{7,8},{8,7},{9,10},{10,9},{11,... | collective-permute-start | bytes 98312 | tf_op jit(solution)/shard_map/ppermute | solution.py:380
  19.6 6.6 %collective-permute-start.5 = (bf16[32,256]{1,0:T(8,128)(2,1)S(1)}, bf16[32,256]{1,0:T(8,128)(2,1)S(1)}, u32[]{:S(2)}, u32[]{:S(2)}) collective-permute-start(bf16[32,256]{1,0:T(8,128)(2,1)S(1)} %get-tuple-element.29), channel_id=1, source_target_pairs={{0,13},{1,12},{2,15},{3,14},{4,9},{5,8},{6,11},{7,10},{8,5},{9,4},... | collective-permute-start | bytes 49160 | tf_op jit(solution)/shard_map/ppermute | solution.py:348
  24.7 4.1 %collective-permute-start.6 = (bf16[32,256]{1,0:T(8,128)(2,1)S(1)}, bf16[32,256]{1,0:T(8,128)(2,1)S(1)}, u32[]{:S(2)}, u32[]{:S(2)}) collective-permute-start(bf16[32,256]{1,0:T(8,128)(2,1)S(1)} %get-tuple-element.30), channel_id=1, source_target_pairs={{0,9},{1,8},{2,11},{3,10},{4,13},{5,12},{6,15},{7,14},{8,1},{9,0},... | collective-permute-start | bytes 49160 | tf_op jit(solution)/shard_map/ppermute | solution.py:348
  24.7 4.1 %collective-permute-start.7 = (bf16[32,256]{1,0:T(8,128)(2,1)S(1)}, bf16[32,256]{1,0:T(8,128)(2,1)S(1)}, u32[]{:S(2)}, u32[]{:S(2)}) collective-permute-start(bf16[32,256]{1,0:T(8,128)(2,1)S(1)} %get-tuple-element.31), channel_id=1, source_target_pairs={{0,4},{1,5},{2,6},{3,7},{4,0},{5,1},{6,2},{7,3},{8,12},{9,13},{10,... | collective-permute-start | bytes 49160 | tf_op jit(solution)/shard_map/ppermute | solution.py:348
  28.8 3.8 %collective-permute-start.8 = (bf16[128,256]{1,0:T(8,128)(2,1)S(1)}, bf16[128,256]{1,0:T(8,128)(2,1)S(1)}, u32[]{:S(2)}, u32[]{:S(2)}) collective-permute-start(bf16[128,256]{1,0:T(8,128)(2,1)S(1)} %constant_dynamic-update-slice_fusion.refs_0_), channel_id=1, source_target_pairs={{0,3},{1,2},{2,1},{3,0},{4,7},{5,6},{6,5},{7,4},{8,11},{9,10},{10,... | collective-permute-start | bytes 196616 | tf_op jit(solution)/shard_map/ppermute | solution.py:348
  28.9 3.7 %collective-permute-start.9 = (bf16[128,256]{1,0:T(8,128)(2,1)S(1)}, bf16[128,256]{1,0:T(8,128)(2,1)S(1)}, u32[]{:S(2)}, u32[]{:S(2)}) collective-permute-start(bf16[128,256]{1,0:T(8,128)(2,1)S(1)} %constant_dynamic-update-slice_fusion.refs_0_), channel_id=1, source_target_pairs={{0,1},{1,0},{2,3},{3,2},{4,5},{5,4},{6,7},{7,6},{8,9},{9,8},{10,11... | collective-permute-start | bytes 196616 | tf_op jit(solution)/shard_map/ppermute | solution.py:348
  32.6 1.3 %collective-permute-start.10 = (bf16[128,256]{1,0:T(8,128)(2,1)S(1)}, bf16[128,256]{1,0:T(8,128)(2,1)S(1)}, u32[]{:S(2)}, u32[]{:S(2)}) collective-permute-start(bf16[128,256]{1,0:T(8,128)(2,1)S(1)} %collective-permute-done.8.refs_1_), channel_id=1, source_target_pairs={{0,1},{1,0},{2,3},{3,2},{4,5},{5,4},{6,7},{7,6},{8,9},{9,8},{10,11... | collective-permute-start | bytes 196616 | tf_op jit(solution)/shard_map/ppermute | solution.py:348
  35.1 5.0 %collective-permute-start.11 = (bf16[32,256]{1,0:T(8,128)(2,1)S(1)}, bf16[32,256]{1,0:T(8,128)(2,1)S(1)}, u32[]{:S(2)}, u32[]{:S(2)}) collective-permute-start(bf16[32,256]{1,0:T(8,128)(2,1)S(1)} %get-tuple-element.34), channel_id=1, source_target_pairs={{0,13},{1,12},{2,15},{3,14},{4,9},{5,8},{6,11},{7,10},{8,5},{9,4},... | collective-permute-start | bytes 49160 | tf_op jit(solution)/shard_map/ppermute | solution.py:348
  36.2 4.5 %collective-permute-start.12 = (bf16[32,256]{1,0:T(8,128)(2,1)S(1)}, bf16[32,256]{1,0:T(8,128)(2,1)S(1)}, u32[]{:S(2)}, u32[]{:S(2)}) collective-permute-start(bf16[32,256]{1,0:T(8,128)(2,1)S(1)} %get-tuple-element.35), channel_id=1, source_target_pairs={{0,9},{1,8},{2,11},{3,10},{4,13},{5,12},{6,15},{7,14},{8,1},{9,0},... | collective-permute-start | bytes 49160 | tf_op jit(solution)/shard_map/ppermute | solution.py:348
  36.6 4.4 %collective-permute-start.13 = (bf16[32,256]{1,0:T(8,128)(2,1)S(1)}, bf16[32,256]{1,0:T(8,128)(2,1)S(1)}, u32[]{:S(2)}, u32[]{:S(2)}) collective-permute-start(bf16[32,256]{1,0:T(8,128)(2,1)S(1)} %get-tuple-element.36), channel_id=1, source_target_pairs={{0,4},{1,5},{2,6},{3,7},{4,0},{5,1},{6,2},{7,3},{8,12},{9,13},{10,... | collective-permute-start | bytes 49160 | tf_op jit(solution)/shard_map/ppermute | solution.py:348

commit v10 on v8

--- a/solution.py
+++ b/solution.py
@@ -58,8 +58,10 @@
         scores = jnp.where(mask[None], scores, -1e30).reshape(HEADS * count, keys.shape[0])
     top = jnp.max(scores, axis=-1, keepdims=True)
     probs = jnp.exp(scores - top)
-    totals = jnp.sum(probs, axis=-1, keepdims=True)
-    mixed = dot(probs.astype(bf16), values) * (1.0 / totals)
+    probs = probs.astype(bf16)
+    totals = dot(probs, jnp.ones((keys.shape[0], LANES), bf16))
+    share = 1.0 / totals
+    mixed = dot(probs, values) * jnp.concatenate([share] * (channels // LANES), axis=-1)
     out = mixed[:count]
     for h in range(1, HEADS):
         out = jnp.where(picks[h], mixed[h * count : (h + 1) * count], out)
@@ -99,8 +101,31 @@
         where = pl.ds(lax.rem(lax.axis_index("lat") + s, nlat) * rows, rows)
         near[where] = jnp.where(even, last, first)
         far[where] = jnp.where(even, first, last)
-    near_ref[...] = near[...].reshape(near_ref.shape).astype(bf16)
-    far_ref[...] = far[...].reshape(far_ref.shape).astype(bf16)
+    for strip, strip_ref, is_last in ((near, near_ref, even), (far, far_ref, ~even)):
+        strip_ref[...] = pack(strip[...], is_last).reshape(strip_ref.shape).astype(bf16)
+
+
+def lower_half():
+    return lax.broadcasted_iota(jnp.int32, (1, STRIP, 1), 1) < SIDE
+
+
+def turn(values):
+    return jnp.concatenate([values[:, SIDE:], values[:, :SIDE]], axis=1)
+
+
+def pack(strip, is_last):
+    half = strip.shape[0] // 2
+    turned = turn(strip)
+    low = jnp.where(is_last, turned, strip)
+    high = jnp.where(is_last, strip, turned)
+    return jnp.where(lower_half(), low[:half], high[half:])
+
+
+def unpack(packed, is_left):
+    turned = turn(packed)
+    low = jnp.where(is_left, turned, packed)
+    high = jnp.where(is_left, packed, turned)
+    return jnp.concatenate([low, high], axis=0)
 
 
 def chain(my_lat, slab, shape, dw_ref, expand_ref, reduce_ref, attn_ref, center, scratch):
@@ -186,21 +211,21 @@
 
 def outer_kernel(nlat, levels, *refs):
     tiles, refs = refs[:nlat], refs[nlat:]
-    near_ref, far_ref, inner_in_ref, dw_ref, expand_ref, reduce_ref, attn_ref = refs[:7]
+    far_ref, near_ref, inner_in_ref, dw_ref, expand_ref, reduce_ref, attn_ref = refs[:7]
     two_ref, *refs = refs[7:]
     sent_refs, (sent, padded, *scratch) = refs[:levels], refs[levels:]
     rows, cols, channels = tiles[0].shape
     all_rows = rows * nlat
     columns = 2 * SIDE
-    strip_shape = (all_rows, STRIP, channels)
-    near = near_ref[...].astype(f32).reshape(strip_shape)
-    far = far_ref[...].astype(f32).reshape(strip_shape)
+    packed = (all_rows // 2, STRIP, channels)
+    near = near_ref[...].astype(f32).reshape(packed)
+    far = far_ref[...].astype(f32).reshape(packed)
     even = lax.axis_index("lon") % 2 == 0
+    my_lat = lax.axis_index("lat")
     clear(padded, all_rows)
-    fill(padded, all_rows, 0, jnp.where(even, far, near))
-    my_lat = lax.axis_index("lat")
+    fill(padded, all_rows, 0, unpack(jnp.where(even, far, near), True))
     fill_tiles(padded, my_lat, STRIP, tiles)
-    fill(padded, all_rows, STRIP + cols, jnp.where(even, near, far))
+    fill(padded, all_rows, STRIP + cols, unpack(jnp.where(even, near, far), False))
     sublane = lax.broadcasted_iota(jnp.int32, (1, columns, 1), 1)
 
     def halves(shift, rows_of, c, width):
@@ -324,7 +349,7 @@
     )
     expand, reduce, lat_proj, lon_proj = staged
 
-    strip = (all_rows * STRIP, channels)
+    strip = (all_rows * SIDE, channels)
     strip_scratch = pltpu.VMEM((all_rows, STRIP, channels), f32)
     near, far = call(
         functools.partial(strip_kernel, nlat),
@@ -332,10 +357,10 @@
         [*tiles, reduce],
         [strip_scratch, strip_scratch],
     )
-    near = swap(near, 1)
     far = lax.ppermute(
         far, "lon", [(j, (j - 1) % nlon if j % 2 == 0 else (j + 1) % nlon) for j in range(nlon)]
     )
+    near = swap(near, 1)
 
     def scratch(width, count):
         return [
@@ -357,7 +382,7 @@
     outer_two, *parts = call(
         functools.partial(outer_kernel, nlat, levels),
         [(rows * columns, channels)] + [piece] * levels,
-        [*tiles, near, far, inner_in, dw_weight, expand, reduce, lat_proj],
+        [*tiles, far, near, inner_in, dw_weight, expand, reduce, lat_proj],
         [pltpu.VMEM((rows, cols, channels), bf16)] + scratch(cols + 2 * STRIP, columns),
         flops=work,
     )

time: 36.6 us -> 35.4 us (0.967)
  starting transfers between devices: 19 us -> 16.7 us
  waiting for transfers between devices: 7.73 us -> 8.5 us
  Pallas kernels: 9.61 us -> 10 us
    ppermute x1, starting transfers between devices: 5.12 us -> 3.37 us  [shards(): lax.ppermute(far, 'lon', [(j, (j - 1) % nlon if j % 2 == 0 else (j + 1) %...]
    ppermute x10, waiting for transfers between devices: 6.94 us -> 7.72 us  [swap(): return lax.ppermute(piece, 'lon', [(j, j ^ mask) for j in range(nlon)])]
    ppermute x10, starting transfers between devices: 11 us -> 10.4 us  [swap(): return lax.ppermute(piece, 'lon', [(j, j ^ mask) for j in range(nlon)])]
    pallas_call x6, Pallas kernels: 9.61 us -> 10 us  [call(): pl.pallas_call(kernel, out_shape=shapes, in_specs=[given] * len(operands)...]
  transfers between devices with their start and end apart: 12 -> 12, of which waited for: 8 -> 9; matrix products, arithmetic and copies ran while one was open for 0% -> 0% of each run, Pallas kernels for 13% -> 14%
where the time goes in v10:
time: 35.4 us; the launch traced here: 35.3 us
  starting transfers between devices  16.7 us (47%)
  Pallas kernels  10 us (28%)
  waiting for transfers between devices  8.5 us (24%)
    ppermute x10, starting transfers between devices, swap(): return lax.ppermute(piece, 'lon', [(j, j ^ mask) for j in range(nlon)])  10.4 us
    pallas_call x6, Pallas kernels, call(): pl.pallas_call(kernel, out_shape=shapes, in_specs=[given] * len(operands)...  10 us
    ppermute x10, waiting for transfers between devices, swap(): return lax.ppermute(piece, 'lon', [(j, j ^ mask) for j in range(nlon)])  7.72 us
    ppermute x1, starting transfers between devices, shards(): lax.ppermute(far, 'lon', [(j, (j - 1) % nlon if j % 2 == 0 else (j + 1) %...  3.37 us
    ppermute x1, starting transfers between devices, shards(): lax.ppermute(field, 'lat', [((i + s) % nlat, i) for i in range(nlat)])  2.94 us
    ppermute x1, waiting for transfers between devices, shards(): lax.ppermute(field, 'lat', [((i + s) % nlat, i) for i in range(nlat)])  0.78 us
  transfers between devices with their start and end apart: 12, of which 9 were waited for; matrix products, arithmetic and copies ran while one was open for 0% of the time, Pallas kernels for 14%

profile of v10, /device:TPU:0, one launch (start us, length us, event | category | flops | bytes accessed | tf_op | source)
XLA Modules:
  0.0 35.3 jit_solution(8701086957562503896)
XLA Ops:
  0.0 0.0 copy-start
  0.0 2.9 %collective-permute-start = (bf16[8,16,256]{2,1,0:T(8,128)(2,1)}, bf16[8,16,256]{2,1,0:T(8,128)(2,1)S(1)}, u32[]{:S(2)}, u32[]{:S(2)}) collective-permute-start(bf16[8,16,256]{2,1,0:T(8,128)(2,1)} %refs_0_.7), channel_id=1, source_target_pairs={{16,0},{0,16},{17,1},{1,17},{18,2},{2,18},{19,3},{3,19},{20,4},{4,... | collective-permute-start | bytes 196616 | tf_op jit(solution)/shard_map/ppermute | solution.py:340
  2.9 1.7 %shard_map.64 = (bf16[256,1024]{1,0:T(8,128)(2,1)S(1)}, bf16[1024,256]{1,0:T(8,128)(2,1)S(1)}, bf16[4,256,256]{2,1,0:T(8,128)(2,1)S(1)}, bf16[4,256,256]{2,1,0:T(8,128)(2,1)S(1)}) custom-call(bf16[256,1024]{1,0:T(8,128)(2,1)} %refs_0_.4, bf16[1024,256]{1,0:T(8,128)(2,1)} %refs_1_.1, bf16[4,256,256]{2,1,0:T(8,128)(2,1)} %refs_2_.2, bf16[4,256,256]{2,1,0:T(8,128)(2,1)} %refs_3_.1), custom_call_target="tpu_custom_call" | custom-call | bytes 2097152 | tf_op jit(solution)/shard_map/pallas_call | solution.py:307
  4.7 0.8 %collective-permute-done.refs_1_ = bf16[8,16,256]{2,1,0:T(8,128)(2,1)S(1)} collective-permute-done((bf16[8,16,256]{2,1,0:T(8,128)(2,1)}, bf16[8,16,256]{2,1,0:T(8,128)(2,1)S(1)}, u32[]{:S(2)}, u32[]{:S(2)}) %collective-permute-start) | collective-permute-done | bytes 65568 | tf_op jit(solution)/shard_map/ppermute | solution.py:340
  5.5 0.0 copy-done
  5.5 0.0 copy-start.1
  5.5 0.1 shard_map.65
  5.5 3.4 %collective-permute-start.1 = (bf16[64,256]{1,0:T(8,128)(2,1)S(1)}, bf16[64,256]{1,0:T(8,128)(2,1)S(1)}, u32[]{:S(2)}, u32[]{:S(2)}) collective-permute-start(bf16[64,256]{1,0:T(8,128)(2,1)S(1)} %get-tuple-element.23), channel_id=1, source_target_pairs={{0,15},{1,2},{2,1},{3,4},{4,3},{5,6},{6,5},{7,8},{8,7},{9,10},{10,... | collective-permute-start | bytes 98312 | tf_op jit(solution)/shard_map/ppermute | solution.py:360
  8.9 0.0 collective-permute-start.2
  8.9 0.0 copy-done.1
  8.9 3.3 %shard_map.66 = (bf16[64,256]{1,0:T(8,128)(2,1)S(1)}, bf16[64,256]{1,0:T(8,128)(2,1)S(1)}) custom-call(bf16[8,16,256]{2,1,0:T(8,128)(2,1)S(1)} %copy-done, bf16[8,16,256]{2,1,0:T(8,128)(2,1)S(1)} %collective-permute-done.refs_1_, bf16[7,7,256]{2,1,0:T(8,128)(2,1)S(1)} %copy-done.1, bf16[256,1024]{1,0:T(8,128)(2,1)S(1)} %get-tuple-element.25.refs_3_.refs_6_, ...), custom_call_target="tpu_custom_call" | custom-call | flops 134217728 | bytes 1729024 | tf_op jit(solution)/shard_map/pallas_call | solution.py:307
  12.2 0.0 collective-permute-done.1.refs_2_
  12.2 0.0 collective-permute-done.2.refs_3_
  12.2 2.8 %shard_map.67 = (bf16[64,256]{1,0:T(8,128)(2,1)S(1)}, bf16[32,256]{1,0:T(8,128)(2,1)S(1)}, bf16[32,256]{1,0:T(8,128)(2,1)S(1)}, bf16[32,256]{1,0:T(8,128)(2,1)S(1)}, bf16[32,256]{1,0:T(8,128)(2,1)S(1)}) custom-call(bf16[8,16,256]{2,1,0:T(8,128)(2,1)S(1)} %copy-done, bf16[8,16,256]{2,1,0:T(8,128)(2,1)S(1)} %collective-permute-done.refs_1_, ...), custom_call_target="tpu_custom_call" | custom-call | flops 134217728 | bytes 1827328 | tf_op jit(solution)/shard_map/pallas_call | solution.py:307
  15.0 2.1 %collective-permute-start.3 = (bf16[32,256]{1,0:T(8,128)(2,1)S(1)}, bf16[32,256]{1,0:T(8,128)(2,1)S(1)}, u32[]{:S(2)}, u32[]{:S(2)}) collective-permute-start(bf16[32,256]{1,0:T(8,128)(2,1)S(1)} %get-tuple-element.29), channel_id=1, source_target_pairs={{0,13},{1,12},{2,15},{3,14},{4,9},{5,8},{6,11},{7,10},{8,5},{9,4},... | collective-permute-start | bytes 49160 | tf_op jit(solution)/shard_map/ppermute | solution.py:329
  17.1 0.0 collective-permute-start.4
  17.1 2.1 %collective-permute-start.5 = (bf16[32,256]{1,0:T(8,128)(2,1)S(1)}, bf16[32,256]{1,0:T(8,128)(2,1)S(1)}, u32[]{:S(2)}, u32[]{:S(2)}) collective-permute-start(bf16[32,256]{1,0:T(8,128)(2,1)S(1)} %get-tuple-element.31), channel_id=1, source_target_pairs={{0,4},{1,5},{2,6},{3,7},{4,0},{5,1},{6,2},{7,3},{8,12},{9,13},{10,... | collective-permute-start | bytes 49160 | tf_op jit(solution)/shard_map/ppermute | solution.py:329
  19.2 0.9 %collective-permute-done.3 = bf16[32,256]{1,0:T(8,128)(2,1)S(1)} collective-permute-done((bf16[32,256]{1,0:T(8,128)(2,1)S(1)}, bf16[32,256]{1,0:T(8,128)(2,1)S(1)}, u32[]{:S(2)}, u32[]{:S(2)}) %collective-permute-start.3) | collective-permute-done | bytes 16416 | tf_op jit(solution)/shard_map/ppermute | solution.py:329
  20.1 1.1 %collective-permute-done.4 = bf16[32,256]{1,0:T(8,128)(2,1)S(1)} collective-permute-done((bf16[32,256]{1,0:T(8,128)(2,1)S(1)}, bf16[32,256]{1,0:T(8,128)(2,1)S(1)}, u32[]{:S(2)}, u32[]{:S(2)}) %collective-permute-start.4) | collective-permute-done | bytes 16416 | tf_op jit(solution)/shard_map/ppermute | solution.py:329
  21.2 0.1 collective-permute-done.5
  21.3 1.1 %collective-permute-start.6 = (bf16[128,256]{1,0:T(8,128)(2,1)S(1)}, bf16[128,256]{1,0:T(8,128)(2,1)S(1)}, u32[]{:S(2)}, u32[]{:S(2)}) collective-permute-start(bf16[128,256]{1,0:T(8,128)(2,1)S(1)} %constant_dynamic-update-slice_fusion.refs_0_), channel_id=1, source_target_pairs={{0,3},{1,2},{2,1},{3,0},{4,7},{5,6},{6,5},{7,4},{8,11},{9,10},{10,... | collective-permute-start | bytes 196616 | tf_op jit(solution)/shard_map/ppermute | solution.py:329
  22.4 0.5 %collective-permute-start.7 = (bf16[128,256]{1,0:T(8,128)(2,1)S(1)}, bf16[128,256]{1,0:T(8,128)(2,1)S(1)}, u32[]{:S(2)}, u32[]{:S(2)}) collective-permute-start(bf16[128,256]{1,0:T(8,128)(2,1)S(1)} %constant_dynamic-update-slice_fusion.refs_0_), channel_id=1, source_target_pairs={{0,1},{1,0},{2,3},{3,2},{4,5},{5,4},{6,7},{7,6},{8,9},{9,8},{10,11... | collective-permute-start | bytes 196616 | tf_op jit(solution)/shard_map/ppermute | solution.py:329
  22.9 2.2 %collective-permute-done.6.refs_1_ = bf16[128,256]{1,0:T(8,128)(2,1)S(1)} collective-permute-done((bf16[128,256]{1,0:T(8,128)(2,1)S(1)}, bf16[128,256]{1,0:T(8,128)(2,1)S(1)}, u32[]{:S(2)}, u32[]{:S(2)}) %collective-permute-start.6) | collective-permute-done | bytes 65568 | tf_op jit(solution)/shard_map/ppermute | solution.py:329
  25.0 0.4 %collective-permute-start.8 = (bf16[128,256]{1,0:T(8,128)(2,1)S(1)}, bf16[128,256]{1,0:T(8,128)(2,1)S(1)}, u32[]{:S(2)}, u32[]{:S(2)}) collective-permute-start(bf16[128,256]{1,0:T(8,128)(2,1)S(1)} %collective-permute-done.6.refs_1_), channel_id=1, source_target_pairs={{0,1},{1,0},{2,3},{3,2},{4,5},{5,4},{6,7},{7,6},{8,9},{9,8},{10,11... | collective-permute-start | bytes 196616 | tf_op jit(solution)/shard_map/ppermute | solution.py:329
  25.5 0.0 collective-permute-done.7.refs_2_
  25.5 0.9 %collective-permute-done.8.refs_3_ = bf16[128,256]{1,0:T(8,128)(2,1)S(1)} collective-permute-done((bf16[128,256]{1,0:T(8,128)(2,1)S(1)}, bf16[128,256]{1,0:T(8,128)(2,1)S(1)}, u32[]{:S(2)}, u32[]{:S(2)}) %collective-permute-start.8) | collective-permute-done | bytes 65568 | tf_op jit(solution)/shard_map/ppermute | solution.py:329
  26.4 1.3 %shard_map.68 = (bf16[32,256]{1,0:T(8,128)(2,1)S(1)}, bf16[32,256]{1,0:T(8,128)(2,1)S(1)}, bf16[32,256]{1,0:T(8,128)(2,1)S(1)}, bf16[32,256]{1,0:T(8,128)(2,1)S(1)}) custom-call(bf16[128,256]{1,0:T(8,128)(2,1)S(1)} %constant_dynamic-update-slice_fusion.refs_0_, bf16[128,256]{1,0:T(8,128)(2,1)S(1)} %collective-permute-done.6.refs_1_, ...), custom_call_target="tpu_custom_call" | custom-call | bytes 786432 | tf_op jit(solution)/shard_map/pallas_call | solution.py:307
  27.7 2.5 %collective-permute-start.9 = (bf16[32,256]{1,0:T(8,128)(2,1)S(1)}, bf16[32,256]{1,0:T(8,128)(2,1)S(1)}, u32[]{:S(2)}, u32[]{:S(2)}) collective-permute-start(bf16[32,256]{1,0:T(8,128)(2,1)S(1)} %get-tuple-element.34), channel_id=1, source_target_pairs={{0,13},{1,12},{2,15},{3,14},{4,9},{5,8},{6,11},{7,10},{8,5},{9,4},... | collective-permute-start | bytes 49160 | tf_op jit(solution)/shard_map/ppermute | solution.py:329
  30.2 0.5 %collective-permute-start.10 = (bf16[32,256]{1,0:T(8,128)(2,1)S(1)}, bf16[32,256]{1,0:T(8,128)(2,1)S(1)}, u32[]{:S(2)}, u32[]{:S(2)}) collective-permute-start(bf16[32,256]{1,0:T(8,128)(2,1)S(1)} %get-tuple-element.35), channel_id=1, source_target_pairs={{0,9},{1,8},{2,11},{3,10},{4,13},{5,12},{6,15},{7,14},{8,1},{9,0},... | collective-permute-start | bytes 49160 | tf_op jit(solution)/shard_map/ppermute | solution.py:329
  30.7 1.2 %collective-permute-start.11 = (bf16[32,256]{1,0:T(8,128)(2,1)S(1)}, bf16[32,256]{1,0:T(8,128)(2,1)S(1)}, u32[]{:S(2)}, u32[]{:S(2)}) collective-permute-start(bf16[32,256]{1,0:T(8,128)(2,1)S(1)} %get-tuple-element.36), channel_id=1, source_target_pairs={{0,4},{1,5},{2,6},{3,7},{4,0},{5,1},{6,2},{7,3},{8,12},{9,13},{10,... | collective-permute-start | bytes 49160 | tf_op jit(solution)/shard_map/ppermute | solution.py:329
  31.9 0.9 %collective-permute-done.9.refs_1_ = bf16[32,256]{1,0:T(8,128)(2,1)S(1)} collective-permute-done((bf16[32,256]{1,0:T(8,128)(2,1)S(1)}, bf16[32,256]{1,0:T(8,128)(2,1)S(1)}, u32[]{:S(2)}, u32[]{:S(2)}) %collective-permute-start.9) | collective-permute-done | bytes 16416 | tf_op jit(solution)/shard_map/ppermute | solution.py:329
  32.7 1.6 %collective-permute-done.10.refs_2_ = bf16[32,256]{1,0:T(8,128)(2,1)S(1)} collective-permute-done((bf16[32,256]{1,0:T(8,128)(2,1)S(1)}, bf16[32,256]{1,0:T(8,128)(2,1)S(1)}, u32[]{:S(2)}, u32[]{:S(2)}) %collective-permute-start.10) | collective-permute-done | bytes 16416 | tf_op jit(solution)/shard_map/ppermute | solution.py:329
  34.3 0.2 collective-permute-done.11.refs_3_
  34.5 0.8 %shard_map.69 = bf16[8,16,256]{2,1,0:T(8,128)(2,1)} custom-call(bf16[32,256]{1,0:T(8,128)(2,1)S(1)} %get-tuple-element.33.refs_0_, bf16[32,256]{1,0:T(8,128)(2,1)S(1)} %collective-permute-done.9.refs_1_, bf16[32,256]{1,0:T(8,128)(2,1)S(1)} %collective-permute-done.10.refs_2_, bf16[32,256]{1,0:T(8,128)(2,1)S(1)} %collective-permute-done.11.refs_3_, ...), custom_call_target="tpu_custom_call" | custom-call | bytes 655360 | tf_op jit(solution)/shard_map/pallas_call | solution.py:307
  (4 shorter events, 0.0 us)
Async XLA Ops:
  0.0 5.5 %copy-start = (bf16[8,16,256]{2,1,0:T(8,128)(2,1)S(1)}, bf16[8,16,256]{2,1,0:T(8,128)(2,1)}, u32[]{:S(2)}) copy-start(bf16[8,16,256]{2,1,0:T(8,128)(2,1)} %refs_0_.7) | copy-start | bytes 196612
  0.0 5.5 %collective-permute-start = (bf16[8,16,256]{2,1,0:T(8,128)(2,1)}, bf16[8,16,256]{2,1,0:T(8,128)(2,1)S(1)}, u32[]{:S(2)}, u32[]{:S(2)}) collective-permute-start(bf16[8,16,256]{2,1,0:T(8,128)(2,1)} %refs_0_.7), channel_id=1, source_target_pairs={{16,0},{0,16},{17,1},{1,17},{18,2},{2,18},{19,3},{3,19},{20,4},{4,... | collective-permute-start | bytes 196616 | tf_op jit(solution)/shard_map/ppermute | solution.py:340
  5.5 3.4 %copy-start.1 = (bf16[7,7,256]{2,1,0:T(8,128)(2,1)S(1)}, bf16[7,7,256]{2,1,0:T(8,128)(2,1)}, u32[]{:S(2)}) copy-start(bf16[7,7,256]{2,1,0:T(8,128)(2,1)} %refs_5_.1) | copy-start | bytes 75268
  5.5 6.7 %collective-permute-start.1 = (bf16[64,256]{1,0:T(8,128)(2,1)S(1)}, bf16[64,256]{1,0:T(8,128)(2,1)S(1)}, u32[]{:S(2)}, u32[]{:S(2)}) collective-permute-start(bf16[64,256]{1,0:T(8,128)(2,1)S(1)} %get-tuple-element.23), channel_id=1, source_target_pairs={{0,15},{1,2},{2,1},{3,4},{4,3},{5,6},{6,5},{7,8},{8,7},{9,10},{10,... | collective-permute-start | bytes 98312 | tf_op jit(solution)/shard_map/ppermute | solution.py:360
  8.9 3.3 %collective-permute-start.2 = (bf16[64,256]{1,0:T(8,128)(2,1)S(1)}, bf16[64,256]{1,0:T(8,128)(2,1)S(1)}, u32[]{:S(2)}, u32[]{:S(2)}) collective-permute-start(bf16[64,256]{1,0:T(8,128)(2,1)S(1)} %get-tuple-element.24), channel_id=1, source_target_pairs={{0,1},{1,0},{2,3},{3,2},{4,5},{5,4},{6,7},{7,6},{8,9},{9,8},{10,11... | collective-permute-start | bytes 98312 | tf_op jit(solution)/shard_map/ppermute | solution.py:329
  15.0 5.0 %collective-permute-start.3 = (bf16[32,256]{1,0:T(8,128)(2,1)S(1)}, bf16[32,256]{1,0:T(8,128)(2,1)S(1)}, u32[]{:S(2)}, u32[]{:S(2)}) collective-permute-start(bf16[32,256]{1,0:T(8,128)(2,1)S(1)} %get-tuple-element.29), channel_id=1, source_target_pairs={{0,13},{1,12},{2,15},{3,14},{4,9},{5,8},{6,11},{7,10},{8,5},{9,4},... | collective-permute-start | bytes 49160 | tf_op jit(solution)/shard_map/ppermute | solution.py:329
  17.1 4.1 %collective-permute-start.4 = (bf16[32,256]{1,0:T(8,128)(2,1)S(1)}, bf16[32,256]{1,0:T(8,128)(2,1)S(1)}, u32[]{:S(2)}, u32[]{:S(2)}) collective-permute-start(bf16[32,256]{1,0:T(8,128)(2,1)S(1)} %get-tuple-element.30), channel_id=1, source_target_pairs={{0,9},{1,8},{2,11},{3,10},{4,13},{5,12},{6,15},{7,14},{8,1},{9,0},... | collective-permute-start | bytes 49160 | tf_op jit(solution)/shard_map/ppermute | solution.py:329
  17.1 4.2 %collective-permute-start.5 = (bf16[32,256]{1,0:T(8,128)(2,1)S(1)}, bf16[32,256]{1,0:T(8,128)(2,1)S(1)}, u32[]{:S(2)}, u32[]{:S(2)}) collective-permute-start(bf16[32,256]{1,0:T(8,128)(2,1)S(1)} %get-tuple-element.31), channel_id=1, source_target_pairs={{0,4},{1,5},{2,6},{3,7},{4,0},{5,1},{6,2},{7,3},{8,12},{9,13},{10,... | collective-permute-start | bytes 49160 | tf_op jit(solution)/shard_map/ppermute | solution.py:329
  21.3 3.8 %collective-permute-start.6 = (bf16[128,256]{1,0:T(8,128)(2,1)S(1)}, bf16[128,256]{1,0:T(8,128)(2,1)S(1)}, u32[]{:S(2)}, u32[]{:S(2)}) collective-permute-start(bf16[128,256]{1,0:T(8,128)(2,1)S(1)} %constant_dynamic-update-slice_fusion.refs_0_), channel_id=1, source_target_pairs={{0,3},{1,2},{2,1},{3,0},{4,7},{5,6},{6,5},{7,4},{8,11},{9,10},{10,... | collective-permute-start | bytes 196616 | tf_op jit(solution)/shard_map/ppermute | solution.py:329
  22.4 3.1 %collective-permute-start.7 = (bf16[128,256]{1,0:T(8,128)(2,1)S(1)}, bf16[128,256]{1,0:T(8,128)(2,1)S(1)}, u32[]{:S(2)}, u32[]{:S(2)}) collective-permute-start(bf16[128,256]{1,0:T(8,128)(2,1)S(1)} %constant_dynamic-update-slice_fusion.refs_0_), channel_id=1, source_target_pairs={{0,1},{1,0},{2,3},{3,2},{4,5},{5,4},{6,7},{7,6},{8,9},{9,8},{10,11... | collective-permute-start | bytes 196616 | tf_op jit(solution)/shard_map/ppermute | solution.py:329
  25.0 1.3 %collective-permute-start.8 = (bf16[128,256]{1,0:T(8,128)(2,1)S(1)}, bf16[128,256]{1,0:T(8,128)(2,1)S(1)}, u32[]{:S(2)}, u32[]{:S(2)}) collective-permute-start(bf16[128,256]{1,0:T(8,128)(2,1)S(1)} %collective-permute-done.6.refs_1_), channel_id=1, source_target_pairs={{0,1},{1,0},{2,3},{3,2},{4,5},{5,4},{6,7},{7,6},{8,9},{9,8},{10,11... | collective-permute-start | bytes 196616 | tf_op jit(solution)/shard_map/ppermute | solution.py:329
  27.7 5.0 %collective-permute-start.9 = (bf16[32,256]{1,0:T(8,128)(2,1)S(1)}, bf16[32,256]{1,0:T(8,128)(2,1)S(1)}, u32[]{:S(2)}, u32[]{:S(2)}) collective-permute-start(bf16[32,256]{1,0:T(8,128)(2,1)S(1)} %get-tuple-element.34), channel_id=1, source_target_pairs={{0,13},{1,12},{2,15},{3,14},{4,9},{5,8},{6,11},{7,10},{8,5},{9,4},... | collective-permute-start | bytes 49160 | tf_op jit(solution)/shard_map/ppermute | solution.py:329
  30.2 4.1 %collective-permute-start.10 = (bf16[32,256]{1,0:T(8,128)(2,1)S(1)}, bf16[32,256]{1,0:T(8,128)(2,1)S(1)}, u32[]{:S(2)}, u32[]{:S(2)}) collective-permute-start(bf16[32,256]{1,0:T(8,128)(2,1)S(1)} %get-tuple-element.35), channel_id=1, source_target_pairs={{0,9},{1,8},{2,11},{3,10},{4,13},{5,12},{6,15},{7,14},{8,1},{9,0},... | collective-permute-start | bytes 49160 | tf_op jit(solution)/shard_map/ppermute | solution.py:329
  30.7 3.8 %collective-permute-start.11 = (bf16[32,256]{1,0:T(8,128)(2,1)S(1)}, bf16[32,256]{1,0:T(8,128)(2,1)S(1)}, u32[]{:S(2)}, u32[]{:S(2)}) collective-permute-start(bf16[32,256]{1,0:T(8,128)(2,1)S(1)} %get-tuple-element.36), channel_id=1, source_target_pairs={{0,4},{1,5},{2,6},{3,7},{4,0},{5,1},{6,2},{7,3},{8,12},{9,13},{10,... | collective-permute-start | bytes 49160 | tf_op jit(solution)/shard_map/ppermute | solution.py:329

commit v11 on v10

--- a/solution.py
+++ b/solution.py
@@ -14,6 +14,7 @@
 SIDE = 4
 LANES = 128
 LEVELS = 4
+STAGES = 4
 EPSILON = 1e-06
 VMEM_BYTES = 24 * 1024 * 1024
 STAGE_BYTES = 103 * 512 * 1024
@@ -58,23 +59,21 @@
         scores = jnp.where(mask[None], scores, -1e30).reshape(HEADS * count, keys.shape[0])
     top = jnp.max(scores, axis=-1, keepdims=True)
     probs = jnp.exp(scores - top)
-    probs = probs.astype(bf16)
-    totals = dot(probs, jnp.ones((keys.shape[0], LANES), bf16))
-    share = 1.0 / totals
-    mixed = dot(probs, values) * jnp.concatenate([share] * (channels // LANES), axis=-1)
+    totals = jnp.sum(probs, axis=-1, keepdims=True)
+    mixed = dot(probs.astype(bf16), values) * (1.0 / totals)
     out = mixed[:count]
     for h in range(1, HEADS):
         out = jnp.where(picks[h], mixed[h * count : (h + 1) * count], out)
     return out.astype(bf16)
 
 
-def stage_kernel(*refs):
-    count = (len(refs) - 1) // 2
-    sems = refs[-1]
-    copies = []
+def stage_kernel(count, *refs):
+    sources, dw_ref = refs[:count], refs[count]
+    targets, taps_ref, dw, sems = refs[count + 1 : 2 * count + 1], *refs[2 * count + 1 :]
+    copies = [pltpu.make_async_copy(dw_ref, dw, sems.at[count, 0])]
+    pieces = sems.shape[1]
     for i in range(count):
-        source, target = refs[i], refs[count + i]
-        pieces = sems.shape[1]
+        source, target = sources[i], targets[i]
         size = source.shape[0] // pieces
         for k in range(pieces):
             part = pl.ds(k * size, size)
@@ -83,6 +82,7 @@
         copy.start()
     for copy in copies:
         copy.wait()
+    taps_ref[...] = dw[...].astype(f32)
 
 
 def peer(levels, k):
@@ -128,18 +128,17 @@
     return jnp.concatenate([low, high], axis=0)
 
 
-def chain(my_lat, slab, shape, dw_ref, expand_ref, reduce_ref, attn_ref, center, scratch):
-    taps, one, lat_in = scratch
+def chain(my_lat, slab, shape, taps_ref, expand_ref, reduce_ref, attn_ref, center, scratch):
+    one, lat_in = scratch
     rows, all_rows, columns, channels = shape
     cells = all_rows * columns
-    taps[...] = dw_ref[...].astype(f32)
     parts = []
     for c in range(0, channels, LANES):
         acc = jnp.zeros((all_rows, columns, LANES), f32)
         for b in range(TAPS):
             block = slab(b, c)
             for a in range(TAPS):
-                tap = taps[a, b : b + 1, c : c + LANES].reshape(1, 1, LANES)
+                tap = taps_ref[a, b : b + 1, c : c + LANES].reshape(1, 1, LANES)
                 acc = acc + block[a : a + all_rows] * tap
         parts.append(acc.reshape(cells, LANES))
     normed = layer_norm(jnp.concatenate(parts, axis=-1)).astype(bf16)
@@ -188,7 +187,7 @@
 
 def inner_kernel(nlat, *refs):
     tiles, refs = refs[:nlat], refs[nlat:]
-    dw_ref, expand_ref, reduce_ref, attn_ref, two_ref, in_ref, padded, *scratch = refs
+    taps_ref, expand_ref, reduce_ref, attn_ref, two_ref, in_ref, padded, *scratch = refs
     rows, cols, channels = tiles[0].shape
     all_rows = rows * nlat
     columns = cols - 2 * SIDE
@@ -203,7 +202,7 @@
     center = padded[HALO : HALO + all_rows, SIDE : SIDE + columns]
     shape = (rows, all_rows, columns, channels)
     block_two, lon_in = chain(
-        my_lat, slab, shape, dw_ref, expand_ref, reduce_ref, attn_ref, center, scratch
+        my_lat, slab, shape, taps_ref, expand_ref, reduce_ref, attn_ref, center, scratch
     )
     two_ref[...] = block_two
     in_ref[...] = lon_in.astype(bf16)
@@ -211,7 +210,7 @@
 
 def outer_kernel(nlat, levels, *refs):
     tiles, refs = refs[:nlat], refs[nlat:]
-    far_ref, near_ref, inner_in_ref, dw_ref, expand_ref, reduce_ref, attn_ref = refs[:7]
+    far_ref, near_ref, inner_in_ref, taps_ref, expand_ref, reduce_ref, attn_ref = refs[:7]
     two_ref, *refs = refs[7:]
     sent_refs, (sent, padded, *scratch) = refs[:levels], refs[levels:]
     rows, cols, channels = tiles[0].shape
@@ -243,7 +242,7 @@
     center = halves(0, slice(HALO, HALO + all_rows), 0, channels)
     shape = (rows, all_rows, columns, channels)
     block_two, lon_in = chain(
-        my_lat, slab, shape, dw_ref, expand_ref, reduce_ref, attn_ref, center, scratch
+        my_lat, slab, shape, taps_ref, expand_ref, reduce_ref, attn_ref, center, scratch
     )
     two_ref[...] = block_two
     inner = inner_in_ref[...].astype(f32).reshape(rows, cols - columns, channels)
@@ -302,7 +301,10 @@
 ):
     vmem = pl.BlockSpec(memory_space=pltpu.VMEM)
     given = pl.BlockSpec(memory_space=pl.ANY) if any_space else vmem
-    shapes = [jax.ShapeDtypeStruct(shape, bf16) for shape in outs]
+    shapes = [
+        out if isinstance(out, jax.ShapeDtypeStruct) else jax.ShapeDtypeStruct(out, bf16)
+        for out in outs
+    ]
     moved = sum(x.size * x.dtype.itemsize for x in operands)
     result = pl.pallas_call(
         kernel,
@@ -332,22 +334,25 @@
         moved = []
         for k in range(1, levels):
             level = levels - k
-            moved.append(swap(pieces[k], level * column + level * 2 // levels))
+            cross = (level ^ (level >> 1)) & 1 if column > 1 else 0
+            moved.append(swap(pieces[k], level * column + cross))
         return [pieces[0]] + moved
 
     tiles = [field]
     for s in range(1, nlat):
         tiles.append(lax.ppermute(field, "lat", [((i + s) % nlat, i) for i in range(nlat)]))
     weights = (w_expand, w_reduce, lat_attn, lon_attn)
-    staged = call(
-        stage_kernel,
-        [w.shape for w in weights],
-        weights,
-        [pltpu.SemaphoreType.DMA((len(weights), 4))],
+    expand, reduce, lat_proj, lon_proj, taps = call(
+        functools.partial(stage_kernel, len(weights)),
+        [w.shape for w in weights] + [jax.ShapeDtypeStruct(dw_weight.shape, f32)],
+        [*weights, dw_weight],
+        [
+            pltpu.VMEM(dw_weight.shape, bf16),
+            pltpu.SemaphoreType.DMA((len(weights) + 1, STAGES)),
+        ],
         any_space=True,
         grant=STAGE_BYTES,
     )
-    expand, reduce, lat_proj, lon_proj = staged
 
     strip = (all_rows * SIDE, channels)
     strip_scratch = pltpu.VMEM((all_rows, STRIP, channels), f32)
@@ -365,7 +370,6 @@
     def scratch(width, count):
         return [
             pltpu.VMEM((all_rows + 2 * HALO, width, channels), f32),
-            pltpu.VMEM(dw_weight.shape, f32),
             pltpu.VMEM((all_rows * count, channels), bf16),
             pltpu.VMEM((all_rows * count, channels), bf16),
         ]
@@ -374,7 +378,7 @@
     inner_two, inner_in = call(
         functools.partial(inner_kernel, nlat),
         [(rows * (cols - columns), channels)] * 2,
-        [*tiles, dw_weight, expand, reduce, lat_proj],
+        [*tiles, taps, expand, reduce, lat_proj],
         scratch(cols, cols - columns),
         flops=work,
     )
@@ -382,7 +386,7 @@
     outer_two, *parts = call(
         functools.partial(outer_kernel, nlat, levels),
         [(rows * columns, channels)] + [piece] * levels,
-        [*tiles, far, near, inner_in, dw_weight, expand, reduce, lat_proj],
+        [*tiles, far, near, inner_in, taps, expand, reduce, lat_proj],
         [pltpu.VMEM((rows, cols, channels), bf16)] + scratch(cols + 2 * STRIP, columns),
         flops=work,
     )

time: 35.4 us -> 35.5 us (level)
  local copies, waits for them, and re-layouts: 0.02 us -> 0.76 us
  starting transfers between devices: 16.7 us -> 16.3 us
    ppermute x10, starting transfers between devices: 10.4 us -> 9.57 us  [swap(): return lax.ppermute(piece, 'lon', [(j, j ^ mask) for j in range(nlon)])]
    ppermute x1, waiting for transfers between devices: 0.78 us -> 0.01 us  [shards(): lax.ppermute(field, 'lat', [((i + s) % nlat, i) for i in range(nlat)])]
    unnamed x7, local copies, waits for them, and re-layouts: 0.01 us -> 0.76 us
    ppermute x10, waiting for transfers between devices: 7.72 us -> 8.28 us  [swap(): return lax.ppermute(piece, 'lon', [(j, j ^ mask) for j in range(nlon)])]
    ppermute x1, starting transfers between devices: 3.37 us -> 3.78 us  [shards(): lax.ppermute(far, 'lon', [(j, (j - 1) % nlon if j % 2 == 0 else (j + 1) %...]
  transfers between devices with their start and end apart: 12 -> 12, of which waited for: 9 -> 6; matrix products, arithmetic and copies ran while one was open for 0% -> 0% of each run, Pallas kernels for 14% -> 14%
where the time goes in v11:
time: 35.5 us; the launch traced here: 35.3 us
  starting transfers between devices  16.3 us (46%)
  Pallas kernels  9.87 us (28%)
  waiting for transfers between devices  8.29 us (23%)
  local copies, waits for them, and re-layouts  0.76 us (2%)
    pallas_call x6, Pallas kernels, call(): pl.pallas_call(kernel, out_shape=shapes, in_specs=[given] * len(operands)...  9.87 us
    ppermute x10, starting transfers between devices, swap(): return lax.ppermute(piece, 'lon', [(j, j ^ mask) for j in range(nlon)])  9.57 us
    ppermute x10, waiting for transfers between devices, swap(): return lax.ppermute(piece, 'lon', [(j, j ^ mask) for j in range(nlon)])  8.28 us
    ppermute x1, starting transfers between devices, shards(): lax.ppermute(far, 'lon', [(j, (j - 1) % nlon if j % 2 == 0 else (j + 1) %...  3.78 us
    ppermute x1, starting transfers between devices, shards(): lax.ppermute(field, 'lat', [((i + s) % nlat, i) for i in range(nlat)])  2.94 us
    unnamed x7, local copies, waits for them, and re-layouts  0.76 us
  transfers between devices with their start and end apart: 12, of which 6 were waited for; matrix products, arithmetic and copies ran while one was open for 0% of the time, Pallas kernels for 14%

profile of v11, /device:TPU:0, one launch (start us, length us, event | category | flops | bytes accessed | tf_op | source)
XLA Modules:
  0.0 35.3 jit_solution(15192411646768150219)
XLA Ops:
  0.0 0.0 copy-start
  0.0 2.9 %collective-permute-start = (bf16[8,16,256]{2,1,0:T(8,128)(2,1)}, bf16[8,16,256]{2,1,0:T(8,128)(2,1)S(1)}, u32[]{:S(2)}, u32[]{:S(2)}) collective-permute-start(bf16[8,16,256]{2,1,0:T(8,128)(2,1)} %refs_0_.7), channel_id=1, source_target_pairs={{16,0},{0,16},{17,1},{1,17},{18,2},{2,18},{19,3},{3,19},{20,4},{4,... | collective-permute-start | bytes 196616 | tf_op jit(solution)/shard_map/ppermute | solution.py:343
  2.9 0.0 copy-start.1
  2.9 0.7 %copy-done.1 = bf16[7,7,256]{2,1,0:T(8,128)(2,1)S(1)} copy-done((bf16[7,7,256]{2,1,0:T(8,128)(2,1)S(1)}, bf16[7,7,256]{2,1,0:T(8,128)(2,1)}, u32[]{:S(2)}) %copy-start.1) | copy-done | bytes 25112
  3.7 1.8 %shard_map.64 = (bf16[256,1024]{1,0:T(8,128)(2,1)S(1)}, bf16[1024,256]{1,0:T(8,128)(2,1)S(1)}, bf16[4,256,256]{2,1,0:T(8,128)(2,1)S(1)}, bf16[4,256,256]{2,1,0:T(8,128)(2,1)S(1)}, f32[7,7,256]{2,1,0:T(8,128)S(1)}) custom-call(bf16[256,1024]{1,0:T(8,128)(2,1)} %refs_0_.4, bf16[1024,256]{1,0:T(8,128)(2,1)} %refs_1_.1, bf16[4,256,256]{2,1,0:T(8,128)(2,1)} %refs_2_.1, ...), custom_call_target="tpu_custom_call" | custom-call | bytes 2122240 | tf_op jit(solution)/shard_map/pallas_call | solution.py:309
  5.5 0.0 collective-permute-done.refs_1_
  5.5 0.0 copy-done
  5.5 0.1 shard_map.65
  5.6 3.8 %collective-permute-start.1 = (bf16[64,256]{1,0:T(8,128)(2,1)S(1)}, bf16[64,256]{1,0:T(8,128)(2,1)S(1)}, u32[]{:S(2)}, u32[]{:S(2)}) collective-permute-start(bf16[64,256]{1,0:T(8,128)(2,1)S(1)} %get-tuple-element.24), channel_id=1, source_target_pairs={{0,15},{1,2},{2,1},{3,4},{4,3},{5,6},{6,5},{7,8},{8,7},{9,10},{10,... | collective-permute-start | bytes 98312 | tf_op jit(solution)/shard_map/ppermute | solution.py:365
  9.4 0.0 collective-permute-start.2
  9.4 3.2 %shard_map.66 = (bf16[64,256]{1,0:T(8,128)(2,1)S(1)}, bf16[64,256]{1,0:T(8,128)(2,1)S(1)}) custom-call(bf16[8,16,256]{2,1,0:T(8,128)(2,1)S(1)} %copy-done, bf16[8,16,256]{2,1,0:T(8,128)(2,1)S(1)} %collective-permute-done.refs_1_, f32[7,7,256]{2,1,0:T(8,128)S(1)} %get-tuple-element.26.refs_2_.refs_5_, ...), custom_call_target="tpu_custom_call" | custom-call | flops 134217728 | bytes 1754112 | tf_op jit(solution)/shard_map/pallas_call | solution.py:309
  12.6 0.0 collective-permute-done.1.refs_2_
  12.6 0.0 collective-permute-done.2.refs_3_
  12.6 2.8 %shard_map.67 = (bf16[64,256]{1,0:T(8,128)(2,1)S(1)}, bf16[32,256]{1,0:T(8,128)(2,1)S(1)}, bf16[32,256]{1,0:T(8,128)(2,1)S(1)}, bf16[32,256]{1,0:T(8,128)(2,1)S(1)}, bf16[32,256]{1,0:T(8,128)(2,1)S(1)}) custom-call(bf16[8,16,256]{2,1,0:T(8,128)(2,1)S(1)} %copy-done, bf16[8,16,256]{2,1,0:T(8,128)(2,1)S(1)} %collective-permute-done.refs_1_, ...), custom_call_target="tpu_custom_call" | custom-call | flops 134217728 | bytes 1852416 | tf_op jit(solution)/shard_map/pallas_call | solution.py:309
  15.4 2.0 %collective-permute-start.3 = (bf16[32,256]{1,0:T(8,128)(2,1)S(1)}, bf16[32,256]{1,0:T(8,128)(2,1)S(1)}, u32[]{:S(2)}, u32[]{:S(2)}) collective-permute-start(bf16[32,256]{1,0:T(8,128)(2,1)S(1)} %get-tuple-element.31), channel_id=1, source_target_pairs={{0,12},{1,13},{2,14},{3,15},{4,8},{5,9},{6,10},{7,11},{8,4},{9,5},... | collective-permute-start | bytes 49160 | tf_op jit(solution)/shard_map/ppermute | solution.py:331
  17.4 0.0 collective-permute-start.4
  17.4 2.2 %collective-permute-start.5 = (bf16[32,256]{1,0:T(8,128)(2,1)S(1)}, bf16[32,256]{1,0:T(8,128)(2,1)S(1)}, u32[]{:S(2)}, u32[]{:S(2)}) collective-permute-start(bf16[32,256]{1,0:T(8,128)(2,1)S(1)} %get-tuple-element.33), channel_id=1, source_target_pairs={{0,5},{1,4},{2,7},{3,6},{4,1},{5,0},{6,3},{7,2},{8,13},{9,12},{10,... | collective-permute-start | bytes 49160 | tf_op jit(solution)/shard_map/ppermute | solution.py:331
  19.6 1.5 %collective-permute-done.3 = bf16[32,256]{1,0:T(8,128)(2,1)S(1)} collective-permute-done((bf16[32,256]{1,0:T(8,128)(2,1)S(1)}, bf16[32,256]{1,0:T(8,128)(2,1)S(1)}, u32[]{:S(2)}, u32[]{:S(2)}) %collective-permute-start.3) | collective-permute-done | bytes 16416 | tf_op jit(solution)/shard_map/ppermute | solution.py:331
  21.1 0.5 %collective-permute-done.4 = bf16[32,256]{1,0:T(8,128)(2,1)S(1)} collective-permute-done((bf16[32,256]{1,0:T(8,128)(2,1)S(1)}, bf16[32,256]{1,0:T(8,128)(2,1)S(1)}, u32[]{:S(2)}, u32[]{:S(2)}) %collective-permute-start.4) | collective-permute-done | bytes 16416 | tf_op jit(solution)/shard_map/ppermute | solution.py:331
  21.6 0.0 collective-permute-done.5
  21.6 1.1 %collective-permute-start.6 = (bf16[128,256]{1,0:T(8,128)(2,1)S(1)}, bf16[128,256]{1,0:T(8,128)(2,1)S(1)}, u32[]{:S(2)}, u32[]{:S(2)}) collective-permute-start(bf16[128,256]{1,0:T(8,128)(2,1)S(1)} %constant_dynamic-update-slice_fusion.refs_0_), channel_id=1, source_target_pairs={{0,3},{1,2},{2,1},{3,0},{4,7},{5,6},{6,5},{7,4},{8,11},{9,10},{10,... | collective-permute-start | bytes 196616 | tf_op jit(solution)/shard_map/ppermute | solution.py:331
  22.7 0.0 collective-permute-start.7
  22.7 3.2 %collective-permute-done.6.refs_1_ = bf16[128,256]{1,0:T(8,128)(2,1)S(1)} collective-permute-done((bf16[128,256]{1,0:T(8,128)(2,1)S(1)}, bf16[128,256]{1,0:T(8,128)(2,1)S(1)}, u32[]{:S(2)}, u32[]{:S(2)}) %collective-permute-start.6) | collective-permute-done | bytes 65568 | tf_op jit(solution)/shard_map/ppermute | solution.py:331
  25.8 0.1 collective-permute-start.8
  26.0 0.0 collective-permute-done.7.refs_2_
  26.0 1.1 %collective-permute-done.8.refs_3_ = bf16[128,256]{1,0:T(8,128)(2,1)S(1)} collective-permute-done((bf16[128,256]{1,0:T(8,128)(2,1)S(1)}, bf16[128,256]{1,0:T(8,128)(2,1)S(1)}, u32[]{:S(2)}, u32[]{:S(2)}) %collective-permute-start.8) | collective-permute-done | bytes 65568 | tf_op jit(solution)/shard_map/ppermute | solution.py:331
  27.1 1.2 %shard_map.68 = (bf16[32,256]{1,0:T(8,128)(2,1)S(1)}, bf16[32,256]{1,0:T(8,128)(2,1)S(1)}, bf16[32,256]{1,0:T(8,128)(2,1)S(1)}, bf16[32,256]{1,0:T(8,128)(2,1)S(1)}) custom-call(bf16[128,256]{1,0:T(8,128)(2,1)S(1)} %constant_dynamic-update-slice_fusion.refs_0_, bf16[128,256]{1,0:T(8,128)(2,1)S(1)} %collective-permute-done.6.refs_1_, ...), custom_call_target="tpu_custom_call" | custom-call | bytes 786432 | tf_op jit(solution)/shard_map/pallas_call | solution.py:309
  28.3 1.7 %collective-permute-start.9 = (bf16[32,256]{1,0:T(8,128)(2,1)S(1)}, bf16[32,256]{1,0:T(8,128)(2,1)S(1)}, u32[]{:S(2)}, u32[]{:S(2)}) collective-permute-start(bf16[32,256]{1,0:T(8,128)(2,1)S(1)} %get-tuple-element.36), channel_id=1, source_target_pairs={{0,12},{1,13},{2,14},{3,15},{4,8},{5,9},{6,10},{7,11},{8,4},{9,5},... | collective-permute-start | bytes 49160 | tf_op jit(solution)/shard_map/ppermute | solution.py:331
  30.1 0.3 collective-permute-start.10
  30.4 2.1 %collective-permute-start.11 = (bf16[32,256]{1,0:T(8,128)(2,1)S(1)}, bf16[32,256]{1,0:T(8,128)(2,1)S(1)}, u32[]{:S(2)}, u32[]{:S(2)}) collective-permute-start(bf16[32,256]{1,0:T(8,128)(2,1)S(1)} %get-tuple-element.38), channel_id=1, source_target_pairs={{0,5},{1,4},{2,7},{3,6},{4,1},{5,0},{6,3},{7,2},{8,13},{9,12},{10,... | collective-permute-start | bytes 49160 | tf_op jit(solution)/shard_map/ppermute | solution.py:331
  32.5 1.5 %collective-permute-done.9.refs_1_ = bf16[32,256]{1,0:T(8,128)(2,1)S(1)} collective-permute-done((bf16[32,256]{1,0:T(8,128)(2,1)S(1)}, bf16[32,256]{1,0:T(8,128)(2,1)S(1)}, u32[]{:S(2)}, u32[]{:S(2)}) %collective-permute-start.9) | collective-permute-done | bytes 16416 | tf_op jit(solution)/shard_map/ppermute | solution.py:331
  34.0 0.4 %collective-permute-done.10.refs_2_ = bf16[32,256]{1,0:T(8,128)(2,1)S(1)} collective-permute-done((bf16[32,256]{1,0:T(8,128)(2,1)S(1)}, bf16[32,256]{1,0:T(8,128)(2,1)S(1)}, u32[]{:S(2)}, u32[]{:S(2)}) %collective-permute-start.10) | collective-permute-done | bytes 16416 | tf_op jit(solution)/shard_map/ppermute | solution.py:331
  34.5 0.0 collective-permute-done.11.refs_3_
  34.5 0.8 %shard_map.69 = bf16[8,16,256]{2,1,0:T(8,128)(2,1)} custom-call(bf16[32,256]{1,0:T(8,128)(2,1)S(1)} %get-tuple-element.35.refs_0_, bf16[32,256]{1,0:T(8,128)(2,1)S(1)} %collective-permute-done.9.refs_1_, bf16[32,256]{1,0:T(8,128)(2,1)S(1)} %collective-permute-done.10.refs_2_, bf16[32,256]{1,0:T(8,128)(2,1)S(1)} %collective-permute-done.11.refs_3_, ...), custom_call_target="tpu_custom_call" | custom-call | bytes 655360 | tf_op jit(solution)/shard_map/pallas_call | solution.py:309
  (4 shorter events, 0.0 us)
Async XLA Ops:
  0.0 5.5 %copy-start = (bf16[8,16,256]{2,1,0:T(8,128)(2,1)S(1)}, bf16[8,16,256]{2,1,0:T(8,128)(2,1)}, u32[]{:S(2)}) copy-start(bf16[8,16,256]{2,1,0:T(8,128)(2,1)} %refs_0_.7) | copy-start | bytes 196612
  0.0 5.5 %collective-permute-start = (bf16[8,16,256]{2,1,0:T(8,128)(2,1)}, bf16[8,16,256]{2,1,0:T(8,128)(2,1)S(1)}, u32[]{:S(2)}, u32[]{:S(2)}) collective-permute-start(bf16[8,16,256]{2,1,0:T(8,128)(2,1)} %refs_0_.7), channel_id=1, source_target_pairs={{16,0},{0,16},{17,1},{1,17},{18,2},{2,18},{19,3},{3,19},{20,4},{4,... | collective-permute-start | bytes 196616 | tf_op jit(solution)/shard_map/ppermute | solution.py:343
  2.9 0.7 %copy-start.1 = (bf16[7,7,256]{2,1,0:T(8,128)(2,1)S(1)}, bf16[7,7,256]{2,1,0:T(8,128)(2,1)}, u32[]{:S(2)}) copy-start(bf16[7,7,256]{2,1,0:T(8,128)(2,1)} %refs_4_.1) | copy-start | bytes 75268
  5.6 7.0 %collective-permute-start.1 = (bf16[64,256]{1,0:T(8,128)(2,1)S(1)}, bf16[64,256]{1,0:T(8,128)(2,1)S(1)}, u32[]{:S(2)}, u32[]{:S(2)}) collective-permute-start(bf16[64,256]{1,0:T(8,128)(2,1)S(1)} %get-tuple-element.24), channel_id=1, source_target_pairs={{0,15},{1,2},{2,1},{3,4},{4,3},{5,6},{6,5},{7,8},{8,7},{9,10},{10,... | collective-permute-start | bytes 98312 | tf_op jit(solution)/shard_map/ppermute | solution.py:365
  9.4 3.2 %collective-permute-start.2 = (bf16[64,256]{1,0:T(8,128)(2,1)S(1)}, bf16[64,256]{1,0:T(8,128)(2,1)S(1)}, u32[]{:S(2)}, u32[]{:S(2)}) collective-permute-start(bf16[64,256]{1,0:T(8,128)(2,1)S(1)} %get-tuple-element.25), channel_id=1, source_target_pairs={{0,1},{1,0},{2,3},{3,2},{4,5},{5,4},{6,7},{7,6},{8,9},{9,8},{10,11... | collective-permute-start | bytes 98312 | tf_op jit(solution)/shard_map/ppermute | solution.py:331
  15.4 5.7 %collective-permute-start.3 = (bf16[32,256]{1,0:T(8,128)(2,1)S(1)}, bf16[32,256]{1,0:T(8,128)(2,1)S(1)}, u32[]{:S(2)}, u32[]{:S(2)}) collective-permute-start(bf16[32,256]{1,0:T(8,128)(2,1)S(1)} %get-tuple-element.31), channel_id=1, source_target_pairs={{0,12},{1,13},{2,14},{3,15},{4,8},{5,9},{6,10},{7,11},{8,4},{9,5},... | collective-permute-start | bytes 49160 | tf_op jit(solution)/shard_map/ppermute | solution.py:331
  17.4 4.2 %collective-permute-start.4 = (bf16[32,256]{1,0:T(8,128)(2,1)S(1)}, bf16[32,256]{1,0:T(8,128)(2,1)S(1)}, u32[]{:S(2)}, u32[]{:S(2)}) collective-permute-start(bf16[32,256]{1,0:T(8,128)(2,1)S(1)} %get-tuple-element.32), channel_id=1, source_target_pairs={{0,9},{1,8},{2,11},{3,10},{4,13},{5,12},{6,15},{7,14},{8,1},{9,0},... | collective-permute-start | bytes 49160 | tf_op jit(solution)/shard_map/ppermute | solution.py:331
  17.4 4.2 %collective-permute-start.5 = (bf16[32,256]{1,0:T(8,128)(2,1)S(1)}, bf16[32,256]{1,0:T(8,128)(2,1)S(1)}, u32[]{:S(2)}, u32[]{:S(2)}) collective-permute-start(bf16[32,256]{1,0:T(8,128)(2,1)S(1)} %get-tuple-element.33), channel_id=1, source_target_pairs={{0,5},{1,4},{2,7},{3,6},{4,1},{5,0},{6,3},{7,2},{8,13},{9,12},{10,... | collective-permute-start | bytes 49160 | tf_op jit(solution)/shard_map/ppermute | solution.py:331
  21.6 4.3 %collective-permute-start.6 = (bf16[128,256]{1,0:T(8,128)(2,1)S(1)}, bf16[128,256]{1,0:T(8,128)(2,1)S(1)}, u32[]{:S(2)}, u32[]{:S(2)}) collective-permute-start(bf16[128,256]{1,0:T(8,128)(2,1)S(1)} %constant_dynamic-update-slice_fusion.refs_0_), channel_id=1, source_target_pairs={{0,3},{1,2},{2,1},{3,0},{4,7},{5,6},{6,5},{7,4},{8,11},{9,10},{10,... | collective-permute-start | bytes 196616 | tf_op jit(solution)/shard_map/ppermute | solution.py:331
  22.7 3.3 %collective-permute-start.7 = (bf16[128,256]{1,0:T(8,128)(2,1)S(1)}, bf16[128,256]{1,0:T(8,128)(2,1)S(1)}, u32[]{:S(2)}, u32[]{:S(2)}) collective-permute-start(bf16[128,256]{1,0:T(8,128)(2,1)S(1)} %constant_dynamic-update-slice_fusion.refs_0_), channel_id=1, source_target_pairs={{0,1},{1,0},{2,3},{3,2},{4,5},{5,4},{6,7},{7,6},{8,9},{9,8},{10,11... | collective-permute-start | bytes 196616 | tf_op jit(solution)/shard_map/ppermute | solution.py:331
  25.8 1.3 %collective-permute-start.8 = (bf16[128,256]{1,0:T(8,128)(2,1)S(1)}, bf16[128,256]{1,0:T(8,128)(2,1)S(1)}, u32[]{:S(2)}, u32[]{:S(2)}) collective-permute-start(bf16[128,256]{1,0:T(8,128)(2,1)S(1)} %collective-permute-done.6.refs_1_), channel_id=1, source_target_pairs={{0,1},{1,0},{2,3},{3,2},{4,5},{5,4},{6,7},{7,6},{8,9},{9,8},{10,11... | collective-permute-start | bytes 196616 | tf_op jit(solution)/shard_map/ppermute | solution.py:331
  28.3 5.7 %collective-permute-start.9 = (bf16[32,256]{1,0:T(8,128)(2,1)S(1)}, bf16[32,256]{1,0:T(8,128)(2,1)S(1)}, u32[]{:S(2)}, u32[]{:S(2)}) collective-permute-start(bf16[32,256]{1,0:T(8,128)(2,1)S(1)} %get-tuple-element.36), channel_id=1, source_target_pairs={{0,12},{1,13},{2,14},{3,15},{4,8},{5,9},{6,10},{7,11},{8,4},{9,5},... | collective-permute-start | bytes 49160 | tf_op jit(solution)/shard_map/ppermute | solution.py:331
  30.1 4.4 %collective-permute-start.10 = (bf16[32,256]{1,0:T(8,128)(2,1)S(1)}, bf16[32,256]{1,0:T(8,128)(2,1)S(1)}, u32[]{:S(2)}, u32[]{:S(2)}) collective-permute-start(bf16[32,256]{1,0:T(8,128)(2,1)S(1)} %get-tuple-element.37), channel_id=1, source_target_pairs={{0,9},{1,8},{2,11},{3,10},{4,13},{5,12},{6,15},{7,14},{8,1},{9,0},... | collective-permute-start | bytes 49160 | tf_op jit(solution)/shard_map/ppermute | solution.py:331
  30.4 4.1 %collective-permute-start.11 = (bf16[32,256]{1,0:T(8,128)(2,1)S(1)}, bf16[32,256]{1,0:T(8,128)(2,1)S(1)}, u32[]{:S(2)}, u32[]{:S(2)}) collective-permute-start(bf16[32,256]{1,0:T(8,128)(2,1)S(1)} %get-tuple-element.38), channel_id=1, source_target_pairs={{0,5},{1,4},{2,7},{3,6},{4,1},{5,0},{6,3},{7,2},{8,13},{9,12},{10,... | collective-permute-start | bytes 49160 | tf_op jit(solution)/shard_map/ppermute | solution.py:331

commit v12 on v11

--- a/solution.py
+++ b/solution.py
@@ -14,6 +14,7 @@
 SIDE = 4
 LANES = 128
 LEVELS = 4
+HALVES = 2
 STAGES = 4
 EPSILON = 1e-06
 VMEM_BYTES = 24 * 1024 * 1024
@@ -132,29 +133,36 @@
     one, lat_in = scratch
     rows, all_rows, columns, channels = shape
     cells = all_rows * columns
-    parts = []
-    for c in range(0, channels, LANES):
-        acc = jnp.zeros((all_rows, columns, LANES), f32)
-        for b in range(TAPS):
-            block = slab(b, c)
-            for a in range(TAPS):
-                tap = taps_ref[a, b : b + 1, c : c + LANES].reshape(1, 1, LANES)
-                acc = acc + block[a : a + all_rows] * tap
-        parts.append(acc.reshape(cells, LANES))
-    normed = layer_norm(jnp.concatenate(parts, axis=-1)).astype(bf16)
-
-    def widen(k, total):
-        part = slice(k * channels, (k + 1) * channels)
-        wide = gelu(dot(normed, expand_ref[:, part])).astype(bf16)
-        return total + dot(wide, reduce_ref[part])
-
-    total = center.reshape(cells, channels)
-    for k in range(expand_ref.shape[1] // channels):
-        total = widen(k, total)
-    block_one = total.astype(bf16)
-    one[...] = block_one
-    every = layer_norm(block_one.astype(f32)).astype(bf16)
-    lat_in[...] = every
+    half = all_rows // HALVES
+
+    def convolve(start):
+        parts = []
+        for c in range(0, channels, LANES):
+            acc = jnp.zeros((half, columns, LANES), f32)
+            for b in range(TAPS):
+                block = slab(start, half + 2 * HALO, b, c)
+                for a in range(TAPS):
+                    tap = taps_ref[a, b : b + 1, c : c + LANES].reshape(1, 1, LANES)
+                    acc = acc + block[a : a + half] * tap
+            parts.append(acc.reshape(half * columns, LANES))
+        return layer_norm(jnp.concatenate(parts, axis=-1)).astype(bf16)
+
+    def widen(normed, total):
+        for k in range(0, expand_ref.shape[1], channels):
+            part = slice(k, k + channels)
+            wide = gelu(dot(normed, expand_ref[:, part])).astype(bf16)
+            total = total + dot(wide, reduce_ref[part])
+        return total
+
+    blocks = []
+    for start in range(0, all_rows, half):
+        total = widen(convolve(start), center(start, half).reshape(half * columns, channels))
+        block_one = total.astype(bf16)
+        place = slice(start * columns, (start + half) * columns)
+        one[place] = block_one
+        blocks.append(layer_norm(block_one.astype(f32)).astype(bf16))
+        lat_in[place] = blocks[-1]
+    every = jnp.concatenate(blocks, axis=0)
     count = rows * columns
     own = pl.ds(pl.multiple_of(my_lat * count, count), count)
     queries = dot(lat_in[own], attn_ref[0]).astype(bf16)
@@ -195,11 +203,13 @@
     my_lat = lax.axis_index("lat")
     fill_tiles(padded, my_lat, 0, tiles)
 
-    def slab(b, c):
+    def slab(start, size, b, c):
         first = SIDE - HALO + b
-        return padded[:, first : first + columns, c : c + LANES]
-
-    center = padded[HALO : HALO + all_rows, SIDE : SIDE + columns]
+        return padded[start : start + size, first : first + columns, c : c + LANES]
+
+    def center(start, size):
+        return padded[HALO + start : HALO + start + size, SIDE : SIDE + columns]
+
     shape = (rows, all_rows, columns, channels)
     block_two, lon_in = chain(
         my_lat, slab, shape, taps_ref, expand_ref, reduce_ref, attn_ref, center, scratch
@@ -236,10 +246,12 @@
             padded[rows_of, left : left + columns, c : c + width],
         )
 
-    def slab(b, c):
-        return halves(b - HALO, slice(None), c, LANES)
-
-    center = halves(0, slice(HALO, HALO + all_rows), 0, channels)
+    def slab(start, size, b, c):
+        return halves(b - HALO, slice(start, start + size), c, LANES)
+
+    def center(start, size):
+        return halves(0, slice(HALO + start, HALO + start + size), 0, channels)
+
     shape = (rows, all_rows, columns, channels)
     block_two, lon_in = chain(
         my_lat, slab, shape, taps_ref, expand_ref, reduce_ref, attn_ref, center, scratch

time: 35.5 us -> 35.6 us (level)
  no operation moved by 1% of the time
where the time goes in v12:
time: 35.6 us; the launch traced here: 35.4 us
  starting transfers between devices  16.3 us (46%)
  Pallas kernels  9.98 us (28%)
  waiting for transfers between devices  8.31 us (23%)
  local copies, waits for them, and re-layouts  0.76 us (2%)
    pallas_call x6, Pallas kernels, call(): pl.pallas_call(kernel, out_shape=shapes, in_specs=[given] * len(operands)...  9.98 us
    ppermute x10, starting transfers between devices, swap(): return lax.ppermute(piece, 'lon', [(j, j ^ mask) for j in range(nlon)])  9.55 us
    ppermute x10, waiting for transfers between devices, swap(): return lax.ppermute(piece, 'lon', [(j, j ^ mask) for j in range(nlon)])  8.31 us
    ppermute x1, starting transfers between devices, shards(): lax.ppermute(far, 'lon', [(j, (j - 1) % nlon if j % 2 == 0 else (j + 1) %...  3.78 us
    ppermute x1, starting transfers between devices, shards(): lax.ppermute(field, 'lat', [((i + s) % nlat, i) for i in range(nlat)])  2.94 us
    unnamed x7, local copies, waits for them, and re-layouts  0.76 us
  transfers between devices with their start and end apart: 12, of which 6 were waited for; matrix products, arithmetic and copies ran while one was open for 0% of the time, Pallas kernels for 14%

profile of v12, /device:TPU:0, one launch (start us, length us, event | category | flops | bytes accessed | tf_op | source)
XLA Modules:
  0.0 35.4 jit_solution(12579353620227930309)
XLA Ops:
  0.0 0.0 copy-start
  0.0 2.9 %collective-permute-start = (bf16[8,16,256]{2,1,0:T(8,128)(2,1)}, bf16[8,16,256]{2,1,0:T(8,128)(2,1)S(1)}, u32[]{:S(2)}, u32[]{:S(2)}) collective-permute-start(bf16[8,16,256]{2,1,0:T(8,128)(2,1)} %refs_0_.7), channel_id=1, source_target_pairs={{16,0},{0,16},{17,1},{1,17},{18,2},{2,18},{19,3},{3,19},{20,4},{4,... | collective-permute-start | bytes 196616 | tf_op jit(solution)/shard_map/ppermute | solution.py:355
  2.9 0.0 copy-start.1
  2.9 0.7 %copy-done.1 = bf16[7,7,256]{2,1,0:T(8,128)(2,1)S(1)} copy-done((bf16[7,7,256]{2,1,0:T(8,128)(2,1)S(1)}, bf16[7,7,256]{2,1,0:T(8,128)(2,1)}, u32[]{:S(2)}) %copy-start.1) | copy-done | bytes 25112
  3.7 1.8 %shard_map.64 = (bf16[256,1024]{1,0:T(8,128)(2,1)S(1)}, bf16[1024,256]{1,0:T(8,128)(2,1)S(1)}, bf16[4,256,256]{2,1,0:T(8,128)(2,1)S(1)}, bf16[4,256,256]{2,1,0:T(8,128)(2,1)S(1)}, f32[7,7,256]{2,1,0:T(8,128)S(1)}) custom-call(bf16[256,1024]{1,0:T(8,128)(2,1)} %refs_0_.4, bf16[1024,256]{1,0:T(8,128)(2,1)} %refs_1_.1, bf16[4,256,256]{2,1,0:T(8,128)(2,1)} %refs_2_.1, ...), custom_call_target="tpu_custom_call" | custom-call | bytes 2122240 | tf_op jit(solution)/shard_map/pallas_call | solution.py:321
  5.5 0.0 collective-permute-done.refs_1_
  5.5 0.0 copy-done
  5.5 0.1 shard_map.65
  5.6 3.8 %collective-permute-start.1 = (bf16[64,256]{1,0:T(8,128)(2,1)S(1)}, bf16[64,256]{1,0:T(8,128)(2,1)S(1)}, u32[]{:S(2)}, u32[]{:S(2)}) collective-permute-start(bf16[64,256]{1,0:T(8,128)(2,1)S(1)} %get-tuple-element.24), channel_id=1, source_target_pairs={{0,15},{1,2},{2,1},{3,4},{4,3},{5,6},{6,5},{7,8},{8,7},{9,10},{10,... | collective-permute-start | bytes 98312 | tf_op jit(solution)/shard_map/ppermute | solution.py:377
  9.4 0.0 collective-permute-start.2
  9.4 3.2 %shard_map.66 = (bf16[64,256]{1,0:T(8,128)(2,1)S(1)}, bf16[64,256]{1,0:T(8,128)(2,1)S(1)}) custom-call(bf16[8,16,256]{2,1,0:T(8,128)(2,1)S(1)} %copy-done, bf16[8,16,256]{2,1,0:T(8,128)(2,1)S(1)} %collective-permute-done.refs_1_, f32[7,7,256]{2,1,0:T(8,128)S(1)} %get-tuple-element.26.refs_2_.refs_5_, ...), custom_call_target="tpu_custom_call" | custom-call | flops 134217728 | bytes 1754112 | tf_op jit(solution)/shard_map/pallas_call | solution.py:321
  12.6 0.0 collective-permute-done.1.refs_2_
  12.6 0.0 collective-permute-done.2.refs_3_
  12.6 2.9 %shard_map.67 = (bf16[64,256]{1,0:T(8,128)(2,1)S(1)}, bf16[32,256]{1,0:T(8,128)(2,1)S(1)}, bf16[32,256]{1,0:T(8,128)(2,1)S(1)}, bf16[32,256]{1,0:T(8,128)(2,1)S(1)}, bf16[32,256]{1,0:T(8,128)(2,1)S(1)}) custom-call(bf16[8,16,256]{2,1,0:T(8,128)(2,1)S(1)} %copy-done, bf16[8,16,256]{2,1,0:T(8,128)(2,1)S(1)} %collective-permute-done.refs_1_, ...), custom_call_target="tpu_custom_call" | custom-call | flops 134217728 | bytes 1852416 | tf_op jit(solution)/shard_map/pallas_call | solution.py:321
  15.5 2.0 %collective-permute-start.3 = (bf16[32,256]{1,0:T(8,128)(2,1)S(1)}, bf16[32,256]{1,0:T(8,128)(2,1)S(1)}, u32[]{:S(2)}, u32[]{:S(2)}) collective-permute-start(bf16[32,256]{1,0:T(8,128)(2,1)S(1)} %get-tuple-element.31), channel_id=1, source_target_pairs={{0,12},{1,13},{2,14},{3,15},{4,8},{5,9},{6,10},{7,11},{8,4},{9,5},... | collective-permute-start | bytes 49160 | tf_op jit(solution)/shard_map/ppermute | solution.py:343
  17.5 0.0 collective-permute-start.4
  17.5 2.2 %collective-permute-start.5 = (bf16[32,256]{1,0:T(8,128)(2,1)S(1)}, bf16[32,256]{1,0:T(8,128)(2,1)S(1)}, u32[]{:S(2)}, u32[]{:S(2)}) collective-permute-start(bf16[32,256]{1,0:T(8,128)(2,1)S(1)} %get-tuple-element.33), channel_id=1, source_target_pairs={{0,5},{1,4},{2,7},{3,6},{4,1},{5,0},{6,3},{7,2},{8,13},{9,12},{10,... | collective-permute-start | bytes 49160 | tf_op jit(solution)/shard_map/ppermute | solution.py:343
  19.7 1.5 %collective-permute-done.3 = bf16[32,256]{1,0:T(8,128)(2,1)S(1)} collective-permute-done((bf16[32,256]{1,0:T(8,128)(2,1)S(1)}, bf16[32,256]{1,0:T(8,128)(2,1)S(1)}, u32[]{:S(2)}, u32[]{:S(2)}) %collective-permute-start.3) | collective-permute-done | bytes 16416 | tf_op jit(solution)/shard_map/ppermute | solution.py:343
  21.2 0.5 %collective-permute-done.4 = bf16[32,256]{1,0:T(8,128)(2,1)S(1)} collective-permute-done((bf16[32,256]{1,0:T(8,128)(2,1)S(1)}, bf16[32,256]{1,0:T(8,128)(2,1)S(1)}, u32[]{:S(2)}, u32[]{:S(2)}) %collective-permute-start.4) | collective-permute-done | bytes 16416 | tf_op jit(solution)/shard_map/ppermute | solution.py:343
  21.7 0.0 collective-permute-done.5
  21.7 1.1 %collective-permute-start.6 = (bf16[128,256]{1,0:T(8,128)(2,1)S(1)}, bf16[128,256]{1,0:T(8,128)(2,1)S(1)}, u32[]{:S(2)}, u32[]{:S(2)}) collective-permute-start(bf16[128,256]{1,0:T(8,128)(2,1)S(1)} %constant_dynamic-update-slice_fusion.refs_0_), channel_id=1, source_target_pairs={{0,3},{1,2},{2,1},{3,0},{4,7},{5,6},{6,5},{7,4},{8,11},{9,10},{10,... | collective-permute-start | bytes 196616 | tf_op jit(solution)/shard_map/ppermute | solution.py:343
  22.8 0.0 collective-permute-start.7
  22.8 3.2 %collective-permute-done.6.refs_1_ = bf16[128,256]{1,0:T(8,128)(2,1)S(1)} collective-permute-done((bf16[128,256]{1,0:T(8,128)(2,1)S(1)}, bf16[128,256]{1,0:T(8,128)(2,1)S(1)}, u32[]{:S(2)}, u32[]{:S(2)}) %collective-permute-start.6) | collective-permute-done | bytes 65568 | tf_op jit(solution)/shard_map/ppermute | solution.py:343
  26.0 0.1 collective-permute-start.8
  26.1 0.0 collective-permute-done.7.refs_2_
  26.1 1.1 %collective-permute-done.8.refs_3_ = bf16[128,256]{1,0:T(8,128)(2,1)S(1)} collective-permute-done((bf16[128,256]{1,0:T(8,128)(2,1)S(1)}, bf16[128,256]{1,0:T(8,128)(2,1)S(1)}, u32[]{:S(2)}, u32[]{:S(2)}) %collective-permute-start.8) | collective-permute-done | bytes 65568 | tf_op jit(solution)/shard_map/ppermute | solution.py:343
  27.2 1.2 %shard_map.68 = (bf16[32,256]{1,0:T(8,128)(2,1)S(1)}, bf16[32,256]{1,0:T(8,128)(2,1)S(1)}, bf16[32,256]{1,0:T(8,128)(2,1)S(1)}, bf16[32,256]{1,0:T(8,128)(2,1)S(1)}) custom-call(bf16[128,256]{1,0:T(8,128)(2,1)S(1)} %constant_dynamic-update-slice_fusion.refs_0_, bf16[128,256]{1,0:T(8,128)(2,1)S(1)} %collective-permute-done.6.refs_1_, ...), custom_call_target="tpu_custom_call" | custom-call | bytes 786432 | tf_op jit(solution)/shard_map/pallas_call | solution.py:321
  28.4 1.7 %collective-permute-start.9 = (bf16[32,256]{1,0:T(8,128)(2,1)S(1)}, bf16[32,256]{1,0:T(8,128)(2,1)S(1)}, u32[]{:S(2)}, u32[]{:S(2)}) collective-permute-start(bf16[32,256]{1,0:T(8,128)(2,1)S(1)} %get-tuple-element.36), channel_id=1, source_target_pairs={{0,12},{1,13},{2,14},{3,15},{4,8},{5,9},{6,10},{7,11},{8,4},{9,5},... | collective-permute-start | bytes 49160 | tf_op jit(solution)/shard_map/ppermute | solution.py:343
  30.2 0.3 collective-permute-start.10
  30.5 2.1 %collective-permute-start.11 = (bf16[32,256]{1,0:T(8,128)(2,1)S(1)}, bf16[32,256]{1,0:T(8,128)(2,1)S(1)}, u32[]{:S(2)}, u32[]{:S(2)}) collective-permute-start(bf16[32,256]{1,0:T(8,128)(2,1)S(1)} %get-tuple-element.38), channel_id=1, source_target_pairs={{0,5},{1,4},{2,7},{3,6},{4,1},{5,0},{6,3},{7,2},{8,13},{9,12},{10,... | collective-permute-start | bytes 49160 | tf_op jit(solution)/shard_map/ppermute | solution.py:343
  32.6 1.5 %collective-permute-done.9.refs_1_ = bf16[32,256]{1,0:T(8,128)(2,1)S(1)} collective-permute-done((bf16[32,256]{1,0:T(8,128)(2,1)S(1)}, bf16[32,256]{1,0:T(8,128)(2,1)S(1)}, u32[]{:S(2)}, u32[]{:S(2)}) %collective-permute-start.9) | collective-permute-done | bytes 16416 | tf_op jit(solution)/shard_map/ppermute | solution.py:343
  34.1 0.5 %collective-permute-done.10.refs_2_ = bf16[32,256]{1,0:T(8,128)(2,1)S(1)} collective-permute-done((bf16[32,256]{1,0:T(8,128)(2,1)S(1)}, bf16[32,256]{1,0:T(8,128)(2,1)S(1)}, u32[]{:S(2)}, u32[]{:S(2)}) %collective-permute-start.10) | collective-permute-done | bytes 16416 | tf_op jit(solution)/shard_map/ppermute | solution.py:343
  34.6 0.0 collective-permute-done.11.refs_3_
  34.6 0.8 %shard_map.69 = bf16[8,16,256]{2,1,0:T(8,128)(2,1)} custom-call(bf16[32,256]{1,0:T(8,128)(2,1)S(1)} %get-tuple-element.35.refs_0_, bf16[32,256]{1,0:T(8,128)(2,1)S(1)} %collective-permute-done.9.refs_1_, bf16[32,256]{1,0:T(8,128)(2,1)S(1)} %collective-permute-done.10.refs_2_, bf16[32,256]{1,0:T(8,128)(2,1)S(1)} %collective-permute-done.11.refs_3_, ...), custom_call_target="tpu_custom_call" | custom-call | bytes 655360 | tf_op jit(solution)/shard_map/pallas_call | solution.py:321
  (4 shorter events, 0.0 us)
Async XLA Ops:
  0.0 5.5 %copy-start = (bf16[8,16,256]{2,1,0:T(8,128)(2,1)S(1)}, bf16[8,16,256]{2,1,0:T(8,128)(2,1)}, u32[]{:S(2)}) copy-start(bf16[8,16,256]{2,1,0:T(8,128)(2,1)} %refs_0_.7) | copy-start | bytes 196612
  0.0 5.5 %collective-permute-start = (bf16[8,16,256]{2,1,0:T(8,128)(2,1)}, bf16[8,16,256]{2,1,0:T(8,128)(2,1)S(1)}, u32[]{:S(2)}, u32[]{:S(2)}) collective-permute-start(bf16[8,16,256]{2,1,0:T(8,128)(2,1)} %refs_0_.7), channel_id=1, source_target_pairs={{16,0},{0,16},{17,1},{1,17},{18,2},{2,18},{19,3},{3,19},{20,4},{4,... | collective-permute-start | bytes 196616 | tf_op jit(solution)/shard_map/ppermute | solution.py:355
  2.9 0.7 %copy-start.1 = (bf16[7,7,256]{2,1,0:T(8,128)(2,1)S(1)}, bf16[7,7,256]{2,1,0:T(8,128)(2,1)}, u32[]{:S(2)}) copy-start(bf16[7,7,256]{2,1,0:T(8,128)(2,1)} %refs_4_.1) | copy-start | bytes 75268
  5.6 7.0 %collective-permute-start.1 = (bf16[64,256]{1,0:T(8,128)(2,1)S(1)}, bf16[64,256]{1,0:T(8,128)(2,1)S(1)}, u32[]{:S(2)}, u32[]{:S(2)}) collective-permute-start(bf16[64,256]{1,0:T(8,128)(2,1)S(1)} %get-tuple-element.24), channel_id=1, source_target_pairs={{0,15},{1,2},{2,1},{3,4},{4,3},{5,6},{6,5},{7,8},{8,7},{9,10},{10,... | collective-permute-start | bytes 98312 | tf_op jit(solution)/shard_map/ppermute | solution.py:377
  9.4 3.2 %collective-permute-start.2 = (bf16[64,256]{1,0:T(8,128)(2,1)S(1)}, bf16[64,256]{1,0:T(8,128)(2,1)S(1)}, u32[]{:S(2)}, u32[]{:S(2)}) collective-permute-start(bf16[64,256]{1,0:T(8,128)(2,1)S(1)} %get-tuple-element.25), channel_id=1, source_target_pairs={{0,1},{1,0},{2,3},{3,2},{4,5},{5,4},{6,7},{7,6},{8,9},{9,8},{10,11... | collective-permute-start | bytes 98312 | tf_op jit(solution)/shard_map/ppermute | solution.py:343
  15.5 5.7 %collective-permute-start.3 = (bf16[32,256]{1,0:T(8,128)(2,1)S(1)}, bf16[32,256]{1,0:T(8,128)(2,1)S(1)}, u32[]{:S(2)}, u32[]{:S(2)}) collective-permute-start(bf16[32,256]{1,0:T(8,128)(2,1)S(1)} %get-tuple-element.31), channel_id=1, source_target_pairs={{0,12},{1,13},{2,14},{3,15},{4,8},{5,9},{6,10},{7,11},{8,4},{9,5},... | collective-permute-start | bytes 49160 | tf_op jit(solution)/shard_map/ppermute | solution.py:343
  17.5 4.2 %collective-permute-start.4 = (bf16[32,256]{1,0:T(8,128)(2,1)S(1)}, bf16[32,256]{1,0:T(8,128)(2,1)S(1)}, u32[]{:S(2)}, u32[]{:S(2)}) collective-permute-start(bf16[32,256]{1,0:T(8,128)(2,1)S(1)} %get-tuple-element.32), channel_id=1, source_target_pairs={{0,9},{1,8},{2,11},{3,10},{4,13},{5,12},{6,15},{7,14},{8,1},{9,0},... | collective-permute-start | bytes 49160 | tf_op jit(solution)/shard_map/ppermute | solution.py:343
  17.5 4.2 %collective-permute-start.5 = (bf16[32,256]{1,0:T(8,128)(2,1)S(1)}, bf16[32,256]{1,0:T(8,128)(2,1)S(1)}, u32[]{:S(2)}, u32[]{:S(2)}) collective-permute-start(bf16[32,256]{1,0:T(8,128)(2,1)S(1)} %get-tuple-element.33), channel_id=1, source_target_pairs={{0,5},{1,4},{2,7},{3,6},{4,1},{5,0},{6,3},{7,2},{8,13},{9,12},{10,... | collective-permute-start | bytes 49160 | tf_op jit(solution)/shard_map/ppermute | solution.py:343
  21.7 4.3 %collective-permute-start.6 = (bf16[128,256]{1,0:T(8,128)(2,1)S(1)}, bf16[128,256]{1,0:T(8,128)(2,1)S(1)}, u32[]{:S(2)}, u32[]{:S(2)}) collective-permute-start(bf16[128,256]{1,0:T(8,128)(2,1)S(1)} %constant_dynamic-update-slice_fusion.refs_0_), channel_id=1, source_target_pairs={{0,3},{1,2},{2,1},{3,0},{4,7},{5,6},{6,5},{7,4},{8,11},{9,10},{10,... | collective-permute-start | bytes 196616 | tf_op jit(solution)/shard_map/ppermute | solution.py:343
  22.8 3.3 %collective-permute-start.7 = (bf16[128,256]{1,0:T(8,128)(2,1)S(1)}, bf16[128,256]{1,0:T(8,128)(2,1)S(1)}, u32[]{:S(2)}, u32[]{:S(2)}) collective-permute-start(bf16[128,256]{1,0:T(8,128)(2,1)S(1)} %constant_dynamic-update-slice_fusion.refs_0_), channel_id=1, source_target_pairs={{0,1},{1,0},{2,3},{3,2},{4,5},{5,4},{6,7},{7,6},{8,9},{9,8},{10,11... | collective-permute-start | bytes 196616 | tf_op jit(solution)/shard_map/ppermute | solution.py:343
  26.0 1.3 %collective-permute-start.8 = (bf16[128,256]{1,0:T(8,128)(2,1)S(1)}, bf16[128,256]{1,0:T(8,128)(2,1)S(1)}, u32[]{:S(2)}, u32[]{:S(2)}) collective-permute-start(bf16[128,256]{1,0:T(8,128)(2,1)S(1)} %collective-permute-done.6.refs_1_), channel_id=1, source_target_pairs={{0,1},{1,0},{2,3},{3,2},{4,5},{5,4},{6,7},{7,6},{8,9},{9,8},{10,11... | collective-permute-start | bytes 196616 | tf_op jit(solution)/shard_map/ppermute | solution.py:343
  28.4 5.7 %collective-permute-start.9 = (bf16[32,256]{1,0:T(8,128)(2,1)S(1)}, bf16[32,256]{1,0:T(8,128)(2,1)S(1)}, u32[]{:S(2)}, u32[]{:S(2)}) collective-permute-start(bf16[32,256]{1,0:T(8,128)(2,1)S(1)} %get-tuple-element.36), channel_id=1, source_target_pairs={{0,12},{1,13},{2,14},{3,15},{4,8},{5,9},{6,10},{7,11},{8,4},{9,5},... | collective-permute-start | bytes 49160 | tf_op jit(solution)/shard_map/ppermute | solution.py:343
  30.2 4.4 %collective-permute-start.10 = (bf16[32,256]{1,0:T(8,128)(2,1)S(1)}, bf16[32,256]{1,0:T(8,128)(2,1)S(1)}, u32[]{:S(2)}, u32[]{:S(2)}) collective-permute-start(bf16[32,256]{1,0:T(8,128)(2,1)S(1)} %get-tuple-element.37), channel_id=1, source_target_pairs={{0,9},{1,8},{2,11},{3,10},{4,13},{5,12},{6,15},{7,14},{8,1},{9,0},... | collective-permute-start | bytes 49160 | tf_op jit(solution)/shard_map/ppermute | solution.py:343
  30.5 4.1 %collective-permute-start.11 = (bf16[32,256]{1,0:T(8,128)(2,1)S(1)}, bf16[32,256]{1,0:T(8,128)(2,1)S(1)}, u32[]{:S(2)}, u32[]{:S(2)}) collective-permute-start(bf16[32,256]{1,0:T(8,128)(2,1)S(1)} %get-tuple-element.38), channel_id=1, source_target_pairs={{0,5},{1,4},{2,7},{3,6},{4,1},{5,0},{6,3},{7,2},{8,13},{9,12},{10,... | collective-permute-start | bytes 49160 | tf_op jit(solution)/shard_map/ppermute | solution.py:343

commit v13 on v11

--- a/solution.py
+++ b/solution.py
@@ -129,19 +129,23 @@
 
 
 def chain(my_lat, slab, shape, taps_ref, expand_ref, reduce_ref, attn_ref, center, scratch):
-    one, lat_in = scratch
+    one, lat_in, conv = scratch
     rows, all_rows, columns, channels = shape
     cells = all_rows * columns
-    parts = []
-    for c in range(0, channels, LANES):
+
+    def convolve(i, carry):
+        place = pl.ds(pl.multiple_of(i * LANES, LANES), LANES)
         acc = jnp.zeros((all_rows, columns, LANES), f32)
         for b in range(TAPS):
-            block = slab(b, c)
+            block = slab(b, place)
             for a in range(TAPS):
-                tap = taps_ref[a, b : b + 1, c : c + LANES].reshape(1, 1, LANES)
+                tap = taps_ref[a, b : b + 1, place].reshape(1, 1, LANES)
                 acc = acc + block[a : a + all_rows] * tap
-        parts.append(acc.reshape(cells, LANES))
-    normed = layer_norm(jnp.concatenate(parts, axis=-1)).astype(bf16)
+        conv[:, place] = acc.reshape(cells, LANES)
+        return carry
+
+    lax.fori_loop(0, channels // LANES, convolve, 0)
+    normed = layer_norm(conv[...]).astype(bf16)
 
     def widen(k, total):
         part = slice(k * channels, (k + 1) * channels)
@@ -197,7 +201,7 @@
 
     def slab(b, c):
         first = SIDE - HALO + b
-        return padded[:, first : first + columns, c : c + LANES]
+        return padded[:, first : first + columns, c]
 
     center = padded[HALO : HALO + all_rows, SIDE : SIDE + columns]
     shape = (rows, all_rows, columns, channels)
@@ -227,19 +231,19 @@
     fill(padded, all_rows, STRIP + cols, unpack(jnp.where(even, near, far), False))
     sublane = lax.broadcasted_iota(jnp.int32, (1, columns, 1), 1)
 
-    def halves(shift, rows_of, c, width):
+    def halves(shift, rows_of, c):
         right = STRIP + cols - SIDE + shift
         left = STRIP - SIDE + shift
         return jnp.where(
             sublane < SIDE,
-            padded[rows_of, right : right + columns, c : c + width],
-            padded[rows_of, left : left + columns, c : c + width],
+            padded[rows_of, right : right + columns, c],
+            padded[rows_of, left : left + columns, c],
         )
 
     def slab(b, c):
-        return halves(b - HALO, slice(None), c, LANES)
-
-    center = halves(0, slice(HALO, HALO + all_rows), 0, channels)
+        return halves(b - HALO, slice(None), c)
+
+    center = halves(0, slice(HALO, HALO + all_rows), slice(None))
     shape = (rows, all_rows, columns, channels)
     block_two, lon_in = chain(
         my_lat, slab, shape, taps_ref, expand_ref, reduce_ref, attn_ref, center, scratch
@@ -372,6 +376,7 @@
             pltpu.VMEM((all_rows + 2 * HALO, width, channels), f32),
             pltpu.VMEM((all_rows * count, channels), bf16),
             pltpu.VMEM((all_rows * count, channels), bf16),
+            pltpu.VMEM((all_rows * count, channels), f32),
         ]
 
     work = 4 * all_rows * columns * channels * w_expand.shape[1]

time: 35.5 us -> 35.6 us (level)
  no operation moved by 1% of the time
where the time goes in v13:
time: 35.6 us; the launch traced here: 35.4 us
  starting transfers between devices  16.2 us (46%)
  Pallas kernels  9.96 us (28%)
  waiting for transfers between devices  8.39 us (24%)
  local copies, waits for them, and re-layouts  0.76 us (2%)
    pallas_call x6, Pallas kernels, call(): pl.pallas_call(kernel, out_shape=shapes, in_specs=[given] * len(operands)...  9.96 us
    ppermute x10, starting transfers between devices, swap(): return lax.ppermute(piece, 'lon', [(j, j ^ mask) for j in range(nlon)])  9.47 us
    ppermute x10, waiting for transfers between devices, swap(): return lax.ppermute(piece, 'lon', [(j, j ^ mask) for j in range(nlon)])  8.39 us
    ppermute x1, starting transfers between devices, shards(): lax.ppermute(far, 'lon', [(j, (j - 1) % nlon if j % 2 == 0 else (j + 1) %...  3.78 us
    ppermute x1, starting transfers between devices, shards(): lax.ppermute(field, 'lat', [((i + s) % nlat, i) for i in range(nlat)])  2.94 us
    unnamed x7, local copies, waits for them, and re-layouts  0.76 us
  transfers between devices with their start and end apart: 12, of which 6 were waited for; matrix products, arithmetic and copies ran while one was open for 0% of the time, Pallas kernels for 14%

profile of v13, /device:TPU:0, one launch (start us, length us, event | category | flops | bytes accessed | tf_op | source)
XLA Modules:
  0.0 35.4 jit_solution(2293024664751162370)
XLA Ops:
  0.0 0.0 copy-start
  0.0 2.9 %collective-permute-start = (bf16[8,16,256]{2,1,0:T(8,128)(2,1)}, bf16[8,16,256]{2,1,0:T(8,128)(2,1)S(1)}, u32[]{:S(2)}, u32[]{:S(2)}) collective-permute-start(bf16[8,16,256]{2,1,0:T(8,128)(2,1)} %refs_0_.7), channel_id=1, source_target_pairs={{16,0},{0,16},{17,1},{1,17},{18,2},{2,18},{19,3},{3,19},{20,4},{4,... | collective-permute-start | bytes 196616 | tf_op jit(solution)/shard_map/ppermute | solution.py:347
  2.9 0.0 copy-start.1
  2.9 0.7 %copy-done.1 = bf16[7,7,256]{2,1,0:T(8,128)(2,1)S(1)} copy-done((bf16[7,7,256]{2,1,0:T(8,128)(2,1)S(1)}, bf16[7,7,256]{2,1,0:T(8,128)(2,1)}, u32[]{:S(2)}) %copy-start.1) | copy-done | bytes 25112
  3.7 1.8 %shard_map.64 = (bf16[256,1024]{1,0:T(8,128)(2,1)S(1)}, bf16[1024,256]{1,0:T(8,128)(2,1)S(1)}, bf16[4,256,256]{2,1,0:T(8,128)(2,1)S(1)}, bf16[4,256,256]{2,1,0:T(8,128)(2,1)S(1)}, f32[7,7,256]{2,1,0:T(8,128)S(1)}) custom-call(bf16[256,1024]{1,0:T(8,128)(2,1)} %refs_0_.4, bf16[1024,256]{1,0:T(8,128)(2,1)} %refs_1_.1, bf16[4,256,256]{2,1,0:T(8,128)(2,1)} %refs_2_.1, ...), custom_call_target="tpu_custom_call" | custom-call | bytes 2122240 | tf_op jit(solution)/shard_map/pallas_call | solution.py:313
  5.5 0.0 collective-permute-done.refs_1_
  5.5 0.0 copy-done
  5.5 0.1 shard_map.65
  5.6 3.8 %collective-permute-start.1 = (bf16[64,256]{1,0:T(8,128)(2,1)S(1)}, bf16[64,256]{1,0:T(8,128)(2,1)S(1)}, u32[]{:S(2)}, u32[]{:S(2)}) collective-permute-start(bf16[64,256]{1,0:T(8,128)(2,1)S(1)} %get-tuple-element.24), channel_id=1, source_target_pairs={{0,15},{1,2},{2,1},{3,4},{4,3},{5,6},{6,5},{7,8},{8,7},{9,10},{10,... | collective-permute-start | bytes 98312 | tf_op jit(solution)/shard_map/ppermute | solution.py:369
  9.4 0.0 collective-permute-start.2
  9.4 3.3 %shard_map.66 = (bf16[64,256]{1,0:T(8,128)(2,1)S(1)}, bf16[64,256]{1,0:T(8,128)(2,1)S(1)}) custom-call(bf16[8,16,256]{2,1,0:T(8,128)(2,1)S(1)} %copy-done, bf16[8,16,256]{2,1,0:T(8,128)(2,1)S(1)} %collective-permute-done.refs_1_, f32[7,7,256]{2,1,0:T(8,128)S(1)} %get-tuple-element.26.refs_2_.refs_5_, ...), custom_call_target="tpu_custom_call" | custom-call | flops 134217728 | bytes 1754112 | tf_op jit(solution)/shard_map/pallas_call | solution.py:313
  12.7 0.0 collective-permute-done.1.refs_2_
  12.7 0.0 collective-permute-done.2.refs_3_
  12.7 2.8 %shard_map.67 = (bf16[64,256]{1,0:T(8,128)(2,1)S(1)}, bf16[32,256]{1,0:T(8,128)(2,1)S(1)}, bf16[32,256]{1,0:T(8,128)(2,1)S(1)}, bf16[32,256]{1,0:T(8,128)(2,1)S(1)}, bf16[32,256]{1,0:T(8,128)(2,1)S(1)}) custom-call(bf16[8,16,256]{2,1,0:T(8,128)(2,1)S(1)} %copy-done, bf16[8,16,256]{2,1,0:T(8,128)(2,1)S(1)} %collective-permute-done.refs_1_, ...), custom_call_target="tpu_custom_call" | custom-call | flops 134217728 | bytes 1852416 | tf_op jit(solution)/shard_map/pallas_call | solution.py:313
  15.5 2.0 %collective-permute-start.3 = (bf16[32,256]{1,0:T(8,128)(2,1)S(1)}, bf16[32,256]{1,0:T(8,128)(2,1)S(1)}, u32[]{:S(2)}, u32[]{:S(2)}) collective-permute-start(bf16[32,256]{1,0:T(8,128)(2,1)S(1)} %get-tuple-element.31), channel_id=1, source_target_pairs={{0,12},{1,13},{2,14},{3,15},{4,8},{5,9},{6,10},{7,11},{8,4},{9,5},... | collective-permute-start | bytes 49160 | tf_op jit(solution)/shard_map/ppermute | solution.py:335
  17.5 0.0 collective-permute-start.4
  17.5 2.2 %collective-permute-start.5 = (bf16[32,256]{1,0:T(8,128)(2,1)S(1)}, bf16[32,256]{1,0:T(8,128)(2,1)S(1)}, u32[]{:S(2)}, u32[]{:S(2)}) collective-permute-start(bf16[32,256]{1,0:T(8,128)(2,1)S(1)} %get-tuple-element.33), channel_id=1, source_target_pairs={{0,5},{1,4},{2,7},{3,6},{4,1},{5,0},{6,3},{7,2},{8,13},{9,12},{10,... | collective-permute-start | bytes 49160 | tf_op jit(solution)/shard_map/ppermute | solution.py:335
  19.7 1.5 %collective-permute-done.3 = bf16[32,256]{1,0:T(8,128)(2,1)S(1)} collective-permute-done((bf16[32,256]{1,0:T(8,128)(2,1)S(1)}, bf16[32,256]{1,0:T(8,128)(2,1)S(1)}, u32[]{:S(2)}, u32[]{:S(2)}) %collective-permute-start.3) | collective-permute-done | bytes 16416 | tf_op jit(solution)/shard_map/ppermute | solution.py:335
  21.2 0.5 %collective-permute-done.4 = bf16[32,256]{1,0:T(8,128)(2,1)S(1)} collective-permute-done((bf16[32,256]{1,0:T(8,128)(2,1)S(1)}, bf16[32,256]{1,0:T(8,128)(2,1)S(1)}, u32[]{:S(2)}, u32[]{:S(2)}) %collective-permute-start.4) | collective-permute-done | bytes 16416 | tf_op jit(solution)/shard_map/ppermute | solution.py:335
  21.7 0.0 collective-permute-done.5
  21.7 1.0 %collective-permute-start.6 = (bf16[128,256]{1,0:T(8,128)(2,1)S(1)}, bf16[128,256]{1,0:T(8,128)(2,1)S(1)}, u32[]{:S(2)}, u32[]{:S(2)}) collective-permute-start(bf16[128,256]{1,0:T(8,128)(2,1)S(1)} %constant_dynamic-update-slice_fusion.refs_0_), channel_id=1, source_target_pairs={{0,3},{1,2},{2,1},{3,0},{4,7},{5,6},{6,5},{7,4},{8,11},{9,10},{10,... | collective-permute-start | bytes 196616 | tf_op jit(solution)/shard_map/ppermute | solution.py:335
  22.7 0.0 collective-permute-start.7
  22.7 3.3 %collective-permute-done.6.refs_1_ = bf16[128,256]{1,0:T(8,128)(2,1)S(1)} collective-permute-done((bf16[128,256]{1,0:T(8,128)(2,1)S(1)}, bf16[128,256]{1,0:T(8,128)(2,1)S(1)}, u32[]{:S(2)}, u32[]{:S(2)}) %collective-permute-start.6) | collective-permute-done | bytes 65568 | tf_op jit(solution)/shard_map/ppermute | solution.py:335
  25.9 0.1 collective-permute-start.8
  26.0 0.0 collective-permute-done.7.refs_2_
  26.1 1.1 %collective-permute-done.8.refs_3_ = bf16[128,256]{1,0:T(8,128)(2,1)S(1)} collective-permute-done((bf16[128,256]{1,0:T(8,128)(2,1)S(1)}, bf16[128,256]{1,0:T(8,128)(2,1)S(1)}, u32[]{:S(2)}, u32[]{:S(2)}) %collective-permute-start.8) | collective-permute-done | bytes 65568 | tf_op jit(solution)/shard_map/ppermute | solution.py:335
  27.2 1.2 %shard_map.68 = (bf16[32,256]{1,0:T(8,128)(2,1)S(1)}, bf16[32,256]{1,0:T(8,128)(2,1)S(1)}, bf16[32,256]{1,0:T(8,128)(2,1)S(1)}, bf16[32,256]{1,0:T(8,128)(2,1)S(1)}) custom-call(bf16[128,256]{1,0:T(8,128)(2,1)S(1)} %constant_dynamic-update-slice_fusion.refs_0_, bf16[128,256]{1,0:T(8,128)(2,1)S(1)} %collective-permute-done.6.refs_1_, ...), custom_call_target="tpu_custom_call" | custom-call | bytes 786432 | tf_op jit(solution)/shard_map/pallas_call | solution.py:313
  28.4 1.7 %collective-permute-start.9 = (bf16[32,256]{1,0:T(8,128)(2,1)S(1)}, bf16[32,256]{1,0:T(8,128)(2,1)S(1)}, u32[]{:S(2)}, u32[]{:S(2)}) collective-permute-start(bf16[32,256]{1,0:T(8,128)(2,1)S(1)} %get-tuple-element.36), channel_id=1, source_target_pairs={{0,12},{1,13},{2,14},{3,15},{4,8},{5,9},{6,10},{7,11},{8,4},{9,5},... | collective-permute-start | bytes 49160 | tf_op jit(solution)/shard_map/ppermute | solution.py:335
  30.2 0.3 collective-permute-start.10
  30.5 2.1 %collective-permute-start.11 = (bf16[32,256]{1,0:T(8,128)(2,1)S(1)}, bf16[32,256]{1,0:T(8,128)(2,1)S(1)}, u32[]{:S(2)}, u32[]{:S(2)}) collective-permute-start(bf16[32,256]{1,0:T(8,128)(2,1)S(1)} %get-tuple-element.38), channel_id=1, source_target_pairs={{0,5},{1,4},{2,7},{3,6},{4,1},{5,0},{6,3},{7,2},{8,13},{9,12},{10,... | collective-permute-start | bytes 49160 | tf_op jit(solution)/shard_map/ppermute | solution.py:335
  32.6 1.5 %collective-permute-done.9.refs_1_ = bf16[32,256]{1,0:T(8,128)(2,1)S(1)} collective-permute-done((bf16[32,256]{1,0:T(8,128)(2,1)S(1)}, bf16[32,256]{1,0:T(8,128)(2,1)S(1)}, u32[]{:S(2)}, u32[]{:S(2)}) %collective-permute-start.9) | collective-permute-done | bytes 16416 | tf_op jit(solution)/shard_map/ppermute | solution.py:335
  34.1 0.5 %collective-permute-done.10.refs_2_ = bf16[32,256]{1,0:T(8,128)(2,1)S(1)} collective-permute-done((bf16[32,256]{1,0:T(8,128)(2,1)S(1)}, bf16[32,256]{1,0:T(8,128)(2,1)S(1)}, u32[]{:S(2)}, u32[]{:S(2)}) %collective-permute-start.10) | collective-permute-done | bytes 16416 | tf_op jit(solution)/shard_map/ppermute | solution.py:335
  34.6 0.0 collective-permute-done.11.refs_3_
  34.6 0.8 %shard_map.69 = bf16[8,16,256]{2,1,0:T(8,128)(2,1)} custom-call(bf16[32,256]{1,0:T(8,128)(2,1)S(1)} %get-tuple-element.35.refs_0_, bf16[32,256]{1,0:T(8,128)(2,1)S(1)} %collective-permute-done.9.refs_1_, bf16[32,256]{1,0:T(8,128)(2,1)S(1)} %collective-permute-done.10.refs_2_, bf16[32,256]{1,0:T(8,128)(2,1)S(1)} %collective-permute-done.11.refs_3_, ...), custom_call_target="tpu_custom_call" | custom-call | bytes 655360 | tf_op jit(solution)/shard_map/pallas_call | solution.py:313
  (4 shorter events, 0.0 us)
Async XLA Ops:
  0.0 5.5 %copy-start = (bf16[8,16,256]{2,1,0:T(8,128)(2,1)S(1)}, bf16[8,16,256]{2,1,0:T(8,128)(2,1)}, u32[]{:S(2)}) copy-start(bf16[8,16,256]{2,1,0:T(8,128)(2,1)} %refs_0_.7) | copy-start | bytes 196612
  0.0 5.5 %collective-permute-start = (bf16[8,16,256]{2,1,0:T(8,128)(2,1)}, bf16[8,16,256]{2,1,0:T(8,128)(2,1)S(1)}, u32[]{:S(2)}, u32[]{:S(2)}) collective-permute-start(bf16[8,16,256]{2,1,0:T(8,128)(2,1)} %refs_0_.7), channel_id=1, source_target_pairs={{16,0},{0,16},{17,1},{1,17},{18,2},{2,18},{19,3},{3,19},{20,4},{4,... | collective-permute-start | bytes 196616 | tf_op jit(solution)/shard_map/ppermute | solution.py:347
  2.9 0.7 %copy-start.1 = (bf16[7,7,256]{2,1,0:T(8,128)(2,1)S(1)}, bf16[7,7,256]{2,1,0:T(8,128)(2,1)}, u32[]{:S(2)}) copy-start(bf16[7,7,256]{2,1,0:T(8,128)(2,1)} %refs_4_.1) | copy-start | bytes 75268
  5.6 7.1 %collective-permute-start.1 = (bf16[64,256]{1,0:T(8,128)(2,1)S(1)}, bf16[64,256]{1,0:T(8,128)(2,1)S(1)}, u32[]{:S(2)}, u32[]{:S(2)}) collective-permute-start(bf16[64,256]{1,0:T(8,128)(2,1)S(1)} %get-tuple-element.24), channel_id=1, source_target_pairs={{0,15},{1,2},{2,1},{3,4},{4,3},{5,6},{6,5},{7,8},{8,7},{9,10},{10,... | collective-permute-start | bytes 98312 | tf_op jit(solution)/shard_map/ppermute | solution.py:369
  9.4 3.3 %collective-permute-start.2 = (bf16[64,256]{1,0:T(8,128)(2,1)S(1)}, bf16[64,256]{1,0:T(8,128)(2,1)S(1)}, u32[]{:S(2)}, u32[]{:S(2)}) collective-permute-start(bf16[64,256]{1,0:T(8,128)(2,1)S(1)} %get-tuple-element.25), channel_id=1, source_target_pairs={{0,1},{1,0},{2,3},{3,2},{4,5},{5,4},{6,7},{7,6},{8,9},{9,8},{10,11... | collective-permute-start | bytes 98312 | tf_op jit(solution)/shard_map/ppermute | solution.py:335
  15.5 5.7 %collective-permute-start.3 = (bf16[32,256]{1,0:T(8,128)(2,1)S(1)}, bf16[32,256]{1,0:T(8,128)(2,1)S(1)}, u32[]{:S(2)}, u32[]{:S(2)}) collective-permute-start(bf16[32,256]{1,0:T(8,128)(2,1)S(1)} %get-tuple-element.31), channel_id=1, source_target_pairs={{0,12},{1,13},{2,14},{3,15},{4,8},{5,9},{6,10},{7,11},{8,4},{9,5},... | collective-permute-start | bytes 49160 | tf_op jit(solution)/shard_map/ppermute | solution.py:335
  17.5 4.2 %collective-permute-start.4 = (bf16[32,256]{1,0:T(8,128)(2,1)S(1)}, bf16[32,256]{1,0:T(8,128)(2,1)S(1)}, u32[]{:S(2)}, u32[]{:S(2)}) collective-permute-start(bf16[32,256]{1,0:T(8,128)(2,1)S(1)} %get-tuple-element.32), channel_id=1, source_target_pairs={{0,9},{1,8},{2,11},{3,10},{4,13},{5,12},{6,15},{7,14},{8,1},{9,0},... | collective-permute-start | bytes 49160 | tf_op jit(solution)/shard_map/ppermute | solution.py:335
  17.5 4.2 %collective-permute-start.5 = (bf16[32,256]{1,0:T(8,128)(2,1)S(1)}, bf16[32,256]{1,0:T(8,128)(2,1)S(1)}, u32[]{:S(2)}, u32[]{:S(2)}) collective-permute-start(bf16[32,256]{1,0:T(8,128)(2,1)S(1)} %get-tuple-element.33), channel_id=1, source_target_pairs={{0,5},{1,4},{2,7},{3,6},{4,1},{5,0},{6,3},{7,2},{8,13},{9,12},{10,... | collective-permute-start | bytes 49160 | tf_op jit(solution)/shard_map/ppermute | solution.py:335
  21.7 4.3 %collective-permute-start.6 = (bf16[128,256]{1,0:T(8,128)(2,1)S(1)}, bf16[128,256]{1,0:T(8,128)(2,1)S(1)}, u32[]{:S(2)}, u32[]{:S(2)}) collective-permute-start(bf16[128,256]{1,0:T(8,128)(2,1)S(1)} %constant_dynamic-update-slice_fusion.refs_0_), channel_id=1, source_target_pairs={{0,3},{1,2},{2,1},{3,0},{4,7},{5,6},{6,5},{7,4},{8,11},{9,10},{10,... | collective-permute-start | bytes 196616 | tf_op jit(solution)/shard_map/ppermute | solution.py:335
  22.7 3.4 %collective-permute-start.7 = (bf16[128,256]{1,0:T(8,128)(2,1)S(1)}, bf16[128,256]{1,0:T(8,128)(2,1)S(1)}, u32[]{:S(2)}, u32[]{:S(2)}) collective-permute-start(bf16[128,256]{1,0:T(8,128)(2,1)S(1)} %constant_dynamic-update-slice_fusion.refs_0_), channel_id=1, source_target_pairs={{0,1},{1,0},{2,3},{3,2},{4,5},{5,4},{6,7},{7,6},{8,9},{9,8},{10,11... | collective-permute-start | bytes 196616 | tf_op jit(solution)/shard_map/ppermute | solution.py:335
  25.9 1.3 %collective-permute-start.8 = (bf16[128,256]{1,0:T(8,128)(2,1)S(1)}, bf16[128,256]{1,0:T(8,128)(2,1)S(1)}, u32[]{:S(2)}, u32[]{:S(2)}) collective-permute-start(bf16[128,256]{1,0:T(8,128)(2,1)S(1)} %collective-permute-done.6.refs_1_), channel_id=1, source_target_pairs={{0,1},{1,0},{2,3},{3,2},{4,5},{5,4},{6,7},{7,6},{8,9},{9,8},{10,11... | collective-permute-start | bytes 196616 | tf_op jit(solution)/shard_map/ppermute | solution.py:335
  28.4 5.7 %collective-permute-start.9 = (bf16[32,256]{1,0:T(8,128)(2,1)S(1)}, bf16[32,256]{1,0:T(8,128)(2,1)S(1)}, u32[]{:S(2)}, u32[]{:S(2)}) collective-permute-start(bf16[32,256]{1,0:T(8,128)(2,1)S(1)} %get-tuple-element.36), channel_id=1, source_target_pairs={{0,12},{1,13},{2,14},{3,15},{4,8},{5,9},{6,10},{7,11},{8,4},{9,5},... | collective-permute-start | bytes 49160 | tf_op jit(solution)/shard_map/ppermute | solution.py:335
  30.2 4.4 %collective-permute-start.10 = (bf16[32,256]{1,0:T(8,128)(2,1)S(1)}, bf16[32,256]{1,0:T(8,128)(2,1)S(1)}, u32[]{:S(2)}, u32[]{:S(2)}) collective-permute-start(bf16[32,256]{1,0:T(8,128)(2,1)S(1)} %get-tuple-element.37), channel_id=1, source_target_pairs={{0,9},{1,8},{2,11},{3,10},{4,13},{5,12},{6,15},{7,14},{8,1},{9,0},... | collective-permute-start | bytes 49160 | tf_op jit(solution)/shard_map/ppermute | solution.py:335
  30.5 4.1 %collective-permute-start.11 = (bf16[32,256]{1,0:T(8,128)(2,1)S(1)}, bf16[32,256]{1,0:T(8,128)(2,1)S(1)}, u32[]{:S(2)}, u32[]{:S(2)}) collective-permute-start(bf16[32,256]{1,0:T(8,128)(2,1)S(1)} %get-tuple-element.38), channel_id=1, source_target_pairs={{0,5},{1,4},{2,7},{3,6},{4,1},{5,0},{6,3},{7,2},{8,13},{9,12},{10,... | collective-permute-start | bytes 49160 | tf_op jit(solution)/shard_map/ppermute | solution.py:335

commit v14 on v11

--- a/solution.py
+++ b/solution.py
@@ -254,24 +254,29 @@
         sent_refs[k][...] = part.reshape(sent_refs[k].shape)
 
 
-def circle_kernel(levels, some, *refs):
-    attn_ref, mix_refs = refs[-levels - 1], refs[-levels:]
-    parts = refs[: -levels - 1]
-    count = parts[0].shape[0] // (some * levels)
-
-    def latitude(part, r):
-        starts = [(k * some + r) * count for k in range(levels)]
-        return jnp.concatenate([part[start : start + count] for start in starts], axis=0)
-
+def join_kernel(levels, some, *refs):
+    parts, joined = refs[:levels], refs[levels:]
+    cols = parts[0].shape[0] // some
     for r in range(some):
-        own = latitude(parts[0], r)
-        every = jnp.concatenate([own] + [latitude(part, r) for part in parts[1:]], axis=0)
-        queries = dot(own, attn_ref[0]).astype(bf16)
-        keys = dot(every, attn_ref[1]).astype(bf16)
-        values = dot(every, attn_ref[2]).astype(bf16)
-        mix = attend(queries, keys, values, None)
         for k in range(levels):
-            mix_refs[k][r * count : (r + 1) * count] = mix[k * count : (k + 1) * count]
+            joined[r][k * cols : (k + 1) * cols] = parts[k][r * cols : (r + 1) * cols]
+
+
+def circle_kernel(levels, before, *refs):
+    attn_ref, refs = refs[0], refs[1:]
+    done, refs = refs[:before], refs[before:]
+    parts, mix_refs = refs[:-levels], refs[-levels:]
+    own = parts[0][...]
+    every = jnp.concatenate([own] + [part[...] for part in parts[1:]], axis=0)
+    queries = dot(own, attn_ref[0]).astype(bf16)
+    keys = dot(every, attn_ref[1]).astype(bf16)
+    values = dot(every, attn_ref[2]).astype(bf16)
+    mix = attend(queries, keys, values, None)
+    cols = own.shape[0] // levels
+    for k in range(levels):
+        for r in range(before // levels):
+            mix_refs[k][r * cols : (r + 1) * cols] = done[r * levels + k][...]
+        mix_refs[k][before // levels * cols :] = mix[k * cols : (k + 1) * cols]
 
 
 def last_kernel(levels, *refs):
@@ -392,14 +397,25 @@
     )
 
     parts = exchange(parts)
-    circle = [jnp.concatenate(parts, axis=0)]
+    joined = call(
+        functools.partial(join_kernel, levels, some), [(levels * cols, channels)] * some, parts
+    )
+    circles = [[part] for part in joined]
     mask = column // 2
     while mask:
-        circle = circle + [swap(part, mask + mask // 2) for part in circle]
+        for circle in circles:
+            circle += [swap(part, mask + mask // 2) for part in circle]
         mask //= 2
-    mixes = call(
-        functools.partial(circle_kernel, levels, some), [piece] * levels, [*circle, lon_proj]
-    )
+    done = []
+    for r, circle in enumerate(circles):
+        last_one = r == some - 1
+        mixes = call(
+            functools.partial(circle_kernel, levels, len(done) if last_one else 0),
+            [piece if last_one else (cols, channels)] * levels,
+            [lon_proj, *(done if last_one else []), *circle],
+            flops=work // 4,
+        )
+        done = done + list(mixes)
     mixes = exchange(mixes)
     (out,) = call(
         functools.partial(last_kernel, levels),

time: 35.5 us -> 35.3 us (level)
  waiting for transfers between devices: 8.29 us -> 6.78 us
  starting transfers between devices: 16.3 us -> 17.4 us
    ppermute x10 -> x13, waiting for transfers between devices: 8.28 us -> 6.77 us  [swap(): return lax.ppermute(piece, 'lon', [(j, j ^ mask) for j in range(nlon)])]
    ppermute x10 -> x13, starting transfers between devices: 9.57 us -> 10.7 us  [swap(): return lax.ppermute(piece, 'lon', [(j, j ^ mask) for j in range(nlon)])]
    pallas_call x6 -> x8, Pallas kernels: 9.87 us -> 10 us  [call(): pl.pallas_call(kernel, out_shape=shapes, in_specs=[given] * len(operands)...]
    unnamed x7 -> x4, local copies, waits for them, and re-layouts: 0.76 us -> 0.75 us
  transfers between devices with their start and end apart: 12 -> 15, of which waited for: 6 -> 8; matrix products, arithmetic and copies ran while one was open for 0% -> 0% of each run, Pallas kernels for 14% -> 16%
where the time goes in v14:
time: 35.3 us; the launch traced here: 35.1 us
  starting transfers between devices  17.4 us (49%)
  Pallas kernels  10 us (28%)
  waiting for transfers between devices  6.78 us (19%)
  local copies, waits for them, and re-layouts  0.75 us (2%)
    ppermute x13, starting transfers between devices, swap(): return lax.ppermute(piece, 'lon', [(j, j ^ mask) for j in range(nlon)])  10.7 us
    pallas_call x8, Pallas kernels, call(): pl.pallas_call(kernel, out_shape=shapes, in_specs=[given] * len(operands)...  10 us
    ppermute x13, waiting for transfers between devices, swap(): return lax.ppermute(piece, 'lon', [(j, j ^ mask) for j in range(nlon)])  6.77 us
    ppermute x1, starting transfers between devices, shards(): lax.ppermute(far, 'lon', [(j, (j - 1) % nlon if j % 2 == 0 else (j + 1) %...  3.78 us
    ppermute x1, starting transfers between devices, shards(): lax.ppermute(field, 'lat', [((i + s) % nlat, i) for i in range(nlat)])  2.94 us
    unnamed x4, local copies, waits for them, and re-layouts  0.75 us
  transfers between devices with their start and end apart: 15, of which 8 were waited for; matrix products, arithmetic and copies ran while one was open for 0% of the time, Pallas kernels for 16%

profile of v14, /device:TPU:0, one launch (start us, length us, event | category | flops | bytes accessed | tf_op | source)
XLA Modules:
  0.0 35.1 jit_solution(10435538431158442128)
XLA Ops:
  0.0 0.0 copy-start
  0.0 2.9 %collective-permute-start = (bf16[8,16,256]{2,1,0:T(8,128)(2,1)}, bf16[8,16,256]{2,1,0:T(8,128)(2,1)S(1)}, u32[]{:S(2)}, u32[]{:S(2)}) collective-permute-start(bf16[8,16,256]{2,1,0:T(8,128)(2,1)} %refs_0_.7), channel_id=1, source_target_pairs={{16,0},{0,16},{17,1},{1,17},{18,2},{2,18},{19,3},{3,19},{20,4},{4,... | collective-permute-start | bytes 196616 | tf_op jit(solution)/shard_map/ppermute | solution.py:348
  2.9 0.0 copy-start.1
  2.9 0.7 %copy-done.1 = bf16[7,7,256]{2,1,0:T(8,128)(2,1)S(1)} copy-done((bf16[7,7,256]{2,1,0:T(8,128)(2,1)S(1)}, bf16[7,7,256]{2,1,0:T(8,128)(2,1)}, u32[]{:S(2)}) %copy-start.1) | copy-done | bytes 25112
  3.7 1.8 %shard_map.64 = (bf16[256,1024]{1,0:T(8,128)(2,1)S(1)}, bf16[1024,256]{1,0:T(8,128)(2,1)S(1)}, bf16[4,256,256]{2,1,0:T(8,128)(2,1)S(1)}, bf16[4,256,256]{2,1,0:T(8,128)(2,1)S(1)}, f32[7,7,256]{2,1,0:T(8,128)S(1)}) custom-call(bf16[256,1024]{1,0:T(8,128)(2,1)} %refs_0_.4, bf16[1024,256]{1,0:T(8,128)(2,1)} %refs_1_.1, bf16[4,256,256]{2,1,0:T(8,128)(2,1)} %refs_2_.1, ...), custom_call_target="tpu_custom_call" | custom-call | bytes 2122240 | tf_op jit(solution)/shard_map/pallas_call | solution.py:314
  5.5 0.0 collective-permute-done.refs_1_
  5.5 0.0 copy-done
  5.5 0.1 shard_map.65
  5.6 3.8 %collective-permute-start.1 = (bf16[64,256]{1,0:T(8,128)(2,1)S(1)}, bf16[64,256]{1,0:T(8,128)(2,1)S(1)}, u32[]{:S(2)}, u32[]{:S(2)}) collective-permute-start(bf16[64,256]{1,0:T(8,128)(2,1)S(1)} %get-tuple-element.31), channel_id=1, source_target_pairs={{0,15},{1,2},{2,1},{3,4},{4,3},{5,6},{6,5},{7,8},{8,7},{9,10},{10,... | collective-permute-start | bytes 98312 | tf_op jit(solution)/shard_map/ppermute | solution.py:370
  9.4 0.0 collective-permute-start.2
  9.4 3.2 %shard_map.66 = (bf16[64,256]{1,0:T(8,128)(2,1)S(1)}, bf16[64,256]{1,0:T(8,128)(2,1)S(1)}) custom-call(bf16[8,16,256]{2,1,0:T(8,128)(2,1)S(1)} %copy-done, bf16[8,16,256]{2,1,0:T(8,128)(2,1)S(1)} %collective-permute-done.refs_1_, f32[7,7,256]{2,1,0:T(8,128)S(1)} %get-tuple-element.33.refs_2_.refs_5_, ...), custom_call_target="tpu_custom_call" | custom-call | flops 134217728 | bytes 1754112 | tf_op jit(solution)/shard_map/pallas_call | solution.py:314
  12.6 0.0 collective-permute-done.1.refs_2_
  12.6 0.0 collective-permute-done.2.refs_3_
  12.6 2.8 %shard_map.67 = (bf16[64,256]{1,0:T(8,128)(2,1)S(1)}, bf16[32,256]{1,0:T(8,128)(2,1)S(1)}, bf16[32,256]{1,0:T(8,128)(2,1)S(1)}, bf16[32,256]{1,0:T(8,128)(2,1)S(1)}, bf16[32,256]{1,0:T(8,128)(2,1)S(1)}) custom-call(bf16[8,16,256]{2,1,0:T(8,128)(2,1)S(1)} %copy-done, bf16[8,16,256]{2,1,0:T(8,128)(2,1)S(1)} %collective-permute-done.refs_1_, ...), custom_call_target="tpu_custom_call" | custom-call | flops 134217728 | bytes 1852416 | tf_op jit(solution)/shard_map/pallas_call | solution.py:314
  15.4 2.0 %collective-permute-start.3 = (bf16[32,256]{1,0:T(8,128)(2,1)S(1)}, bf16[32,256]{1,0:T(8,128)(2,1)S(1)}, u32[]{:S(2)}, u32[]{:S(2)}) collective-permute-start(bf16[32,256]{1,0:T(8,128)(2,1)S(1)} %get-tuple-element.38), channel_id=1, source_target_pairs={{0,12},{1,13},{2,14},{3,15},{4,8},{5,9},{6,10},{7,11},{8,4},{9,5},... | collective-permute-start | bytes 49160 | tf_op jit(solution)/shard_map/ppermute | solution.py:336
  17.4 0.0 collective-permute-start.4
  17.4 2.2 %collective-permute-start.5 = (bf16[32,256]{1,0:T(8,128)(2,1)S(1)}, bf16[32,256]{1,0:T(8,128)(2,1)S(1)}, u32[]{:S(2)}, u32[]{:S(2)}) collective-permute-start(bf16[32,256]{1,0:T(8,128)(2,1)S(1)} %get-tuple-element.40), channel_id=1, source_target_pairs={{0,5},{1,4},{2,7},{3,6},{4,1},{5,0},{6,3},{7,2},{8,13},{9,12},{10,... | collective-permute-start | bytes 49160 | tf_op jit(solution)/shard_map/ppermute | solution.py:336
  19.6 1.5 %collective-permute-done.3.refs_1_ = bf16[32,256]{1,0:T(8,128)(2,1)S(1)} collective-permute-done((bf16[32,256]{1,0:T(8,128)(2,1)S(1)}, bf16[32,256]{1,0:T(8,128)(2,1)S(1)}, u32[]{:S(2)}, u32[]{:S(2)}) %collective-permute-start.3) | collective-permute-done | bytes 16416 | tf_op jit(solution)/shard_map/ppermute | solution.py:336
  21.1 0.5 %collective-permute-done.4.refs_2_ = bf16[32,256]{1,0:T(8,128)(2,1)S(1)} collective-permute-done((bf16[32,256]{1,0:T(8,128)(2,1)S(1)}, bf16[32,256]{1,0:T(8,128)(2,1)S(1)}, u32[]{:S(2)}, u32[]{:S(2)}) %collective-permute-start.4) | collective-permute-done | bytes 16416 | tf_op jit(solution)/shard_map/ppermute | solution.py:336
  21.6 0.0 collective-permute-done.5.refs_3_
  21.6 1.1 %collective-permute-start.6 = (bf16[64,256]{1,0:T(8,128)(2,1)S(1)}, bf16[64,256]{1,0:T(8,128)(2,1)S(1)}, u32[]{:S(2)}, u32[]{:S(2)}) collective-permute-start(bf16[64,256]{1,0:T(8,128)(2,1)S(1)} %get-tuple-element.41.refs_1_), channel_id=1, source_target_pairs={{0,3},{1,2},{2,1},{3,0},{4,7},{5,6},{6,5},{7,4},{8,11},{9,10},{10,... | collective-permute-start | bytes 98312 | tf_op jit(solution)/shard_map/ppermute | solution.py:336
  22.7 0.7 %collective-permute-start.9 = (bf16[64,256]{1,0:T(8,128)(2,1)S(1)}, bf16[64,256]{1,0:T(8,128)(2,1)S(1)}, u32[]{:S(2)}, u32[]{:S(2)}) collective-permute-start(bf16[64,256]{1,0:T(8,128)(2,1)S(1)} %get-tuple-element.46.refs_5_), channel_id=1, source_target_pairs={{0,3},{1,2},{2,1},{3,0},{4,7},{5,6},{6,5},{7,4},{8,11},{9,10},{10,... | collective-permute-start | bytes 98312 | tf_op jit(solution)/shard_map/ppermute | solution.py:336
  23.4 0.0 collective-permute-start.7
  23.4 1.7 %collective-permute-done.6.refs_2_ = bf16[64,256]{1,0:T(8,128)(2,1)S(1)} collective-permute-done((bf16[64,256]{1,0:T(8,128)(2,1)S(1)}, bf16[64,256]{1,0:T(8,128)(2,1)S(1)}, u32[]{:S(2)}, u32[]{:S(2)}) %collective-permute-start.6) | collective-permute-done | bytes 32800 | tf_op jit(solution)/shard_map/ppermute | solution.py:336
  25.1 0.1 collective-permute-start.8
  25.3 0.4 %collective-permute-start.10 = (bf16[64,256]{1,0:T(8,128)(2,1)S(1)}, bf16[64,256]{1,0:T(8,128)(2,1)S(1)}, u32[]{:S(2)}, u32[]{:S(2)}) collective-permute-start(bf16[64,256]{1,0:T(8,128)(2,1)S(1)} %get-tuple-element.46.refs_5_), channel_id=1, source_target_pairs={{0,1},{1,0},{2,3},{3,2},{4,5},{5,4},{6,7},{7,6},{8,9},{9,8},{10,11... | collective-permute-start | bytes 98312 | tf_op jit(solution)/shard_map/ppermute | solution.py:336
  25.7 0.4 %collective-permute-done.9.refs_6_ = bf16[64,256]{1,0:T(8,128)(2,1)S(1)} collective-permute-done((bf16[64,256]{1,0:T(8,128)(2,1)S(1)}, bf16[64,256]{1,0:T(8,128)(2,1)S(1)}, u32[]{:S(2)}, u32[]{:S(2)}) %collective-permute-start.9) | collective-permute-done | bytes 32800 | tf_op jit(solution)/shard_map/ppermute | solution.py:336
  26.0 0.0 collective-permute-start.11
  26.0 0.0 collective-permute-done.7.refs_3_
  26.0 0.3 collective-permute-done.8.refs_4_
  26.4 0.7 %shard_map.69 = (bf16[16,256]{1,0:T(8,128)(2,1)S(1)}, bf16[16,256]{1,0:T(8,128)(2,1)S(1)}, bf16[16,256]{1,0:T(8,128)(2,1)S(1)}, bf16[16,256]{1,0:T(8,128)(2,1)S(1)}) custom-call(bf16[4,256,256]{2,1,0:T(8,128)(2,1)S(1)} %get-tuple-element.29.refs_0_.refs_6_, bf16[64,256]{1,0:T(8,128)(2,1)S(1)} %get-tuple-element.41.refs_1_, ...), custom_call_target="tpu_custom_call" | custom-call | flops 33554432 | bytes 655360 | tf_op jit(solution)/shard_map/pallas_call | solution.py:314
  27.0 0.0 collective-permute-done.10.refs_7_
  27.1 0.2 collective-permute-done.11.refs_8_
  27.2 0.7 %shard_map.70 = (bf16[32,256]{1,0:T(8,128)(2,1)S(1)}, bf16[32,256]{1,0:T(8,128)(2,1)S(1)}, bf16[32,256]{1,0:T(8,128)(2,1)S(1)}, bf16[32,256]{1,0:T(8,128)(2,1)S(1)}) custom-call(bf16[4,256,256]{2,1,0:T(8,128)(2,1)S(1)} %get-tuple-element.29.refs_0_.refs_6_, bf16[16,256]{1,0:T(8,128)(2,1)S(1)} %get-tuple-element.42.refs_1_, ...), custom_call_target="tpu_custom_call" | custom-call | flops 33554432 | bytes 688128 | tf_op jit(solution)/shard_map/pallas_call | solution.py:314
  27.9 1.8 %collective-permute-start.12 = (bf16[32,256]{1,0:T(8,128)(2,1)S(1)}, bf16[32,256]{1,0:T(8,128)(2,1)S(1)}, u32[]{:S(2)}, u32[]{:S(2)}) collective-permute-start(bf16[32,256]{1,0:T(8,128)(2,1)S(1)} %get-tuple-element.48), channel_id=1, source_target_pairs={{0,12},{1,13},{2,14},{3,15},{4,8},{5,9},{6,10},{7,11},{8,4},{9,5},... | collective-permute-start | bytes 49160 | tf_op jit(solution)/shard_map/ppermute | solution.py:336
  29.7 0.7 %collective-permute-start.13 = (bf16[32,256]{1,0:T(8,128)(2,1)S(1)}, bf16[32,256]{1,0:T(8,128)(2,1)S(1)}, u32[]{:S(2)}, u32[]{:S(2)}) collective-permute-start(bf16[32,256]{1,0:T(8,128)(2,1)S(1)} %get-tuple-element.49), channel_id=1, source_target_pairs={{0,9},{1,8},{2,11},{3,10},{4,13},{5,12},{6,15},{7,14},{8,1},{9,0},... | collective-permute-start | bytes 49160 | tf_op jit(solution)/shard_map/ppermute | solution.py:336
  30.5 1.6 %collective-permute-start.14 = (bf16[32,256]{1,0:T(8,128)(2,1)S(1)}, bf16[32,256]{1,0:T(8,128)(2,1)S(1)}, u32[]{:S(2)}, u32[]{:S(2)}) collective-permute-start(bf16[32,256]{1,0:T(8,128)(2,1)S(1)} %get-tuple-element.50), channel_id=1, source_target_pairs={{0,5},{1,4},{2,7},{3,6},{4,1},{5,0},{6,3},{7,2},{8,13},{9,12},{10,... | collective-permute-start | bytes 49160 | tf_op jit(solution)/shard_map/ppermute | solution.py:336
  32.1 1.4 %collective-permute-done.12.refs_1_ = bf16[32,256]{1,0:T(8,128)(2,1)S(1)} collective-permute-done((bf16[32,256]{1,0:T(8,128)(2,1)S(1)}, bf16[32,256]{1,0:T(8,128)(2,1)S(1)}, u32[]{:S(2)}, u32[]{:S(2)}) %collective-permute-start.12) | collective-permute-done | bytes 16416 | tf_op jit(solution)/shard_map/ppermute | solution.py:336
  33.6 0.7 %collective-permute-done.13.refs_2_ = bf16[32,256]{1,0:T(8,128)(2,1)S(1)} collective-permute-done((bf16[32,256]{1,0:T(8,128)(2,1)S(1)}, bf16[32,256]{1,0:T(8,128)(2,1)S(1)}, u32[]{:S(2)}, u32[]{:S(2)}) %collective-permute-start.13) | collective-permute-done | bytes 16416 | tf_op jit(solution)/shard_map/ppermute | solution.py:336
  34.3 0.0 collective-permute-done.14.refs_3_
  34.3 0.8 %shard_map.71 = bf16[8,16,256]{2,1,0:T(8,128)(2,1)} custom-call(bf16[32,256]{1,0:T(8,128)(2,1)S(1)} %get-tuple-element.47.refs_0_, bf16[32,256]{1,0:T(8,128)(2,1)S(1)} %collective-permute-done.12.refs_1_, bf16[32,256]{1,0:T(8,128)(2,1)S(1)} %collective-permute-done.13.refs_2_, bf16[32,256]{1,0:T(8,128)(2,1)S(1)} %collective-permute-done.14.refs_3_, ...), custom_call_target="tpu_custom_call" | custom-call | bytes 655360 | tf_op jit(solution)/shard_map/pallas_call | solution.py:314
  (1 shorter events, 0.0 us)
Async XLA Ops:
  0.0 5.5 %copy-start = (bf16[8,16,256]{2,1,0:T(8,128)(2,1)S(1)}, bf16[8,16,256]{2,1,0:T(8,128)(2,1)}, u32[]{:S(2)}) copy-start(bf16[8,16,256]{2,1,0:T(8,128)(2,1)} %refs_0_.7) | copy-start | bytes 196612
  0.0 5.5 %collective-permute-start = (bf16[8,16,256]{2,1,0:T(8,128)(2,1)}, bf16[8,16,256]{2,1,0:T(8,128)(2,1)S(1)}, u32[]{:S(2)}, u32[]{:S(2)}) collective-permute-start(bf16[8,16,256]{2,1,0:T(8,128)(2,1)} %refs_0_.7), channel_id=1, source_target_pairs={{16,0},{0,16},{17,1},{1,17},{18,2},{2,18},{19,3},{3,19},{20,4},{4,... | collective-permute-start | bytes 196616 | tf_op jit(solution)/shard_map/ppermute | solution.py:348
  2.9 0.7 %copy-start.1 = (bf16[7,7,256]{2,1,0:T(8,128)(2,1)S(1)}, bf16[7,7,256]{2,1,0:T(8,128)(2,1)}, u32[]{:S(2)}) copy-start(bf16[7,7,256]{2,1,0:T(8,128)(2,1)} %refs_4_.1) | copy-start | bytes 75268
  5.6 7.0 %collective-permute-start.1 = (bf16[64,256]{1,0:T(8,128)(2,1)S(1)}, bf16[64,256]{1,0:T(8,128)(2,1)S(1)}, u32[]{:S(2)}, u32[]{:S(2)}) collective-permute-start(bf16[64,256]{1,0:T(8,128)(2,1)S(1)} %get-tuple-element.31), channel_id=1, source_target_pairs={{0,15},{1,2},{2,1},{3,4},{4,3},{5,6},{6,5},{7,8},{8,7},{9,10},{10,... | collective-permute-start | bytes 98312 | tf_op jit(solution)/shard_map/ppermute | solution.py:370
  9.4 3.2 %collective-permute-start.2 = (bf16[64,256]{1,0:T(8,128)(2,1)S(1)}, bf16[64,256]{1,0:T(8,128)(2,1)S(1)}, u32[]{:S(2)}, u32[]{:S(2)}) collective-permute-start(bf16[64,256]{1,0:T(8,128)(2,1)S(1)} %get-tuple-element.32), channel_id=1, source_target_pairs={{0,1},{1,0},{2,3},{3,2},{4,5},{5,4},{6,7},{7,6},{8,9},{9,8},{10,11... | collective-permute-start | bytes 98312 | tf_op jit(solution)/shard_map/ppermute | solution.py:336
  15.4 5.7 %collective-permute-start.3 = (bf16[32,256]{1,0:T(8,128)(2,1)S(1)}, bf16[32,256]{1,0:T(8,128)(2,1)S(1)}, u32[]{:S(2)}, u32[]{:S(2)}) collective-permute-start(bf16[32,256]{1,0:T(8,128)(2,1)S(1)} %get-tuple-element.38), channel_id=1, source_target_pairs={{0,12},{1,13},{2,14},{3,15},{4,8},{5,9},{6,10},{7,11},{8,4},{9,5},... | collective-permute-start | bytes 49160 | tf_op jit(solution)/shard_map/ppermute | solution.py:336
  17.4 4.2 %collective-permute-start.4 = (bf16[32,256]{1,0:T(8,128)(2,1)S(1)}, bf16[32,256]{1,0:T(8,128)(2,1)S(1)}, u32[]{:S(2)}, u32[]{:S(2)}) collective-permute-start(bf16[32,256]{1,0:T(8,128)(2,1)S(1)} %get-tuple-element.39), channel_id=1, source_target_pairs={{0,9},{1,8},{2,11},{3,10},{4,13},{5,12},{6,15},{7,14},{8,1},{9,0},... | collective-permute-start | bytes 49160 | tf_op jit(solution)/shard_map/ppermute | solution.py:336
  17.4 4.2 %collective-permute-start.5 = (bf16[32,256]{1,0:T(8,128)(2,1)S(1)}, bf16[32,256]{1,0:T(8,128)(2,1)S(1)}, u32[]{:S(2)}, u32[]{:S(2)}) collective-permute-start(bf16[32,256]{1,0:T(8,128)(2,1)S(1)} %get-tuple-element.40), channel_id=1, source_target_pairs={{0,5},{1,4},{2,7},{3,6},{4,1},{5,0},{6,3},{7,2},{8,13},{9,12},{10,... | collective-permute-start | bytes 49160 | tf_op jit(solution)/shard_map/ppermute | solution.py:336
  21.6 3.6 %collective-permute-start.6 = (bf16[64,256]{1,0:T(8,128)(2,1)S(1)}, bf16[64,256]{1,0:T(8,128)(2,1)S(1)}, u32[]{:S(2)}, u32[]{:S(2)}) collective-permute-start(bf16[64,256]{1,0:T(8,128)(2,1)S(1)} %get-tuple-element.41.refs_1_), channel_id=1, source_target_pairs={{0,3},{1,2},{2,1},{3,0},{4,7},{5,6},{6,5},{7,4},{8,11},{9,10},{10,... | collective-permute-start | bytes 98312 | tf_op jit(solution)/shard_map/ppermute | solution.py:336
  22.7 3.4 %collective-permute-start.9 = (bf16[64,256]{1,0:T(8,128)(2,1)S(1)}, bf16[64,256]{1,0:T(8,128)(2,1)S(1)}, u32[]{:S(2)}, u32[]{:S(2)}) collective-permute-start(bf16[64,256]{1,0:T(8,128)(2,1)S(1)} %get-tuple-element.46.refs_5_), channel_id=1, source_target_pairs={{0,3},{1,2},{2,1},{3,0},{4,7},{5,6},{6,5},{7,4},{8,11},{9,10},{10,... | collective-permute-start | bytes 98312 | tf_op jit(solution)/shard_map/ppermute | solution.py:336
  23.4 2.7 %collective-permute-start.7 = (bf16[64,256]{1,0:T(8,128)(2,1)S(1)}, bf16[64,256]{1,0:T(8,128)(2,1)S(1)}, u32[]{:S(2)}, u32[]{:S(2)}) collective-permute-start(bf16[64,256]{1,0:T(8,128)(2,1)S(1)} %get-tuple-element.41.refs_1_), channel_id=1, source_target_pairs={{0,1},{1,0},{2,3},{3,2},{4,5},{5,4},{6,7},{7,6},{8,9},{9,8},{10,11... | collective-permute-start | bytes 98312 | tf_op jit(solution)/shard_map/ppermute | solution.py:336
  25.1 1.2 %collective-permute-start.8 = (bf16[64,256]{1,0:T(8,128)(2,1)S(1)}, bf16[64,256]{1,0:T(8,128)(2,1)S(1)}, u32[]{:S(2)}, u32[]{:S(2)}) collective-permute-start(bf16[64,256]{1,0:T(8,128)(2,1)S(1)} %collective-permute-done.6.refs_2_), channel_id=1, source_target_pairs={{0,1},{1,0},{2,3},{3,2},{4,5},{5,4},{6,7},{7,6},{8,9},{9,8},{10,11... | collective-permute-start | bytes 98312 | tf_op jit(solution)/shard_map/ppermute | solution.py:336
  25.3 1.8 %collective-permute-start.10 = (bf16[64,256]{1,0:T(8,128)(2,1)S(1)}, bf16[64,256]{1,0:T(8,128)(2,1)S(1)}, u32[]{:S(2)}, u32[]{:S(2)}) collective-permute-start(bf16[64,256]{1,0:T(8,128)(2,1)S(1)} %get-tuple-element.46.refs_5_), channel_id=1, source_target_pairs={{0,1},{1,0},{2,3},{3,2},{4,5},{5,4},{6,7},{7,6},{8,9},{9,8},{10,11... | collective-permute-start | bytes 98312 | tf_op jit(solution)/shard_map/ppermute | solution.py:336
  26.0 1.2 %collective-permute-start.11 = (bf16[64,256]{1,0:T(8,128)(2,1)S(1)}, bf16[64,256]{1,0:T(8,128)(2,1)S(1)}, u32[]{:S(2)}, u32[]{:S(2)}) collective-permute-start(bf16[64,256]{1,0:T(8,128)(2,1)S(1)} %collective-permute-done.9.refs_6_), channel_id=1, source_target_pairs={{0,1},{1,0},{2,3},{3,2},{4,5},{5,4},{6,7},{7,6},{8,9},{9,8},{10,11... | collective-permute-start | bytes 98312 | tf_op jit(solution)/shard_map/ppermute | solution.py:336
  27.9 5.6 %collective-permute-start.12 = (bf16[32,256]{1,0:T(8,128)(2,1)S(1)}, bf16[32,256]{1,0:T(8,128)(2,1)S(1)}, u32[]{:S(2)}, u32[]{:S(2)}) collective-permute-start(bf16[32,256]{1,0:T(8,128)(2,1)S(1)} %get-tuple-element.48), channel_id=1, source_target_pairs={{0,12},{1,13},{2,14},{3,15},{4,8},{5,9},{6,10},{7,11},{8,4},{9,5},... | collective-permute-start | bytes 49160 | tf_op jit(solution)/shard_map/ppermute | solution.py:336
  29.7 4.5 %collective-permute-start.13 = (bf16[32,256]{1,0:T(8,128)(2,1)S(1)}, bf16[32,256]{1,0:T(8,128)(2,1)S(1)}, u32[]{:S(2)}, u32[]{:S(2)}) collective-permute-start(bf16[32,256]{1,0:T(8,128)(2,1)S(1)} %get-tuple-element.49), channel_id=1, source_target_pairs={{0,9},{1,8},{2,11},{3,10},{4,13},{5,12},{6,15},{7,14},{8,1},{9,0},... | collective-permute-start | bytes 49160 | tf_op jit(solution)/shard_map/ppermute | solution.py:336
  30.5 3.8 %collective-permute-start.14 = (bf16[32,256]{1,0:T(8,128)(2,1)S(1)}, bf16[32,256]{1,0:T(8,128)(2,1)S(1)}, u32[]{:S(2)}, u32[]{:S(2)}) collective-permute-start(bf16[32,256]{1,0:T(8,128)(2,1)S(1)} %get-tuple-element.50), channel_id=1, source_target_pairs={{0,5},{1,4},{2,7},{3,6},{4,1},{5,0},{6,3},{7,2},{8,13},{9,12},{10,... | collective-permute-start | bytes 49160 | tf_op jit(solution)/shard_map/ppermute | solution.py:336

commit v15 on v14

--- a/solution.py
+++ b/solution.py
@@ -339,8 +339,7 @@
         moved = []
         for k in range(1, levels):
             level = levels - k
-            cross = (level ^ (level >> 1)) & 1 if column > 1 else 0
-            moved.append(swap(pieces[k], level * column + cross))
+            moved.append(swap(pieces[k], level * column + min(1, column - 1)))
         return [pieces[0]] + moved
 
     tiles = [field]

time: 35.3 us -> 35 us (level)
  waiting for transfers between devices: 6.78 us -> 5.47 us
  starting transfers between devices: 17.4 us -> 18.4 us
    ppermute x13, waiting for transfers between devices: 6.77 us -> 5.46 us  [swap(): return lax.ppermute(piece, 'lon', [(j, j ^ mask) for j in range(nlon)])]
    ppermute x13, starting transfers between devices: 10.7 us -> 11.7 us  [swap(): return lax.ppermute(piece, 'lon', [(j, j ^ mask) for j in range(nlon)])]
  transfers between devices with their start and end apart: 15 -> 15, of which waited for: 8 -> 7; matrix products, arithmetic and copies ran while one was open for 0% -> 0% of each run, Pallas kernels for 16% -> 16%
where the time goes in v15:
time: 35 us; the launch traced here: 34.8 us
  starting transfers between devices  18.4 us (53%)
  Pallas kernels  10 us (29%)
  waiting for transfers between devices  5.47 us (16%)
  local copies, waits for them, and re-layouts  0.75 us (2%)
    ppermute x13, starting transfers between devices, swap(): return lax.ppermute(piece, 'lon', [(j, j ^ mask) for j in range(nlon)])  11.7 us
    pallas_call x8, Pallas kernels, call(): pl.pallas_call(kernel, out_shape=shapes, in_specs=[given] * len(operands)...  10 us
    ppermute x13, waiting for transfers between devices, swap(): return lax.ppermute(piece, 'lon', [(j, j ^ mask) for j in range(nlon)])  5.46 us
    ppermute x1, starting transfers between devices, shards(): lax.ppermute(far, 'lon', [(j, (j - 1) % nlon if j % 2 == 0 else (j + 1) %...  3.78 us
    ppermute x1, starting transfers between devices, shards(): lax.ppermute(field, 'lat', [((i + s) % nlat, i) for i in range(nlat)])  2.94 us
    unnamed x4, local copies, waits for them, and re-layouts  0.75 us
  transfers between devices with their start and end apart: 15, of which 7 were waited for; matrix products, arithmetic and copies ran while one was open for 0% of the time, Pallas kernels for 16%

profile of v15, /device:TPU:0, one launch (start us, length us, event | category | flops | bytes accessed | tf_op | source)
XLA Modules:
  0.0 34.8 jit_solution(14301466589603887458)
XLA Ops:
  0.0 0.0 copy-start
  0.0 2.9 %collective-permute-start = (bf16[8,16,256]{2,1,0:T(8,128)(2,1)}, bf16[8,16,256]{2,1,0:T(8,128)(2,1)S(1)}, u32[]{:S(2)}, u32[]{:S(2)}) collective-permute-start(bf16[8,16,256]{2,1,0:T(8,128)(2,1)} %refs_0_.7), channel_id=1, source_target_pairs={{16,0},{0,16},{17,1},{1,17},{18,2},{2,18},{19,3},{3,19},{20,4},{4,... | collective-permute-start | bytes 196616 | tf_op jit(solution)/shard_map/ppermute | solution.py:347
  2.9 0.0 copy-start.1
  2.9 0.7 %copy-done.1 = bf16[7,7,256]{2,1,0:T(8,128)(2,1)S(1)} copy-done((bf16[7,7,256]{2,1,0:T(8,128)(2,1)S(1)}, bf16[7,7,256]{2,1,0:T(8,128)(2,1)}, u32[]{:S(2)}) %copy-start.1) | copy-done | bytes 25112
  3.7 1.8 %shard_map.64 = (bf16[256,1024]{1,0:T(8,128)(2,1)S(1)}, bf16[1024,256]{1,0:T(8,128)(2,1)S(1)}, bf16[4,256,256]{2,1,0:T(8,128)(2,1)S(1)}, bf16[4,256,256]{2,1,0:T(8,128)(2,1)S(1)}, f32[7,7,256]{2,1,0:T(8,128)S(1)}) custom-call(bf16[256,1024]{1,0:T(8,128)(2,1)} %refs_0_.4, bf16[1024,256]{1,0:T(8,128)(2,1)} %refs_1_.1, bf16[4,256,256]{2,1,0:T(8,128)(2,1)} %refs_2_.1, ...), custom_call_target="tpu_custom_call" | custom-call | bytes 2122240 | tf_op jit(solution)/shard_map/pallas_call | solution.py:314
  5.5 0.0 collective-permute-done.refs_1_
  5.5 0.0 copy-done
  5.5 0.1 shard_map.65
  5.6 3.8 %collective-permute-start.1 = (bf16[64,256]{1,0:T(8,128)(2,1)S(1)}, bf16[64,256]{1,0:T(8,128)(2,1)S(1)}, u32[]{:S(2)}, u32[]{:S(2)}) collective-permute-start(bf16[64,256]{1,0:T(8,128)(2,1)S(1)} %get-tuple-element.31), channel_id=1, source_target_pairs={{0,15},{1,2},{2,1},{3,4},{4,3},{5,6},{6,5},{7,8},{8,7},{9,10},{10,... | collective-permute-start | bytes 98312 | tf_op jit(solution)/shard_map/ppermute | solution.py:369
  9.4 0.0 collective-permute-start.2
  9.4 3.2 %shard_map.66 = (bf16[64,256]{1,0:T(8,128)(2,1)S(1)}, bf16[64,256]{1,0:T(8,128)(2,1)S(1)}) custom-call(bf16[8,16,256]{2,1,0:T(8,128)(2,1)S(1)} %copy-done, bf16[8,16,256]{2,1,0:T(8,128)(2,1)S(1)} %collective-permute-done.refs_1_, f32[7,7,256]{2,1,0:T(8,128)S(1)} %get-tuple-element.33.refs_2_.refs_5_, ...), custom_call_target="tpu_custom_call" | custom-call | flops 134217728 | bytes 1754112 | tf_op jit(solution)/shard_map/pallas_call | solution.py:314
  12.6 0.0 collective-permute-done.1.refs_2_
  12.6 0.0 collective-permute-done.2.refs_3_
  12.6 2.8 %shard_map.67 = (bf16[64,256]{1,0:T(8,128)(2,1)S(1)}, bf16[32,256]{1,0:T(8,128)(2,1)S(1)}, bf16[32,256]{1,0:T(8,128)(2,1)S(1)}, bf16[32,256]{1,0:T(8,128)(2,1)S(1)}, bf16[32,256]{1,0:T(8,128)(2,1)S(1)}) custom-call(bf16[8,16,256]{2,1,0:T(8,128)(2,1)S(1)} %copy-done, bf16[8,16,256]{2,1,0:T(8,128)(2,1)S(1)} %collective-permute-done.refs_1_, ...), custom_call_target="tpu_custom_call" | custom-call | flops 134217728 | bytes 1852416 | tf_op jit(solution)/shard_map/pallas_call | solution.py:314
  15.4 1.6 %collective-permute-start.3 = (bf16[32,256]{1,0:T(8,128)(2,1)S(1)}, bf16[32,256]{1,0:T(8,128)(2,1)S(1)}, u32[]{:S(2)}, u32[]{:S(2)}) collective-permute-start(bf16[32,256]{1,0:T(8,128)(2,1)S(1)} %get-tuple-element.38), channel_id=1, source_target_pairs={{0,13},{1,12},{2,15},{3,14},{4,9},{5,8},{6,11},{7,10},{8,5},{9,4},... | collective-permute-start | bytes 49160 | tf_op jit(solution)/shard_map/ppermute | solution.py:336
  17.0 0.0 collective-permute-start.4
  17.0 2.7 %collective-permute-start.5 = (bf16[32,256]{1,0:T(8,128)(2,1)S(1)}, bf16[32,256]{1,0:T(8,128)(2,1)S(1)}, u32[]{:S(2)}, u32[]{:S(2)}) collective-permute-start(bf16[32,256]{1,0:T(8,128)(2,1)S(1)} %get-tuple-element.40), channel_id=1, source_target_pairs={{0,5},{1,4},{2,7},{3,6},{4,1},{5,0},{6,3},{7,2},{8,13},{9,12},{10,... | collective-permute-start | bytes 49160 | tf_op jit(solution)/shard_map/ppermute | solution.py:336
  19.7 0.7 %collective-permute-done.3.refs_1_ = bf16[32,256]{1,0:T(8,128)(2,1)S(1)} collective-permute-done((bf16[32,256]{1,0:T(8,128)(2,1)S(1)}, bf16[32,256]{1,0:T(8,128)(2,1)S(1)}, u32[]{:S(2)}, u32[]{:S(2)}) %collective-permute-start.3) | collective-permute-done | bytes 16416 | tf_op jit(solution)/shard_map/ppermute | solution.py:336
  20.4 1.0 %collective-permute-done.4.refs_2_ = bf16[32,256]{1,0:T(8,128)(2,1)S(1)} collective-permute-done((bf16[32,256]{1,0:T(8,128)(2,1)S(1)}, bf16[32,256]{1,0:T(8,128)(2,1)S(1)}, u32[]{:S(2)}, u32[]{:S(2)}) %collective-permute-start.4) | collective-permute-done | bytes 16416 | tf_op jit(solution)/shard_map/ppermute | solution.py:336
  21.4 0.2 collective-permute-done.5.refs_3_
  21.6 0.0 collective-permute-start.6
  21.6 1.8 %collective-permute-start.9 = (bf16[64,256]{1,0:T(8,128)(2,1)S(1)}, bf16[64,256]{1,0:T(8,128)(2,1)S(1)}, u32[]{:S(2)}, u32[]{:S(2)}) collective-permute-start(bf16[64,256]{1,0:T(8,128)(2,1)S(1)} %get-tuple-element.46.refs_5_), channel_id=1, source_target_pairs={{0,3},{1,2},{2,1},{3,0},{4,7},{5,6},{6,5},{7,4},{8,11},{9,10},{10,... | collective-permute-start | bytes 98312 | tf_op jit(solution)/shard_map/ppermute | solution.py:336
  23.4 0.1 collective-permute-start.7
  23.4 1.5 %collective-permute-done.6.refs_2_ = bf16[64,256]{1,0:T(8,128)(2,1)S(1)} collective-permute-done((bf16[64,256]{1,0:T(8,128)(2,1)S(1)}, bf16[64,256]{1,0:T(8,128)(2,1)S(1)}, u32[]{:S(2)}, u32[]{:S(2)}) %collective-permute-start.6) | collective-permute-done | bytes 32800 | tf_op jit(solution)/shard_map/ppermute | solution.py:336
  25.0 0.7 %collective-permute-start.8 = (bf16[64,256]{1,0:T(8,128)(2,1)S(1)}, bf16[64,256]{1,0:T(8,128)(2,1)S(1)}, u32[]{:S(2)}, u32[]{:S(2)}) collective-permute-start(bf16[64,256]{1,0:T(8,128)(2,1)S(1)} %collective-permute-done.6.refs_2_), channel_id=1, source_target_pairs={{0,1},{1,0},{2,3},{3,2},{4,5},{5,4},{6,7},{7,6},{8,9},{9,8},{10,11... | collective-permute-start | bytes 98312 | tf_op jit(solution)/shard_map/ppermute | solution.py:336
  25.7 0.0 collective-permute-start.10
  25.7 0.0 collective-permute-done.9.refs_6_
  25.7 0.7 %collective-permute-start.11 = (bf16[64,256]{1,0:T(8,128)(2,1)S(1)}, bf16[64,256]{1,0:T(8,128)(2,1)S(1)}, u32[]{:S(2)}, u32[]{:S(2)}) collective-permute-start(bf16[64,256]{1,0:T(8,128)(2,1)S(1)} %collective-permute-done.9.refs_6_), channel_id=1, source_target_pairs={{0,1},{1,0},{2,3},{3,2},{4,5},{5,4},{6,7},{7,6},{8,9},{9,8},{10,11... | collective-permute-start | bytes 98312 | tf_op jit(solution)/shard_map/ppermute | solution.py:336
  26.4 0.0 collective-permute-done.7.refs_3_
  26.4 0.1 collective-permute-done.8.refs_4_
  26.5 0.7 %shard_map.69 = (bf16[16,256]{1,0:T(8,128)(2,1)S(1)}, bf16[16,256]{1,0:T(8,128)(2,1)S(1)}, bf16[16,256]{1,0:T(8,128)(2,1)S(1)}, bf16[16,256]{1,0:T(8,128)(2,1)S(1)}) custom-call(bf16[4,256,256]{2,1,0:T(8,128)(2,1)S(1)} %get-tuple-element.29.refs_0_.refs_6_, bf16[64,256]{1,0:T(8,128)(2,1)S(1)} %get-tuple-element.41.refs_1_, ...), custom_call_target="tpu_custom_call" | custom-call | flops 33554432 | bytes 655360 | tf_op jit(solution)/shard_map/pallas_call | solution.py:314
  27.2 0.0 collective-permute-done.10.refs_7_
  27.2 0.0 collective-permute-done.11.refs_8_
  27.3 0.7 %shard_map.70 = (bf16[32,256]{1,0:T(8,128)(2,1)S(1)}, bf16[32,256]{1,0:T(8,128)(2,1)S(1)}, bf16[32,256]{1,0:T(8,128)(2,1)S(1)}, bf16[32,256]{1,0:T(8,128)(2,1)S(1)}) custom-call(bf16[4,256,256]{2,1,0:T(8,128)(2,1)S(1)} %get-tuple-element.29.refs_0_.refs_6_, bf16[16,256]{1,0:T(8,128)(2,1)S(1)} %get-tuple-element.42.refs_1_, ...), custom_call_target="tpu_custom_call" | custom-call | flops 33554432 | bytes 688128 | tf_op jit(solution)/shard_map/pallas_call | solution.py:314
  28.0 1.9 %collective-permute-start.12 = (bf16[32,256]{1,0:T(8,128)(2,1)S(1)}, bf16[32,256]{1,0:T(8,128)(2,1)S(1)}, u32[]{:S(2)}, u32[]{:S(2)}) collective-permute-start(bf16[32,256]{1,0:T(8,128)(2,1)S(1)} %get-tuple-element.48), channel_id=1, source_target_pairs={{0,13},{1,12},{2,15},{3,14},{4,9},{5,8},{6,11},{7,10},{8,5},{9,4},... | collective-permute-start | bytes 49160 | tf_op jit(solution)/shard_map/ppermute | solution.py:336
  29.9 0.2 collective-permute-start.13
  30.1 2.0 %collective-permute-start.14 = (bf16[32,256]{1,0:T(8,128)(2,1)S(1)}, bf16[32,256]{1,0:T(8,128)(2,1)S(1)}, u32[]{:S(2)}, u32[]{:S(2)}) collective-permute-start(bf16[32,256]{1,0:T(8,128)(2,1)S(1)} %get-tuple-element.50), channel_id=1, source_target_pairs={{0,5},{1,4},{2,7},{3,6},{4,1},{5,0},{6,3},{7,2},{8,13},{9,12},{10,... | collective-permute-start | bytes 49160 | tf_op jit(solution)/shard_map/ppermute | solution.py:336
  32.1 0.9 %collective-permute-done.12.refs_1_ = bf16[32,256]{1,0:T(8,128)(2,1)S(1)} collective-permute-done((bf16[32,256]{1,0:T(8,128)(2,1)S(1)}, bf16[32,256]{1,0:T(8,128)(2,1)S(1)}, u32[]{:S(2)}, u32[]{:S(2)}) %collective-permute-start.12) | collective-permute-done | bytes 16416 | tf_op jit(solution)/shard_map/ppermute | solution.py:336
  33.0 1.0 %collective-permute-done.13.refs_2_ = bf16[32,256]{1,0:T(8,128)(2,1)S(1)} collective-permute-done((bf16[32,256]{1,0:T(8,128)(2,1)S(1)}, bf16[32,256]{1,0:T(8,128)(2,1)S(1)}, u32[]{:S(2)}, u32[]{:S(2)}) %collective-permute-start.13) | collective-permute-done | bytes 16416 | tf_op jit(solution)/shard_map/ppermute | solution.py:336
  34.0 0.0 collective-permute-done.14.refs_3_
  34.0 0.8 %shard_map.71 = bf16[8,16,256]{2,1,0:T(8,128)(2,1)} custom-call(bf16[32,256]{1,0:T(8,128)(2,1)S(1)} %get-tuple-element.47.refs_0_, bf16[32,256]{1,0:T(8,128)(2,1)S(1)} %collective-permute-done.12.refs_1_, bf16[32,256]{1,0:T(8,128)(2,1)S(1)} %collective-permute-done.13.refs_2_, bf16[32,256]{1,0:T(8,128)(2,1)S(1)} %collective-permute-done.14.refs_3_, ...), custom_call_target="tpu_custom_call" | custom-call | bytes 655360 | tf_op jit(solution)/shard_map/pallas_call | solution.py:314
  (1 shorter events, 0.0 us)
Async XLA Ops:
  0.0 5.5 %copy-start = (bf16[8,16,256]{2,1,0:T(8,128)(2,1)S(1)}, bf16[8,16,256]{2,1,0:T(8,128)(2,1)}, u32[]{:S(2)}) copy-start(bf16[8,16,256]{2,1,0:T(8,128)(2,1)} %refs_0_.7) | copy-start | bytes 196612
  0.0 5.5 %collective-permute-start = (bf16[8,16,256]{2,1,0:T(8,128)(2,1)}, bf16[8,16,256]{2,1,0:T(8,128)(2,1)S(1)}, u32[]{:S(2)}, u32[]{:S(2)}) collective-permute-start(bf16[8,16,256]{2,1,0:T(8,128)(2,1)} %refs_0_.7), channel_id=1, source_target_pairs={{16,0},{0,16},{17,1},{1,17},{18,2},{2,18},{19,3},{3,19},{20,4},{4,... | collective-permute-start | bytes 196616 | tf_op jit(solution)/shard_map/ppermute | solution.py:347
  2.9 0.7 %copy-start.1 = (bf16[7,7,256]{2,1,0:T(8,128)(2,1)S(1)}, bf16[7,7,256]{2,1,0:T(8,128)(2,1)}, u32[]{:S(2)}) copy-start(bf16[7,7,256]{2,1,0:T(8,128)(2,1)} %refs_4_.1) | copy-start | bytes 75268
  5.6 7.0 %collective-permute-start.1 = (bf16[64,256]{1,0:T(8,128)(2,1)S(1)}, bf16[64,256]{1,0:T(8,128)(2,1)S(1)}, u32[]{:S(2)}, u32[]{:S(2)}) collective-permute-start(bf16[64,256]{1,0:T(8,128)(2,1)S(1)} %get-tuple-element.31), channel_id=1, source_target_pairs={{0,15},{1,2},{2,1},{3,4},{4,3},{5,6},{6,5},{7,8},{8,7},{9,10},{10,... | collective-permute-start | bytes 98312 | tf_op jit(solution)/shard_map/ppermute | solution.py:369
  9.4 3.2 %collective-permute-start.2 = (bf16[64,256]{1,0:T(8,128)(2,1)S(1)}, bf16[64,256]{1,0:T(8,128)(2,1)S(1)}, u32[]{:S(2)}, u32[]{:S(2)}) collective-permute-start(bf16[64,256]{1,0:T(8,128)(2,1)S(1)} %get-tuple-element.32), channel_id=1, source_target_pairs={{0,1},{1,0},{2,3},{3,2},{4,5},{5,4},{6,7},{7,6},{8,9},{9,8},{10,11... | collective-permute-start | bytes 98312 | tf_op jit(solution)/shard_map/ppermute | solution.py:336
  15.4 5.0 %collective-permute-start.3 = (bf16[32,256]{1,0:T(8,128)(2,1)S(1)}, bf16[32,256]{1,0:T(8,128)(2,1)S(1)}, u32[]{:S(2)}, u32[]{:S(2)}) collective-permute-start(bf16[32,256]{1,0:T(8,128)(2,1)S(1)} %get-tuple-element.38), channel_id=1, source_target_pairs={{0,13},{1,12},{2,15},{3,14},{4,9},{5,8},{6,11},{7,10},{8,5},{9,4},... | collective-permute-start | bytes 49160 | tf_op jit(solution)/shard_map/ppermute | solution.py:336
  17.0 4.4 %collective-permute-start.4 = (bf16[32,256]{1,0:T(8,128)(2,1)S(1)}, bf16[32,256]{1,0:T(8,128)(2,1)S(1)}, u32[]{:S(2)}, u32[]{:S(2)}) collective-permute-start(bf16[32,256]{1,0:T(8,128)(2,1)S(1)} %get-tuple-element.39), channel_id=1, source_target_pairs={{0,9},{1,8},{2,11},{3,10},{4,13},{5,12},{6,15},{7,14},{8,1},{9,0},... | collective-permute-start | bytes 49160 | tf_op jit(solution)/shard_map/ppermute | solution.py:336
  17.0 4.6 %collective-permute-start.5 = (bf16[32,256]{1,0:T(8,128)(2,1)S(1)}, bf16[32,256]{1,0:T(8,128)(2,1)S(1)}, u32[]{:S(2)}, u32[]{:S(2)}) collective-permute-start(bf16[32,256]{1,0:T(8,128)(2,1)S(1)} %get-tuple-element.40), channel_id=1, source_target_pairs={{0,5},{1,4},{2,7},{3,6},{4,1},{5,0},{6,3},{7,2},{8,13},{9,12},{10,... | collective-permute-start | bytes 49160 | tf_op jit(solution)/shard_map/ppermute | solution.py:336
  21.6 3.4 %collective-permute-start.6 = (bf16[64,256]{1,0:T(8,128)(2,1)S(1)}, bf16[64,256]{1,0:T(8,128)(2,1)S(1)}, u32[]{:S(2)}, u32[]{:S(2)}) collective-permute-start(bf16[64,256]{1,0:T(8,128)(2,1)S(1)} %get-tuple-element.41.refs_1_), channel_id=1, source_target_pairs={{0,3},{1,2},{2,1},{3,0},{4,7},{5,6},{6,5},{7,4},{8,11},{9,10},{10,... | collective-permute-start | bytes 98312 | tf_op jit(solution)/shard_map/ppermute | solution.py:336
  21.6 4.1 %collective-permute-start.9 = (bf16[64,256]{1,0:T(8,128)(2,1)S(1)}, bf16[64,256]{1,0:T(8,128)(2,1)S(1)}, u32[]{:S(2)}, u32[]{:S(2)}) collective-permute-start(bf16[64,256]{1,0:T(8,128)(2,1)S(1)} %get-tuple-element.46.refs_5_), channel_id=1, source_target_pairs={{0,3},{1,2},{2,1},{3,0},{4,7},{5,6},{6,5},{7,4},{8,11},{9,10},{10,... | collective-permute-start | bytes 98312 | tf_op jit(solution)/shard_map/ppermute | solution.py:336
  23.4 3.1 %collective-permute-start.7 = (bf16[64,256]{1,0:T(8,128)(2,1)S(1)}, bf16[64,256]{1,0:T(8,128)(2,1)S(1)}, u32[]{:S(2)}, u32[]{:S(2)}) collective-permute-start(bf16[64,256]{1,0:T(8,128)(2,1)S(1)} %get-tuple-element.41.refs_1_), channel_id=1, source_target_pairs={{0,1},{1,0},{2,3},{3,2},{4,5},{5,4},{6,7},{7,6},{8,9},{9,8},{10,11... | collective-permute-start | bytes 98312 | tf_op jit(solution)/shard_map/ppermute | solution.py:336
  25.0 1.6 %collective-permute-start.8 = (bf16[64,256]{1,0:T(8,128)(2,1)S(1)}, bf16[64,256]{1,0:T(8,128)(2,1)S(1)}, u32[]{:S(2)}, u32[]{:S(2)}) collective-permute-start(bf16[64,256]{1,0:T(8,128)(2,1)S(1)} %collective-permute-done.6.refs_2_), channel_id=1, source_target_pairs={{0,1},{1,0},{2,3},{3,2},{4,5},{5,4},{6,7},{7,6},{8,9},{9,8},{10,11... | collective-permute-start | bytes 98312 | tf_op jit(solution)/shard_map/ppermute | solution.py:336
  25.7 1.6 %collective-permute-start.10 = (bf16[64,256]{1,0:T(8,128)(2,1)S(1)}, bf16[64,256]{1,0:T(8,128)(2,1)S(1)}, u32[]{:S(2)}, u32[]{:S(2)}) collective-permute-start(bf16[64,256]{1,0:T(8,128)(2,1)S(1)} %get-tuple-element.46.refs_5_), channel_id=1, source_target_pairs={{0,1},{1,0},{2,3},{3,2},{4,5},{5,4},{6,7},{7,6},{8,9},{9,8},{10,11... | collective-permute-start | bytes 98312 | tf_op jit(solution)/shard_map/ppermute | solution.py:336
  25.7 1.6 %collective-permute-start.11 = (bf16[64,256]{1,0:T(8,128)(2,1)S(1)}, bf16[64,256]{1,0:T(8,128)(2,1)S(1)}, u32[]{:S(2)}, u32[]{:S(2)}) collective-permute-start(bf16[64,256]{1,0:T(8,128)(2,1)S(1)} %collective-permute-done.9.refs_6_), channel_id=1, source_target_pairs={{0,1},{1,0},{2,3},{3,2},{4,5},{5,4},{6,7},{7,6},{8,9},{9,8},{10,11... | collective-permute-start | bytes 98312 | tf_op jit(solution)/shard_map/ppermute | solution.py:336
  28.0 5.0 %collective-permute-start.12 = (bf16[32,256]{1,0:T(8,128)(2,1)S(1)}, bf16[32,256]{1,0:T(8,128)(2,1)S(1)}, u32[]{:S(2)}, u32[]{:S(2)}) collective-permute-start(bf16[32,256]{1,0:T(8,128)(2,1)S(1)} %get-tuple-element.48), channel_id=1, source_target_pairs={{0,13},{1,12},{2,15},{3,14},{4,9},{5,8},{6,11},{7,10},{8,5},{9,4},... | collective-permute-start | bytes 49160 | tf_op jit(solution)/shard_map/ppermute | solution.py:336
  29.9 4.1 %collective-permute-start.13 = (bf16[32,256]{1,0:T(8,128)(2,1)S(1)}, bf16[32,256]{1,0:T(8,128)(2,1)S(1)}, u32[]{:S(2)}, u32[]{:S(2)}) collective-permute-start(bf16[32,256]{1,0:T(8,128)(2,1)S(1)} %get-tuple-element.49), channel_id=1, source_target_pairs={{0,9},{1,8},{2,11},{3,10},{4,13},{5,12},{6,15},{7,14},{8,1},{9,0},... | collective-permute-start | bytes 49160 | tf_op jit(solution)/shard_map/ppermute | solution.py:336
  30.1 3.9 %collective-permute-start.14 = (bf16[32,256]{1,0:T(8,128)(2,1)S(1)}, bf16[32,256]{1,0:T(8,128)(2,1)S(1)}, u32[]{:S(2)}, u32[]{:S(2)}) collective-permute-start(bf16[32,256]{1,0:T(8,128)(2,1)S(1)} %get-tuple-element.50), channel_id=1, source_target_pairs={{0,5},{1,4},{2,7},{3,6},{4,1},{5,0},{6,3},{7,2},{8,13},{9,12},{10,... | collective-permute-start | bytes 49160 | tf_op jit(solution)/shard_map/ppermute | solution.py:336

commit v16 on v15

--- a/solution.py
+++ b/solution.py
@@ -38,7 +38,7 @@
 
 def gelu(values):
     size = jnp.abs(values)
-    t = 1.0 / (1.0 + (0.3275911 * 0.5**0.5) * size)
+    t = pl.reciprocal(1.0 + (0.3275911 * 0.5**0.5) * size, approx=True)
     tail = 1.061405429 * t - 1.453152027
     for coefficient in (1.421413741, -0.284496736, 0.254829592):
         tail = tail * t + coefficient
@@ -60,7 +60,7 @@
     top = jnp.max(scores, axis=-1, keepdims=True)
     probs = jnp.exp(scores - top)
     totals = jnp.sum(probs, axis=-1, keepdims=True)
-    mixed = dot(probs.astype(bf16), values) * (1.0 / totals)
+    mixed = dot(probs.astype(bf16), values) * pl.reciprocal(totals, approx=True)
     out = mixed[:count]
     for h in range(1, HEADS):
         out = jnp.where(picks[h], mixed[h * count : (h + 1) * count], out)

time: 35 us -> 35 us (level)
  no operation moved by 1% of the time
where the time goes in v16:
time: 35 us; the launch traced here: 34.8 us
  starting transfers between devices  18.4 us (53%)
  Pallas kernels  10 us (29%)
  waiting for transfers between devices  5.47 us (16%)
  local copies, waits for them, and re-layouts  0.75 us (2%)
    ppermute x13, starting transfers between devices, swap(): return lax.ppermute(piece, 'lon', [(j, j ^ mask) for j in range(nlon)])  11.7 us
    pallas_call x8, Pallas kernels, call(): pl.pallas_call(kernel, out_shape=shapes, in_specs=[given] * len(operands)...  10 us
    ppermute x13, waiting for transfers between devices, swap(): return lax.ppermute(piece, 'lon', [(j, j ^ mask) for j in range(nlon)])  5.46 us
    ppermute x1, starting transfers between devices, shards(): lax.ppermute(far, 'lon', [(j, (j - 1) % nlon if j % 2 == 0 else (j + 1) %...  3.78 us
    ppermute x1, starting transfers between devices, shards(): lax.ppermute(field, 'lat', [((i + s) % nlat, i) for i in range(nlat)])  2.94 us
    unnamed x4, local copies, waits for them, and re-layouts  0.75 us
  transfers between devices with their start and end apart: 15, of which 7 were waited for; matrix products, arithmetic and copies ran while one was open for 0% of the time, Pallas kernels for 16%

profile of v16, /device:TPU:0, one launch (start us, length us, event | category | flops | bytes accessed | tf_op | source)
XLA Modules:
  0.0 34.8 jit_solution(14301466589603887458)
XLA Ops:
  0.0 0.0 copy-start
  0.0 2.9 %collective-permute-start = (bf16[8,16,256]{2,1,0:T(8,128)(2,1)}, bf16[8,16,256]{2,1,0:T(8,128)(2,1)S(1)}, u32[]{:S(2)}, u32[]{:S(2)}) collective-permute-start(bf16[8,16,256]{2,1,0:T(8,128)(2,1)} %refs_0_.7), channel_id=1, source_target_pairs={{16,0},{0,16},{17,1},{1,17},{18,2},{2,18},{19,3},{3,19},{20,4},{4,... | collective-permute-start | bytes 196616 | tf_op jit(solution)/shard_map/ppermute | solution.py:347
  2.9 0.0 copy-start.1
  2.9 0.7 %copy-done.1 = bf16[7,7,256]{2,1,0:T(8,128)(2,1)S(1)} copy-done((bf16[7,7,256]{2,1,0:T(8,128)(2,1)S(1)}, bf16[7,7,256]{2,1,0:T(8,128)(2,1)}, u32[]{:S(2)}) %copy-start.1) | copy-done | bytes 25112
  3.7 1.8 %shard_map.64 = (bf16[256,1024]{1,0:T(8,128)(2,1)S(1)}, bf16[1024,256]{1,0:T(8,128)(2,1)S(1)}, bf16[4,256,256]{2,1,0:T(8,128)(2,1)S(1)}, bf16[4,256,256]{2,1,0:T(8,128)(2,1)S(1)}, f32[7,7,256]{2,1,0:T(8,128)S(1)}) custom-call(bf16[256,1024]{1,0:T(8,128)(2,1)} %refs_0_.4, bf16[1024,256]{1,0:T(8,128)(2,1)} %refs_1_.1, bf16[4,256,256]{2,1,0:T(8,128)(2,1)} %refs_2_.1, ...), custom_call_target="tpu_custom_call" | custom-call | bytes 2122240 | tf_op jit(solution)/shard_map/pallas_call | solution.py:314
  5.5 0.0 collective-permute-done.refs_1_
  5.5 0.0 copy-done
  5.5 0.1 shard_map.65
  5.6 3.8 %collective-permute-start.1 = (bf16[64,256]{1,0:T(8,128)(2,1)S(1)}, bf16[64,256]{1,0:T(8,128)(2,1)S(1)}, u32[]{:S(2)}, u32[]{:S(2)}) collective-permute-start(bf16[64,256]{1,0:T(8,128)(2,1)S(1)} %get-tuple-element.31), channel_id=1, source_target_pairs={{0,15},{1,2},{2,1},{3,4},{4,3},{5,6},{6,5},{7,8},{8,7},{9,10},{10,... | collective-permute-start | bytes 98312 | tf_op jit(solution)/shard_map/ppermute | solution.py:369
  9.4 0.0 collective-permute-start.2
  9.4 3.2 %shard_map.66 = (bf16[64,256]{1,0:T(8,128)(2,1)S(1)}, bf16[64,256]{1,0:T(8,128)(2,1)S(1)}) custom-call(bf16[8,16,256]{2,1,0:T(8,128)(2,1)S(1)} %copy-done, bf16[8,16,256]{2,1,0:T(8,128)(2,1)S(1)} %collective-permute-done.refs_1_, f32[7,7,256]{2,1,0:T(8,128)S(1)} %get-tuple-element.33.refs_2_.refs_5_, ...), custom_call_target="tpu_custom_call" | custom-call | flops 134217728 | bytes 1754112 | tf_op jit(solution)/shard_map/pallas_call | solution.py:314
  12.6 0.0 collective-permute-done.1.refs_2_
  12.6 0.0 collective-permute-done.2.refs_3_
  12.6 2.8 %shard_map.67 = (bf16[64,256]{1,0:T(8,128)(2,1)S(1)}, bf16[32,256]{1,0:T(8,128)(2,1)S(1)}, bf16[32,256]{1,0:T(8,128)(2,1)S(1)}, bf16[32,256]{1,0:T(8,128)(2,1)S(1)}, bf16[32,256]{1,0:T(8,128)(2,1)S(1)}) custom-call(bf16[8,16,256]{2,1,0:T(8,128)(2,1)S(1)} %copy-done, bf16[8,16,256]{2,1,0:T(8,128)(2,1)S(1)} %collective-permute-done.refs_1_, ...), custom_call_target="tpu_custom_call" | custom-call | flops 134217728 | bytes 1852416 | tf_op jit(solution)/shard_map/pallas_call | solution.py:314
  15.4 1.6 %collective-permute-start.3 = (bf16[32,256]{1,0:T(8,128)(2,1)S(1)}, bf16[32,256]{1,0:T(8,128)(2,1)S(1)}, u32[]{:S(2)}, u32[]{:S(2)}) collective-permute-start(bf16[32,256]{1,0:T(8,128)(2,1)S(1)} %get-tuple-element.38), channel_id=1, source_target_pairs={{0,13},{1,12},{2,15},{3,14},{4,9},{5,8},{6,11},{7,10},{8,5},{9,4},... | collective-permute-start | bytes 49160 | tf_op jit(solution)/shard_map/ppermute | solution.py:336
  17.0 0.0 collective-permute-start.4
  17.0 2.7 %collective-permute-start.5 = (bf16[32,256]{1,0:T(8,128)(2,1)S(1)}, bf16[32,256]{1,0:T(8,128)(2,1)S(1)}, u32[]{:S(2)}, u32[]{:S(2)}) collective-permute-start(bf16[32,256]{1,0:T(8,128)(2,1)S(1)} %get-tuple-element.40), channel_id=1, source_target_pairs={{0,5},{1,4},{2,7},{3,6},{4,1},{5,0},{6,3},{7,2},{8,13},{9,12},{10,... | collective-permute-start | bytes 49160 | tf_op jit(solution)/shard_map/ppermute | solution.py:336
  19.7 0.7 %collective-permute-done.3.refs_1_ = bf16[32,256]{1,0:T(8,128)(2,1)S(1)} collective-permute-done((bf16[32,256]{1,0:T(8,128)(2,1)S(1)}, bf16[32,256]{1,0:T(8,128)(2,1)S(1)}, u32[]{:S(2)}, u32[]{:S(2)}) %collective-permute-start.3) | collective-permute-done | bytes 16416 | tf_op jit(solution)/shard_map/ppermute | solution.py:336
  20.4 1.0 %collective-permute-done.4.refs_2_ = bf16[32,256]{1,0:T(8,128)(2,1)S(1)} collective-permute-done((bf16[32,256]{1,0:T(8,128)(2,1)S(1)}, bf16[32,256]{1,0:T(8,128)(2,1)S(1)}, u32[]{:S(2)}, u32[]{:S(2)}) %collective-permute-start.4) | collective-permute-done | bytes 16416 | tf_op jit(solution)/shard_map/ppermute | solution.py:336
  21.4 0.2 collective-permute-done.5.refs_3_
  21.6 0.0 collective-permute-start.6
  21.6 1.8 %collective-permute-start.9 = (bf16[64,256]{1,0:T(8,128)(2,1)S(1)}, bf16[64,256]{1,0:T(8,128)(2,1)S(1)}, u32[]{:S(2)}, u32[]{:S(2)}) collective-permute-start(bf16[64,256]{1,0:T(8,128)(2,1)S(1)} %get-tuple-element.46.refs_5_), channel_id=1, source_target_pairs={{0,3},{1,2},{2,1},{3,0},{4,7},{5,6},{6,5},{7,4},{8,11},{9,10},{10,... | collective-permute-start | bytes 98312 | tf_op jit(solution)/shard_map/ppermute | solution.py:336
  23.4 0.1 collective-permute-start.7
  23.4 1.5 %collective-permute-done.6.refs_2_ = bf16[64,256]{1,0:T(8,128)(2,1)S(1)} collective-permute-done((bf16[64,256]{1,0:T(8,128)(2,1)S(1)}, bf16[64,256]{1,0:T(8,128)(2,1)S(1)}, u32[]{:S(2)}, u32[]{:S(2)}) %collective-permute-start.6) | collective-permute-done | bytes 32800 | tf_op jit(solution)/shard_map/ppermute | solution.py:336
  25.0 0.7 %collective-permute-start.8 = (bf16[64,256]{1,0:T(8,128)(2,1)S(1)}, bf16[64,256]{1,0:T(8,128)(2,1)S(1)}, u32[]{:S(2)}, u32[]{:S(2)}) collective-permute-start(bf16[64,256]{1,0:T(8,128)(2,1)S(1)} %collective-permute-done.6.refs_2_), channel_id=1, source_target_pairs={{0,1},{1,0},{2,3},{3,2},{4,5},{5,4},{6,7},{7,6},{8,9},{9,8},{10,11... | collective-permute-start | bytes 98312 | tf_op jit(solution)/shard_map/ppermute | solution.py:336
  25.7 0.0 collective-permute-start.10
  25.7 0.0 collective-permute-done.9.refs_6_
  25.7 0.7 %collective-permute-start.11 = (bf16[64,256]{1,0:T(8,128)(2,1)S(1)}, bf16[64,256]{1,0:T(8,128)(2,1)S(1)}, u32[]{:S(2)}, u32[]{:S(2)}) collective-permute-start(bf16[64,256]{1,0:T(8,128)(2,1)S(1)} %collective-permute-done.9.refs_6_), channel_id=1, source_target_pairs={{0,1},{1,0},{2,3},{3,2},{4,5},{5,4},{6,7},{7,6},{8,9},{9,8},{10,11... | collective-permute-start | bytes 98312 | tf_op jit(solution)/shard_map/ppermute | solution.py:336
  26.4 0.0 collective-permute-done.7.refs_3_
  26.4 0.1 collective-permute-done.8.refs_4_
  26.5 0.7 %shard_map.69 = (bf16[16,256]{1,0:T(8,128)(2,1)S(1)}, bf16[16,256]{1,0:T(8,128)(2,1)S(1)}, bf16[16,256]{1,0:T(8,128)(2,1)S(1)}, bf16[16,256]{1,0:T(8,128)(2,1)S(1)}) custom-call(bf16[4,256,256]{2,1,0:T(8,128)(2,1)S(1)} %get-tuple-element.29.refs_0_.refs_6_, bf16[64,256]{1,0:T(8,128)(2,1)S(1)} %get-tuple-element.41.refs_1_, ...), custom_call_target="tpu_custom_call" | custom-call | flops 33554432 | bytes 655360 | tf_op jit(solution)/shard_map/pallas_call | solution.py:314
  27.2 0.0 collective-permute-done.10.refs_7_
  27.2 0.0 collective-permute-done.11.refs_8_
  27.3 0.7 %shard_map.70 = (bf16[32,256]{1,0:T(8,128)(2,1)S(1)}, bf16[32,256]{1,0:T(8,128)(2,1)S(1)}, bf16[32,256]{1,0:T(8,128)(2,1)S(1)}, bf16[32,256]{1,0:T(8,128)(2,1)S(1)}) custom-call(bf16[4,256,256]{2,1,0:T(8,128)(2,1)S(1)} %get-tuple-element.29.refs_0_.refs_6_, bf16[16,256]{1,0:T(8,128)(2,1)S(1)} %get-tuple-element.42.refs_1_, ...), custom_call_target="tpu_custom_call" | custom-call | flops 33554432 | bytes 688128 | tf_op jit(solution)/shard_map/pallas_call | solution.py:314
  28.0 1.9 %collective-permute-start.12 = (bf16[32,256]{1,0:T(8,128)(2,1)S(1)}, bf16[32,256]{1,0:T(8,128)(2,1)S(1)}, u32[]{:S(2)}, u32[]{:S(2)}) collective-permute-start(bf16[32,256]{1,0:T(8,128)(2,1)S(1)} %get-tuple-element.48), channel_id=1, source_target_pairs={{0,13},{1,12},{2,15},{3,14},{4,9},{5,8},{6,11},{7,10},{8,5},{9,4},... | collective-permute-start | bytes 49160 | tf_op jit(solution)/shard_map/ppermute | solution.py:336
  29.9 0.2 collective-permute-start.13
  30.1 2.0 %collective-permute-start.14 = (bf16[32,256]{1,0:T(8,128)(2,1)S(1)}, bf16[32,256]{1,0:T(8,128)(2,1)S(1)}, u32[]{:S(2)}, u32[]{:S(2)}) collective-permute-start(bf16[32,256]{1,0:T(8,128)(2,1)S(1)} %get-tuple-element.50), channel_id=1, source_target_pairs={{0,5},{1,4},{2,7},{3,6},{4,1},{5,0},{6,3},{7,2},{8,13},{9,12},{10,... | collective-permute-start | bytes 49160 | tf_op jit(solution)/shard_map/ppermute | solution.py:336
  32.1 0.9 %collective-permute-done.12.refs_1_ = bf16[32,256]{1,0:T(8,128)(2,1)S(1)} collective-permute-done((bf16[32,256]{1,0:T(8,128)(2,1)S(1)}, bf16[32,256]{1,0:T(8,128)(2,1)S(1)}, u32[]{:S(2)}, u32[]{:S(2)}) %collective-permute-start.12) | collective-permute-done | bytes 16416 | tf_op jit(solution)/shard_map/ppermute | solution.py:336
  33.0 1.0 %collective-permute-done.13.refs_2_ = bf16[32,256]{1,0:T(8,128)(2,1)S(1)} collective-permute-done((bf16[32,256]{1,0:T(8,128)(2,1)S(1)}, bf16[32,256]{1,0:T(8,128)(2,1)S(1)}, u32[]{:S(2)}, u32[]{:S(2)}) %collective-permute-start.13) | collective-permute-done | bytes 16416 | tf_op jit(solution)/shard_map/ppermute | solution.py:336
  34.0 0.0 collective-permute-done.14.refs_3_
  34.0 0.8 %shard_map.71 = bf16[8,16,256]{2,1,0:T(8,128)(2,1)} custom-call(bf16[32,256]{1,0:T(8,128)(2,1)S(1)} %get-tuple-element.47.refs_0_, bf16[32,256]{1,0:T(8,128)(2,1)S(1)} %collective-permute-done.12.refs_1_, bf16[32,256]{1,0:T(8,128)(2,1)S(1)} %collective-permute-done.13.refs_2_, bf16[32,256]{1,0:T(8,128)(2,1)S(1)} %collective-permute-done.14.refs_3_, ...), custom_call_target="tpu_custom_call" | custom-call | bytes 655360 | tf_op jit(solution)/shard_map/pallas_call | solution.py:314
  (1 shorter events, 0.0 us)
Async XLA Ops:
  0.0 5.5 %copy-start = (bf16[8,16,256]{2,1,0:T(8,128)(2,1)S(1)}, bf16[8,16,256]{2,1,0:T(8,128)(2,1)}, u32[]{:S(2)}) copy-start(bf16[8,16,256]{2,1,0:T(8,128)(2,1)} %refs_0_.7) | copy-start | bytes 196612
  0.0 5.5 %collective-permute-start = (bf16[8,16,256]{2,1,0:T(8,128)(2,1)}, bf16[8,16,256]{2,1,0:T(8,128)(2,1)S(1)}, u32[]{:S(2)}, u32[]{:S(2)}) collective-permute-start(bf16[8,16,256]{2,1,0:T(8,128)(2,1)} %refs_0_.7), channel_id=1, source_target_pairs={{16,0},{0,16},{17,1},{1,17},{18,2},{2,18},{19,3},{3,19},{20,4},{4,... | collective-permute-start | bytes 196616 | tf_op jit(solution)/shard_map/ppermute | solution.py:347
  2.9 0.7 %copy-start.1 = (bf16[7,7,256]{2,1,0:T(8,128)(2,1)S(1)}, bf16[7,7,256]{2,1,0:T(8,128)(2,1)}, u32[]{:S(2)}) copy-start(bf16[7,7,256]{2,1,0:T(8,128)(2,1)} %refs_4_.1) | copy-start | bytes 75268
  5.6 7.0 %collective-permute-start.1 = (bf16[64,256]{1,0:T(8,128)(2,1)S(1)}, bf16[64,256]{1,0:T(8,128)(2,1)S(1)}, u32[]{:S(2)}, u32[]{:S(2)}) collective-permute-start(bf16[64,256]{1,0:T(8,128)(2,1)S(1)} %get-tuple-element.31), channel_id=1, source_target_pairs={{0,15},{1,2},{2,1},{3,4},{4,3},{5,6},{6,5},{7,8},{8,7},{9,10},{10,... | collective-permute-start | bytes 98312 | tf_op jit(solution)/shard_map/ppermute | solution.py:369
  9.4 3.2 %collective-permute-start.2 = (bf16[64,256]{1,0:T(8,128)(2,1)S(1)}, bf16[64,256]{1,0:T(8,128)(2,1)S(1)}, u32[]{:S(2)}, u32[]{:S(2)}) collective-permute-start(bf16[64,256]{1,0:T(8,128)(2,1)S(1)} %get-tuple-element.32), channel_id=1, source_target_pairs={{0,1},{1,0},{2,3},{3,2},{4,5},{5,4},{6,7},{7,6},{8,9},{9,8},{10,11... | collective-permute-start | bytes 98312 | tf_op jit(solution)/shard_map/ppermute | solution.py:336
  15.4 5.0 %collective-permute-start.3 = (bf16[32,256]{1,0:T(8,128)(2,1)S(1)}, bf16[32,256]{1,0:T(8,128)(2,1)S(1)}, u32[]{:S(2)}, u32[]{:S(2)}) collective-permute-start(bf16[32,256]{1,0:T(8,128)(2,1)S(1)} %get-tuple-element.38), channel_id=1, source_target_pairs={{0,13},{1,12},{2,15},{3,14},{4,9},{5,8},{6,11},{7,10},{8,5},{9,4},... | collective-permute-start | bytes 49160 | tf_op jit(solution)/shard_map/ppermute | solution.py:336
  17.0 4.4 %collective-permute-start.4 = (bf16[32,256]{1,0:T(8,128)(2,1)S(1)}, bf16[32,256]{1,0:T(8,128)(2,1)S(1)}, u32[]{:S(2)}, u32[]{:S(2)}) collective-permute-start(bf16[32,256]{1,0:T(8,128)(2,1)S(1)} %get-tuple-element.39), channel_id=1, source_target_pairs={{0,9},{1,8},{2,11},{3,10},{4,13},{5,12},{6,15},{7,14},{8,1},{9,0},... | collective-permute-start | bytes 49160 | tf_op jit(solution)/shard_map/ppermute | solution.py:336
  17.0 4.6 %collective-permute-start.5 = (bf16[32,256]{1,0:T(8,128)(2,1)S(1)}, bf16[32,256]{1,0:T(8,128)(2,1)S(1)}, u32[]{:S(2)}, u32[]{:S(2)}) collective-permute-start(bf16[32,256]{1,0:T(8,128)(2,1)S(1)} %get-tuple-element.40), channel_id=1, source_target_pairs={{0,5},{1,4},{2,7},{3,6},{4,1},{5,0},{6,3},{7,2},{8,13},{9,12},{10,... | collective-permute-start | bytes 49160 | tf_op jit(solution)/shard_map/ppermute | solution.py:336
  21.6 3.4 %collective-permute-start.6 = (bf16[64,256]{1,0:T(8,128)(2,1)S(1)}, bf16[64,256]{1,0:T(8,128)(2,1)S(1)}, u32[]{:S(2)}, u32[]{:S(2)}) collective-permute-start(bf16[64,256]{1,0:T(8,128)(2,1)S(1)} %get-tuple-element.41.refs_1_), channel_id=1, source_target_pairs={{0,3},{1,2},{2,1},{3,0},{4,7},{5,6},{6,5},{7,4},{8,11},{9,10},{10,... | collective-permute-start | bytes 98312 | tf_op jit(solution)/shard_map/ppermute | solution.py:336
  21.6 4.1 %collective-permute-start.9 = (bf16[64,256]{1,0:T(8,128)(2,1)S(1)}, bf16[64,256]{1,0:T(8,128)(2,1)S(1)}, u32[]{:S(2)}, u32[]{:S(2)}) collective-permute-start(bf16[64,256]{1,0:T(8,128)(2,1)S(1)} %get-tuple-element.46.refs_5_), channel_id=1, source_target_pairs={{0,3},{1,2},{2,1},{3,0},{4,7},{5,6},{6,5},{7,4},{8,11},{9,10},{10,... | collective-permute-start | bytes 98312 | tf_op jit(solution)/shard_map/ppermute | solution.py:336
  23.4 3.1 %collective-permute-start.7 = (bf16[64,256]{1,0:T(8,128)(2,1)S(1)}, bf16[64,256]{1,0:T(8,128)(2,1)S(1)}, u32[]{:S(2)}, u32[]{:S(2)}) collective-permute-start(bf16[64,256]{1,0:T(8,128)(2,1)S(1)} %get-tuple-element.41.refs_1_), channel_id=1, source_target_pairs={{0,1},{1,0},{2,3},{3,2},{4,5},{5,4},{6,7},{7,6},{8,9},{9,8},{10,11... | collective-permute-start | bytes 98312 | tf_op jit(solution)/shard_map/ppermute | solution.py:336
  25.0 1.6 %collective-permute-start.8 = (bf16[64,256]{1,0:T(8,128)(2,1)S(1)}, bf16[64,256]{1,0:T(8,128)(2,1)S(1)}, u32[]{:S(2)}, u32[]{:S(2)}) collective-permute-start(bf16[64,256]{1,0:T(8,128)(2,1)S(1)} %collective-permute-done.6.refs_2_), channel_id=1, source_target_pairs={{0,1},{1,0},{2,3},{3,2},{4,5},{5,4},{6,7},{7,6},{8,9},{9,8},{10,11... | collective-permute-start | bytes 98312 | tf_op jit(solution)/shard_map/ppermute | solution.py:336
  25.7 1.6 %collective-permute-start.10 = (bf16[64,256]{1,0:T(8,128)(2,1)S(1)}, bf16[64,256]{1,0:T(8,128)(2,1)S(1)}, u32[]{:S(2)}, u32[]{:S(2)}) collective-permute-start(bf16[64,256]{1,0:T(8,128)(2,1)S(1)} %get-tuple-element.46.refs_5_), channel_id=1, source_target_pairs={{0,1},{1,0},{2,3},{3,2},{4,5},{5,4},{6,7},{7,6},{8,9},{9,8},{10,11... | collective-permute-start | bytes 98312 | tf_op jit(solution)/shard_map/ppermute | solution.py:336
  25.7 1.6 %collective-permute-start.11 = (bf16[64,256]{1,0:T(8,128)(2,1)S(1)}, bf16[64,256]{1,0:T(8,128)(2,1)S(1)}, u32[]{:S(2)}, u32[]{:S(2)}) collective-permute-start(bf16[64,256]{1,0:T(8,128)(2,1)S(1)} %collective-permute-done.9.refs_6_), channel_id=1, source_target_pairs={{0,1},{1,0},{2,3},{3,2},{4,5},{5,4},{6,7},{7,6},{8,9},{9,8},{10,11... | collective-permute-start | bytes 98312 | tf_op jit(solution)/shard_map/ppermute | solution.py:336
  28.0 5.0 %collective-permute-start.12 = (bf16[32,256]{1,0:T(8,128)(2,1)S(1)}, bf16[32,256]{1,0:T(8,128)(2,1)S(1)}, u32[]{:S(2)}, u32[]{:S(2)}) collective-permute-start(bf16[32,256]{1,0:T(8,128)(2,1)S(1)} %get-tuple-element.48), channel_id=1, source_target_pairs={{0,13},{1,12},{2,15},{3,14},{4,9},{5,8},{6,11},{7,10},{8,5},{9,4},... | collective-permute-start | bytes 49160 | tf_op jit(solution)/shard_map/ppermute | solution.py:336
  29.9 4.1 %collective-permute-start.13 = (bf16[32,256]{1,0:T(8,128)(2,1)S(1)}, bf16[32,256]{1,0:T(8,128)(2,1)S(1)}, u32[]{:S(2)}, u32[]{:S(2)}) collective-permute-start(bf16[32,256]{1,0:T(8,128)(2,1)S(1)} %get-tuple-element.49), channel_id=1, source_target_pairs={{0,9},{1,8},{2,11},{3,10},{4,13},{5,12},{6,15},{7,14},{8,1},{9,0},... | collective-permute-start | bytes 49160 | tf_op jit(solution)/shard_map/ppermute | solution.py:336
  30.1 3.9 %collective-permute-start.14 = (bf16[32,256]{1,0:T(8,128)(2,1)S(1)}, bf16[32,256]{1,0:T(8,128)(2,1)S(1)}, u32[]{:S(2)}, u32[]{:S(2)}) collective-permute-start(bf16[32,256]{1,0:T(8,128)(2,1)S(1)} %get-tuple-element.50), channel_id=1, source_target_pairs={{0,5},{1,4},{2,7},{3,6},{4,1},{5,0},{6,3},{7,2},{8,13},{9,12},{10,... | collective-permute-start | bytes 49160 | tf_op jit(solution)/shard_map/ppermute | solution.py:336

commit v17 on v15

--- a/solution.py
+++ b/solution.py
@@ -145,7 +145,7 @@
 
     def widen(k, total):
         part = slice(k * channels, (k + 1) * channels)
-        wide = gelu(dot(normed, expand_ref[:, part])).astype(bf16)
+        wide = gelu(dot(normed, expand_ref[:, part]).astype(bf16))
         return total + dot(wide, reduce_ref[part])
 
     total = center.reshape(cells, channels)

time: 35 us -> 35 us (level)
  transfers between devices with their start and end apart: 15 -> 15, of which waited for: 7 -> 8; matrix products, arithmetic and copies ran while one was open for 0% -> 0% of each run, Pallas kernels for 16% -> 16%
where the time goes in v17:
time: 35 us; the launch traced here: 34.8 us
  starting transfers between devices  18.6 us (53%)
  Pallas kernels  9.73 us (28%)
  waiting for transfers between devices  5.61 us (16%)
  local copies, waits for them, and re-layouts  0.75 us (2%)
    ppermute x13, starting transfers between devices, swap(): return lax.ppermute(piece, 'lon', [(j, j ^ mask) for j in range(nlon)])  11.9 us
    pallas_call x8, Pallas kernels, call(): pl.pallas_call(kernel, out_shape=shapes, in_specs=[given] * len(operands)...  9.73 us
    ppermute x13, waiting for transfers between devices, swap(): return lax.ppermute(piece, 'lon', [(j, j ^ mask) for j in range(nlon)])  5.6 us
    ppermute x1, starting transfers between devices, shards(): lax.ppermute(far, 'lon', [(j, (j - 1) % nlon if j % 2 == 0 else (j + 1) %...  3.78 us
    ppermute x1, starting transfers between devices, shards(): lax.ppermute(field, 'lat', [((i + s) % nlat, i) for i in range(nlat)])  2.94 us
    unnamed x4, local copies, waits for them, and re-layouts  0.75 us
  transfers between devices with their start and end apart: 15, of which 8 were waited for; matrix products, arithmetic and copies ran while one was open for 0% of the time, Pallas kernels for 16%

profile of v17, /device:TPU:0, one launch (start us, length us, event | category | flops | bytes accessed | tf_op | source)
XLA Modules:
  0.0 34.8 jit_solution(2519597277326063509)
XLA Ops:
  0.0 0.0 copy-start
  0.0 2.9 %collective-permute-start = (bf16[8,16,256]{2,1,0:T(8,128)(2,1)}, bf16[8,16,256]{2,1,0:T(8,128)(2,1)S(1)}, u32[]{:S(2)}, u32[]{:S(2)}) collective-permute-start(bf16[8,16,256]{2,1,0:T(8,128)(2,1)} %refs_0_.7), channel_id=1, source_target_pairs={{16,0},{0,16},{17,1},{1,17},{18,2},{2,18},{19,3},{3,19},{20,4},{4,... | collective-permute-start | bytes 196616 | tf_op jit(solution)/shard_map/ppermute | solution.py:347
  2.9 0.0 copy-start.1
  2.9 0.7 %copy-done.1 = bf16[7,7,256]{2,1,0:T(8,128)(2,1)S(1)} copy-done((bf16[7,7,256]{2,1,0:T(8,128)(2,1)S(1)}, bf16[7,7,256]{2,1,0:T(8,128)(2,1)}, u32[]{:S(2)}) %copy-start.1) | copy-done | bytes 25112
  3.7 1.8 %shard_map.64 = (bf16[256,1024]{1,0:T(8,128)(2,1)S(1)}, bf16[1024,256]{1,0:T(8,128)(2,1)S(1)}, bf16[4,256,256]{2,1,0:T(8,128)(2,1)S(1)}, bf16[4,256,256]{2,1,0:T(8,128)(2,1)S(1)}, f32[7,7,256]{2,1,0:T(8,128)S(1)}) custom-call(bf16[256,1024]{1,0:T(8,128)(2,1)} %refs_0_.4, bf16[1024,256]{1,0:T(8,128)(2,1)} %refs_1_.1, bf16[4,256,256]{2,1,0:T(8,128)(2,1)} %refs_2_.1, ...), custom_call_target="tpu_custom_call" | custom-call | bytes 2122240 | tf_op jit(solution)/shard_map/pallas_call | solution.py:314
  5.5 0.0 collective-permute-done.refs_1_
  5.5 0.0 copy-done
  5.5 0.1 shard_map.65
  5.6 3.8 %collective-permute-start.1 = (bf16[64,256]{1,0:T(8,128)(2,1)S(1)}, bf16[64,256]{1,0:T(8,128)(2,1)S(1)}, u32[]{:S(2)}, u32[]{:S(2)}) collective-permute-start(bf16[64,256]{1,0:T(8,128)(2,1)S(1)} %get-tuple-element.31), channel_id=1, source_target_pairs={{0,15},{1,2},{2,1},{3,4},{4,3},{5,6},{6,5},{7,8},{8,7},{9,10},{10,... | collective-permute-start | bytes 98312 | tf_op jit(solution)/shard_map/ppermute | solution.py:369
  9.4 0.0 collective-permute-start.2
  9.4 3.1 %shard_map.66 = (bf16[64,256]{1,0:T(8,128)(2,1)S(1)}, bf16[64,256]{1,0:T(8,128)(2,1)S(1)}) custom-call(bf16[8,16,256]{2,1,0:T(8,128)(2,1)S(1)} %copy-done, bf16[8,16,256]{2,1,0:T(8,128)(2,1)S(1)} %collective-permute-done.refs_1_, f32[7,7,256]{2,1,0:T(8,128)S(1)} %get-tuple-element.33.refs_2_.refs_5_, ...), custom_call_target="tpu_custom_call" | custom-call | flops 134217728 | bytes 1754112 | tf_op jit(solution)/shard_map/pallas_call | solution.py:314
  12.4 0.0 collective-permute-done.1.refs_2_
  12.4 0.0 collective-permute-done.2.refs_3_
  12.4 2.7 %shard_map.67 = (bf16[64,256]{1,0:T(8,128)(2,1)S(1)}, bf16[32,256]{1,0:T(8,128)(2,1)S(1)}, bf16[32,256]{1,0:T(8,128)(2,1)S(1)}, bf16[32,256]{1,0:T(8,128)(2,1)S(1)}, bf16[32,256]{1,0:T(8,128)(2,1)S(1)}) custom-call(bf16[8,16,256]{2,1,0:T(8,128)(2,1)S(1)} %copy-done, bf16[8,16,256]{2,1,0:T(8,128)(2,1)S(1)} %collective-permute-done.refs_1_, ...), custom_call_target="tpu_custom_call" | custom-call | flops 134217728 | bytes 1852416 | tf_op jit(solution)/shard_map/pallas_call | solution.py:314
  15.1 1.6 %collective-permute-start.3 = (bf16[32,256]{1,0:T(8,128)(2,1)S(1)}, bf16[32,256]{1,0:T(8,128)(2,1)S(1)}, u32[]{:S(2)}, u32[]{:S(2)}) collective-permute-start(bf16[32,256]{1,0:T(8,128)(2,1)S(1)} %get-tuple-element.38), channel_id=1, source_target_pairs={{0,13},{1,12},{2,15},{3,14},{4,9},{5,8},{6,11},{7,10},{8,5},{9,4},... | collective-permute-start | bytes 49160 | tf_op jit(solution)/shard_map/ppermute | solution.py:336
  16.7 0.0 collective-permute-start.4
  16.7 2.7 %collective-permute-start.5 = (bf16[32,256]{1,0:T(8,128)(2,1)S(1)}, bf16[32,256]{1,0:T(8,128)(2,1)S(1)}, u32[]{:S(2)}, u32[]{:S(2)}) collective-permute-start(bf16[32,256]{1,0:T(8,128)(2,1)S(1)} %get-tuple-element.40), channel_id=1, source_target_pairs={{0,5},{1,4},{2,7},{3,6},{4,1},{5,0},{6,3},{7,2},{8,13},{9,12},{10,... | collective-permute-start | bytes 49160 | tf_op jit(solution)/shard_map/ppermute | solution.py:336
  19.4 0.7 %collective-permute-done.3.refs_1_ = bf16[32,256]{1,0:T(8,128)(2,1)S(1)} collective-permute-done((bf16[32,256]{1,0:T(8,128)(2,1)S(1)}, bf16[32,256]{1,0:T(8,128)(2,1)S(1)}, u32[]{:S(2)}, u32[]{:S(2)}) %collective-permute-start.3) | collective-permute-done | bytes 16416 | tf_op jit(solution)/shard_map/ppermute | solution.py:336
  20.1 1.0 %collective-permute-done.4.refs_2_ = bf16[32,256]{1,0:T(8,128)(2,1)S(1)} collective-permute-done((bf16[32,256]{1,0:T(8,128)(2,1)S(1)}, bf16[32,256]{1,0:T(8,128)(2,1)S(1)}, u32[]{:S(2)}, u32[]{:S(2)}) %collective-permute-start.4) | collective-permute-done | bytes 16416 | tf_op jit(solution)/shard_map/ppermute | solution.py:336
  21.1 0.2 collective-permute-done.5.refs_3_
  21.3 0.0 collective-permute-start.6
  21.3 1.8 %collective-permute-start.9 = (bf16[64,256]{1,0:T(8,128)(2,1)S(1)}, bf16[64,256]{1,0:T(8,128)(2,1)S(1)}, u32[]{:S(2)}, u32[]{:S(2)}) collective-permute-start(bf16[64,256]{1,0:T(8,128)(2,1)S(1)} %get-tuple-element.46.refs_5_), channel_id=1, source_target_pairs={{0,3},{1,2},{2,1},{3,0},{4,7},{5,6},{6,5},{7,4},{8,11},{9,10},{10,... | collective-permute-start | bytes 98312 | tf_op jit(solution)/shard_map/ppermute | solution.py:336
  23.1 0.1 collective-permute-start.7
  23.1 1.5 %collective-permute-done.6.refs_2_ = bf16[64,256]{1,0:T(8,128)(2,1)S(1)} collective-permute-done((bf16[64,256]{1,0:T(8,128)(2,1)S(1)}, bf16[64,256]{1,0:T(8,128)(2,1)S(1)}, u32[]{:S(2)}, u32[]{:S(2)}) %collective-permute-start.6) | collective-permute-done | bytes 32800 | tf_op jit(solution)/shard_map/ppermute | solution.py:336
  24.7 0.7 %collective-permute-start.8 = (bf16[64,256]{1,0:T(8,128)(2,1)S(1)}, bf16[64,256]{1,0:T(8,128)(2,1)S(1)}, u32[]{:S(2)}, u32[]{:S(2)}) collective-permute-start(bf16[64,256]{1,0:T(8,128)(2,1)S(1)} %collective-permute-done.6.refs_2_), channel_id=1, source_target_pairs={{0,1},{1,0},{2,3},{3,2},{4,5},{5,4},{6,7},{7,6},{8,9},{9,8},{10,11... | collective-permute-start | bytes 98312 | tf_op jit(solution)/shard_map/ppermute | solution.py:336
  25.4 0.0 collective-permute-start.10
  25.4 0.0 collective-permute-done.9.refs_6_
  25.4 0.9 %collective-permute-start.11 = (bf16[64,256]{1,0:T(8,128)(2,1)S(1)}, bf16[64,256]{1,0:T(8,128)(2,1)S(1)}, u32[]{:S(2)}, u32[]{:S(2)}) collective-permute-start(bf16[64,256]{1,0:T(8,128)(2,1)S(1)} %collective-permute-done.9.refs_6_), channel_id=1, source_target_pairs={{0,1},{1,0},{2,3},{3,2},{4,5},{5,4},{6,7},{7,6},{8,9},{9,8},{10,11... | collective-permute-start | bytes 98312 | tf_op jit(solution)/shard_map/ppermute | solution.py:336
  26.3 0.0 collective-permute-done.7.refs_3_
  26.3 0.0 collective-permute-done.8.refs_4_
  26.3 0.7 %shard_map.69 = (bf16[16,256]{1,0:T(8,128)(2,1)S(1)}, bf16[16,256]{1,0:T(8,128)(2,1)S(1)}, bf16[16,256]{1,0:T(8,128)(2,1)S(1)}, bf16[16,256]{1,0:T(8,128)(2,1)S(1)}) custom-call(bf16[4,256,256]{2,1,0:T(8,128)(2,1)S(1)} %get-tuple-element.29.refs_0_.refs_6_, bf16[64,256]{1,0:T(8,128)(2,1)S(1)} %get-tuple-element.41.refs_1_, ...), custom_call_target="tpu_custom_call" | custom-call | flops 33554432 | bytes 655360 | tf_op jit(solution)/shard_map/pallas_call | solution.py:314
  27.0 0.0 collective-permute-done.10.refs_7_
  27.0 0.1 collective-permute-done.11.refs_8_
  27.1 0.7 %shard_map.70 = (bf16[32,256]{1,0:T(8,128)(2,1)S(1)}, bf16[32,256]{1,0:T(8,128)(2,1)S(1)}, bf16[32,256]{1,0:T(8,128)(2,1)S(1)}, bf16[32,256]{1,0:T(8,128)(2,1)S(1)}) custom-call(bf16[4,256,256]{2,1,0:T(8,128)(2,1)S(1)} %get-tuple-element.29.refs_0_.refs_6_, bf16[16,256]{1,0:T(8,128)(2,1)S(1)} %get-tuple-element.42.refs_1_, ...), custom_call_target="tpu_custom_call" | custom-call | flops 33554432 | bytes 688128 | tf_op jit(solution)/shard_map/pallas_call | solution.py:314
  27.8 1.6 %collective-permute-start.12 = (bf16[32,256]{1,0:T(8,128)(2,1)S(1)}, bf16[32,256]{1,0:T(8,128)(2,1)S(1)}, u32[]{:S(2)}, u32[]{:S(2)}) collective-permute-start(bf16[32,256]{1,0:T(8,128)(2,1)S(1)} %get-tuple-element.48), channel_id=1, source_target_pairs={{0,13},{1,12},{2,15},{3,14},{4,9},{5,8},{6,11},{7,10},{8,5},{9,4},... | collective-permute-start | bytes 49160 | tf_op jit(solution)/shard_map/ppermute | solution.py:336
  29.4 0.4 %collective-permute-start.13 = (bf16[32,256]{1,0:T(8,128)(2,1)S(1)}, bf16[32,256]{1,0:T(8,128)(2,1)S(1)}, u32[]{:S(2)}, u32[]{:S(2)}) collective-permute-start(bf16[32,256]{1,0:T(8,128)(2,1)S(1)} %get-tuple-element.49), channel_id=1, source_target_pairs={{0,9},{1,8},{2,11},{3,10},{4,13},{5,12},{6,15},{7,14},{8,1},{9,0},... | collective-permute-start | bytes 49160 | tf_op jit(solution)/shard_map/ppermute | solution.py:336
  29.8 2.1 %collective-permute-start.14 = (bf16[32,256]{1,0:T(8,128)(2,1)S(1)}, bf16[32,256]{1,0:T(8,128)(2,1)S(1)}, u32[]{:S(2)}, u32[]{:S(2)}) collective-permute-start(bf16[32,256]{1,0:T(8,128)(2,1)S(1)} %get-tuple-element.50), channel_id=1, source_target_pairs={{0,5},{1,4},{2,7},{3,6},{4,1},{5,0},{6,3},{7,2},{8,13},{9,12},{10,... | collective-permute-start | bytes 49160 | tf_op jit(solution)/shard_map/ppermute | solution.py:336
  32.0 0.9 %collective-permute-done.12.refs_1_ = bf16[32,256]{1,0:T(8,128)(2,1)S(1)} collective-permute-done((bf16[32,256]{1,0:T(8,128)(2,1)S(1)}, bf16[32,256]{1,0:T(8,128)(2,1)S(1)}, u32[]{:S(2)}, u32[]{:S(2)}) %collective-permute-start.12) | collective-permute-done | bytes 16416 | tf_op jit(solution)/shard_map/ppermute | solution.py:336
  32.9 1.0 %collective-permute-done.13.refs_2_ = bf16[32,256]{1,0:T(8,128)(2,1)S(1)} collective-permute-done((bf16[32,256]{1,0:T(8,128)(2,1)S(1)}, bf16[32,256]{1,0:T(8,128)(2,1)S(1)}, u32[]{:S(2)}, u32[]{:S(2)}) %collective-permute-start.13) | collective-permute-done | bytes 16416 | tf_op jit(solution)/shard_map/ppermute | solution.py:336
  33.8 0.2 collective-permute-done.14.refs_3_
  34.0 0.8 %shard_map.71 = bf16[8,16,256]{2,1,0:T(8,128)(2,1)} custom-call(bf16[32,256]{1,0:T(8,128)(2,1)S(1)} %get-tuple-element.47.refs_0_, bf16[32,256]{1,0:T(8,128)(2,1)S(1)} %collective-permute-done.12.refs_1_, bf16[32,256]{1,0:T(8,128)(2,1)S(1)} %collective-permute-done.13.refs_2_, bf16[32,256]{1,0:T(8,128)(2,1)S(1)} %collective-permute-done.14.refs_3_, ...), custom_call_target="tpu_custom_call" | custom-call | bytes 655360 | tf_op jit(solution)/shard_map/pallas_call | solution.py:314
  (1 shorter events, 0.0 us)
Async XLA Ops:
  0.0 5.5 %copy-start = (bf16[8,16,256]{2,1,0:T(8,128)(2,1)S(1)}, bf16[8,16,256]{2,1,0:T(8,128)(2,1)}, u32[]{:S(2)}) copy-start(bf16[8,16,256]{2,1,0:T(8,128)(2,1)} %refs_0_.7) | copy-start | bytes 196612
  0.0 5.5 %collective-permute-start = (bf16[8,16,256]{2,1,0:T(8,128)(2,1)}, bf16[8,16,256]{2,1,0:T(8,128)(2,1)S(1)}, u32[]{:S(2)}, u32[]{:S(2)}) collective-permute-start(bf16[8,16,256]{2,1,0:T(8,128)(2,1)} %refs_0_.7), channel_id=1, source_target_pairs={{16,0},{0,16},{17,1},{1,17},{18,2},{2,18},{19,3},{3,19},{20,4},{4,... | collective-permute-start | bytes 196616 | tf_op jit(solution)/shard_map/ppermute | solution.py:347
  2.9 0.7 %copy-start.1 = (bf16[7,7,256]{2,1,0:T(8,128)(2,1)S(1)}, bf16[7,7,256]{2,1,0:T(8,128)(2,1)}, u32[]{:S(2)}) copy-start(bf16[7,7,256]{2,1,0:T(8,128)(2,1)} %refs_4_.1) | copy-start | bytes 75268
  5.6 6.8 %collective-permute-start.1 = (bf16[64,256]{1,0:T(8,128)(2,1)S(1)}, bf16[64,256]{1,0:T(8,128)(2,1)S(1)}, u32[]{:S(2)}, u32[]{:S(2)}) collective-permute-start(bf16[64,256]{1,0:T(8,128)(2,1)S(1)} %get-tuple-element.31), channel_id=1, source_target_pairs={{0,15},{1,2},{2,1},{3,4},{4,3},{5,6},{6,5},{7,8},{8,7},{9,10},{10,... | collective-permute-start | bytes 98312 | tf_op jit(solution)/shard_map/ppermute | solution.py:369
  9.4 3.1 %collective-permute-start.2 = (bf16[64,256]{1,0:T(8,128)(2,1)S(1)}, bf16[64,256]{1,0:T(8,128)(2,1)S(1)}, u32[]{:S(2)}, u32[]{:S(2)}) collective-permute-start(bf16[64,256]{1,0:T(8,128)(2,1)S(1)} %get-tuple-element.32), channel_id=1, source_target_pairs={{0,1},{1,0},{2,3},{3,2},{4,5},{5,4},{6,7},{7,6},{8,9},{9,8},{10,11... | collective-permute-start | bytes 98312 | tf_op jit(solution)/shard_map/ppermute | solution.py:336
  15.1 5.0 %collective-permute-start.3 = (bf16[32,256]{1,0:T(8,128)(2,1)S(1)}, bf16[32,256]{1,0:T(8,128)(2,1)S(1)}, u32[]{:S(2)}, u32[]{:S(2)}) collective-permute-start(bf16[32,256]{1,0:T(8,128)(2,1)S(1)} %get-tuple-element.38), channel_id=1, source_target_pairs={{0,13},{1,12},{2,15},{3,14},{4,9},{5,8},{6,11},{7,10},{8,5},{9,4},... | collective-permute-start | bytes 49160 | tf_op jit(solution)/shard_map/ppermute | solution.py:336
  16.7 4.4 %collective-permute-start.4 = (bf16[32,256]{1,0:T(8,128)(2,1)S(1)}, bf16[32,256]{1,0:T(8,128)(2,1)S(1)}, u32[]{:S(2)}, u32[]{:S(2)}) collective-permute-start(bf16[32,256]{1,0:T(8,128)(2,1)S(1)} %get-tuple-element.39), channel_id=1, source_target_pairs={{0,9},{1,8},{2,11},{3,10},{4,13},{5,12},{6,15},{7,14},{8,1},{9,0},... | collective-permute-start | bytes 49160 | tf_op jit(solution)/shard_map/ppermute | solution.py:336
  16.7 4.6 %collective-permute-start.5 = (bf16[32,256]{1,0:T(8,128)(2,1)S(1)}, bf16[32,256]{1,0:T(8,128)(2,1)S(1)}, u32[]{:S(2)}, u32[]{:S(2)}) collective-permute-start(bf16[32,256]{1,0:T(8,128)(2,1)S(1)} %get-tuple-element.40), channel_id=1, source_target_pairs={{0,5},{1,4},{2,7},{3,6},{4,1},{5,0},{6,3},{7,2},{8,13},{9,12},{10,... | collective-permute-start | bytes 49160 | tf_op jit(solution)/shard_map/ppermute | solution.py:336
  21.3 3.4 %collective-permute-start.6 = (bf16[64,256]{1,0:T(8,128)(2,1)S(1)}, bf16[64,256]{1,0:T(8,128)(2,1)S(1)}, u32[]{:S(2)}, u32[]{:S(2)}) collective-permute-start(bf16[64,256]{1,0:T(8,128)(2,1)S(1)} %get-tuple-element.41.refs_1_), channel_id=1, source_target_pairs={{0,3},{1,2},{2,1},{3,0},{4,7},{5,6},{6,5},{7,4},{8,11},{9,10},{10,... | collective-permute-start | bytes 98312 | tf_op jit(solution)/shard_map/ppermute | solution.py:336
  21.3 4.1 %collective-permute-start.9 = (bf16[64,256]{1,0:T(8,128)(2,1)S(1)}, bf16[64,256]{1,0:T(8,128)(2,1)S(1)}, u32[]{:S(2)}, u32[]{:S(2)}) collective-permute-start(bf16[64,256]{1,0:T(8,128)(2,1)S(1)} %get-tuple-element.46.refs_5_), channel_id=1, source_target_pairs={{0,3},{1,2},{2,1},{3,0},{4,7},{5,6},{6,5},{7,4},{8,11},{9,10},{10,... | collective-permute-start | bytes 98312 | tf_op jit(solution)/shard_map/ppermute | solution.py:336
  23.1 3.2 %collective-permute-start.7 = (bf16[64,256]{1,0:T(8,128)(2,1)S(1)}, bf16[64,256]{1,0:T(8,128)(2,1)S(1)}, u32[]{:S(2)}, u32[]{:S(2)}) collective-permute-start(bf16[64,256]{1,0:T(8,128)(2,1)S(1)} %get-tuple-element.41.refs_1_), channel_id=1, source_target_pairs={{0,1},{1,0},{2,3},{3,2},{4,5},{5,4},{6,7},{7,6},{8,9},{9,8},{10,11... | collective-permute-start | bytes 98312 | tf_op jit(solution)/shard_map/ppermute | solution.py:336
  24.7 1.6 %collective-permute-start.8 = (bf16[64,256]{1,0:T(8,128)(2,1)S(1)}, bf16[64,256]{1,0:T(8,128)(2,1)S(1)}, u32[]{:S(2)}, u32[]{:S(2)}) collective-permute-start(bf16[64,256]{1,0:T(8,128)(2,1)S(1)} %collective-permute-done.6.refs_2_), channel_id=1, source_target_pairs={{0,1},{1,0},{2,3},{3,2},{4,5},{5,4},{6,7},{7,6},{8,9},{9,8},{10,11... | collective-permute-start | bytes 98312 | tf_op jit(solution)/shard_map/ppermute | solution.py:336
  25.4 1.6 %collective-permute-start.10 = (bf16[64,256]{1,0:T(8,128)(2,1)S(1)}, bf16[64,256]{1,0:T(8,128)(2,1)S(1)}, u32[]{:S(2)}, u32[]{:S(2)}) collective-permute-start(bf16[64,256]{1,0:T(8,128)(2,1)S(1)} %get-tuple-element.46.refs_5_), channel_id=1, source_target_pairs={{0,1},{1,0},{2,3},{3,2},{4,5},{5,4},{6,7},{7,6},{8,9},{9,8},{10,11... | collective-permute-start | bytes 98312 | tf_op jit(solution)/shard_map/ppermute | solution.py:336
  25.4 1.7 %collective-permute-start.11 = (bf16[64,256]{1,0:T(8,128)(2,1)S(1)}, bf16[64,256]{1,0:T(8,128)(2,1)S(1)}, u32[]{:S(2)}, u32[]{:S(2)}) collective-permute-start(bf16[64,256]{1,0:T(8,128)(2,1)S(1)} %collective-permute-done.9.refs_6_), channel_id=1, source_target_pairs={{0,1},{1,0},{2,3},{3,2},{4,5},{5,4},{6,7},{7,6},{8,9},{9,8},{10,11... | collective-permute-start | bytes 98312 | tf_op jit(solution)/shard_map/ppermute | solution.py:336
  27.8 5.0 %collective-permute-start.12 = (bf16[32,256]{1,0:T(8,128)(2,1)S(1)}, bf16[32,256]{1,0:T(8,128)(2,1)S(1)}, u32[]{:S(2)}, u32[]{:S(2)}) collective-permute-start(bf16[32,256]{1,0:T(8,128)(2,1)S(1)} %get-tuple-element.48), channel_id=1, source_target_pairs={{0,13},{1,12},{2,15},{3,14},{4,9},{5,8},{6,11},{7,10},{8,5},{9,4},... | collective-permute-start | bytes 49160 | tf_op jit(solution)/shard_map/ppermute | solution.py:336
  29.4 4.4 %collective-permute-start.13 = (bf16[32,256]{1,0:T(8,128)(2,1)S(1)}, bf16[32,256]{1,0:T(8,128)(2,1)S(1)}, u32[]{:S(2)}, u32[]{:S(2)}) collective-permute-start(bf16[32,256]{1,0:T(8,128)(2,1)S(1)} %get-tuple-element.49), channel_id=1, source_target_pairs={{0,9},{1,8},{2,11},{3,10},{4,13},{5,12},{6,15},{7,14},{8,1},{9,0},... | collective-permute-start | bytes 49160 | tf_op jit(solution)/shard_map/ppermute | solution.py:336
  29.8 4.1 %collective-permute-start.14 = (bf16[32,256]{1,0:T(8,128)(2,1)S(1)}, bf16[32,256]{1,0:T(8,128)(2,1)S(1)}, u32[]{:S(2)}, u32[]{:S(2)}) collective-permute-start(bf16[32,256]{1,0:T(8,128)(2,1)S(1)} %get-tuple-element.50), channel_id=1, source_target_pairs={{0,5},{1,4},{2,7},{3,6},{4,1},{5,0},{6,3},{7,2},{8,13},{9,12},{10,... | collective-permute-start | bytes 49160 | tf_op jit(solution)/shard_map/ppermute | solution.py:336

commit v18 on v15

--- a/solution.py
+++ b/solution.py
@@ -255,27 +255,33 @@
 
 
 def join_kernel(levels, some, *refs):
-    parts, joined = refs[:levels], refs[levels:]
+    parts, joined, whole_ref = refs[:levels], refs[levels:-1], refs[-1]
     cols = parts[0].shape[0] // some
     for r in range(some):
         for k in range(levels):
-            joined[r][k * cols : (k + 1) * cols] = parts[k][r * cols : (r + 1) * cols]
-
-
-def circle_kernel(levels, before, *refs):
+            part = parts[k][r * cols : (r + 1) * cols]
+            start = (r * levels + k) * cols
+            joined[r][k * cols : (k + 1) * cols] = part
+            whole_ref[start : start + cols] = part
+
+
+def circle_kernel(levels, r, before, beside, *refs):
     attn_ref, refs = refs[0], refs[1:]
     done, refs = refs[:before], refs[before:]
     parts, mix_refs = refs[:-levels], refs[-levels:]
     own = parts[0][...]
-    every = jnp.concatenate([own] + [part[...] for part in parts[1:]], axis=0)
+    pieces = [own] + [part[...] for part in parts[1 + beside :]]
+    if beside:
+        pieces.append(parts[1][r * own.shape[0] : (r + 1) * own.shape[0]])
+    every = jnp.concatenate(pieces, axis=0)
     queries = dot(own, attn_ref[0]).astype(bf16)
     keys = dot(every, attn_ref[1]).astype(bf16)
     values = dot(every, attn_ref[2]).astype(bf16)
     mix = attend(queries, keys, values, None)
     cols = own.shape[0] // levels
     for k in range(levels):
-        for r in range(before // levels):
-            mix_refs[k][r * cols : (r + 1) * cols] = done[r * levels + k][...]
+        for i in range(before // levels):
+            mix_refs[k][i * cols : (i + 1) * cols] = done[i * levels + k][...]
         mix_refs[k][before // levels * cols :] = mix[k * cols : (k + 1) * cols]
 
 
@@ -396,22 +402,28 @@
     )
 
     parts = exchange(parts)
-    joined = call(
-        functools.partial(join_kernel, levels, some), [(levels * cols, channels)] * some, parts
+    block = (levels * cols, channels)
+    *joined, whole = call(
+        functools.partial(join_kernel, levels, some),
+        [block] * some + [(some * levels * cols, channels)],
+        parts,
     )
     circles = [[part] for part in joined]
     mask = column // 2
-    while mask:
+    while mask > 1:
         for circle in circles:
             circle += [swap(part, mask + mask // 2) for part in circle]
         mask //= 2
+    beside = [swap(whole, 1)] if column > 1 else []
     done = []
     for r, circle in enumerate(circles):
-        last_one = r == some - 1
+        if beside:
+            circle += [swap(part, 1) for part in circle[1:]]
+        earlier = done if r == some - 1 else []
         mixes = call(
-            functools.partial(circle_kernel, levels, len(done) if last_one else 0),
-            [piece if last_one else (cols, channels)] * levels,
-            [lon_proj, *(done if last_one else []), *circle],
+            functools.partial(circle_kernel, levels, r, len(earlier), len(beside)),
+            [piece if r == some - 1 else (cols, channels)] * levels,
+            [lon_proj, *earlier, circle[0], *beside, *circle[1:]],
             flops=work // 4,
         )
         done = done + list(mixes)

time: 35 us -> 35.2 us (level)
  waiting for transfers between devices: 5.47 us -> 7.04 us
  starting transfers between devices: 18.4 us -> 17.1 us
    ppermute x13 -> x12, waiting for transfers between devices: 5.46 us -> 7.03 us  [swap(): return lax.ppermute(piece, 'lon', [(j, j ^ mask) for j in range(nlon)])]
    ppermute x13 -> x12, starting transfers between devices: 11.7 us -> 10.4 us  [swap(): return lax.ppermute(piece, 'lon', [(j, j ^ mask) for j in range(nlon)])]
  transfers between devices with their start and end apart: 15 -> 14, of which waited for: 7 -> 8; matrix products, arithmetic and copies ran while one was open for 0% -> 0% of each run, Pallas kernels for 16% -> 16%
where the time goes in v18:
time: 35.2 us; the launch traced here: 35 us
  starting transfers between devices  17.1 us (49%)
  Pallas kernels  10 us (28%)
  waiting for transfers between devices  7.04 us (20%)
  local copies, waits for them, and re-layouts  0.75 us (2%)
    ppermute x12, starting transfers between devices, swap(): return lax.ppermute(piece, 'lon', [(j, j ^ mask) for j in range(nlon)])  10.4 us
    pallas_call x8, Pallas kernels, call(): pl.pallas_call(kernel, out_shape=shapes, in_specs=[given] * len(operands)...  10 us
    ppermute x12, waiting for transfers between devices, swap(): return lax.ppermute(piece, 'lon', [(j, j ^ mask) for j in range(nlon)])  7.03 us
    ppermute x1, starting transfers between devices, shards(): lax.ppermute(far, 'lon', [(j, (j - 1) % nlon if j % 2 == 0 else (j + 1) %...  3.78 us
    ppermute x1, starting transfers between devices, shards(): lax.ppermute(field, 'lat', [((i + s) % nlat, i) for i in range(nlat)])  2.94 us
    unnamed x4, local copies, waits for them, and re-layouts  0.75 us
  transfers between devices with their start and end apart: 14, of which 8 were waited for; matrix products, arithmetic and copies ran while one was open for 0% of the time, Pallas kernels for 16%

profile of v18, /device:TPU:0, one launch (start us, length us, event | category | flops | bytes accessed | tf_op | source)
XLA Modules:
  0.0 35.0 jit_solution(7842400123107540182)
XLA Ops:
  0.0 0.0 copy-start
  0.0 2.9 %collective-permute-start = (bf16[8,16,256]{2,1,0:T(8,128)(2,1)}, bf16[8,16,256]{2,1,0:T(8,128)(2,1)S(1)}, u32[]{:S(2)}, u32[]{:S(2)}) collective-permute-start(bf16[8,16,256]{2,1,0:T(8,128)(2,1)} %refs_0_.7), channel_id=1, source_target_pairs={{16,0},{0,16},{17,1},{1,17},{18,2},{2,18},{19,3},{3,19},{20,4},{4,... | collective-permute-start | bytes 196616 | tf_op jit(solution)/shard_map/ppermute | solution.py:353
  2.9 0.0 copy-start.1
  2.9 0.7 %copy-done.1 = bf16[7,7,256]{2,1,0:T(8,128)(2,1)S(1)} copy-done((bf16[7,7,256]{2,1,0:T(8,128)(2,1)S(1)}, bf16[7,7,256]{2,1,0:T(8,128)(2,1)}, u32[]{:S(2)}) %copy-start.1) | copy-done | bytes 25112
  3.7 1.8 %shard_map.64 = (bf16[256,1024]{1,0:T(8,128)(2,1)S(1)}, bf16[1024,256]{1,0:T(8,128)(2,1)S(1)}, bf16[4,256,256]{2,1,0:T(8,128)(2,1)S(1)}, bf16[4,256,256]{2,1,0:T(8,128)(2,1)S(1)}, f32[7,7,256]{2,1,0:T(8,128)S(1)}) custom-call(bf16[256,1024]{1,0:T(8,128)(2,1)} %refs_0_.4, bf16[1024,256]{1,0:T(8,128)(2,1)} %refs_1_.1, bf16[4,256,256]{2,1,0:T(8,128)(2,1)} %refs_2_.1, ...), custom_call_target="tpu_custom_call" | custom-call | bytes 2122240 | tf_op jit(solution)/shard_map/pallas_call | solution.py:320
  5.5 0.0 collective-permute-done.refs_1_
  5.5 0.0 copy-done
  5.5 0.1 shard_map.65
  5.6 3.8 %collective-permute-start.1 = (bf16[64,256]{1,0:T(8,128)(2,1)S(1)}, bf16[64,256]{1,0:T(8,128)(2,1)S(1)}, u32[]{:S(2)}, u32[]{:S(2)}) collective-permute-start(bf16[64,256]{1,0:T(8,128)(2,1)S(1)} %get-tuple-element.32), channel_id=1, source_target_pairs={{0,15},{1,2},{2,1},{3,4},{4,3},{5,6},{6,5},{7,8},{8,7},{9,10},{10,... | collective-permute-start | bytes 98312 | tf_op jit(solution)/shard_map/ppermute | solution.py:375
  9.4 0.0 collective-permute-start.2
  9.4 3.2 %shard_map.66 = (bf16[64,256]{1,0:T(8,128)(2,1)S(1)}, bf16[64,256]{1,0:T(8,128)(2,1)S(1)}) custom-call(bf16[8,16,256]{2,1,0:T(8,128)(2,1)S(1)} %copy-done, bf16[8,16,256]{2,1,0:T(8,128)(2,1)S(1)} %collective-permute-done.refs_1_, f32[7,7,256]{2,1,0:T(8,128)S(1)} %get-tuple-element.34.refs_2_.refs_5_, ...), custom_call_target="tpu_custom_call" | custom-call | flops 134217728 | bytes 1754112 | tf_op jit(solution)/shard_map/pallas_call | solution.py:320
  12.6 0.0 collective-permute-done.1.refs_2_
  12.6 0.0 collective-permute-done.2.refs_3_
  12.6 2.8 %shard_map.67 = (bf16[64,256]{1,0:T(8,128)(2,1)S(1)}, bf16[32,256]{1,0:T(8,128)(2,1)S(1)}, bf16[32,256]{1,0:T(8,128)(2,1)S(1)}, bf16[32,256]{1,0:T(8,128)(2,1)S(1)}, bf16[32,256]{1,0:T(8,128)(2,1)S(1)}) custom-call(bf16[8,16,256]{2,1,0:T(8,128)(2,1)S(1)} %copy-done, bf16[8,16,256]{2,1,0:T(8,128)(2,1)S(1)} %collective-permute-done.refs_1_, ...), custom_call_target="tpu_custom_call" | custom-call | flops 134217728 | bytes 1852416 | tf_op jit(solution)/shard_map/pallas_call | solution.py:320
  15.4 1.6 %collective-permute-start.3 = (bf16[32,256]{1,0:T(8,128)(2,1)S(1)}, bf16[32,256]{1,0:T(8,128)(2,1)S(1)}, u32[]{:S(2)}, u32[]{:S(2)}) collective-permute-start(bf16[32,256]{1,0:T(8,128)(2,1)S(1)} %get-tuple-element.39), channel_id=1, source_target_pairs={{0,13},{1,12},{2,15},{3,14},{4,9},{5,8},{6,11},{7,10},{8,5},{9,4},... | collective-permute-start | bytes 49160 | tf_op jit(solution)/shard_map/ppermute | solution.py:342
  17.0 0.0 collective-permute-start.4
  17.0 2.7 %collective-permute-start.5 = (bf16[32,256]{1,0:T(8,128)(2,1)S(1)}, bf16[32,256]{1,0:T(8,128)(2,1)S(1)}, u32[]{:S(2)}, u32[]{:S(2)}) collective-permute-start(bf16[32,256]{1,0:T(8,128)(2,1)S(1)} %get-tuple-element.41), channel_id=1, source_target_pairs={{0,5},{1,4},{2,7},{3,6},{4,1},{5,0},{6,3},{7,2},{8,13},{9,12},{10,... | collective-permute-start | bytes 49160 | tf_op jit(solution)/shard_map/ppermute | solution.py:342
  19.7 0.7 %collective-permute-done.3.refs_1_ = bf16[32,256]{1,0:T(8,128)(2,1)S(1)} collective-permute-done((bf16[32,256]{1,0:T(8,128)(2,1)S(1)}, bf16[32,256]{1,0:T(8,128)(2,1)S(1)}, u32[]{:S(2)}, u32[]{:S(2)}) %collective-permute-start.3) | collective-permute-done | bytes 16416 | tf_op jit(solution)/shard_map/ppermute | solution.py:342
  20.4 1.0 %collective-permute-done.4.refs_2_ = bf16[32,256]{1,0:T(8,128)(2,1)S(1)} collective-permute-done((bf16[32,256]{1,0:T(8,128)(2,1)S(1)}, bf16[32,256]{1,0:T(8,128)(2,1)S(1)}, u32[]{:S(2)}, u32[]{:S(2)}) %collective-permute-start.4) | collective-permute-done | bytes 16416 | tf_op jit(solution)/shard_map/ppermute | solution.py:342
  21.4 0.2 collective-permute-done.5.refs_3_
  21.6 0.1 collective-permute-start.7
  21.7 1.4 %collective-permute-start.6 = (bf16[128,256]{1,0:T(8,128)(2,1)S(1)}, bf16[128,256]{1,0:T(8,128)(2,1)S(1)}, u32[]{:S(2)}, u32[]{:S(2)}) collective-permute-start(bf16[128,256]{1,0:T(8,128)(2,1)S(1)} %get-tuple-element.43), channel_id=1, source_target_pairs={{0,1},{1,0},{2,3},{3,2},{4,5},{5,4},{6,7},{7,6},{8,9},{9,8},{10,11... | collective-permute-start | bytes 196616 | tf_op jit(solution)/shard_map/ppermute | solution.py:342
  23.1 0.4 %collective-permute-start.9 = (bf16[64,256]{1,0:T(8,128)(2,1)S(1)}, bf16[64,256]{1,0:T(8,128)(2,1)S(1)}, u32[]{:S(2)}, u32[]{:S(2)}) collective-permute-start(bf16[64,256]{1,0:T(8,128)(2,1)S(1)} %get-tuple-element.48.refs_5_), channel_id=1, source_target_pairs={{0,3},{1,2},{2,1},{3,0},{4,7},{5,6},{6,5},{7,4},{8,11},{9,10},{10,... | collective-permute-start | bytes 98312 | tf_op jit(solution)/shard_map/ppermute | solution.py:342
  23.5 1.5 %collective-permute-done.7.refs_3_ = bf16[64,256]{1,0:T(8,128)(2,1)S(1)} collective-permute-done((bf16[64,256]{1,0:T(8,128)(2,1)S(1)}, bf16[64,256]{1,0:T(8,128)(2,1)S(1)}, u32[]{:S(2)}, u32[]{:S(2)}) %collective-permute-start.7) | collective-permute-done | bytes 32800 | tf_op jit(solution)/shard_map/ppermute | solution.py:342
  25.0 0.1 collective-permute-start.8
  25.2 1.4 %collective-permute-done.9.refs_7_ = bf16[64,256]{1,0:T(8,128)(2,1)S(1)} collective-permute-done((bf16[64,256]{1,0:T(8,128)(2,1)S(1)}, bf16[64,256]{1,0:T(8,128)(2,1)S(1)}, u32[]{:S(2)}, u32[]{:S(2)}) %collective-permute-start.9) | collective-permute-done | bytes 32800 | tf_op jit(solution)/shard_map/ppermute | solution.py:342
  26.6 0.1 collective-permute-start.10
  26.7 0.0 collective-permute-done.6.refs_2_.refs_6_
  26.7 0.0 collective-permute-done.8.refs_4_
  26.7 0.7 %shard_map.69 = (bf16[16,256]{1,0:T(8,128)(2,1)S(1)}, bf16[16,256]{1,0:T(8,128)(2,1)S(1)}, bf16[16,256]{1,0:T(8,128)(2,1)S(1)}, bf16[16,256]{1,0:T(8,128)(2,1)S(1)}) custom-call(bf16[4,256,256]{2,1,0:T(8,128)(2,1)S(1)} %get-tuple-element.30.refs_0_.refs_6_, bf16[64,256]{1,0:T(8,128)(2,1)S(1)} %get-tuple-element.42.refs_1_, ...), custom_call_target="tpu_custom_call" | custom-call | flops 33554432 | bytes 688128 | tf_op jit(solution)/shard_map/pallas_call | solution.py:320
  27.4 0.4 %collective-permute-done.10.refs_8_ = bf16[64,256]{1,0:T(8,128)(2,1)S(1)} collective-permute-done((bf16[64,256]{1,0:T(8,128)(2,1)S(1)}, bf16[64,256]{1,0:T(8,128)(2,1)S(1)}, u32[]{:S(2)}, u32[]{:S(2)}) %collective-permute-start.10) | collective-permute-done | bytes 32800 | tf_op jit(solution)/shard_map/ppermute | solution.py:342
  27.8 0.7 %shard_map.70 = (bf16[32,256]{1,0:T(8,128)(2,1)S(1)}, bf16[32,256]{1,0:T(8,128)(2,1)S(1)}, bf16[32,256]{1,0:T(8,128)(2,1)S(1)}, bf16[32,256]{1,0:T(8,128)(2,1)S(1)}) custom-call(bf16[4,256,256]{2,1,0:T(8,128)(2,1)S(1)} %get-tuple-element.30.refs_0_.refs_6_, bf16[16,256]{1,0:T(8,128)(2,1)S(1)} %get-tuple-element.44.refs_1_, ...), custom_call_target="tpu_custom_call" | custom-call | flops 33554432 | bytes 720896 | tf_op jit(solution)/shard_map/pallas_call | solution.py:320
  28.5 1.5 %collective-permute-start.11 = (bf16[32,256]{1,0:T(8,128)(2,1)S(1)}, bf16[32,256]{1,0:T(8,128)(2,1)S(1)}, u32[]{:S(2)}, u32[]{:S(2)}) collective-permute-start(bf16[32,256]{1,0:T(8,128)(2,1)S(1)} %get-tuple-element.50), channel_id=1, source_target_pairs={{0,13},{1,12},{2,15},{3,14},{4,9},{5,8},{6,11},{7,10},{8,5},{9,4},... | collective-permute-start | bytes 49160 | tf_op jit(solution)/shard_map/ppermute | solution.py:342
  30.0 0.6 %collective-permute-start.12 = (bf16[32,256]{1,0:T(8,128)(2,1)S(1)}, bf16[32,256]{1,0:T(8,128)(2,1)S(1)}, u32[]{:S(2)}, u32[]{:S(2)}) collective-permute-start(bf16[32,256]{1,0:T(8,128)(2,1)S(1)} %get-tuple-element.51), channel_id=1, source_target_pairs={{0,9},{1,8},{2,11},{3,10},{4,13},{5,12},{6,15},{7,14},{8,1},{9,0},... | collective-permute-start | bytes 49160 | tf_op jit(solution)/shard_map/ppermute | solution.py:342
  30.6 1.8 %collective-permute-start.13 = (bf16[32,256]{1,0:T(8,128)(2,1)S(1)}, bf16[32,256]{1,0:T(8,128)(2,1)S(1)}, u32[]{:S(2)}, u32[]{:S(2)}) collective-permute-start(bf16[32,256]{1,0:T(8,128)(2,1)S(1)} %get-tuple-element.52), channel_id=1, source_target_pairs={{0,5},{1,4},{2,7},{3,6},{4,1},{5,0},{6,3},{7,2},{8,13},{9,12},{10,... | collective-permute-start | bytes 49160 | tf_op jit(solution)/shard_map/ppermute | solution.py:342
  32.4 1.1 %collective-permute-done.11.refs_1_ = bf16[32,256]{1,0:T(8,128)(2,1)S(1)} collective-permute-done((bf16[32,256]{1,0:T(8,128)(2,1)S(1)}, bf16[32,256]{1,0:T(8,128)(2,1)S(1)}, u32[]{:S(2)}, u32[]{:S(2)}) %collective-permute-start.11) | collective-permute-done | bytes 16416 | tf_op jit(solution)/shard_map/ppermute | solution.py:342
  33.5 0.7 %collective-permute-done.12.refs_2_ = bf16[32,256]{1,0:T(8,128)(2,1)S(1)} collective-permute-done((bf16[32,256]{1,0:T(8,128)(2,1)S(1)}, bf16[32,256]{1,0:T(8,128)(2,1)S(1)}, u32[]{:S(2)}, u32[]{:S(2)}) %collective-permute-start.12) | collective-permute-done | bytes 16416 | tf_op jit(solution)/shard_map/ppermute | solution.py:342
  34.2 0.0 collective-permute-done.13.refs_3_
  34.2 0.8 %shard_map.71 = bf16[8,16,256]{2,1,0:T(8,128)(2,1)} custom-call(bf16[32,256]{1,0:T(8,128)(2,1)S(1)} %get-tuple-element.49.refs_0_, bf16[32,256]{1,0:T(8,128)(2,1)S(1)} %collective-permute-done.11.refs_1_, bf16[32,256]{1,0:T(8,128)(2,1)S(1)} %collective-permute-done.12.refs_2_, bf16[32,256]{1,0:T(8,128)(2,1)S(1)} %collective-permute-done.13.refs_3_, ...), custom_call_target="tpu_custom_call" | custom-call | bytes 655360 | tf_op jit(solution)/shard_map/pallas_call | solution.py:320
  (1 shorter events, 0.0 us)
Async XLA Ops:
  0.0 5.5 %copy-start = (bf16[8,16,256]{2,1,0:T(8,128)(2,1)S(1)}, bf16[8,16,256]{2,1,0:T(8,128)(2,1)}, u32[]{:S(2)}) copy-start(bf16[8,16,256]{2,1,0:T(8,128)(2,1)} %refs_0_.7) | copy-start | bytes 196612
  0.0 5.5 %collective-permute-start = (bf16[8,16,256]{2,1,0:T(8,128)(2,1)}, bf16[8,16,256]{2,1,0:T(8,128)(2,1)S(1)}, u32[]{:S(2)}, u32[]{:S(2)}) collective-permute-start(bf16[8,16,256]{2,1,0:T(8,128)(2,1)} %refs_0_.7), channel_id=1, source_target_pairs={{16,0},{0,16},{17,1},{1,17},{18,2},{2,18},{19,3},{3,19},{20,4},{4,... | collective-permute-start | bytes 196616 | tf_op jit(solution)/shard_map/ppermute | solution.py:353
  2.9 0.7 %copy-start.1 = (bf16[7,7,256]{2,1,0:T(8,128)(2,1)S(1)}, bf16[7,7,256]{2,1,0:T(8,128)(2,1)}, u32[]{:S(2)}) copy-start(bf16[7,7,256]{2,1,0:T(8,128)(2,1)} %refs_4_.1) | copy-start | bytes 75268
  5.6 7.0 %collective-permute-start.1 = (bf16[64,256]{1,0:T(8,128)(2,1)S(1)}, bf16[64,256]{1,0:T(8,128)(2,1)S(1)}, u32[]{:S(2)}, u32[]{:S(2)}) collective-permute-start(bf16[64,256]{1,0:T(8,128)(2,1)S(1)} %get-tuple-element.32), channel_id=1, source_target_pairs={{0,15},{1,2},{2,1},{3,4},{4,3},{5,6},{6,5},{7,8},{8,7},{9,10},{10,... | collective-permute-start | bytes 98312 | tf_op jit(solution)/shard_map/ppermute | solution.py:375
  9.4 3.2 %collective-permute-start.2 = (bf16[64,256]{1,0:T(8,128)(2,1)S(1)}, bf16[64,256]{1,0:T(8,128)(2,1)S(1)}, u32[]{:S(2)}, u32[]{:S(2)}) collective-permute-start(bf16[64,256]{1,0:T(8,128)(2,1)S(1)} %get-tuple-element.33), channel_id=1, source_target_pairs={{0,1},{1,0},{2,3},{3,2},{4,5},{5,4},{6,7},{7,6},{8,9},{9,8},{10,11... | collective-permute-start | bytes 98312 | tf_op jit(solution)/shard_map/ppermute | solution.py:342
  15.4 5.0 %collective-permute-start.3 = (bf16[32,256]{1,0:T(8,128)(2,1)S(1)}, bf16[32,256]{1,0:T(8,128)(2,1)S(1)}, u32[]{:S(2)}, u32[]{:S(2)}) collective-permute-start(bf16[32,256]{1,0:T(8,128)(2,1)S(1)} %get-tuple-element.39), channel_id=1, source_target_pairs={{0,13},{1,12},{2,15},{3,14},{4,9},{5,8},{6,11},{7,10},{8,5},{9,4},... | collective-permute-start | bytes 49160 | tf_op jit(solution)/shard_map/ppermute | solution.py:342
  17.0 4.4 %collective-permute-start.4 = (bf16[32,256]{1,0:T(8,128)(2,1)S(1)}, bf16[32,256]{1,0:T(8,128)(2,1)S(1)}, u32[]{:S(2)}, u32[]{:S(2)}) collective-permute-start(bf16[32,256]{1,0:T(8,128)(2,1)S(1)} %get-tuple-element.40), channel_id=1, source_target_pairs={{0,9},{1,8},{2,11},{3,10},{4,13},{5,12},{6,15},{7,14},{8,1},{9,0},... | collective-permute-start | bytes 49160 | tf_op jit(solution)/shard_map/ppermute | solution.py:342
  17.0 4.6 %collective-permute-start.5 = (bf16[32,256]{1,0:T(8,128)(2,1)S(1)}, bf16[32,256]{1,0:T(8,128)(2,1)S(1)}, u32[]{:S(2)}, u32[]{:S(2)}) collective-permute-start(bf16[32,256]{1,0:T(8,128)(2,1)S(1)} %get-tuple-element.41), channel_id=1, source_target_pairs={{0,5},{1,4},{2,7},{3,6},{4,1},{5,0},{6,3},{7,2},{8,13},{9,12},{10,... | collective-permute-start | bytes 49160 | tf_op jit(solution)/shard_map/ppermute | solution.py:342
  21.6 3.5 %collective-permute-start.7 = (bf16[64,256]{1,0:T(8,128)(2,1)S(1)}, bf16[64,256]{1,0:T(8,128)(2,1)S(1)}, u32[]{:S(2)}, u32[]{:S(2)}) collective-permute-start(bf16[64,256]{1,0:T(8,128)(2,1)S(1)} %get-tuple-element.42.refs_1_), channel_id=1, source_target_pairs={{0,3},{1,2},{2,1},{3,0},{4,7},{5,6},{6,5},{7,4},{8,11},{9,10},{10,... | collective-permute-start | bytes 98312 | tf_op jit(solution)/shard_map/ppermute | solution.py:342
  21.7 5.0 %collective-permute-start.6 = (bf16[128,256]{1,0:T(8,128)(2,1)S(1)}, bf16[128,256]{1,0:T(8,128)(2,1)S(1)}, u32[]{:S(2)}, u32[]{:S(2)}) collective-permute-start(bf16[128,256]{1,0:T(8,128)(2,1)S(1)} %get-tuple-element.43), channel_id=1, source_target_pairs={{0,1},{1,0},{2,3},{3,2},{4,5},{5,4},{6,7},{7,6},{8,9},{9,8},{10,11... | collective-permute-start | bytes 196616 | tf_op jit(solution)/shard_map/ppermute | solution.py:342
  23.1 3.5 %collective-permute-start.9 = (bf16[64,256]{1,0:T(8,128)(2,1)S(1)}, bf16[64,256]{1,0:T(8,128)(2,1)S(1)}, u32[]{:S(2)}, u32[]{:S(2)}) collective-permute-start(bf16[64,256]{1,0:T(8,128)(2,1)S(1)} %get-tuple-element.48.refs_5_), channel_id=1, source_target_pairs={{0,3},{1,2},{2,1},{3,0},{4,7},{5,6},{6,5},{7,4},{8,11},{9,10},{10,... | collective-permute-start | bytes 98312 | tf_op jit(solution)/shard_map/ppermute | solution.py:342
  25.0 1.7 %collective-permute-start.8 = (bf16[64,256]{1,0:T(8,128)(2,1)S(1)}, bf16[64,256]{1,0:T(8,128)(2,1)S(1)}, u32[]{:S(2)}, u32[]{:S(2)}) collective-permute-start(bf16[64,256]{1,0:T(8,128)(2,1)S(1)} %collective-permute-done.7.refs_3_), channel_id=1, source_target_pairs={{0,1},{1,0},{2,3},{3,2},{4,5},{5,4},{6,7},{7,6},{8,9},{9,8},{10,11... | collective-permute-start | bytes 98312 | tf_op jit(solution)/shard_map/ppermute | solution.py:342
  26.6 1.2 %collective-permute-start.10 = (bf16[64,256]{1,0:T(8,128)(2,1)S(1)}, bf16[64,256]{1,0:T(8,128)(2,1)S(1)}, u32[]{:S(2)}, u32[]{:S(2)}) collective-permute-start(bf16[64,256]{1,0:T(8,128)(2,1)S(1)} %collective-permute-done.9.refs_7_), channel_id=1, source_target_pairs={{0,1},{1,0},{2,3},{3,2},{4,5},{5,4},{6,7},{7,6},{8,9},{9,8},{10,11... | collective-permute-start | bytes 98312 | tf_op jit(solution)/shard_map/ppermute | solution.py:342
  28.5 5.0 %collective-permute-start.11 = (bf16[32,256]{1,0:T(8,128)(2,1)S(1)}, bf16[32,256]{1,0:T(8,128)(2,1)S(1)}, u32[]{:S(2)}, u32[]{:S(2)}) collective-permute-start(bf16[32,256]{1,0:T(8,128)(2,1)S(1)} %get-tuple-element.50), channel_id=1, source_target_pairs={{0,13},{1,12},{2,15},{3,14},{4,9},{5,8},{6,11},{7,10},{8,5},{9,4},... | collective-permute-start | bytes 49160 | tf_op jit(solution)/shard_map/ppermute | solution.py:342
  30.0 4.3 %collective-permute-start.12 = (bf16[32,256]{1,0:T(8,128)(2,1)S(1)}, bf16[32,256]{1,0:T(8,128)(2,1)S(1)}, u32[]{:S(2)}, u32[]{:S(2)}) collective-permute-start(bf16[32,256]{1,0:T(8,128)(2,1)S(1)} %get-tuple-element.51), channel_id=1, source_target_pairs={{0,9},{1,8},{2,11},{3,10},{4,13},{5,12},{6,15},{7,14},{8,1},{9,0},... | collective-permute-start | bytes 49160 | tf_op jit(solution)/shard_map/ppermute | solution.py:342
  30.6 3.6 %collective-permute-start.13 = (bf16[32,256]{1,0:T(8,128)(2,1)S(1)}, bf16[32,256]{1,0:T(8,128)(2,1)S(1)}, u32[]{:S(2)}, u32[]{:S(2)}) collective-permute-start(bf16[32,256]{1,0:T(8,128)(2,1)S(1)} %get-tuple-element.52), channel_id=1, source_target_pairs={{0,5},{1,4},{2,7},{3,6},{4,1},{5,0},{6,3},{7,2},{8,13},{9,12},{10,... | collective-permute-start | bytes 49160 | tf_op jit(solution)/shard_map/ppermute | solution.py:342

commit v19 on v15

--- a/solution.py
+++ b/solution.py
@@ -110,7 +110,7 @@
 
 
 def turn(values):
-    return jnp.concatenate([values[:, SIDE:], values[:, :SIDE]], axis=1)
+    return pltpu.roll(values, SIDE, axis=1)
 
 
 def pack(strip, is_last):
@@ -295,9 +295,10 @@
             place = pl.ds(pl.multiple_of(start * width, count), count)
             return ref[place].astype(f32).reshape(some, width, channels)
 
-        inner = state(inner_ref, cols - columns) + change[k, :, : cols - columns]
-        outer = state(outer_ref, columns) + change[k, :, cols - columns :]
-        total = jnp.concatenate([outer[:, SIDE:], inner, outer[:, :SIDE]], axis=1)
+        before = jnp.concatenate(
+            [state(inner_ref, cols - columns), state(outer_ref, columns)], axis=1
+        )
+        total = pltpu.roll(before + change[k], SIDE, axis=1)
         out_ref[pl.ds(start, some)] = total.astype(bf16)
 
 

time: 35 us -> 35 us (level)
  no operation moved by 1% of the time
where the time goes in v19:
time: 35 us; the launch traced here: 34.8 us
  starting transfers between devices  18.4 us (53%)
  Pallas kernels  10 us (29%)
  waiting for transfers between devices  5.47 us (16%)
  local copies, waits for them, and re-layouts  0.75 us (2%)
    ppermute x13, starting transfers between devices, swap(): return lax.ppermute(piece, 'lon', [(j, j ^ mask) for j in range(nlon)])  11.7 us
    pallas_call x8, Pallas kernels, call(): pl.pallas_call(kernel, out_shape=shapes, in_specs=[given] * len(operands)...  10 us
    ppermute x13, waiting for transfers between devices, swap(): return lax.ppermute(piece, 'lon', [(j, j ^ mask) for j in range(nlon)])  5.46 us
    ppermute x1, starting transfers between devices, shards(): lax.ppermute(far, 'lon', [(j, (j - 1) % nlon if j % 2 == 0 else (j + 1) %...  3.78 us
    ppermute x1, starting transfers between devices, shards(): lax.ppermute(field, 'lat', [((i + s) % nlat, i) for i in range(nlat)])  2.94 us
    unnamed x4, local copies, waits for them, and re-layouts  0.75 us
  transfers between devices with their start and end apart: 15, of which 7 were waited for; matrix products, arithmetic and copies ran while one was open for 0% of the time, Pallas kernels for 16%

profile of v19, /device:TPU:0, one launch (start us, length us, event | category | flops | bytes accessed | tf_op | source)
XLA Modules:
  0.0 34.8 jit_solution(8449475292192539967)
XLA Ops:
  0.0 0.0 copy-start
  0.0 2.9 %collective-permute-start = (bf16[8,16,256]{2,1,0:T(8,128)(2,1)}, bf16[8,16,256]{2,1,0:T(8,128)(2,1)S(1)}, u32[]{:S(2)}, u32[]{:S(2)}) collective-permute-start(bf16[8,16,256]{2,1,0:T(8,128)(2,1)} %refs_0_.7), channel_id=1, source_target_pairs={{16,0},{0,16},{17,1},{1,17},{18,2},{2,18},{19,3},{3,19},{20,4},{4,... | collective-permute-start | bytes 196616 | tf_op jit(solution)/shard_map/ppermute | solution.py:348
  2.9 0.0 copy-start.1
  2.9 0.7 %copy-done.1 = bf16[7,7,256]{2,1,0:T(8,128)(2,1)S(1)} copy-done((bf16[7,7,256]{2,1,0:T(8,128)(2,1)S(1)}, bf16[7,7,256]{2,1,0:T(8,128)(2,1)}, u32[]{:S(2)}) %copy-start.1) | copy-done | bytes 25112
  3.7 1.8 %shard_map.64 = (bf16[256,1024]{1,0:T(8,128)(2,1)S(1)}, bf16[1024,256]{1,0:T(8,128)(2,1)S(1)}, bf16[4,256,256]{2,1,0:T(8,128)(2,1)S(1)}, bf16[4,256,256]{2,1,0:T(8,128)(2,1)S(1)}, f32[7,7,256]{2,1,0:T(8,128)S(1)}) custom-call(bf16[256,1024]{1,0:T(8,128)(2,1)} %refs_0_.4, bf16[1024,256]{1,0:T(8,128)(2,1)} %refs_1_.1, bf16[4,256,256]{2,1,0:T(8,128)(2,1)} %refs_2_.1, ...), custom_call_target="tpu_custom_call" | custom-call | bytes 2122240 | tf_op jit(solution)/shard_map/pallas_call | solution.py:315
  5.5 0.0 collective-permute-done.refs_1_
  5.5 0.0 copy-done
  5.5 0.1 shard_map.65
  5.6 3.8 %collective-permute-start.1 = (bf16[64,256]{1,0:T(8,128)(2,1)S(1)}, bf16[64,256]{1,0:T(8,128)(2,1)S(1)}, u32[]{:S(2)}, u32[]{:S(2)}) collective-permute-start(bf16[64,256]{1,0:T(8,128)(2,1)S(1)} %get-tuple-element.31), channel_id=1, source_target_pairs={{0,15},{1,2},{2,1},{3,4},{4,3},{5,6},{6,5},{7,8},{8,7},{9,10},{10,... | collective-permute-start | bytes 98312 | tf_op jit(solution)/shard_map/ppermute | solution.py:370
  9.4 0.0 collective-permute-start.2
  9.4 3.2 %shard_map.66 = (bf16[64,256]{1,0:T(8,128)(2,1)S(1)}, bf16[64,256]{1,0:T(8,128)(2,1)S(1)}) custom-call(bf16[8,16,256]{2,1,0:T(8,128)(2,1)S(1)} %copy-done, bf16[8,16,256]{2,1,0:T(8,128)(2,1)S(1)} %collective-permute-done.refs_1_, f32[7,7,256]{2,1,0:T(8,128)S(1)} %get-tuple-element.33.refs_2_.refs_5_, ...), custom_call_target="tpu_custom_call" | custom-call | flops 134217728 | bytes 1754112 | tf_op jit(solution)/shard_map/pallas_call | solution.py:315
  12.6 0.0 collective-permute-done.1.refs_2_
  12.6 0.0 collective-permute-done.2.refs_3_
  12.6 2.8 %shard_map.67 = (bf16[64,256]{1,0:T(8,128)(2,1)S(1)}, bf16[32,256]{1,0:T(8,128)(2,1)S(1)}, bf16[32,256]{1,0:T(8,128)(2,1)S(1)}, bf16[32,256]{1,0:T(8,128)(2,1)S(1)}, bf16[32,256]{1,0:T(8,128)(2,1)S(1)}) custom-call(bf16[8,16,256]{2,1,0:T(8,128)(2,1)S(1)} %copy-done, bf16[8,16,256]{2,1,0:T(8,128)(2,1)S(1)} %collective-permute-done.refs_1_, ...), custom_call_target="tpu_custom_call" | custom-call | flops 134217728 | bytes 1852416 | tf_op jit(solution)/shard_map/pallas_call | solution.py:315
  15.4 1.6 %collective-permute-start.3 = (bf16[32,256]{1,0:T(8,128)(2,1)S(1)}, bf16[32,256]{1,0:T(8,128)(2,1)S(1)}, u32[]{:S(2)}, u32[]{:S(2)}) collective-permute-start(bf16[32,256]{1,0:T(8,128)(2,1)S(1)} %get-tuple-element.38), channel_id=1, source_target_pairs={{0,13},{1,12},{2,15},{3,14},{4,9},{5,8},{6,11},{7,10},{8,5},{9,4},... | collective-permute-start | bytes 49160 | tf_op jit(solution)/shard_map/ppermute | solution.py:337
  17.0 0.0 collective-permute-start.4
  17.0 2.7 %collective-permute-start.5 = (bf16[32,256]{1,0:T(8,128)(2,1)S(1)}, bf16[32,256]{1,0:T(8,128)(2,1)S(1)}, u32[]{:S(2)}, u32[]{:S(2)}) collective-permute-start(bf16[32,256]{1,0:T(8,128)(2,1)S(1)} %get-tuple-element.40), channel_id=1, source_target_pairs={{0,5},{1,4},{2,7},{3,6},{4,1},{5,0},{6,3},{7,2},{8,13},{9,12},{10,... | collective-permute-start | bytes 49160 | tf_op jit(solution)/shard_map/ppermute | solution.py:337
  19.7 0.7 %collective-permute-done.3.refs_1_ = bf16[32,256]{1,0:T(8,128)(2,1)S(1)} collective-permute-done((bf16[32,256]{1,0:T(8,128)(2,1)S(1)}, bf16[32,256]{1,0:T(8,128)(2,1)S(1)}, u32[]{:S(2)}, u32[]{:S(2)}) %collective-permute-start.3) | collective-permute-done | bytes 16416 | tf_op jit(solution)/shard_map/ppermute | solution.py:337
  20.4 1.0 %collective-permute-done.4.refs_2_ = bf16[32,256]{1,0:T(8,128)(2,1)S(1)} collective-permute-done((bf16[32,256]{1,0:T(8,128)(2,1)S(1)}, bf16[32,256]{1,0:T(8,128)(2,1)S(1)}, u32[]{:S(2)}, u32[]{:S(2)}) %collective-permute-start.4) | collective-permute-done | bytes 16416 | tf_op jit(solution)/shard_map/ppermute | solution.py:337
  21.4 0.2 collective-permute-done.5.refs_3_
  21.6 0.0 collective-permute-start.6
  21.6 1.8 %collective-permute-start.9 = (bf16[64,256]{1,0:T(8,128)(2,1)S(1)}, bf16[64,256]{1,0:T(8,128)(2,1)S(1)}, u32[]{:S(2)}, u32[]{:S(2)}) collective-permute-start(bf16[64,256]{1,0:T(8,128)(2,1)S(1)} %get-tuple-element.46.refs_5_), channel_id=1, source_target_pairs={{0,3},{1,2},{2,1},{3,0},{4,7},{5,6},{6,5},{7,4},{8,11},{9,10},{10,... | collective-permute-start | bytes 98312 | tf_op jit(solution)/shard_map/ppermute | solution.py:337
  23.4 0.1 collective-permute-start.7
  23.4 1.5 %collective-permute-done.6.refs_2_ = bf16[64,256]{1,0:T(8,128)(2,1)S(1)} collective-permute-done((bf16[64,256]{1,0:T(8,128)(2,1)S(1)}, bf16[64,256]{1,0:T(8,128)(2,1)S(1)}, u32[]{:S(2)}, u32[]{:S(2)}) %collective-permute-start.6) | collective-permute-done | bytes 32800 | tf_op jit(solution)/shard_map/ppermute | solution.py:337
  25.0 0.7 %collective-permute-start.8 = (bf16[64,256]{1,0:T(8,128)(2,1)S(1)}, bf16[64,256]{1,0:T(8,128)(2,1)S(1)}, u32[]{:S(2)}, u32[]{:S(2)}) collective-permute-start(bf16[64,256]{1,0:T(8,128)(2,1)S(1)} %collective-permute-done.6.refs_2_), channel_id=1, source_target_pairs={{0,1},{1,0},{2,3},{3,2},{4,5},{5,4},{6,7},{7,6},{8,9},{9,8},{10,11... | collective-permute-start | bytes 98312 | tf_op jit(solution)/shard_map/ppermute | solution.py:337
  25.7 0.0 collective-permute-start.10
  25.7 0.0 collective-permute-done.9.refs_6_
  25.7 0.7 %collective-permute-start.11 = (bf16[64,256]{1,0:T(8,128)(2,1)S(1)}, bf16[64,256]{1,0:T(8,128)(2,1)S(1)}, u32[]{:S(2)}, u32[]{:S(2)}) collective-permute-start(bf16[64,256]{1,0:T(8,128)(2,1)S(1)} %collective-permute-done.9.refs_6_), channel_id=1, source_target_pairs={{0,1},{1,0},{2,3},{3,2},{4,5},{5,4},{6,7},{7,6},{8,9},{9,8},{10,11... | collective-permute-start | bytes 98312 | tf_op jit(solution)/shard_map/ppermute | solution.py:337
  26.4 0.0 collective-permute-done.7.refs_3_
  26.4 0.1 collective-permute-done.8.refs_4_
  26.5 0.7 %shard_map.69 = (bf16[16,256]{1,0:T(8,128)(2,1)S(1)}, bf16[16,256]{1,0:T(8,128)(2,1)S(1)}, bf16[16,256]{1,0:T(8,128)(2,1)S(1)}, bf16[16,256]{1,0:T(8,128)(2,1)S(1)}) custom-call(bf16[4,256,256]{2,1,0:T(8,128)(2,1)S(1)} %get-tuple-element.29.refs_0_.refs_6_, bf16[64,256]{1,0:T(8,128)(2,1)S(1)} %get-tuple-element.41.refs_1_, ...), custom_call_target="tpu_custom_call" | custom-call | flops 33554432 | bytes 655360 | tf_op jit(solution)/shard_map/pallas_call | solution.py:315
  27.2 0.0 collective-permute-done.10.refs_7_
  27.2 0.0 collective-permute-done.11.refs_8_
  27.3 0.7 %shard_map.70 = (bf16[32,256]{1,0:T(8,128)(2,1)S(1)}, bf16[32,256]{1,0:T(8,128)(2,1)S(1)}, bf16[32,256]{1,0:T(8,128)(2,1)S(1)}, bf16[32,256]{1,0:T(8,128)(2,1)S(1)}) custom-call(bf16[4,256,256]{2,1,0:T(8,128)(2,1)S(1)} %get-tuple-element.29.refs_0_.refs_6_, bf16[16,256]{1,0:T(8,128)(2,1)S(1)} %get-tuple-element.42.refs_1_, ...), custom_call_target="tpu_custom_call" | custom-call | flops 33554432 | bytes 688128 | tf_op jit(solution)/shard_map/pallas_call | solution.py:315
  28.0 1.9 %collective-permute-start.12 = (bf16[32,256]{1,0:T(8,128)(2,1)S(1)}, bf16[32,256]{1,0:T(8,128)(2,1)S(1)}, u32[]{:S(2)}, u32[]{:S(2)}) collective-permute-start(bf16[32,256]{1,0:T(8,128)(2,1)S(1)} %get-tuple-element.48), channel_id=1, source_target_pairs={{0,13},{1,12},{2,15},{3,14},{4,9},{5,8},{6,11},{7,10},{8,5},{9,4},... | collective-permute-start | bytes 49160 | tf_op jit(solution)/shard_map/ppermute | solution.py:337
  29.9 0.2 collective-permute-start.13
  30.1 2.0 %collective-permute-start.14 = (bf16[32,256]{1,0:T(8,128)(2,1)S(1)}, bf16[32,256]{1,0:T(8,128)(2,1)S(1)}, u32[]{:S(2)}, u32[]{:S(2)}) collective-permute-start(bf16[32,256]{1,0:T(8,128)(2,1)S(1)} %get-tuple-element.50), channel_id=1, source_target_pairs={{0,5},{1,4},{2,7},{3,6},{4,1},{5,0},{6,3},{7,2},{8,13},{9,12},{10,... | collective-permute-start | bytes 49160 | tf_op jit(solution)/shard_map/ppermute | solution.py:337
  32.1 0.9 %collective-permute-done.12.refs_1_ = bf16[32,256]{1,0:T(8,128)(2,1)S(1)} collective-permute-done((bf16[32,256]{1,0:T(8,128)(2,1)S(1)}, bf16[32,256]{1,0:T(8,128)(2,1)S(1)}, u32[]{:S(2)}, u32[]{:S(2)}) %collective-permute-start.12) | collective-permute-done | bytes 16416 | tf_op jit(solution)/shard_map/ppermute | solution.py:337
  33.0 1.0 %collective-permute-done.13.refs_2_ = bf16[32,256]{1,0:T(8,128)(2,1)S(1)} collective-permute-done((bf16[32,256]{1,0:T(8,128)(2,1)S(1)}, bf16[32,256]{1,0:T(8,128)(2,1)S(1)}, u32[]{:S(2)}, u32[]{:S(2)}) %collective-permute-start.13) | collective-permute-done | bytes 16416 | tf_op jit(solution)/shard_map/ppermute | solution.py:337
  34.0 0.0 collective-permute-done.14.refs_3_
  34.0 0.8 %shard_map.71 = bf16[8,16,256]{2,1,0:T(8,128)(2,1)} custom-call(bf16[32,256]{1,0:T(8,128)(2,1)S(1)} %get-tuple-element.47.refs_0_, bf16[32,256]{1,0:T(8,128)(2,1)S(1)} %collective-permute-done.12.refs_1_, bf16[32,256]{1,0:T(8,128)(2,1)S(1)} %collective-permute-done.13.refs_2_, bf16[32,256]{1,0:T(8,128)(2,1)S(1)} %collective-permute-done.14.refs_3_, ...), custom_call_target="tpu_custom_call" | custom-call | bytes 655360 | tf_op jit(solution)/shard_map/pallas_call | solution.py:315
  (1 shorter events, 0.0 us)
Async XLA Ops:
  0.0 5.5 %copy-start = (bf16[8,16,256]{2,1,0:T(8,128)(2,1)S(1)}, bf16[8,16,256]{2,1,0:T(8,128)(2,1)}, u32[]{:S(2)}) copy-start(bf16[8,16,256]{2,1,0:T(8,128)(2,1)} %refs_0_.7) | copy-start | bytes 196612
  0.0 5.5 %collective-permute-start = (bf16[8,16,256]{2,1,0:T(8,128)(2,1)}, bf16[8,16,256]{2,1,0:T(8,128)(2,1)S(1)}, u32[]{:S(2)}, u32[]{:S(2)}) collective-permute-start(bf16[8,16,256]{2,1,0:T(8,128)(2,1)} %refs_0_.7), channel_id=1, source_target_pairs={{16,0},{0,16},{17,1},{1,17},{18,2},{2,18},{19,3},{3,19},{20,4},{4,... | collective-permute-start | bytes 196616 | tf_op jit(solution)/shard_map/ppermute | solution.py:348
  2.9 0.7 %copy-start.1 = (bf16[7,7,256]{2,1,0:T(8,128)(2,1)S(1)}, bf16[7,7,256]{2,1,0:T(8,128)(2,1)}, u32[]{:S(2)}) copy-start(bf16[7,7,256]{2,1,0:T(8,128)(2,1)} %refs_4_.1) | copy-start | bytes 75268
  5.6 7.0 %collective-permute-start.1 = (bf16[64,256]{1,0:T(8,128)(2,1)S(1)}, bf16[64,256]{1,0:T(8,128)(2,1)S(1)}, u32[]{:S(2)}, u32[]{:S(2)}) collective-permute-start(bf16[64,256]{1,0:T(8,128)(2,1)S(1)} %get-tuple-element.31), channel_id=1, source_target_pairs={{0,15},{1,2},{2,1},{3,4},{4,3},{5,6},{6,5},{7,8},{8,7},{9,10},{10,... | collective-permute-start | bytes 98312 | tf_op jit(solution)/shard_map/ppermute | solution.py:370
  9.4 3.2 %collective-permute-start.2 = (bf16[64,256]{1,0:T(8,128)(2,1)S(1)}, bf16[64,256]{1,0:T(8,128)(2,1)S(1)}, u32[]{:S(2)}, u32[]{:S(2)}) collective-permute-start(bf16[64,256]{1,0:T(8,128)(2,1)S(1)} %get-tuple-element.32), channel_id=1, source_target_pairs={{0,1},{1,0},{2,3},{3,2},{4,5},{5,4},{6,7},{7,6},{8,9},{9,8},{10,11... | collective-permute-start | bytes 98312 | tf_op jit(solution)/shard_map/ppermute | solution.py:337
  15.4 5.0 %collective-permute-start.3 = (bf16[32,256]{1,0:T(8,128)(2,1)S(1)}, bf16[32,256]{1,0:T(8,128)(2,1)S(1)}, u32[]{:S(2)}, u32[]{:S(2)}) collective-permute-start(bf16[32,256]{1,0:T(8,128)(2,1)S(1)} %get-tuple-element.38), channel_id=1, source_target_pairs={{0,13},{1,12},{2,15},{3,14},{4,9},{5,8},{6,11},{7,10},{8,5},{9,4},... | collective-permute-start | bytes 49160 | tf_op jit(solution)/shard_map/ppermute | solution.py:337
  17.0 4.4 %collective-permute-start.4 = (bf16[32,256]{1,0:T(8,128)(2,1)S(1)}, bf16[32,256]{1,0:T(8,128)(2,1)S(1)}, u32[]{:S(2)}, u32[]{:S(2)}) collective-permute-start(bf16[32,256]{1,0:T(8,128)(2,1)S(1)} %get-tuple-element.39), channel_id=1, source_target_pairs={{0,9},{1,8},{2,11},{3,10},{4,13},{5,12},{6,15},{7,14},{8,1},{9,0},... | collective-permute-start | bytes 49160 | tf_op jit(solution)/shard_map/ppermute | solution.py:337
  17.0 4.6 %collective-permute-start.5 = (bf16[32,256]{1,0:T(8,128)(2,1)S(1)}, bf16[32,256]{1,0:T(8,128)(2,1)S(1)}, u32[]{:S(2)}, u32[]{:S(2)}) collective-permute-start(bf16[32,256]{1,0:T(8,128)(2,1)S(1)} %get-tuple-element.40), channel_id=1, source_target_pairs={{0,5},{1,4},{2,7},{3,6},{4,1},{5,0},{6,3},{7,2},{8,13},{9,12},{10,... | collective-permute-start | bytes 49160 | tf_op jit(solution)/shard_map/ppermute | solution.py:337
  21.6 3.4 %collective-permute-start.6 = (bf16[64,256]{1,0:T(8,128)(2,1)S(1)}, bf16[64,256]{1,0:T(8,128)(2,1)S(1)}, u32[]{:S(2)}, u32[]{:S(2)}) collective-permute-start(bf16[64,256]{1,0:T(8,128)(2,1)S(1)} %get-tuple-element.41.refs_1_), channel_id=1, source_target_pairs={{0,3},{1,2},{2,1},{3,0},{4,7},{5,6},{6,5},{7,4},{8,11},{9,10},{10,... | collective-permute-start | bytes 98312 | tf_op jit(solution)/shard_map/ppermute | solution.py:337
  21.6 4.1 %collective-permute-start.9 = (bf16[64,256]{1,0:T(8,128)(2,1)S(1)}, bf16[64,256]{1,0:T(8,128)(2,1)S(1)}, u32[]{:S(2)}, u32[]{:S(2)}) collective-permute-start(bf16[64,256]{1,0:T(8,128)(2,1)S(1)} %get-tuple-element.46.refs_5_), channel_id=1, source_target_pairs={{0,3},{1,2},{2,1},{3,0},{4,7},{5,6},{6,5},{7,4},{8,11},{9,10},{10,... | collective-permute-start | bytes 98312 | tf_op jit(solution)/shard_map/ppermute | solution.py:337
  23.4 3.1 %collective-permute-start.7 = (bf16[64,256]{1,0:T(8,128)(2,1)S(1)}, bf16[64,256]{1,0:T(8,128)(2,1)S(1)}, u32[]{:S(2)}, u32[]{:S(2)}) collective-permute-start(bf16[64,256]{1,0:T(8,128)(2,1)S(1)} %get-tuple-element.41.refs_1_), channel_id=1, source_target_pairs={{0,1},{1,0},{2,3},{3,2},{4,5},{5,4},{6,7},{7,6},{8,9},{9,8},{10,11... | collective-permute-start | bytes 98312 | tf_op jit(solution)/shard_map/ppermute | solution.py:337
  25.0 1.6 %collective-permute-start.8 = (bf16[64,256]{1,0:T(8,128)(2,1)S(1)}, bf16[64,256]{1,0:T(8,128)(2,1)S(1)}, u32[]{:S(2)}, u32[]{:S(2)}) collective-permute-start(bf16[64,256]{1,0:T(8,128)(2,1)S(1)} %collective-permute-done.6.refs_2_), channel_id=1, source_target_pairs={{0,1},{1,0},{2,3},{3,2},{4,5},{5,4},{6,7},{7,6},{8,9},{9,8},{10,11... | collective-permute-start | bytes 98312 | tf_op jit(solution)/shard_map/ppermute | solution.py:337
  25.7 1.6 %collective-permute-start.10 = (bf16[64,256]{1,0:T(8,128)(2,1)S(1)}, bf16[64,256]{1,0:T(8,128)(2,1)S(1)}, u32[]{:S(2)}, u32[]{:S(2)}) collective-permute-start(bf16[64,256]{1,0:T(8,128)(2,1)S(1)} %get-tuple-element.46.refs_5_), channel_id=1, source_target_pairs={{0,1},{1,0},{2,3},{3,2},{4,5},{5,4},{6,7},{7,6},{8,9},{9,8},{10,11... | collective-permute-start | bytes 98312 | tf_op jit(solution)/shard_map/ppermute | solution.py:337
  25.7 1.6 %collective-permute-start.11 = (bf16[64,256]{1,0:T(8,128)(2,1)S(1)}, bf16[64,256]{1,0:T(8,128)(2,1)S(1)}, u32[]{:S(2)}, u32[]{:S(2)}) collective-permute-start(bf16[64,256]{1,0:T(8,128)(2,1)S(1)} %collective-permute-done.9.refs_6_), channel_id=1, source_target_pairs={{0,1},{1,0},{2,3},{3,2},{4,5},{5,4},{6,7},{7,6},{8,9},{9,8},{10,11... | collective-permute-start | bytes 98312 | tf_op jit(solution)/shard_map/ppermute | solution.py:337
  28.0 5.0 %collective-permute-start.12 = (bf16[32,256]{1,0:T(8,128)(2,1)S(1)}, bf16[32,256]{1,0:T(8,128)(2,1)S(1)}, u32[]{:S(2)}, u32[]{:S(2)}) collective-permute-start(bf16[32,256]{1,0:T(8,128)(2,1)S(1)} %get-tuple-element.48), channel_id=1, source_target_pairs={{0,13},{1,12},{2,15},{3,14},{4,9},{5,8},{6,11},{7,10},{8,5},{9,4},... | collective-permute-start | bytes 49160 | tf_op jit(solution)/shard_map/ppermute | solution.py:337
  29.9 4.1 %collective-permute-start.13 = (bf16[32,256]{1,0:T(8,128)(2,1)S(1)}, bf16[32,256]{1,0:T(8,128)(2,1)S(1)}, u32[]{:S(2)}, u32[]{:S(2)}) collective-permute-start(bf16[32,256]{1,0:T(8,128)(2,1)S(1)} %get-tuple-element.49), channel_id=1, source_target_pairs={{0,9},{1,8},{2,11},{3,10},{4,13},{5,12},{6,15},{7,14},{8,1},{9,0},... | collective-permute-start | bytes 49160 | tf_op jit(solution)/shard_map/ppermute | solution.py:337
  30.1 3.9 %collective-permute-start.14 = (bf16[32,256]{1,0:T(8,128)(2,1)S(1)}, bf16[32,256]{1,0:T(8,128)(2,1)S(1)}, u32[]{:S(2)}, u32[]{:S(2)}) collective-permute-start(bf16[32,256]{1,0:T(8,128)(2,1)S(1)} %get-tuple-element.50), channel_id=1, source_target_pairs={{0,5},{1,4},{2,7},{3,6},{4,1},{5,0},{6,3},{7,2},{8,13},{9,12},{10,... | collective-permute-start | bytes 49160 | tf_op jit(solution)/shard_map/ppermute | solution.py:337

commit v20 on v19

--- a/solution.py
+++ b/solution.py
@@ -85,9 +85,13 @@
     taps_ref[...] = dw[...].astype(f32)
 
 
+def hops_of(levels):
+    return [0] + [h for h in (*range(levels // 2, levels), *range(1, levels // 2)) if h]
+
+
 def peer(levels, k):
     level = lax.axis_index("lon") // (lax.axis_size("lon") // levels)
-    return level ^ ((levels - k) % levels)
+    return level ^ hops_of(levels)[k]
 
 
 def strip_kernel(nlat, *refs):
@@ -337,11 +341,11 @@
         return lax.ppermute(piece, "lon", [(j, j ^ mask) for j in range(nlon)])
 
     def exchange(pieces):
-        moved = []
-        for k in range(1, levels):
-            level = levels - k
-            moved.append(swap(pieces[k], level * column + min(1, column - 1)))
-        return [pieces[0]] + moved
+        cross = min(1, column - 1)
+        return [
+            swap(piece, hops * column + cross) if hops else piece
+            for piece, hops in zip(pieces, hops_of(levels))
+        ]
 
     tiles = [field]
     for s in range(1, nlat):

time: 35 us -> 34.9 us (level)
  starting transfers between devices: 18.4 us -> 16 us
  waiting for transfers between devices: 5.47 us -> 7.79 us
    ppermute x13, starting transfers between devices: 11.7 us -> 9.32 us  [swap(): return lax.ppermute(piece, 'lon', [(j, j ^ mask) for j in range(nlon)])]
    ppermute x13, waiting for transfers between devices: 5.46 us -> 7.78 us  [swap(): return lax.ppermute(piece, 'lon', [(j, j ^ mask) for j in range(nlon)])]
where the time goes in v20:
time: 34.9 us; the launch traced here: 34.7 us
  starting transfers between devices  16 us (46%)
  Pallas kernels  10 us (29%)
  waiting for transfers between devices  7.79 us (22%)
  local copies, waits for them, and re-layouts  0.75 us (2%)
    pallas_call x8, Pallas kernels, call(): pl.pallas_call(kernel, out_shape=shapes, in_specs=[given] * len(operands)...  10 us
    ppermute x13, starting transfers between devices, swap(): return lax.ppermute(piece, 'lon', [(j, j ^ mask) for j in range(nlon)])  9.32 us
    ppermute x13, waiting for transfers between devices, swap(): return lax.ppermute(piece, 'lon', [(j, j ^ mask) for j in range(nlon)])  7.78 us
    ppermute x1, starting transfers between devices, shards(): lax.ppermute(far, 'lon', [(j, (j - 1) % nlon if j % 2 == 0 else (j + 1) %...  3.78 us
    ppermute x1, starting transfers between devices, shards(): lax.ppermute(field, 'lat', [((i + s) % nlat, i) for i in range(nlat)])  2.94 us
    unnamed x4, local copies, waits for them, and re-layouts  0.75 us
  transfers between devices with their start and end apart: 15, of which 7 were waited for; matrix products, arithmetic and copies ran while one was open for 0% of the time, Pallas kernels for 16%

profile of v20, /device:TPU:0, one launch (start us, length us, event | category | flops | bytes accessed | tf_op | source)
XLA Modules:
  0.0 34.7 jit_solution(8501831579584784841)
XLA Ops:
  0.0 0.0 copy-start
  0.0 2.9 %collective-permute-start = (bf16[8,16,256]{2,1,0:T(8,128)(2,1)}, bf16[8,16,256]{2,1,0:T(8,128)(2,1)S(1)}, u32[]{:S(2)}, u32[]{:S(2)}) collective-permute-start(bf16[8,16,256]{2,1,0:T(8,128)(2,1)} %refs_0_.7), channel_id=1, source_target_pairs={{16,0},{0,16},{17,1},{1,17},{18,2},{2,18},{19,3},{3,19},{20,4},{4,... | collective-permute-start | bytes 196616 | tf_op jit(solution)/shard_map/ppermute | solution.py:352
  2.9 0.0 copy-start.1
  2.9 0.7 %copy-done.1 = bf16[7,7,256]{2,1,0:T(8,128)(2,1)S(1)} copy-done((bf16[7,7,256]{2,1,0:T(8,128)(2,1)S(1)}, bf16[7,7,256]{2,1,0:T(8,128)(2,1)}, u32[]{:S(2)}) %copy-start.1) | copy-done | bytes 25112
  3.7 1.8 %shard_map.64 = (bf16[256,1024]{1,0:T(8,128)(2,1)S(1)}, bf16[1024,256]{1,0:T(8,128)(2,1)S(1)}, bf16[4,256,256]{2,1,0:T(8,128)(2,1)S(1)}, bf16[4,256,256]{2,1,0:T(8,128)(2,1)S(1)}, f32[7,7,256]{2,1,0:T(8,128)S(1)}) custom-call(bf16[256,1024]{1,0:T(8,128)(2,1)} %refs_0_.4, bf16[1024,256]{1,0:T(8,128)(2,1)} %refs_1_.1, bf16[4,256,256]{2,1,0:T(8,128)(2,1)} %refs_2_.1, ...), custom_call_target="tpu_custom_call" | custom-call | bytes 2122240 | tf_op jit(solution)/shard_map/pallas_call | solution.py:319
  5.5 0.0 collective-permute-done.refs_1_
  5.5 0.0 copy-done
  5.5 0.1 shard_map.65
  5.6 3.8 %collective-permute-start.1 = (bf16[64,256]{1,0:T(8,128)(2,1)S(1)}, bf16[64,256]{1,0:T(8,128)(2,1)S(1)}, u32[]{:S(2)}, u32[]{:S(2)}) collective-permute-start(bf16[64,256]{1,0:T(8,128)(2,1)S(1)} %get-tuple-element.31), channel_id=1, source_target_pairs={{0,15},{1,2},{2,1},{3,4},{4,3},{5,6},{6,5},{7,8},{8,7},{9,10},{10,... | collective-permute-start | bytes 98312 | tf_op jit(solution)/shard_map/ppermute | solution.py:374
  9.4 0.0 collective-permute-start.2
  9.4 3.2 %shard_map.66 = (bf16[64,256]{1,0:T(8,128)(2,1)S(1)}, bf16[64,256]{1,0:T(8,128)(2,1)S(1)}) custom-call(bf16[8,16,256]{2,1,0:T(8,128)(2,1)S(1)} %copy-done, bf16[8,16,256]{2,1,0:T(8,128)(2,1)S(1)} %collective-permute-done.refs_1_, f32[7,7,256]{2,1,0:T(8,128)S(1)} %get-tuple-element.33.refs_2_.refs_5_, ...), custom_call_target="tpu_custom_call" | custom-call | flops 134217728 | bytes 1754112 | tf_op jit(solution)/shard_map/pallas_call | solution.py:319
  12.6 0.0 collective-permute-done.1.refs_2_
  12.6 0.0 collective-permute-done.2.refs_3_
  12.6 2.8 %shard_map.67 = (bf16[64,256]{1,0:T(8,128)(2,1)S(1)}, bf16[32,256]{1,0:T(8,128)(2,1)S(1)}, bf16[32,256]{1,0:T(8,128)(2,1)S(1)}, bf16[32,256]{1,0:T(8,128)(2,1)S(1)}, bf16[32,256]{1,0:T(8,128)(2,1)S(1)}) custom-call(bf16[8,16,256]{2,1,0:T(8,128)(2,1)S(1)} %copy-done, bf16[8,16,256]{2,1,0:T(8,128)(2,1)S(1)} %collective-permute-done.refs_1_, ...), custom_call_target="tpu_custom_call" | custom-call | flops 134217728 | bytes 1852416 | tf_op jit(solution)/shard_map/pallas_call | solution.py:319
  15.4 0.6 %collective-permute-start.3 = (bf16[32,256]{1,0:T(8,128)(2,1)S(1)}, bf16[32,256]{1,0:T(8,128)(2,1)S(1)}, u32[]{:S(2)}, u32[]{:S(2)}) collective-permute-start(bf16[32,256]{1,0:T(8,128)(2,1)S(1)} %get-tuple-element.38), channel_id=1, source_target_pairs={{0,9},{1,8},{2,11},{3,10},{4,13},{5,12},{6,15},{7,14},{8,1},{9,0},... | collective-permute-start | bytes 49160 | tf_op jit(solution)/shard_map/ppermute | solution.py:341
  16.0 1.5 %collective-permute-start.4 = (bf16[32,256]{1,0:T(8,128)(2,1)S(1)}, bf16[32,256]{1,0:T(8,128)(2,1)S(1)}, u32[]{:S(2)}, u32[]{:S(2)}) collective-permute-start(bf16[32,256]{1,0:T(8,128)(2,1)S(1)} %get-tuple-element.39), channel_id=1, source_target_pairs={{0,13},{1,12},{2,15},{3,14},{4,9},{5,8},{6,11},{7,10},{8,5},{9,4},... | collective-permute-start | bytes 49160 | tf_op jit(solution)/shard_map/ppermute | solution.py:341
  17.5 1.3 %collective-permute-start.5 = (bf16[32,256]{1,0:T(8,128)(2,1)S(1)}, bf16[32,256]{1,0:T(8,128)(2,1)S(1)}, u32[]{:S(2)}, u32[]{:S(2)}) collective-permute-start(bf16[32,256]{1,0:T(8,128)(2,1)S(1)} %get-tuple-element.40), channel_id=1, source_target_pairs={{0,5},{1,4},{2,7},{3,6},{4,1},{5,0},{6,3},{7,2},{8,13},{9,12},{10,... | collective-permute-start | bytes 49160 | tf_op jit(solution)/shard_map/ppermute | solution.py:341
  18.8 0.7 %collective-permute-done.3.refs_1_ = bf16[32,256]{1,0:T(8,128)(2,1)S(1)} collective-permute-done((bf16[32,256]{1,0:T(8,128)(2,1)S(1)}, bf16[32,256]{1,0:T(8,128)(2,1)S(1)}, u32[]{:S(2)}, u32[]{:S(2)}) %collective-permute-start.3) | collective-permute-done | bytes 16416 | tf_op jit(solution)/shard_map/ppermute | solution.py:341
  19.5 1.6 %collective-permute-done.4.refs_2_ = bf16[32,256]{1,0:T(8,128)(2,1)S(1)} collective-permute-done((bf16[32,256]{1,0:T(8,128)(2,1)S(1)}, bf16[32,256]{1,0:T(8,128)(2,1)S(1)}, u32[]{:S(2)}, u32[]{:S(2)}) %collective-permute-start.4) | collective-permute-done | bytes 16416 | tf_op jit(solution)/shard_map/ppermute | solution.py:341
  21.1 0.0 collective-permute-done.5.refs_3_
  21.1 1.6 %collective-permute-start.6 = (bf16[64,256]{1,0:T(8,128)(2,1)S(1)}, bf16[64,256]{1,0:T(8,128)(2,1)S(1)}, u32[]{:S(2)}, u32[]{:S(2)}) collective-permute-start(bf16[64,256]{1,0:T(8,128)(2,1)S(1)} %get-tuple-element.41.refs_1_), channel_id=1, source_target_pairs={{0,3},{1,2},{2,1},{3,0},{4,7},{5,6},{6,5},{7,4},{8,11},{9,10},{10,... | collective-permute-start | bytes 98312 | tf_op jit(solution)/shard_map/ppermute | solution.py:341
  22.7 0.2 collective-permute-start.9
  22.9 0.5 %collective-permute-start.7 = (bf16[64,256]{1,0:T(8,128)(2,1)S(1)}, bf16[64,256]{1,0:T(8,128)(2,1)S(1)}, u32[]{:S(2)}, u32[]{:S(2)}) collective-permute-start(bf16[64,256]{1,0:T(8,128)(2,1)S(1)} %get-tuple-element.41.refs_1_), channel_id=1, source_target_pairs={{0,1},{1,0},{2,3},{3,2},{4,5},{5,4},{6,7},{7,6},{8,9},{9,8},{10,11... | collective-permute-start | bytes 98312 | tf_op jit(solution)/shard_map/ppermute | solution.py:341
  23.4 1.1 %collective-permute-done.6.refs_2_ = bf16[64,256]{1,0:T(8,128)(2,1)S(1)} collective-permute-done((bf16[64,256]{1,0:T(8,128)(2,1)S(1)}, bf16[64,256]{1,0:T(8,128)(2,1)S(1)}, u32[]{:S(2)}, u32[]{:S(2)}) %collective-permute-start.6) | collective-permute-done | bytes 32800 | tf_op jit(solution)/shard_map/ppermute | solution.py:341
  24.5 0.5 %collective-permute-start.8 = (bf16[64,256]{1,0:T(8,128)(2,1)S(1)}, bf16[64,256]{1,0:T(8,128)(2,1)S(1)}, u32[]{:S(2)}, u32[]{:S(2)}) collective-permute-start(bf16[64,256]{1,0:T(8,128)(2,1)S(1)} %collective-permute-done.6.refs_2_), channel_id=1, source_target_pairs={{0,1},{1,0},{2,3},{3,2},{4,5},{5,4},{6,7},{7,6},{8,9},{9,8},{10,11... | collective-permute-start | bytes 98312 | tf_op jit(solution)/shard_map/ppermute | solution.py:341
  25.0 0.1 collective-permute-start.10
  25.0 1.1 %collective-permute-done.9.refs_6_ = bf16[64,256]{1,0:T(8,128)(2,1)S(1)} collective-permute-done((bf16[64,256]{1,0:T(8,128)(2,1)S(1)}, bf16[64,256]{1,0:T(8,128)(2,1)S(1)}, u32[]{:S(2)}, u32[]{:S(2)}) %collective-permute-start.9) | collective-permute-done | bytes 32800 | tf_op jit(solution)/shard_map/ppermute | solution.py:341
  26.1 0.1 collective-permute-start.11
  26.3 0.0 collective-permute-done.7.refs_3_
  26.3 0.0 collective-permute-done.8.refs_4_
  26.3 0.7 %shard_map.69 = (bf16[16,256]{1,0:T(8,128)(2,1)S(1)}, bf16[16,256]{1,0:T(8,128)(2,1)S(1)}, bf16[16,256]{1,0:T(8,128)(2,1)S(1)}, bf16[16,256]{1,0:T(8,128)(2,1)S(1)}) custom-call(bf16[4,256,256]{2,1,0:T(8,128)(2,1)S(1)} %get-tuple-element.29.refs_0_.refs_6_, bf16[64,256]{1,0:T(8,128)(2,1)S(1)} %get-tuple-element.41.refs_1_, ...), custom_call_target="tpu_custom_call" | custom-call | flops 33554432 | bytes 655360 | tf_op jit(solution)/shard_map/pallas_call | solution.py:319
  27.0 0.0 collective-permute-done.10.refs_7_
  27.0 0.4 %collective-permute-done.11.refs_8_ = bf16[64,256]{1,0:T(8,128)(2,1)S(1)} collective-permute-done((bf16[64,256]{1,0:T(8,128)(2,1)S(1)}, bf16[64,256]{1,0:T(8,128)(2,1)S(1)}, u32[]{:S(2)}, u32[]{:S(2)}) %collective-permute-start.11) | collective-permute-done | bytes 32800 | tf_op jit(solution)/shard_map/ppermute | solution.py:341
  27.4 0.7 %shard_map.70 = (bf16[32,256]{1,0:T(8,128)(2,1)S(1)}, bf16[32,256]{1,0:T(8,128)(2,1)S(1)}, bf16[32,256]{1,0:T(8,128)(2,1)S(1)}, bf16[32,256]{1,0:T(8,128)(2,1)S(1)}) custom-call(bf16[4,256,256]{2,1,0:T(8,128)(2,1)S(1)} %get-tuple-element.29.refs_0_.refs_6_, bf16[16,256]{1,0:T(8,128)(2,1)S(1)} %get-tuple-element.42.refs_1_, ...), custom_call_target="tpu_custom_call" | custom-call | flops 33554432 | bytes 688128 | tf_op jit(solution)/shard_map/pallas_call | solution.py:319
  28.1 0.9 %collective-permute-start.12 = (bf16[32,256]{1,0:T(8,128)(2,1)S(1)}, bf16[32,256]{1,0:T(8,128)(2,1)S(1)}, u32[]{:S(2)}, u32[]{:S(2)}) collective-permute-start(bf16[32,256]{1,0:T(8,128)(2,1)S(1)} %get-tuple-element.48), channel_id=1, source_target_pairs={{0,9},{1,8},{2,11},{3,10},{4,13},{5,12},{6,15},{7,14},{8,1},{9,0},... | collective-permute-start | bytes 49160 | tf_op jit(solution)/shard_map/ppermute | solution.py:341
  28.9 1.4 %collective-permute-start.13 = (bf16[32,256]{1,0:T(8,128)(2,1)S(1)}, bf16[32,256]{1,0:T(8,128)(2,1)S(1)}, u32[]{:S(2)}, u32[]{:S(2)}) collective-permute-start(bf16[32,256]{1,0:T(8,128)(2,1)S(1)} %get-tuple-element.49), channel_id=1, source_target_pairs={{0,13},{1,12},{2,15},{3,14},{4,9},{5,8},{6,11},{7,10},{8,5},{9,4},... | collective-permute-start | bytes 49160 | tf_op jit(solution)/shard_map/ppermute | solution.py:341
  30.4 0.7 %collective-permute-start.14 = (bf16[32,256]{1,0:T(8,128)(2,1)S(1)}, bf16[32,256]{1,0:T(8,128)(2,1)S(1)}, u32[]{:S(2)}, u32[]{:S(2)}) collective-permute-start(bf16[32,256]{1,0:T(8,128)(2,1)S(1)} %get-tuple-element.50), channel_id=1, source_target_pairs={{0,5},{1,4},{2,7},{3,6},{4,1},{5,0},{6,3},{7,2},{8,13},{9,12},{10,... | collective-permute-start | bytes 49160 | tf_op jit(solution)/shard_map/ppermute | solution.py:341
  31.1 1.1 %collective-permute-done.12.refs_1_ = bf16[32,256]{1,0:T(8,128)(2,1)S(1)} collective-permute-done((bf16[32,256]{1,0:T(8,128)(2,1)S(1)}, bf16[32,256]{1,0:T(8,128)(2,1)S(1)}, u32[]{:S(2)}, u32[]{:S(2)}) %collective-permute-start.12) | collective-permute-done | bytes 16416 | tf_op jit(solution)/shard_map/ppermute | solution.py:341
  32.2 1.7 %collective-permute-done.13.refs_2_ = bf16[32,256]{1,0:T(8,128)(2,1)S(1)} collective-permute-done((bf16[32,256]{1,0:T(8,128)(2,1)S(1)}, bf16[32,256]{1,0:T(8,128)(2,1)S(1)}, u32[]{:S(2)}, u32[]{:S(2)}) %collective-permute-start.13) | collective-permute-done | bytes 16416 | tf_op jit(solution)/shard_map/ppermute | solution.py:341
  33.9 0.0 collective-permute-done.14.refs_3_
  33.9 0.8 %shard_map.71 = bf16[8,16,256]{2,1,0:T(8,128)(2,1)} custom-call(bf16[32,256]{1,0:T(8,128)(2,1)S(1)} %get-tuple-element.47.refs_0_, bf16[32,256]{1,0:T(8,128)(2,1)S(1)} %collective-permute-done.12.refs_1_, bf16[32,256]{1,0:T(8,128)(2,1)S(1)} %collective-permute-done.13.refs_2_, bf16[32,256]{1,0:T(8,128)(2,1)S(1)} %collective-permute-done.14.refs_3_, ...), custom_call_target="tpu_custom_call" | custom-call | bytes 655360 | tf_op jit(solution)/shard_map/pallas_call | solution.py:319
  (1 shorter events, 0.0 us)
Async XLA Ops:
  0.0 5.5 %copy-start = (bf16[8,16,256]{2,1,0:T(8,128)(2,1)S(1)}, bf16[8,16,256]{2,1,0:T(8,128)(2,1)}, u32[]{:S(2)}) copy-start(bf16[8,16,256]{2,1,0:T(8,128)(2,1)} %refs_0_.7) | copy-start | bytes 196612
  0.0 5.5 %collective-permute-start = (bf16[8,16,256]{2,1,0:T(8,128)(2,1)}, bf16[8,16,256]{2,1,0:T(8,128)(2,1)S(1)}, u32[]{:S(2)}, u32[]{:S(2)}) collective-permute-start(bf16[8,16,256]{2,1,0:T(8,128)(2,1)} %refs_0_.7), channel_id=1, source_target_pairs={{16,0},{0,16},{17,1},{1,17},{18,2},{2,18},{19,3},{3,19},{20,4},{4,... | collective-permute-start | bytes 196616 | tf_op jit(solution)/shard_map/ppermute | solution.py:352
  2.9 0.7 %copy-start.1 = (bf16[7,7,256]{2,1,0:T(8,128)(2,1)S(1)}, bf16[7,7,256]{2,1,0:T(8,128)(2,1)}, u32[]{:S(2)}) copy-start(bf16[7,7,256]{2,1,0:T(8,128)(2,1)} %refs_4_.1) | copy-start | bytes 75268
  5.6 7.0 %collective-permute-start.1 = (bf16[64,256]{1,0:T(8,128)(2,1)S(1)}, bf16[64,256]{1,0:T(8,128)(2,1)S(1)}, u32[]{:S(2)}, u32[]{:S(2)}) collective-permute-start(bf16[64,256]{1,0:T(8,128)(2,1)S(1)} %get-tuple-element.31), channel_id=1, source_target_pairs={{0,15},{1,2},{2,1},{3,4},{4,3},{5,6},{6,5},{7,8},{8,7},{9,10},{10,... | collective-permute-start | bytes 98312 | tf_op jit(solution)/shard_map/ppermute | solution.py:374
  9.4 3.2 %collective-permute-start.2 = (bf16[64,256]{1,0:T(8,128)(2,1)S(1)}, bf16[64,256]{1,0:T(8,128)(2,1)S(1)}, u32[]{:S(2)}, u32[]{:S(2)}) collective-permute-start(bf16[64,256]{1,0:T(8,128)(2,1)S(1)} %get-tuple-element.32), channel_id=1, source_target_pairs={{0,1},{1,0},{2,3},{3,2},{4,5},{5,4},{6,7},{7,6},{8,9},{9,8},{10,11... | collective-permute-start | bytes 98312 | tf_op jit(solution)/shard_map/ppermute | solution.py:341
  15.4 4.1 %collective-permute-start.3 = (bf16[32,256]{1,0:T(8,128)(2,1)S(1)}, bf16[32,256]{1,0:T(8,128)(2,1)S(1)}, u32[]{:S(2)}, u32[]{:S(2)}) collective-permute-start(bf16[32,256]{1,0:T(8,128)(2,1)S(1)} %get-tuple-element.38), channel_id=1, source_target_pairs={{0,9},{1,8},{2,11},{3,10},{4,13},{5,12},{6,15},{7,14},{8,1},{9,0},... | collective-permute-start | bytes 49160 | tf_op jit(solution)/shard_map/ppermute | solution.py:341
  16.0 5.1 %collective-permute-start.4 = (bf16[32,256]{1,0:T(8,128)(2,1)S(1)}, bf16[32,256]{1,0:T(8,128)(2,1)S(1)}, u32[]{:S(2)}, u32[]{:S(2)}) collective-permute-start(bf16[32,256]{1,0:T(8,128)(2,1)S(1)} %get-tuple-element.39), channel_id=1, source_target_pairs={{0,13},{1,12},{2,15},{3,14},{4,9},{5,8},{6,11},{7,10},{8,5},{9,4},... | collective-permute-start | bytes 49160 | tf_op jit(solution)/shard_map/ppermute | solution.py:341
  17.5 3.6 %collective-permute-start.5 = (bf16[32,256]{1,0:T(8,128)(2,1)S(1)}, bf16[32,256]{1,0:T(8,128)(2,1)S(1)}, u32[]{:S(2)}, u32[]{:S(2)}) collective-permute-start(bf16[32,256]{1,0:T(8,128)(2,1)S(1)} %get-tuple-element.40), channel_id=1, source_target_pairs={{0,5},{1,4},{2,7},{3,6},{4,1},{5,0},{6,3},{7,2},{8,13},{9,12},{10,... | collective-permute-start | bytes 49160 | tf_op jit(solution)/shard_map/ppermute | solution.py:341
  21.1 3.4 %collective-permute-start.6 = (bf16[64,256]{1,0:T(8,128)(2,1)S(1)}, bf16[64,256]{1,0:T(8,128)(2,1)S(1)}, u32[]{:S(2)}, u32[]{:S(2)}) collective-permute-start(bf16[64,256]{1,0:T(8,128)(2,1)S(1)} %get-tuple-element.41.refs_1_), channel_id=1, source_target_pairs={{0,3},{1,2},{2,1},{3,0},{4,7},{5,6},{6,5},{7,4},{8,11},{9,10},{10,... | collective-permute-start | bytes 98312 | tf_op jit(solution)/shard_map/ppermute | solution.py:341
  22.7 3.5 %collective-permute-start.9 = (bf16[64,256]{1,0:T(8,128)(2,1)S(1)}, bf16[64,256]{1,0:T(8,128)(2,1)S(1)}, u32[]{:S(2)}, u32[]{:S(2)}) collective-permute-start(bf16[64,256]{1,0:T(8,128)(2,1)S(1)} %get-tuple-element.46.refs_5_), channel_id=1, source_target_pairs={{0,3},{1,2},{2,1},{3,0},{4,7},{5,6},{6,5},{7,4},{8,11},{9,10},{10,... | collective-permute-start | bytes 98312 | tf_op jit(solution)/shard_map/ppermute | solution.py:341
  22.9 3.4 %collective-permute-start.7 = (bf16[64,256]{1,0:T(8,128)(2,1)S(1)}, bf16[64,256]{1,0:T(8,128)(2,1)S(1)}, u32[]{:S(2)}, u32[]{:S(2)}) collective-permute-start(bf16[64,256]{1,0:T(8,128)(2,1)S(1)} %get-tuple-element.41.refs_1_), channel_id=1, source_target_pairs={{0,1},{1,0},{2,3},{3,2},{4,5},{5,4},{6,7},{7,6},{8,9},{9,8},{10,11... | collective-permute-start | bytes 98312 | tf_op jit(solution)/shard_map/ppermute | solution.py:341
  24.5 1.8 %collective-permute-start.8 = (bf16[64,256]{1,0:T(8,128)(2,1)S(1)}, bf16[64,256]{1,0:T(8,128)(2,1)S(1)}, u32[]{:S(2)}, u32[]{:S(2)}) collective-permute-start(bf16[64,256]{1,0:T(8,128)(2,1)S(1)} %collective-permute-done.6.refs_2_), channel_id=1, source_target_pairs={{0,1},{1,0},{2,3},{3,2},{4,5},{5,4},{6,7},{7,6},{8,9},{9,8},{10,11... | collective-permute-start | bytes 98312 | tf_op jit(solution)/shard_map/ppermute | solution.py:341
  25.0 2.0 %collective-permute-start.10 = (bf16[64,256]{1,0:T(8,128)(2,1)S(1)}, bf16[64,256]{1,0:T(8,128)(2,1)S(1)}, u32[]{:S(2)}, u32[]{:S(2)}) collective-permute-start(bf16[64,256]{1,0:T(8,128)(2,1)S(1)} %get-tuple-element.46.refs_5_), channel_id=1, source_target_pairs={{0,1},{1,0},{2,3},{3,2},{4,5},{5,4},{6,7},{7,6},{8,9},{9,8},{10,11... | collective-permute-start | bytes 98312 | tf_op jit(solution)/shard_map/ppermute | solution.py:341
  26.1 1.2 %collective-permute-start.11 = (bf16[64,256]{1,0:T(8,128)(2,1)S(1)}, bf16[64,256]{1,0:T(8,128)(2,1)S(1)}, u32[]{:S(2)}, u32[]{:S(2)}) collective-permute-start(bf16[64,256]{1,0:T(8,128)(2,1)S(1)} %collective-permute-done.9.refs_6_), channel_id=1, source_target_pairs={{0,1},{1,0},{2,3},{3,2},{4,5},{5,4},{6,7},{7,6},{8,9},{9,8},{10,11... | collective-permute-start | bytes 98312 | tf_op jit(solution)/shard_map/ppermute | solution.py:341
  28.1 4.1 %collective-permute-start.12 = (bf16[32,256]{1,0:T(8,128)(2,1)S(1)}, bf16[32,256]{1,0:T(8,128)(2,1)S(1)}, u32[]{:S(2)}, u32[]{:S(2)}) collective-permute-start(bf16[32,256]{1,0:T(8,128)(2,1)S(1)} %get-tuple-element.48), channel_id=1, source_target_pairs={{0,9},{1,8},{2,11},{3,10},{4,13},{5,12},{6,15},{7,14},{8,1},{9,0},... | collective-permute-start | bytes 49160 | tf_op jit(solution)/shard_map/ppermute | solution.py:341
  28.9 5.0 %collective-permute-start.13 = (bf16[32,256]{1,0:T(8,128)(2,1)S(1)}, bf16[32,256]{1,0:T(8,128)(2,1)S(1)}, u32[]{:S(2)}, u32[]{:S(2)}) collective-permute-start(bf16[32,256]{1,0:T(8,128)(2,1)S(1)} %get-tuple-element.49), channel_id=1, source_target_pairs={{0,13},{1,12},{2,15},{3,14},{4,9},{5,8},{6,11},{7,10},{8,5},{9,4},... | collective-permute-start | bytes 49160 | tf_op jit(solution)/shard_map/ppermute | solution.py:341
  30.4 3.5 %collective-permute-start.14 = (bf16[32,256]{1,0:T(8,128)(2,1)S(1)}, bf16[32,256]{1,0:T(8,128)(2,1)S(1)}, u32[]{:S(2)}, u32[]{:S(2)}) collective-permute-start(bf16[32,256]{1,0:T(8,128)(2,1)S(1)} %get-tuple-element.50), channel_id=1, source_target_pairs={{0,5},{1,4},{2,7},{3,6},{4,1},{5,0},{6,3},{7,2},{8,13},{9,12},{10,... | collective-permute-start | bytes 49160 | tf_op jit(solution)/shard_map/ppermute | solution.py:341

commit v21 on v20

--- a/solution.py
+++ b/solution.py
@@ -85,13 +85,16 @@
     taps_ref[...] = dw[...].astype(f32)
 
 
-def hops_of(levels):
+def hops_in(levels):
+    return [0, *range(levels - 1, 0, -1)]
+
+
+def hops_back(levels):
     return [0] + [h for h in (*range(levels // 2, levels), *range(1, levels // 2)) if h]
 
 
-def peer(levels, k):
-    level = lax.axis_index("lon") // (lax.axis_size("lon") // levels)
-    return level ^ hops_of(levels)[k]
+def peer(levels, hops):
+    return (lax.axis_index("lon") // (lax.axis_size("lon") // levels)) ^ hops
 
 
 def strip_kernel(nlat, *refs):
@@ -254,7 +257,7 @@
     sent[...] = jnp.concatenate([inner, outer], axis=1).astype(bf16)
     some = rows // levels
     for k in range(levels):
-        part = sent[pl.ds(peer(levels, k) * some, some)]
+        part = sent[pl.ds(peer(levels, hops_in(levels)[k]) * some, some)]
         sent_refs[k][...] = part.reshape(sent_refs[k].shape)
 
 
@@ -292,7 +295,7 @@
     every = jnp.concatenate([part[...] for part in parts], axis=0)
     change = dot(every, attn_ref[3]).reshape(levels, some, cols, channels)
     for k in range(levels):
-        start = peer(levels, k) * some
+        start = peer(levels, hops_back(levels)[k]) * some
 
         def state(ref, width):
             count = some * width
@@ -340,12 +343,9 @@
     def swap(piece, mask):
         return lax.ppermute(piece, "lon", [(j, j ^ mask) for j in range(nlon)])
 
-    def exchange(pieces):
+    def exchange(pieces, hops):
         cross = min(1, column - 1)
-        return [
-            swap(piece, hops * column + cross) if hops else piece
-            for piece, hops in zip(pieces, hops_of(levels))
-        ]
+        return [swap(p, h * column + cross) if h else p for p, h in zip(pieces, hops)]
 
     tiles = [field]
     for s in range(1, nlat):
@@ -400,7 +400,7 @@
         flops=work,
     )
 
-    parts = exchange(parts)
+    parts = exchange(parts, hops_in(levels))
     joined = call(
         functools.partial(join_kernel, levels, some), [(levels * cols, channels)] * some, parts
     )
@@ -420,7 +420,8 @@
             flops=work // 4,
         )
         done = done + list(mixes)
-    mixes = exchange(mixes)
+    mixes = dict(zip(hops_in(levels), mixes))
+    mixes = exchange([mixes[h] for h in hops_back(levels)], hops_back(levels))
     (out,) = call(
         functools.partial(last_kernel, levels),
         [(rows, cols, channels)],

time: 34.9 us -> 35.7 us (1.023)
  starting transfers between devices: 16 us -> 17.5 us
  waiting for transfers between devices: 7.79 us -> 7.08 us
    ppermute x13, starting transfers between devices: 9.32 us -> 10.8 us  [swap(): return lax.ppermute(piece, 'lon', [(j, j ^ mask) for j in range(nlon)])]
    ppermute x13, waiting for transfers between devices: 7.78 us -> 7.08 us  [swap(): return lax.ppermute(piece, 'lon', [(j, j ^ mask) for j in range(nlon)])]
where the time goes in v21:
time: 35.7 us; the launch traced here: 35.5 us
  starting transfers between devices  17.5 us (49%)
  Pallas kernels  10 us (28%)
  waiting for transfers between devices  7.08 us (20%)
  local copies, waits for them, and re-layouts  0.75 us (2%)
    ppermute x13, starting transfers between devices, swap(): return lax.ppermute(piece, 'lon', [(j, j ^ mask) for j in range(nlon)])  10.8 us
    pallas_call x8, Pallas kernels, call(): pl.pallas_call(kernel, out_shape=shapes, in_specs=[given] * len(operands)...  10 us
    ppermute x13, waiting for transfers between devices, swap(): return lax.ppermute(piece, 'lon', [(j, j ^ mask) for j in range(nlon)])  7.08 us
    ppermute x1, starting transfers between devices, shards(): lax.ppermute(far, 'lon', [(j, (j - 1) % nlon if j % 2 == 0 else (j + 1) %...  3.78 us
    ppermute x1, starting transfers between devices, shards(): lax.ppermute(field, 'lat', [((i + s) % nlat, i) for i in range(nlat)])  2.94 us
    unnamed x4, local copies, waits for them, and re-layouts  0.75 us
  transfers between devices with their start and end apart: 15, of which 7 were waited for; matrix products, arithmetic and copies ran while one was open for 0% of the time, Pallas kernels for 16%

profile of v21, /device:TPU:0, one launch (start us, length us, event | category | flops | bytes accessed | tf_op | source)
XLA Modules:
  0.0 35.5 jit_solution(14645571440474578118)
XLA Ops:
  0.0 0.0 copy-start
  0.0 2.9 %collective-permute-start = (bf16[8,16,256]{2,1,0:T(8,128)(2,1)}, bf16[8,16,256]{2,1,0:T(8,128)(2,1)S(1)}, u32[]{:S(2)}, u32[]{:S(2)}) collective-permute-start(bf16[8,16,256]{2,1,0:T(8,128)(2,1)} %refs_0_.7), channel_id=1, source_target_pairs={{16,0},{0,16},{17,1},{1,17},{18,2},{2,18},{19,3},{3,19},{20,4},{4,... | collective-permute-start | bytes 196616 | tf_op jit(solution)/shard_map/ppermute | solution.py:352
  2.9 0.0 copy-start.1
  2.9 0.7 %copy-done.1 = bf16[7,7,256]{2,1,0:T(8,128)(2,1)S(1)} copy-done((bf16[7,7,256]{2,1,0:T(8,128)(2,1)S(1)}, bf16[7,7,256]{2,1,0:T(8,128)(2,1)}, u32[]{:S(2)}) %copy-start.1) | copy-done | bytes 25112
  3.7 1.8 %shard_map.64 = (bf16[256,1024]{1,0:T(8,128)(2,1)S(1)}, bf16[1024,256]{1,0:T(8,128)(2,1)S(1)}, bf16[4,256,256]{2,1,0:T(8,128)(2,1)S(1)}, bf16[4,256,256]{2,1,0:T(8,128)(2,1)S(1)}, f32[7,7,256]{2,1,0:T(8,128)S(1)}) custom-call(bf16[256,1024]{1,0:T(8,128)(2,1)} %refs_0_.4, bf16[1024,256]{1,0:T(8,128)(2,1)} %refs_1_.1, bf16[4,256,256]{2,1,0:T(8,128)(2,1)} %refs_2_.1, ...), custom_call_target="tpu_custom_call" | custom-call | bytes 2122240 | tf_op jit(solution)/shard_map/pallas_call | solution.py:322
  5.5 0.0 collective-permute-done.refs_1_
  5.5 0.0 copy-done
  5.5 0.1 shard_map.65
  5.6 3.8 %collective-permute-start.1 = (bf16[64,256]{1,0:T(8,128)(2,1)S(1)}, bf16[64,256]{1,0:T(8,128)(2,1)S(1)}, u32[]{:S(2)}, u32[]{:S(2)}) collective-permute-start(bf16[64,256]{1,0:T(8,128)(2,1)S(1)} %get-tuple-element.31), channel_id=1, source_target_pairs={{0,15},{1,2},{2,1},{3,4},{4,3},{5,6},{6,5},{7,8},{8,7},{9,10},{10,... | collective-permute-start | bytes 98312 | tf_op jit(solution)/shard_map/ppermute | solution.py:374
  9.4 0.0 collective-permute-start.2
  9.4 3.2 %shard_map.66 = (bf16[64,256]{1,0:T(8,128)(2,1)S(1)}, bf16[64,256]{1,0:T(8,128)(2,1)S(1)}) custom-call(bf16[8,16,256]{2,1,0:T(8,128)(2,1)S(1)} %copy-done, bf16[8,16,256]{2,1,0:T(8,128)(2,1)S(1)} %collective-permute-done.refs_1_, f32[7,7,256]{2,1,0:T(8,128)S(1)} %get-tuple-element.33.refs_2_.refs_5_, ...), custom_call_target="tpu_custom_call" | custom-call | flops 134217728 | bytes 1754112 | tf_op jit(solution)/shard_map/pallas_call | solution.py:322
  12.6 0.0 collective-permute-done.1.refs_2_
  12.6 0.0 collective-permute-done.2.refs_3_
  12.6 2.8 %shard_map.67 = (bf16[64,256]{1,0:T(8,128)(2,1)S(1)}, bf16[32,256]{1,0:T(8,128)(2,1)S(1)}, bf16[32,256]{1,0:T(8,128)(2,1)S(1)}, bf16[32,256]{1,0:T(8,128)(2,1)S(1)}, bf16[32,256]{1,0:T(8,128)(2,1)S(1)}) custom-call(bf16[8,16,256]{2,1,0:T(8,128)(2,1)S(1)} %copy-done, bf16[8,16,256]{2,1,0:T(8,128)(2,1)S(1)} %collective-permute-done.refs_1_, ...), custom_call_target="tpu_custom_call" | custom-call | flops 134217728 | bytes 1852416 | tf_op jit(solution)/shard_map/pallas_call | solution.py:322
  15.4 1.6 %collective-permute-start.3 = (bf16[32,256]{1,0:T(8,128)(2,1)S(1)}, bf16[32,256]{1,0:T(8,128)(2,1)S(1)}, u32[]{:S(2)}, u32[]{:S(2)}) collective-permute-start(bf16[32,256]{1,0:T(8,128)(2,1)S(1)} %get-tuple-element.38), channel_id=1, source_target_pairs={{0,13},{1,12},{2,15},{3,14},{4,9},{5,8},{6,11},{7,10},{8,5},{9,4},... | collective-permute-start | bytes 49160 | tf_op jit(solution)/shard_map/ppermute | solution.py:344
  17.0 0.0 collective-permute-start.4
  17.0 2.7 %collective-permute-start.5 = (bf16[32,256]{1,0:T(8,128)(2,1)S(1)}, bf16[32,256]{1,0:T(8,128)(2,1)S(1)}, u32[]{:S(2)}, u32[]{:S(2)}) collective-permute-start(bf16[32,256]{1,0:T(8,128)(2,1)S(1)} %get-tuple-element.40), channel_id=1, source_target_pairs={{0,5},{1,4},{2,7},{3,6},{4,1},{5,0},{6,3},{7,2},{8,13},{9,12},{10,... | collective-permute-start | bytes 49160 | tf_op jit(solution)/shard_map/ppermute | solution.py:344
  19.7 0.7 %collective-permute-done.3.refs_1_ = bf16[32,256]{1,0:T(8,128)(2,1)S(1)} collective-permute-done((bf16[32,256]{1,0:T(8,128)(2,1)S(1)}, bf16[32,256]{1,0:T(8,128)(2,1)S(1)}, u32[]{:S(2)}, u32[]{:S(2)}) %collective-permute-start.3) | collective-permute-done | bytes 16416 | tf_op jit(solution)/shard_map/ppermute | solution.py:344
  20.4 1.0 %collective-permute-done.4.refs_2_ = bf16[32,256]{1,0:T(8,128)(2,1)S(1)} collective-permute-done((bf16[32,256]{1,0:T(8,128)(2,1)S(1)}, bf16[32,256]{1,0:T(8,128)(2,1)S(1)}, u32[]{:S(2)}, u32[]{:S(2)}) %collective-permute-start.4) | collective-permute-done | bytes 16416 | tf_op jit(solution)/shard_map/ppermute | solution.py:344
  21.4 0.2 collective-permute-done.5.refs_3_
  21.6 0.0 collective-permute-start.6
  21.6 1.8 %collective-permute-start.9 = (bf16[64,256]{1,0:T(8,128)(2,1)S(1)}, bf16[64,256]{1,0:T(8,128)(2,1)S(1)}, u32[]{:S(2)}, u32[]{:S(2)}) collective-permute-start(bf16[64,256]{1,0:T(8,128)(2,1)S(1)} %get-tuple-element.46.refs_5_), channel_id=1, source_target_pairs={{0,3},{1,2},{2,1},{3,0},{4,7},{5,6},{6,5},{7,4},{8,11},{9,10},{10,... | collective-permute-start | bytes 98312 | tf_op jit(solution)/shard_map/ppermute | solution.py:344
  23.4 0.1 collective-permute-start.7
  23.4 1.5 %collective-permute-done.6.refs_2_ = bf16[64,256]{1,0:T(8,128)(2,1)S(1)} collective-permute-done((bf16[64,256]{1,0:T(8,128)(2,1)S(1)}, bf16[64,256]{1,0:T(8,128)(2,1)S(1)}, u32[]{:S(2)}, u32[]{:S(2)}) %collective-permute-start.6) | collective-permute-done | bytes 32800 | tf_op jit(solution)/shard_map/ppermute | solution.py:344
  25.0 0.7 %collective-permute-start.8 = (bf16[64,256]{1,0:T(8,128)(2,1)S(1)}, bf16[64,256]{1,0:T(8,128)(2,1)S(1)}, u32[]{:S(2)}, u32[]{:S(2)}) collective-permute-start(bf16[64,256]{1,0:T(8,128)(2,1)S(1)} %collective-permute-done.6.refs_2_), channel_id=1, source_target_pairs={{0,1},{1,0},{2,3},{3,2},{4,5},{5,4},{6,7},{7,6},{8,9},{9,8},{10,11... | collective-permute-start | bytes 98312 | tf_op jit(solution)/shard_map/ppermute | solution.py:344
  25.7 0.0 collective-permute-start.10
  25.7 0.0 collective-permute-done.9.refs_6_
  25.7 0.7 %collective-permute-start.11 = (bf16[64,256]{1,0:T(8,128)(2,1)S(1)}, bf16[64,256]{1,0:T(8,128)(2,1)S(1)}, u32[]{:S(2)}, u32[]{:S(2)}) collective-permute-start(bf16[64,256]{1,0:T(8,128)(2,1)S(1)} %collective-permute-done.9.refs_6_), channel_id=1, source_target_pairs={{0,1},{1,0},{2,3},{3,2},{4,5},{5,4},{6,7},{7,6},{8,9},{9,8},{10,11... | collective-permute-start | bytes 98312 | tf_op jit(solution)/shard_map/ppermute | solution.py:344
  26.4 0.0 collective-permute-done.7.refs_3_
  26.4 0.1 collective-permute-done.8.refs_4_
  26.5 0.7 %shard_map.69 = (bf16[16,256]{1,0:T(8,128)(2,1)S(1)}, bf16[16,256]{1,0:T(8,128)(2,1)S(1)}, bf16[16,256]{1,0:T(8,128)(2,1)S(1)}, bf16[16,256]{1,0:T(8,128)(2,1)S(1)}) custom-call(bf16[4,256,256]{2,1,0:T(8,128)(2,1)S(1)} %get-tuple-element.29.refs_0_.refs_6_, bf16[64,256]{1,0:T(8,128)(2,1)S(1)} %get-tuple-element.41.refs_1_, ...), custom_call_target="tpu_custom_call" | custom-call | flops 33554432 | bytes 655360 | tf_op jit(solution)/shard_map/pallas_call | solution.py:322
  27.2 0.0 collective-permute-done.10.refs_7_
  27.2 0.0 collective-permute-done.11.refs_8_
  27.3 0.7 %shard_map.70 = (bf16[32,256]{1,0:T(8,128)(2,1)S(1)}, bf16[32,256]{1,0:T(8,128)(2,1)S(1)}, bf16[32,256]{1,0:T(8,128)(2,1)S(1)}, bf16[32,256]{1,0:T(8,128)(2,1)S(1)}) custom-call(bf16[4,256,256]{2,1,0:T(8,128)(2,1)S(1)} %get-tuple-element.29.refs_0_.refs_6_, bf16[16,256]{1,0:T(8,128)(2,1)S(1)} %get-tuple-element.42.refs_1_, ...), custom_call_target="tpu_custom_call" | custom-call | flops 33554432 | bytes 688128 | tf_op jit(solution)/shard_map/pallas_call | solution.py:322
  28.0 1.7 %collective-permute-start.12 = (bf16[32,256]{1,0:T(8,128)(2,1)S(1)}, bf16[32,256]{1,0:T(8,128)(2,1)S(1)}, u32[]{:S(2)}, u32[]{:S(2)}) collective-permute-start(bf16[32,256]{1,0:T(8,128)(2,1)S(1)} %get-tuple-element.48), channel_id=1, source_target_pairs={{0,9},{1,8},{2,11},{3,10},{4,13},{5,12},{6,15},{7,14},{8,1},{9,0},... | collective-permute-start | bytes 49160 | tf_op jit(solution)/shard_map/ppermute | solution.py:344
  29.7 1.3 %collective-permute-start.13 = (bf16[32,256]{1,0:T(8,128)(2,1)S(1)}, bf16[32,256]{1,0:T(8,128)(2,1)S(1)}, u32[]{:S(2)}, u32[]{:S(2)}) collective-permute-start(bf16[32,256]{1,0:T(8,128)(2,1)S(1)} %get-tuple-element.49), channel_id=1, source_target_pairs={{0,13},{1,12},{2,15},{3,14},{4,9},{5,8},{6,11},{7,10},{8,5},{9,4},... | collective-permute-start | bytes 49160 | tf_op jit(solution)/shard_map/ppermute | solution.py:344
  31.0 0.2 collective-permute-start.14
  31.2 0.9 %collective-permute-done.12.refs_1_ = bf16[32,256]{1,0:T(8,128)(2,1)S(1)} collective-permute-done((bf16[32,256]{1,0:T(8,128)(2,1)S(1)}, bf16[32,256]{1,0:T(8,128)(2,1)S(1)}, u32[]{:S(2)}, u32[]{:S(2)}) %collective-permute-start.12) | collective-permute-done | bytes 16416 | tf_op jit(solution)/shard_map/ppermute | solution.py:344
  32.1 2.6 %collective-permute-done.13.refs_2_ = bf16[32,256]{1,0:T(8,128)(2,1)S(1)} collective-permute-done((bf16[32,256]{1,0:T(8,128)(2,1)S(1)}, bf16[32,256]{1,0:T(8,128)(2,1)S(1)}, u32[]{:S(2)}, u32[]{:S(2)}) %collective-permute-start.13) | collective-permute-done | bytes 16416 | tf_op jit(solution)/shard_map/ppermute | solution.py:344
  34.7 0.0 collective-permute-done.14.refs_3_
  34.7 0.8 %shard_map.71 = bf16[8,16,256]{2,1,0:T(8,128)(2,1)} custom-call(bf16[32,256]{1,0:T(8,128)(2,1)S(1)} %get-tuple-element.47.refs_0_, bf16[32,256]{1,0:T(8,128)(2,1)S(1)} %collective-permute-done.12.refs_1_, bf16[32,256]{1,0:T(8,128)(2,1)S(1)} %collective-permute-done.13.refs_2_, bf16[32,256]{1,0:T(8,128)(2,1)S(1)} %collective-permute-done.14.refs_3_, ...), custom_call_target="tpu_custom_call" | custom-call | bytes 655360 | tf_op jit(solution)/shard_map/pallas_call | solution.py:322
  (1 shorter events, 0.0 us)
Async XLA Ops:
  0.0 5.5 %copy-start = (bf16[8,16,256]{2,1,0:T(8,128)(2,1)S(1)}, bf16[8,16,256]{2,1,0:T(8,128)(2,1)}, u32[]{:S(2)}) copy-start(bf16[8,16,256]{2,1,0:T(8,128)(2,1)} %refs_0_.7) | copy-start | bytes 196612
  0.0 5.5 %collective-permute-start = (bf16[8,16,256]{2,1,0:T(8,128)(2,1)}, bf16[8,16,256]{2,1,0:T(8,128)(2,1)S(1)}, u32[]{:S(2)}, u32[]{:S(2)}) collective-permute-start(bf16[8,16,256]{2,1,0:T(8,128)(2,1)} %refs_0_.7), channel_id=1, source_target_pairs={{16,0},{0,16},{17,1},{1,17},{18,2},{2,18},{19,3},{3,19},{20,4},{4,... | collective-permute-start | bytes 196616 | tf_op jit(solution)/shard_map/ppermute | solution.py:352
  2.9 0.7 %copy-start.1 = (bf16[7,7,256]{2,1,0:T(8,128)(2,1)S(1)}, bf16[7,7,256]{2,1,0:T(8,128)(2,1)}, u32[]{:S(2)}) copy-start(bf16[7,7,256]{2,1,0:T(8,128)(2,1)} %refs_4_.1) | copy-start | bytes 75268
  5.6 7.0 %collective-permute-start.1 = (bf16[64,256]{1,0:T(8,128)(2,1)S(1)}, bf16[64,256]{1,0:T(8,128)(2,1)S(1)}, u32[]{:S(2)}, u32[]{:S(2)}) collective-permute-start(bf16[64,256]{1,0:T(8,128)(2,1)S(1)} %get-tuple-element.31), channel_id=1, source_target_pairs={{0,15},{1,2},{2,1},{3,4},{4,3},{5,6},{6,5},{7,8},{8,7},{9,10},{10,... | collective-permute-start | bytes 98312 | tf_op jit(solution)/shard_map/ppermute | solution.py:374
  9.4 3.2 %collective-permute-start.2 = (bf16[64,256]{1,0:T(8,128)(2,1)S(1)}, bf16[64,256]{1,0:T(8,128)(2,1)S(1)}, u32[]{:S(2)}, u32[]{:S(2)}) collective-permute-start(bf16[64,256]{1,0:T(8,128)(2,1)S(1)} %get-tuple-element.32), channel_id=1, source_target_pairs={{0,1},{1,0},{2,3},{3,2},{4,5},{5,4},{6,7},{7,6},{8,9},{9,8},{10,11... | collective-permute-start | bytes 98312 | tf_op jit(solution)/shard_map/ppermute | solution.py:344
  15.4 5.0 %collective-permute-start.3 = (bf16[32,256]{1,0:T(8,128)(2,1)S(1)}, bf16[32,256]{1,0:T(8,128)(2,1)S(1)}, u32[]{:S(2)}, u32[]{:S(2)}) collective-permute-start(bf16[32,256]{1,0:T(8,128)(2,1)S(1)} %get-tuple-element.38), channel_id=1, source_target_pairs={{0,13},{1,12},{2,15},{3,14},{4,9},{5,8},{6,11},{7,10},{8,5},{9,4},... | collective-permute-start | bytes 49160 | tf_op jit(solution)/shard_map/ppermute | solution.py:344
  17.0 4.4 %collective-permute-start.4 = (bf16[32,256]{1,0:T(8,128)(2,1)S(1)}, bf16[32,256]{1,0:T(8,128)(2,1)S(1)}, u32[]{:S(2)}, u32[]{:S(2)}) collective-permute-start(bf16[32,256]{1,0:T(8,128)(2,1)S(1)} %get-tuple-element.39), channel_id=1, source_target_pairs={{0,9},{1,8},{2,11},{3,10},{4,13},{5,12},{6,15},{7,14},{8,1},{9,0},... | collective-permute-start | bytes 49160 | tf_op jit(solution)/shard_map/ppermute | solution.py:344
  17.0 4.6 %collective-permute-start.5 = (bf16[32,256]{1,0:T(8,128)(2,1)S(1)}, bf16[32,256]{1,0:T(8,128)(2,1)S(1)}, u32[]{:S(2)}, u32[]{:S(2)}) collective-permute-start(bf16[32,256]{1,0:T(8,128)(2,1)S(1)} %get-tuple-element.40), channel_id=1, source_target_pairs={{0,5},{1,4},{2,7},{3,6},{4,1},{5,0},{6,3},{7,2},{8,13},{9,12},{10,... | collective-permute-start | bytes 49160 | tf_op jit(solution)/shard_map/ppermute | solution.py:344
  21.6 3.4 %collective-permute-start.6 = (bf16[64,256]{1,0:T(8,128)(2,1)S(1)}, bf16[64,256]{1,0:T(8,128)(2,1)S(1)}, u32[]{:S(2)}, u32[]{:S(2)}) collective-permute-start(bf16[64,256]{1,0:T(8,128)(2,1)S(1)} %get-tuple-element.41.refs_1_), channel_id=1, source_target_pairs={{0,3},{1,2},{2,1},{3,0},{4,7},{5,6},{6,5},{7,4},{8,11},{9,10},{10,... | collective-permute-start | bytes 98312 | tf_op jit(solution)/shard_map/ppermute | solution.py:344
  21.6 4.1 %collective-permute-start.9 = (bf16[64,256]{1,0:T(8,128)(2,1)S(1)}, bf16[64,256]{1,0:T(8,128)(2,1)S(1)}, u32[]{:S(2)}, u32[]{:S(2)}) collective-permute-start(bf16[64,256]{1,0:T(8,128)(2,1)S(1)} %get-tuple-element.46.refs_5_), channel_id=1, source_target_pairs={{0,3},{1,2},{2,1},{3,0},{4,7},{5,6},{6,5},{7,4},{8,11},{9,10},{10,... | collective-permute-start | bytes 98312 | tf_op jit(solution)/shard_map/ppermute | solution.py:344
  23.4 3.1 %collective-permute-start.7 = (bf16[64,256]{1,0:T(8,128)(2,1)S(1)}, bf16[64,256]{1,0:T(8,128)(2,1)S(1)}, u32[]{:S(2)}, u32[]{:S(2)}) collective-permute-start(bf16[64,256]{1,0:T(8,128)(2,1)S(1)} %get-tuple-element.41.refs_1_), channel_id=1, source_target_pairs={{0,1},{1,0},{2,3},{3,2},{4,5},{5,4},{6,7},{7,6},{8,9},{9,8},{10,11... | collective-permute-start | bytes 98312 | tf_op jit(solution)/shard_map/ppermute | solution.py:344
  25.0 1.6 %collective-permute-start.8 = (bf16[64,256]{1,0:T(8,128)(2,1)S(1)}, bf16[64,256]{1,0:T(8,128)(2,1)S(1)}, u32[]{:S(2)}, u32[]{:S(2)}) collective-permute-start(bf16[64,256]{1,0:T(8,128)(2,1)S(1)} %collective-permute-done.6.refs_2_), channel_id=1, source_target_pairs={{0,1},{1,0},{2,3},{3,2},{4,5},{5,4},{6,7},{7,6},{8,9},{9,8},{10,11... | collective-permute-start | bytes 98312 | tf_op jit(solution)/shard_map/ppermute | solution.py:344
  25.7 1.6 %collective-permute-start.10 = (bf16[64,256]{1,0:T(8,128)(2,1)S(1)}, bf16[64,256]{1,0:T(8,128)(2,1)S(1)}, u32[]{:S(2)}, u32[]{:S(2)}) collective-permute-start(bf16[64,256]{1,0:T(8,128)(2,1)S(1)} %get-tuple-element.46.refs_5_), channel_id=1, source_target_pairs={{0,1},{1,0},{2,3},{3,2},{4,5},{5,4},{6,7},{7,6},{8,9},{9,8},{10,11... | collective-permute-start | bytes 98312 | tf_op jit(solution)/shard_map/ppermute | solution.py:344
  25.7 1.6 %collective-permute-start.11 = (bf16[64,256]{1,0:T(8,128)(2,1)S(1)}, bf16[64,256]{1,0:T(8,128)(2,1)S(1)}, u32[]{:S(2)}, u32[]{:S(2)}) collective-permute-start(bf16[64,256]{1,0:T(8,128)(2,1)S(1)} %collective-permute-done.9.refs_6_), channel_id=1, source_target_pairs={{0,1},{1,0},{2,3},{3,2},{4,5},{5,4},{6,7},{7,6},{8,9},{9,8},{10,11... | collective-permute-start | bytes 98312 | tf_op jit(solution)/shard_map/ppermute | solution.py:344
  28.0 4.1 %collective-permute-start.12 = (bf16[32,256]{1,0:T(8,128)(2,1)S(1)}, bf16[32,256]{1,0:T(8,128)(2,1)S(1)}, u32[]{:S(2)}, u32[]{:S(2)}) collective-permute-start(bf16[32,256]{1,0:T(8,128)(2,1)S(1)} %get-tuple-element.48), channel_id=1, source_target_pairs={{0,9},{1,8},{2,11},{3,10},{4,13},{5,12},{6,15},{7,14},{8,1},{9,0},... | collective-permute-start | bytes 49160 | tf_op jit(solution)/shard_map/ppermute | solution.py:344
  29.7 5.0 %collective-permute-start.13 = (bf16[32,256]{1,0:T(8,128)(2,1)S(1)}, bf16[32,256]{1,0:T(8,128)(2,1)S(1)}, u32[]{:S(2)}, u32[]{:S(2)}) collective-permute-start(bf16[32,256]{1,0:T(8,128)(2,1)S(1)} %get-tuple-element.49), channel_id=1, source_target_pairs={{0,13},{1,12},{2,15},{3,14},{4,9},{5,8},{6,11},{7,10},{8,5},{9,4},... | collective-permute-start | bytes 49160 | tf_op jit(solution)/shard_map/ppermute | solution.py:344
  31.0 3.7 %collective-permute-start.14 = (bf16[32,256]{1,0:T(8,128)(2,1)S(1)}, bf16[32,256]{1,0:T(8,128)(2,1)S(1)}, u32[]{:S(2)}, u32[]{:S(2)}) collective-permute-start(bf16[32,256]{1,0:T(8,128)(2,1)S(1)} %get-tuple-element.50), channel_id=1, source_target_pairs={{0,5},{1,4},{2,7},{3,6},{4,1},{5,0},{6,3},{7,2},{8,13},{9,12},{10,... | collective-permute-start | bytes 49160 | tf_op jit(solution)/shard_map/ppermute | solution.py:344

commit v22 on v21

--- a/solution.py
+++ b/solution.py
@@ -85,11 +85,11 @@
     taps_ref[...] = dw[...].astype(f32)
 
 
+def hops_back(levels):
+    return [0, *range(levels - 1, 0, -1)]
+
+
 def hops_in(levels):
-    return [0, *range(levels - 1, 0, -1)]
-
-
-def hops_back(levels):
     return [0] + [h for h in (*range(levels // 2, levels), *range(1, levels // 2)) if h]
 
 

time: 35.7 us -> 35 us (0.980)
  starting transfers between devices: 17.5 us -> 16.9 us
    ppermute x13, starting transfers between devices: 10.8 us -> 10.2 us  [swap(): return lax.ppermute(piece, 'lon', [(j, j ^ mask) for j in range(nlon)])]
where the time goes in v22:
time: 35 us; the launch traced here: 34.7 us
  starting transfers between devices  16.9 us (48%)
  Pallas kernels  10 us (29%)
  waiting for transfers between devices  6.92 us (20%)
  local copies, waits for them, and re-layouts  0.75 us (2%)
    ppermute x13, starting transfers between devices, swap(): return lax.ppermute(piece, 'lon', [(j, j ^ mask) for j in range(nlon)])  10.2 us
    pallas_call x8, Pallas kernels, call(): pl.pallas_call(kernel, out_shape=shapes, in_specs=[given] * len(operands)...  10 us
    ppermute x13, waiting for transfers between devices, swap(): return lax.ppermute(piece, 'lon', [(j, j ^ mask) for j in range(nlon)])  6.91 us
    ppermute x1, starting transfers between devices, shards(): lax.ppermute(far, 'lon', [(j, (j - 1) % nlon if j % 2 == 0 else (j + 1) %...  3.78 us
    ppermute x1, starting transfers between devices, shards(): lax.ppermute(field, 'lat', [((i + s) % nlat, i) for i in range(nlat)])  2.94 us
    unnamed x4, local copies, waits for them, and re-layouts  0.75 us
  transfers between devices with their start and end apart: 15, of which 7 were waited for; matrix products, arithmetic and copies ran while one was open for 0% of the time, Pallas kernels for 16%

profile of v22, /device:TPU:0, one launch (start us, length us, event | category | flops | bytes accessed | tf_op | source)
XLA Modules:
  0.0 34.7 jit_solution(8590503118674056677)
XLA Ops:
  0.0 0.0 copy-start
  0.0 2.9 %collective-permute-start = (bf16[8,16,256]{2,1,0:T(8,128)(2,1)}, bf16[8,16,256]{2,1,0:T(8,128)(2,1)S(1)}, u32[]{:S(2)}, u32[]{:S(2)}) collective-permute-start(bf16[8,16,256]{2,1,0:T(8,128)(2,1)} %refs_0_.7), channel_id=1, source_target_pairs={{16,0},{0,16},{17,1},{1,17},{18,2},{2,18},{19,3},{3,19},{20,4},{4,... | collective-permute-start | bytes 196616 | tf_op jit(solution)/shard_map/ppermute | solution.py:352
  2.9 0.0 copy-start.1
  2.9 0.7 %copy-done.1 = bf16[7,7,256]{2,1,0:T(8,128)(2,1)S(1)} copy-done((bf16[7,7,256]{2,1,0:T(8,128)(2,1)S(1)}, bf16[7,7,256]{2,1,0:T(8,128)(2,1)}, u32[]{:S(2)}) %copy-start.1) | copy-done | bytes 25112
  3.7 1.8 %shard_map.64 = (bf16[256,1024]{1,0:T(8,128)(2,1)S(1)}, bf16[1024,256]{1,0:T(8,128)(2,1)S(1)}, bf16[4,256,256]{2,1,0:T(8,128)(2,1)S(1)}, bf16[4,256,256]{2,1,0:T(8,128)(2,1)S(1)}, f32[7,7,256]{2,1,0:T(8,128)S(1)}) custom-call(bf16[256,1024]{1,0:T(8,128)(2,1)} %refs_0_.4, bf16[1024,256]{1,0:T(8,128)(2,1)} %refs_1_.1, bf16[4,256,256]{2,1,0:T(8,128)(2,1)} %refs_2_.1, ...), custom_call_target="tpu_custom_call" | custom-call | bytes 2122240 | tf_op jit(solution)/shard_map/pallas_call | solution.py:322
  5.5 0.0 collective-permute-done.refs_1_
  5.5 0.0 copy-done
  5.5 0.1 shard_map.65
  5.6 3.8 %collective-permute-start.1 = (bf16[64,256]{1,0:T(8,128)(2,1)S(1)}, bf16[64,256]{1,0:T(8,128)(2,1)S(1)}, u32[]{:S(2)}, u32[]{:S(2)}) collective-permute-start(bf16[64,256]{1,0:T(8,128)(2,1)S(1)} %get-tuple-element.31), channel_id=1, source_target_pairs={{0,15},{1,2},{2,1},{3,4},{4,3},{5,6},{6,5},{7,8},{8,7},{9,10},{10,... | collective-permute-start | bytes 98312 | tf_op jit(solution)/shard_map/ppermute | solution.py:374
  9.4 0.0 collective-permute-start.2
  9.4 3.2 %shard_map.66 = (bf16[64,256]{1,0:T(8,128)(2,1)S(1)}, bf16[64,256]{1,0:T(8,128)(2,1)S(1)}) custom-call(bf16[8,16,256]{2,1,0:T(8,128)(2,1)S(1)} %copy-done, bf16[8,16,256]{2,1,0:T(8,128)(2,1)S(1)} %collective-permute-done.refs_1_, f32[7,7,256]{2,1,0:T(8,128)S(1)} %get-tuple-element.33.refs_2_.refs_5_, ...), custom_call_target="tpu_custom_call" | custom-call | flops 134217728 | bytes 1754112 | tf_op jit(solution)/shard_map/pallas_call | solution.py:322
  12.6 0.0 collective-permute-done.1.refs_2_
  12.6 0.0 collective-permute-done.2.refs_3_
  12.6 2.8 %shard_map.67 = (bf16[64,256]{1,0:T(8,128)(2,1)S(1)}, bf16[32,256]{1,0:T(8,128)(2,1)S(1)}, bf16[32,256]{1,0:T(8,128)(2,1)S(1)}, bf16[32,256]{1,0:T(8,128)(2,1)S(1)}, bf16[32,256]{1,0:T(8,128)(2,1)S(1)}) custom-call(bf16[8,16,256]{2,1,0:T(8,128)(2,1)S(1)} %copy-done, bf16[8,16,256]{2,1,0:T(8,128)(2,1)S(1)} %collective-permute-done.refs_1_, ...), custom_call_target="tpu_custom_call" | custom-call | flops 134217728 | bytes 1852416 | tf_op jit(solution)/shard_map/pallas_call | solution.py:322
  15.4 0.6 %collective-permute-start.3 = (bf16[32,256]{1,0:T(8,128)(2,1)S(1)}, bf16[32,256]{1,0:T(8,128)(2,1)S(1)}, u32[]{:S(2)}, u32[]{:S(2)}) collective-permute-start(bf16[32,256]{1,0:T(8,128)(2,1)S(1)} %get-tuple-element.38), channel_id=1, source_target_pairs={{0,9},{1,8},{2,11},{3,10},{4,13},{5,12},{6,15},{7,14},{8,1},{9,0},... | collective-permute-start | bytes 49160 | tf_op jit(solution)/shard_map/ppermute | solution.py:344
  16.0 1.5 %collective-permute-start.4 = (bf16[32,256]{1,0:T(8,128)(2,1)S(1)}, bf16[32,256]{1,0:T(8,128)(2,1)S(1)}, u32[]{:S(2)}, u32[]{:S(2)}) collective-permute-start(bf16[32,256]{1,0:T(8,128)(2,1)S(1)} %get-tuple-element.39), channel_id=1, source_target_pairs={{0,13},{1,12},{2,15},{3,14},{4,9},{5,8},{6,11},{7,10},{8,5},{9,4},... | collective-permute-start | bytes 49160 | tf_op jit(solution)/shard_map/ppermute | solution.py:344
  17.5 1.3 %collective-permute-start.5 = (bf16[32,256]{1,0:T(8,128)(2,1)S(1)}, bf16[32,256]{1,0:T(8,128)(2,1)S(1)}, u32[]{:S(2)}, u32[]{:S(2)}) collective-permute-start(bf16[32,256]{1,0:T(8,128)(2,1)S(1)} %get-tuple-element.40), channel_id=1, source_target_pairs={{0,5},{1,4},{2,7},{3,6},{4,1},{5,0},{6,3},{7,2},{8,13},{9,12},{10,... | collective-permute-start | bytes 49160 | tf_op jit(solution)/shard_map/ppermute | solution.py:344
  18.8 0.7 %collective-permute-done.3.refs_1_ = bf16[32,256]{1,0:T(8,128)(2,1)S(1)} collective-permute-done((bf16[32,256]{1,0:T(8,128)(2,1)S(1)}, bf16[32,256]{1,0:T(8,128)(2,1)S(1)}, u32[]{:S(2)}, u32[]{:S(2)}) %collective-permute-start.3) | collective-permute-done | bytes 16416 | tf_op jit(solution)/shard_map/ppermute | solution.py:344
  19.5 1.6 %collective-permute-done.4.refs_2_ = bf16[32,256]{1,0:T(8,128)(2,1)S(1)} collective-permute-done((bf16[32,256]{1,0:T(8,128)(2,1)S(1)}, bf16[32,256]{1,0:T(8,128)(2,1)S(1)}, u32[]{:S(2)}, u32[]{:S(2)}) %collective-permute-start.4) | collective-permute-done | bytes 16416 | tf_op jit(solution)/shard_map/ppermute | solution.py:344
  21.1 0.0 collective-permute-done.5.refs_3_
  21.1 1.6 %collective-permute-start.6 = (bf16[64,256]{1,0:T(8,128)(2,1)S(1)}, bf16[64,256]{1,0:T(8,128)(2,1)S(1)}, u32[]{:S(2)}, u32[]{:S(2)}) collective-permute-start(bf16[64,256]{1,0:T(8,128)(2,1)S(1)} %get-tuple-element.41.refs_1_), channel_id=1, source_target_pairs={{0,3},{1,2},{2,1},{3,0},{4,7},{5,6},{6,5},{7,4},{8,11},{9,10},{10,... | collective-permute-start | bytes 98312 | tf_op jit(solution)/shard_map/ppermute | solution.py:344
  22.7 0.2 collective-permute-start.9
  22.9 0.5 %collective-permute-start.7 = (bf16[64,256]{1,0:T(8,128)(2,1)S(1)}, bf16[64,256]{1,0:T(8,128)(2,1)S(1)}, u32[]{:S(2)}, u32[]{:S(2)}) collective-permute-start(bf16[64,256]{1,0:T(8,128)(2,1)S(1)} %get-tuple-element.41.refs_1_), channel_id=1, source_target_pairs={{0,1},{1,0},{2,3},{3,2},{4,5},{5,4},{6,7},{7,6},{8,9},{9,8},{10,11... | collective-permute-start | bytes 98312 | tf_op jit(solution)/shard_map/ppermute | solution.py:344
  23.4 1.1 %collective-permute-done.6.refs_2_ = bf16[64,256]{1,0:T(8,128)(2,1)S(1)} collective-permute-done((bf16[64,256]{1,0:T(8,128)(2,1)S(1)}, bf16[64,256]{1,0:T(8,128)(2,1)S(1)}, u32[]{:S(2)}, u32[]{:S(2)}) %collective-permute-start.6) | collective-permute-done | bytes 32800 | tf_op jit(solution)/shard_map/ppermute | solution.py:344
  24.5 0.5 %collective-permute-start.8 = (bf16[64,256]{1,0:T(8,128)(2,1)S(1)}, bf16[64,256]{1,0:T(8,128)(2,1)S(1)}, u32[]{:S(2)}, u32[]{:S(2)}) collective-permute-start(bf16[64,256]{1,0:T(8,128)(2,1)S(1)} %collective-permute-done.6.refs_2_), channel_id=1, source_target_pairs={{0,1},{1,0},{2,3},{3,2},{4,5},{5,4},{6,7},{7,6},{8,9},{9,8},{10,11... | collective-permute-start | bytes 98312 | tf_op jit(solution)/shard_map/ppermute | solution.py:344
  25.0 0.1 collective-permute-start.10
  25.0 1.1 %collective-permute-done.9.refs_6_ = bf16[64,256]{1,0:T(8,128)(2,1)S(1)} collective-permute-done((bf16[64,256]{1,0:T(8,128)(2,1)S(1)}, bf16[64,256]{1,0:T(8,128)(2,1)S(1)}, u32[]{:S(2)}, u32[]{:S(2)}) %collective-permute-start.9) | collective-permute-done | bytes 32800 | tf_op jit(solution)/shard_map/ppermute | solution.py:344
  26.1 0.1 collective-permute-start.11
  26.3 0.0 collective-permute-done.7.refs_3_
  26.3 0.0 collective-permute-done.8.refs_4_
  26.3 0.7 %shard_map.69 = (bf16[16,256]{1,0:T(8,128)(2,1)S(1)}, bf16[16,256]{1,0:T(8,128)(2,1)S(1)}, bf16[16,256]{1,0:T(8,128)(2,1)S(1)}, bf16[16,256]{1,0:T(8,128)(2,1)S(1)}) custom-call(bf16[4,256,256]{2,1,0:T(8,128)(2,1)S(1)} %get-tuple-element.29.refs_0_.refs_6_, bf16[64,256]{1,0:T(8,128)(2,1)S(1)} %get-tuple-element.41.refs_1_, ...), custom_call_target="tpu_custom_call" | custom-call | flops 33554432 | bytes 655360 | tf_op jit(solution)/shard_map/pallas_call | solution.py:322
  27.0 0.0 collective-permute-done.10.refs_7_
  27.0 0.4 %collective-permute-done.11.refs_8_ = bf16[64,256]{1,0:T(8,128)(2,1)S(1)} collective-permute-done((bf16[64,256]{1,0:T(8,128)(2,1)S(1)}, bf16[64,256]{1,0:T(8,128)(2,1)S(1)}, u32[]{:S(2)}, u32[]{:S(2)}) %collective-permute-start.11) | collective-permute-done | bytes 32800 | tf_op jit(solution)/shard_map/ppermute | solution.py:344
  27.4 0.7 %shard_map.70 = (bf16[32,256]{1,0:T(8,128)(2,1)S(1)}, bf16[32,256]{1,0:T(8,128)(2,1)S(1)}, bf16[32,256]{1,0:T(8,128)(2,1)S(1)}, bf16[32,256]{1,0:T(8,128)(2,1)S(1)}) custom-call(bf16[4,256,256]{2,1,0:T(8,128)(2,1)S(1)} %get-tuple-element.29.refs_0_.refs_6_, bf16[16,256]{1,0:T(8,128)(2,1)S(1)} %get-tuple-element.42.refs_1_, ...), custom_call_target="tpu_custom_call" | custom-call | flops 33554432 | bytes 688128 | tf_op jit(solution)/shard_map/pallas_call | solution.py:322
  28.1 1.8 %collective-permute-start.12 = (bf16[32,256]{1,0:T(8,128)(2,1)S(1)}, bf16[32,256]{1,0:T(8,128)(2,1)S(1)}, u32[]{:S(2)}, u32[]{:S(2)}) collective-permute-start(bf16[32,256]{1,0:T(8,128)(2,1)S(1)} %get-tuple-element.48), channel_id=1, source_target_pairs={{0,13},{1,12},{2,15},{3,14},{4,9},{5,8},{6,11},{7,10},{8,5},{9,4},... | collective-permute-start | bytes 49160 | tf_op jit(solution)/shard_map/ppermute | solution.py:344
  29.9 0.0 collective-permute-start.13
  29.9 2.1 %collective-permute-start.14 = (bf16[32,256]{1,0:T(8,128)(2,1)S(1)}, bf16[32,256]{1,0:T(8,128)(2,1)S(1)}, u32[]{:S(2)}, u32[]{:S(2)}) collective-permute-start(bf16[32,256]{1,0:T(8,128)(2,1)S(1)} %get-tuple-element.50), channel_id=1, source_target_pairs={{0,5},{1,4},{2,7},{3,6},{4,1},{5,0},{6,3},{7,2},{8,13},{9,12},{10,... | collective-permute-start | bytes 49160 | tf_op jit(solution)/shard_map/ppermute | solution.py:344
  32.0 1.1 %collective-permute-done.12.refs_1_ = bf16[32,256]{1,0:T(8,128)(2,1)S(1)} collective-permute-done((bf16[32,256]{1,0:T(8,128)(2,1)S(1)}, bf16[32,256]{1,0:T(8,128)(2,1)S(1)}, u32[]{:S(2)}, u32[]{:S(2)}) %collective-permute-start.12) | collective-permute-done | bytes 16416 | tf_op jit(solution)/shard_map/ppermute | solution.py:344
  33.1 0.9 %collective-permute-done.13.refs_2_ = bf16[32,256]{1,0:T(8,128)(2,1)S(1)} collective-permute-done((bf16[32,256]{1,0:T(8,128)(2,1)S(1)}, bf16[32,256]{1,0:T(8,128)(2,1)S(1)}, u32[]{:S(2)}, u32[]{:S(2)}) %collective-permute-start.13) | collective-permute-done | bytes 16416 | tf_op jit(solution)/shard_map/ppermute | solution.py:344
  33.9 0.0 collective-permute-done.14.refs_3_
  33.9 0.8 %shard_map.71 = bf16[8,16,256]{2,1,0:T(8,128)(2,1)} custom-call(bf16[32,256]{1,0:T(8,128)(2,1)S(1)} %get-tuple-element.47.refs_0_, bf16[32,256]{1,0:T(8,128)(2,1)S(1)} %collective-permute-done.12.refs_1_, bf16[32,256]{1,0:T(8,128)(2,1)S(1)} %collective-permute-done.13.refs_2_, bf16[32,256]{1,0:T(8,128)(2,1)S(1)} %collective-permute-done.14.refs_3_, ...), custom_call_target="tpu_custom_call" | custom-call | bytes 655360 | tf_op jit(solution)/shard_map/pallas_call | solution.py:322
  (1 shorter events, 0.0 us)
Async XLA Ops:
  0.0 5.5 %copy-start = (bf16[8,16,256]{2,1,0:T(8,128)(2,1)S(1)}, bf16[8,16,256]{2,1,0:T(8,128)(2,1)}, u32[]{:S(2)}) copy-start(bf16[8,16,256]{2,1,0:T(8,128)(2,1)} %refs_0_.7) | copy-start | bytes 196612
  0.0 5.5 %collective-permute-start = (bf16[8,16,256]{2,1,0:T(8,128)(2,1)}, bf16[8,16,256]{2,1,0:T(8,128)(2,1)S(1)}, u32[]{:S(2)}, u32[]{:S(2)}) collective-permute-start(bf16[8,16,256]{2,1,0:T(8,128)(2,1)} %refs_0_.7), channel_id=1, source_target_pairs={{16,0},{0,16},{17,1},{1,17},{18,2},{2,18},{19,3},{3,19},{20,4},{4,... | collective-permute-start | bytes 196616 | tf_op jit(solution)/shard_map/ppermute | solution.py:352
  2.9 0.7 %copy-start.1 = (bf16[7,7,256]{2,1,0:T(8,128)(2,1)S(1)}, bf16[7,7,256]{2,1,0:T(8,128)(2,1)}, u32[]{:S(2)}) copy-start(bf16[7,7,256]{2,1,0:T(8,128)(2,1)} %refs_4_.1) | copy-start | bytes 75268
  5.6 7.0 %collective-permute-start.1 = (bf16[64,256]{1,0:T(8,128)(2,1)S(1)}, bf16[64,256]{1,0:T(8,128)(2,1)S(1)}, u32[]{:S(2)}, u32[]{:S(2)}) collective-permute-start(bf16[64,256]{1,0:T(8,128)(2,1)S(1)} %get-tuple-element.31), channel_id=1, source_target_pairs={{0,15},{1,2},{2,1},{3,4},{4,3},{5,6},{6,5},{7,8},{8,7},{9,10},{10,... | collective-permute-start | bytes 98312 | tf_op jit(solution)/shard_map/ppermute | solution.py:374
  9.4 3.2 %collective-permute-start.2 = (bf16[64,256]{1,0:T(8,128)(2,1)S(1)}, bf16[64,256]{1,0:T(8,128)(2,1)S(1)}, u32[]{:S(2)}, u32[]{:S(2)}) collective-permute-start(bf16[64,256]{1,0:T(8,128)(2,1)S(1)} %get-tuple-element.32), channel_id=1, source_target_pairs={{0,1},{1,0},{2,3},{3,2},{4,5},{5,4},{6,7},{7,6},{8,9},{9,8},{10,11... | collective-permute-start | bytes 98312 | tf_op jit(solution)/shard_map/ppermute | solution.py:344
  15.4 4.1 %collective-permute-start.3 = (bf16[32,256]{1,0:T(8,128)(2,1)S(1)}, bf16[32,256]{1,0:T(8,128)(2,1)S(1)}, u32[]{:S(2)}, u32[]{:S(2)}) collective-permute-start(bf16[32,256]{1,0:T(8,128)(2,1)S(1)} %get-tuple-element.38), channel_id=1, source_target_pairs={{0,9},{1,8},{2,11},{3,10},{4,13},{5,12},{6,15},{7,14},{8,1},{9,0},... | collective-permute-start | bytes 49160 | tf_op jit(solution)/shard_map/ppermute | solution.py:344
  16.0 5.1 %collective-permute-start.4 = (bf16[32,256]{1,0:T(8,128)(2,1)S(1)}, bf16[32,256]{1,0:T(8,128)(2,1)S(1)}, u32[]{:S(2)}, u32[]{:S(2)}) collective-permute-start(bf16[32,256]{1,0:T(8,128)(2,1)S(1)} %get-tuple-element.39), channel_id=1, source_target_pairs={{0,13},{1,12},{2,15},{3,14},{4,9},{5,8},{6,11},{7,10},{8,5},{9,4},... | collective-permute-start | bytes 49160 | tf_op jit(solution)/shard_map/ppermute | solution.py:344
  17.5 3.6 %collective-permute-start.5 = (bf16[32,256]{1,0:T(8,128)(2,1)S(1)}, bf16[32,256]{1,0:T(8,128)(2,1)S(1)}, u32[]{:S(2)}, u32[]{:S(2)}) collective-permute-start(bf16[32,256]{1,0:T(8,128)(2,1)S(1)} %get-tuple-element.40), channel_id=1, source_target_pairs={{0,5},{1,4},{2,7},{3,6},{4,1},{5,0},{6,3},{7,2},{8,13},{9,12},{10,... | collective-permute-start | bytes 49160 | tf_op jit(solution)/shard_map/ppermute | solution.py:344
  21.1 3.4 %collective-permute-start.6 = (bf16[64,256]{1,0:T(8,128)(2,1)S(1)}, bf16[64,256]{1,0:T(8,128)(2,1)S(1)}, u32[]{:S(2)}, u32[]{:S(2)}) collective-permute-start(bf16[64,256]{1,0:T(8,128)(2,1)S(1)} %get-tuple-element.41.refs_1_), channel_id=1, source_target_pairs={{0,3},{1,2},{2,1},{3,0},{4,7},{5,6},{6,5},{7,4},{8,11},{9,10},{10,... | collective-permute-start | bytes 98312 | tf_op jit(solution)/shard_map/ppermute | solution.py:344
  22.7 3.5 %collective-permute-start.9 = (bf16[64,256]{1,0:T(8,128)(2,1)S(1)}, bf16[64,256]{1,0:T(8,128)(2,1)S(1)}, u32[]{:S(2)}, u32[]{:S(2)}) collective-permute-start(bf16[64,256]{1,0:T(8,128)(2,1)S(1)} %get-tuple-element.46.refs_5_), channel_id=1, source_target_pairs={{0,3},{1,2},{2,1},{3,0},{4,7},{5,6},{6,5},{7,4},{8,11},{9,10},{10,... | collective-permute-start | bytes 98312 | tf_op jit(solution)/shard_map/ppermute | solution.py:344
  22.9 3.4 %collective-permute-start.7 = (bf16[64,256]{1,0:T(8,128)(2,1)S(1)}, bf16[64,256]{1,0:T(8,128)(2,1)S(1)}, u32[]{:S(2)}, u32[]{:S(2)}) collective-permute-start(bf16[64,256]{1,0:T(8,128)(2,1)S(1)} %get-tuple-element.41.refs_1_), channel_id=1, source_target_pairs={{0,1},{1,0},{2,3},{3,2},{4,5},{5,4},{6,7},{7,6},{8,9},{9,8},{10,11... | collective-permute-start | bytes 98312 | tf_op jit(solution)/shard_map/ppermute | solution.py:344
  24.5 1.8 %collective-permute-start.8 = (bf16[64,256]{1,0:T(8,128)(2,1)S(1)}, bf16[64,256]{1,0:T(8,128)(2,1)S(1)}, u32[]{:S(2)}, u32[]{:S(2)}) collective-permute-start(bf16[64,256]{1,0:T(8,128)(2,1)S(1)} %collective-permute-done.6.refs_2_), channel_id=1, source_target_pairs={{0,1},{1,0},{2,3},{3,2},{4,5},{5,4},{6,7},{7,6},{8,9},{9,8},{10,11... | collective-permute-start | bytes 98312 | tf_op jit(solution)/shard_map/ppermute | solution.py:344
  25.0 2.0 %collective-permute-start.10 = (bf16[64,256]{1,0:T(8,128)(2,1)S(1)}, bf16[64,256]{1,0:T(8,128)(2,1)S(1)}, u32[]{:S(2)}, u32[]{:S(2)}) collective-permute-start(bf16[64,256]{1,0:T(8,128)(2,1)S(1)} %get-tuple-element.46.refs_5_), channel_id=1, source_target_pairs={{0,1},{1,0},{2,3},{3,2},{4,5},{5,4},{6,7},{7,6},{8,9},{9,8},{10,11... | collective-permute-start | bytes 98312 | tf_op jit(solution)/shard_map/ppermute | solution.py:344
  26.1 1.2 %collective-permute-start.11 = (bf16[64,256]{1,0:T(8,128)(2,1)S(1)}, bf16[64,256]{1,0:T(8,128)(2,1)S(1)}, u32[]{:S(2)}, u32[]{:S(2)}) collective-permute-start(bf16[64,256]{1,0:T(8,128)(2,1)S(1)} %collective-permute-done.9.refs_6_), channel_id=1, source_target_pairs={{0,1},{1,0},{2,3},{3,2},{4,5},{5,4},{6,7},{7,6},{8,9},{9,8},{10,11... | collective-permute-start | bytes 98312 | tf_op jit(solution)/shard_map/ppermute | solution.py:344
  28.1 5.0 %collective-permute-start.12 = (bf16[32,256]{1,0:T(8,128)(2,1)S(1)}, bf16[32,256]{1,0:T(8,128)(2,1)S(1)}, u32[]{:S(2)}, u32[]{:S(2)}) collective-permute-start(bf16[32,256]{1,0:T(8,128)(2,1)S(1)} %get-tuple-element.48), channel_id=1, source_target_pairs={{0,13},{1,12},{2,15},{3,14},{4,9},{5,8},{6,11},{7,10},{8,5},{9,4},... | collective-permute-start | bytes 49160 | tf_op jit(solution)/shard_map/ppermute | solution.py:344
  29.9 4.1 %collective-permute-start.13 = (bf16[32,256]{1,0:T(8,128)(2,1)S(1)}, bf16[32,256]{1,0:T(8,128)(2,1)S(1)}, u32[]{:S(2)}, u32[]{:S(2)}) collective-permute-start(bf16[32,256]{1,0:T(8,128)(2,1)S(1)} %get-tuple-element.49), channel_id=1, source_target_pairs={{0,9},{1,8},{2,11},{3,10},{4,13},{5,12},{6,15},{7,14},{8,1},{9,0},... | collective-permute-start | bytes 49160 | tf_op jit(solution)/shard_map/ppermute | solution.py:344
  29.9 4.1 %collective-permute-start.14 = (bf16[32,256]{1,0:T(8,128)(2,1)S(1)}, bf16[32,256]{1,0:T(8,128)(2,1)S(1)}, u32[]{:S(2)}, u32[]{:S(2)}) collective-permute-start(bf16[32,256]{1,0:T(8,128)(2,1)S(1)} %get-tuple-element.50), channel_id=1, source_target_pairs={{0,5},{1,4},{2,7},{3,6},{4,1},{5,0},{6,3},{7,2},{8,13},{9,12},{10,... | collective-permute-start | bytes 49160 | tf_op jit(solution)/shard_map/ppermute | solution.py:344

commit v23 on v20

--- a/solution.py
+++ b/solution.py
@@ -68,12 +68,11 @@
 
 
 def stage_kernel(count, *refs):
-    sources, dw_ref = refs[:count], refs[count]
-    targets, taps_ref, dw, sems = refs[count + 1 : 2 * count + 1], *refs[2 * count + 1 :]
-    copies = [pltpu.make_async_copy(dw_ref, dw, sems.at[count, 0])]
-    pieces = sems.shape[1]
+    sources, targets, sems = refs[:count], refs[count : 2 * count], refs[-1]
+    copies = []
     for i in range(count):
         source, target = sources[i], targets[i]
+        pieces = sems.shape[1] if source.shape[0] % sems.shape[1] == 0 else 1
         size = source.shape[0] // pieces
         for k in range(pieces):
             part = pl.ds(k * size, size)
@@ -82,7 +81,6 @@
         copy.start()
     for copy in copies:
         copy.wait()
-    taps_ref[...] = dw[...].astype(f32)
 
 
 def hops_of(levels):
@@ -132,8 +130,9 @@
     return jnp.concatenate([low, high], axis=0)
 
 
-def chain(my_lat, slab, shape, taps_ref, expand_ref, reduce_ref, attn_ref, center, scratch):
-    one, lat_in = scratch
+def chain(my_lat, slab, shape, dw_ref, expand_ref, reduce_ref, attn_ref, center, scratch):
+    taps, one, lat_in = scratch
+    taps[...] = dw_ref[...].astype(f32)
     rows, all_rows, columns, channels = shape
     cells = all_rows * columns
     parts = []
@@ -142,7 +141,7 @@
         for b in range(TAPS):
             block = slab(b, c)
             for a in range(TAPS):
-                tap = taps_ref[a, b : b + 1, c : c + LANES].reshape(1, 1, LANES)
+                tap = taps[a, b : b + 1, c : c + LANES].reshape(1, 1, LANES)
                 acc = acc + block[a : a + all_rows] * tap
         parts.append(acc.reshape(cells, LANES))
     normed = layer_norm(jnp.concatenate(parts, axis=-1)).astype(bf16)
@@ -191,7 +190,7 @@
 
 def inner_kernel(nlat, *refs):
     tiles, refs = refs[:nlat], refs[nlat:]
-    taps_ref, expand_ref, reduce_ref, attn_ref, two_ref, in_ref, padded, *scratch = refs
+    dw_ref, expand_ref, reduce_ref, attn_ref, two_ref, in_ref, padded, *scratch = refs
     rows, cols, channels = tiles[0].shape
     all_rows = rows * nlat
     columns = cols - 2 * SIDE
@@ -206,7 +205,7 @@
     center = padded[HALO : HALO + all_rows, SIDE : SIDE + columns]
     shape = (rows, all_rows, columns, channels)
     block_two, lon_in = chain(
-        my_lat, slab, shape, taps_ref, expand_ref, reduce_ref, attn_ref, center, scratch
+        my_lat, slab, shape, dw_ref, expand_ref, reduce_ref, attn_ref, center, scratch
     )
     two_ref[...] = block_two
     in_ref[...] = lon_in.astype(bf16)
@@ -214,7 +213,7 @@
 
 def outer_kernel(nlat, levels, *refs):
     tiles, refs = refs[:nlat], refs[nlat:]
-    far_ref, near_ref, inner_in_ref, taps_ref, expand_ref, reduce_ref, attn_ref = refs[:7]
+    far_ref, near_ref, inner_in_ref, dw_ref, expand_ref, reduce_ref, attn_ref = refs[:7]
     two_ref, *refs = refs[7:]
     sent_refs, (sent, padded, *scratch) = refs[:levels], refs[levels:]
     rows, cols, channels = tiles[0].shape
@@ -246,7 +245,7 @@
     center = halves(0, slice(HALO, HALO + all_rows), 0, channels)
     shape = (rows, all_rows, columns, channels)
     block_two, lon_in = chain(
-        my_lat, slab, shape, taps_ref, expand_ref, reduce_ref, attn_ref, center, scratch
+        my_lat, slab, shape, dw_ref, expand_ref, reduce_ref, attn_ref, center, scratch
     )
     two_ref[...] = block_two
     inner = inner_in_ref[...].astype(f32).reshape(rows, cols - columns, channels)
@@ -350,15 +349,12 @@
     tiles = [field]
     for s in range(1, nlat):
         tiles.append(lax.ppermute(field, "lat", [((i + s) % nlat, i) for i in range(nlat)]))
-    weights = (w_expand, w_reduce, lat_attn, lon_attn)
-    expand, reduce, lat_proj, lon_proj, taps = call(
+    weights = (dw_weight, w_expand, w_reduce, lat_attn, lon_attn)
+    taps, expand, reduce, lat_proj, lon_proj = call(
         functools.partial(stage_kernel, len(weights)),
-        [w.shape for w in weights] + [jax.ShapeDtypeStruct(dw_weight.shape, f32)],
-        [*weights, dw_weight],
-        [
-            pltpu.VMEM(dw_weight.shape, bf16),
-            pltpu.SemaphoreType.DMA((len(weights) + 1, STAGES)),
-        ],
+        [w.shape for w in weights],
+        weights,
+        [pltpu.SemaphoreType.DMA((len(weights), STAGES))],
         any_space=True,
         grant=STAGE_BYTES,
     )
@@ -379,6 +375,7 @@
     def scratch(width, count):
         return [
             pltpu.VMEM((all_rows + 2 * HALO, width, channels), f32),
+            pltpu.VMEM(dw_weight.shape, f32),
             pltpu.VMEM((all_rows * count, channels), bf16),
             pltpu.VMEM((all_rows * count, channels), bf16),
         ]

time: 34.9 us -> 34.7 us (level)
  no operation moved by 1% of the time
where the time goes in v23:
time: 34.7 us; the launch traced here: 34.5 us
  starting transfers between devices  16 us (46%)
  Pallas kernels  9.86 us (28%)
  waiting for transfers between devices  7.79 us (22%)
  local copies, waits for them, and re-layouts  0.75 us (2%)
    pallas_call x8, Pallas kernels, call(): pl.pallas_call(kernel, out_shape=shapes, in_specs=[given] * len(operands)...  9.86 us
    ppermute x13, starting transfers between devices, swap(): return lax.ppermute(piece, 'lon', [(j, j ^ mask) for j in range(nlon)])  9.32 us
    ppermute x13, waiting for transfers between devices, swap(): return lax.ppermute(piece, 'lon', [(j, j ^ mask) for j in range(nlon)])  7.78 us
    ppermute x1, starting transfers between devices, shards(): lax.ppermute(far, 'lon', [(j, (j - 1) % nlon if j % 2 == 0 else (j + 1) %...  3.78 us
    ppermute x1, starting transfers between devices, shards(): lax.ppermute(field, 'lat', [((i + s) % nlat, i) for i in range(nlat)])  2.94 us
    unnamed x4, local copies, waits for them, and re-layouts  0.75 us
  transfers between devices with their start and end apart: 15, of which 7 were waited for; matrix products, arithmetic and copies ran while one was open for 0% of the time, Pallas kernels for 16%

profile of v23, /device:TPU:0, one launch (start us, length us, event | category | flops | bytes accessed | tf_op | source)
XLA Modules:
  0.0 34.5 jit_solution(18072707339603130500)
XLA Ops:
  0.0 0.0 copy-start
  0.0 2.9 %collective-permute-start = (bf16[8,16,256]{2,1,0:T(8,128)(2,1)}, bf16[8,16,256]{2,1,0:T(8,128)(2,1)S(1)}, u32[]{:S(2)}, u32[]{:S(2)}) collective-permute-start(bf16[8,16,256]{2,1,0:T(8,128)(2,1)} %refs_0_.7), channel_id=1, source_target_pairs={{16,0},{0,16},{17,1},{1,17},{18,2},{2,18},{19,3},{3,19},{20,4},{4,... | collective-permute-start | bytes 196616 | tf_op jit(solution)/shard_map/ppermute | solution.py:351
  2.9 0.0 copy-start.1
  2.9 0.7 %copy-done.1 = bf16[7,7,256]{2,1,0:T(8,128)(2,1)S(1)} copy-done((bf16[7,7,256]{2,1,0:T(8,128)(2,1)S(1)}, bf16[7,7,256]{2,1,0:T(8,128)(2,1)}, u32[]{:S(2)}) %copy-start.1) | copy-done | bytes 25112
  3.7 1.8 %shard_map.64 = (bf16[7,7,256]{2,1,0:T(8,128)(2,1)S(1)}, bf16[256,1024]{1,0:T(8,128)(2,1)S(1)}, bf16[1024,256]{1,0:T(8,128)(2,1)S(1)}, bf16[4,256,256]{2,1,0:T(8,128)(2,1)S(1)}, bf16[4,256,256]{2,1,0:T(8,128)(2,1)S(1)}) custom-call(bf16[7,7,256]{2,1,0:T(8,128)(2,1)S(1)} %copy-done.1, bf16[256,1024]{1,0:T(8,128)(2,1)} %refs_1_.1, bf16[1024,256]{1,0:T(8,128)(2,1)} %refs_2_.1, ...), custom_call_target="tpu_custom_call" | custom-call | bytes 2122240 | tf_op jit(solution)/shard_map/pallas_call | solution.py:318
  5.5 0.0 collective-permute-done.refs_1_
  5.5 0.0 copy-done
  5.5 0.1 shard_map.65
  5.6 3.8 %collective-permute-start.1 = (bf16[64,256]{1,0:T(8,128)(2,1)S(1)}, bf16[64,256]{1,0:T(8,128)(2,1)S(1)}, u32[]{:S(2)}, u32[]{:S(2)}) collective-permute-start(bf16[64,256]{1,0:T(8,128)(2,1)S(1)} %get-tuple-element.31), channel_id=1, source_target_pairs={{0,15},{1,2},{2,1},{3,4},{4,3},{5,6},{6,5},{7,8},{8,7},{9,10},{10,... | collective-permute-start | bytes 98312 | tf_op jit(solution)/shard_map/ppermute | solution.py:370
  9.3 0.0 collective-permute-start.2
  9.4 3.2 %shard_map.66 = (bf16[64,256]{1,0:T(8,128)(2,1)S(1)}, bf16[64,256]{1,0:T(8,128)(2,1)S(1)}) custom-call(bf16[8,16,256]{2,1,0:T(8,128)(2,1)S(1)} %copy-done, bf16[8,16,256]{2,1,0:T(8,128)(2,1)S(1)} %collective-permute-done.refs_1_, bf16[7,7,256]{2,1,0:T(8,128)(2,1)S(1)} %get-tuple-element.33.refs_2_.refs_5_, ...), custom_call_target="tpu_custom_call" | custom-call | flops 134217728 | bytes 1729024 | tf_op jit(solution)/shard_map/pallas_call | solution.py:318
  12.6 0.0 collective-permute-done.1.refs_2_
  12.6 0.0 collective-permute-done.2.refs_3_
  12.6 2.6 %shard_map.67 = (bf16[64,256]{1,0:T(8,128)(2,1)S(1)}, bf16[32,256]{1,0:T(8,128)(2,1)S(1)}, bf16[32,256]{1,0:T(8,128)(2,1)S(1)}, bf16[32,256]{1,0:T(8,128)(2,1)S(1)}, bf16[32,256]{1,0:T(8,128)(2,1)S(1)}) custom-call(bf16[8,16,256]{2,1,0:T(8,128)(2,1)S(1)} %copy-done, bf16[8,16,256]{2,1,0:T(8,128)(2,1)S(1)} %collective-permute-done.refs_1_, ...), custom_call_target="tpu_custom_call" | custom-call | flops 134217728 | bytes 1827328 | tf_op jit(solution)/shard_map/pallas_call | solution.py:318
  15.2 0.6 %collective-permute-start.3 = (bf16[32,256]{1,0:T(8,128)(2,1)S(1)}, bf16[32,256]{1,0:T(8,128)(2,1)S(1)}, u32[]{:S(2)}, u32[]{:S(2)}) collective-permute-start(bf16[32,256]{1,0:T(8,128)(2,1)S(1)} %get-tuple-element.38), channel_id=1, source_target_pairs={{0,9},{1,8},{2,11},{3,10},{4,13},{5,12},{6,15},{7,14},{8,1},{9,0},... | collective-permute-start | bytes 49160 | tf_op jit(solution)/shard_map/ppermute | solution.py:340
  15.8 1.5 %collective-permute-start.4 = (bf16[32,256]{1,0:T(8,128)(2,1)S(1)}, bf16[32,256]{1,0:T(8,128)(2,1)S(1)}, u32[]{:S(2)}, u32[]{:S(2)}) collective-permute-start(bf16[32,256]{1,0:T(8,128)(2,1)S(1)} %get-tuple-element.39), channel_id=1, source_target_pairs={{0,13},{1,12},{2,15},{3,14},{4,9},{5,8},{6,11},{7,10},{8,5},{9,4},... | collective-permute-start | bytes 49160 | tf_op jit(solution)/shard_map/ppermute | solution.py:340
  17.3 1.3 %collective-permute-start.5 = (bf16[32,256]{1,0:T(8,128)(2,1)S(1)}, bf16[32,256]{1,0:T(8,128)(2,1)S(1)}, u32[]{:S(2)}, u32[]{:S(2)}) collective-permute-start(bf16[32,256]{1,0:T(8,128)(2,1)S(1)} %get-tuple-element.40), channel_id=1, source_target_pairs={{0,5},{1,4},{2,7},{3,6},{4,1},{5,0},{6,3},{7,2},{8,13},{9,12},{10,... | collective-permute-start | bytes 49160 | tf_op jit(solution)/shard_map/ppermute | solution.py:340
  18.6 0.7 %collective-permute-done.3.refs_1_ = bf16[32,256]{1,0:T(8,128)(2,1)S(1)} collective-permute-done((bf16[32,256]{1,0:T(8,128)(2,1)S(1)}, bf16[32,256]{1,0:T(8,128)(2,1)S(1)}, u32[]{:S(2)}, u32[]{:S(2)}) %collective-permute-start.3) | collective-permute-done | bytes 16416 | tf_op jit(solution)/shard_map/ppermute | solution.py:340
  19.4 1.6 %collective-permute-done.4.refs_2_ = bf16[32,256]{1,0:T(8,128)(2,1)S(1)} collective-permute-done((bf16[32,256]{1,0:T(8,128)(2,1)S(1)}, bf16[32,256]{1,0:T(8,128)(2,1)S(1)}, u32[]{:S(2)}, u32[]{:S(2)}) %collective-permute-start.4) | collective-permute-done | bytes 16416 | tf_op jit(solution)/shard_map/ppermute | solution.py:340
  20.9 0.0 collective-permute-done.5.refs_3_
  20.9 1.6 %collective-permute-start.6 = (bf16[64,256]{1,0:T(8,128)(2,1)S(1)}, bf16[64,256]{1,0:T(8,128)(2,1)S(1)}, u32[]{:S(2)}, u32[]{:S(2)}) collective-permute-start(bf16[64,256]{1,0:T(8,128)(2,1)S(1)} %get-tuple-element.41.refs_1_), channel_id=1, source_target_pairs={{0,3},{1,2},{2,1},{3,0},{4,7},{5,6},{6,5},{7,4},{8,11},{9,10},{10,... | collective-permute-start | bytes 98312 | tf_op jit(solution)/shard_map/ppermute | solution.py:340
  22.5 0.2 collective-permute-start.9
  22.7 0.5 %collective-permute-start.7 = (bf16[64,256]{1,0:T(8,128)(2,1)S(1)}, bf16[64,256]{1,0:T(8,128)(2,1)S(1)}, u32[]{:S(2)}, u32[]{:S(2)}) collective-permute-start(bf16[64,256]{1,0:T(8,128)(2,1)S(1)} %get-tuple-element.41.refs_1_), channel_id=1, source_target_pairs={{0,1},{1,0},{2,3},{3,2},{4,5},{5,4},{6,7},{7,6},{8,9},{9,8},{10,11... | collective-permute-start | bytes 98312 | tf_op jit(solution)/shard_map/ppermute | solution.py:340
  23.2 1.1 %collective-permute-done.6.refs_2_ = bf16[64,256]{1,0:T(8,128)(2,1)S(1)} collective-permute-done((bf16[64,256]{1,0:T(8,128)(2,1)S(1)}, bf16[64,256]{1,0:T(8,128)(2,1)S(1)}, u32[]{:S(2)}, u32[]{:S(2)}) %collective-permute-start.6) | collective-permute-done | bytes 32800 | tf_op jit(solution)/shard_map/ppermute | solution.py:340
  24.3 0.5 %collective-permute-start.8 = (bf16[64,256]{1,0:T(8,128)(2,1)S(1)}, bf16[64,256]{1,0:T(8,128)(2,1)S(1)}, u32[]{:S(2)}, u32[]{:S(2)}) collective-permute-start(bf16[64,256]{1,0:T(8,128)(2,1)S(1)} %collective-permute-done.6.refs_2_), channel_id=1, source_target_pairs={{0,1},{1,0},{2,3},{3,2},{4,5},{5,4},{6,7},{7,6},{8,9},{9,8},{10,11... | collective-permute-start | bytes 98312 | tf_op jit(solution)/shard_map/ppermute | solution.py:340
  24.8 0.1 collective-permute-start.10
  24.8 1.1 %collective-permute-done.9.refs_6_ = bf16[64,256]{1,0:T(8,128)(2,1)S(1)} collective-permute-done((bf16[64,256]{1,0:T(8,128)(2,1)S(1)}, bf16[64,256]{1,0:T(8,128)(2,1)S(1)}, u32[]{:S(2)}, u32[]{:S(2)}) %collective-permute-start.9) | collective-permute-done | bytes 32800 | tf_op jit(solution)/shard_map/ppermute | solution.py:340
  26.0 0.1 collective-permute-start.11
  26.1 0.0 collective-permute-done.7.refs_3_
  26.1 0.0 collective-permute-done.8.refs_4_
  26.1 0.7 %shard_map.69 = (bf16[16,256]{1,0:T(8,128)(2,1)S(1)}, bf16[16,256]{1,0:T(8,128)(2,1)S(1)}, bf16[16,256]{1,0:T(8,128)(2,1)S(1)}, bf16[16,256]{1,0:T(8,128)(2,1)S(1)}) custom-call(bf16[4,256,256]{2,1,0:T(8,128)(2,1)S(1)} %get-tuple-element.29.refs_0_.refs_6_, bf16[64,256]{1,0:T(8,128)(2,1)S(1)} %get-tuple-element.41.refs_1_, ...), custom_call_target="tpu_custom_call" | custom-call | flops 33554432 | bytes 655360 | tf_op jit(solution)/shard_map/pallas_call | solution.py:318
  26.8 0.0 collective-permute-done.10.refs_7_
  26.8 0.4 %collective-permute-done.11.refs_8_ = bf16[64,256]{1,0:T(8,128)(2,1)S(1)} collective-permute-done((bf16[64,256]{1,0:T(8,128)(2,1)S(1)}, bf16[64,256]{1,0:T(8,128)(2,1)S(1)}, u32[]{:S(2)}, u32[]{:S(2)}) %collective-permute-start.11) | collective-permute-done | bytes 32800 | tf_op jit(solution)/shard_map/ppermute | solution.py:340
  27.2 0.7 %shard_map.70 = (bf16[32,256]{1,0:T(8,128)(2,1)S(1)}, bf16[32,256]{1,0:T(8,128)(2,1)S(1)}, bf16[32,256]{1,0:T(8,128)(2,1)S(1)}, bf16[32,256]{1,0:T(8,128)(2,1)S(1)}) custom-call(bf16[4,256,256]{2,1,0:T(8,128)(2,1)S(1)} %get-tuple-element.29.refs_0_.refs_6_, bf16[16,256]{1,0:T(8,128)(2,1)S(1)} %get-tuple-element.42.refs_1_, ...), custom_call_target="tpu_custom_call" | custom-call | flops 33554432 | bytes 688128 | tf_op jit(solution)/shard_map/pallas_call | solution.py:318
  27.9 0.9 %collective-permute-start.12 = (bf16[32,256]{1,0:T(8,128)(2,1)S(1)}, bf16[32,256]{1,0:T(8,128)(2,1)S(1)}, u32[]{:S(2)}, u32[]{:S(2)}) collective-permute-start(bf16[32,256]{1,0:T(8,128)(2,1)S(1)} %get-tuple-element.48), channel_id=1, source_target_pairs={{0,9},{1,8},{2,11},{3,10},{4,13},{5,12},{6,15},{7,14},{8,1},{9,0},... | collective-permute-start | bytes 49160 | tf_op jit(solution)/shard_map/ppermute | solution.py:340
  28.8 1.5 %collective-permute-start.13 = (bf16[32,256]{1,0:T(8,128)(2,1)S(1)}, bf16[32,256]{1,0:T(8,128)(2,1)S(1)}, u32[]{:S(2)}, u32[]{:S(2)}) collective-permute-start(bf16[32,256]{1,0:T(8,128)(2,1)S(1)} %get-tuple-element.49), channel_id=1, source_target_pairs={{0,13},{1,12},{2,15},{3,14},{4,9},{5,8},{6,11},{7,10},{8,5},{9,4},... | collective-permute-start | bytes 49160 | tf_op jit(solution)/shard_map/ppermute | solution.py:340
  30.2 0.7 %collective-permute-start.14 = (bf16[32,256]{1,0:T(8,128)(2,1)S(1)}, bf16[32,256]{1,0:T(8,128)(2,1)S(1)}, u32[]{:S(2)}, u32[]{:S(2)}) collective-permute-start(bf16[32,256]{1,0:T(8,128)(2,1)S(1)} %get-tuple-element.50), channel_id=1, source_target_pairs={{0,5},{1,4},{2,7},{3,6},{4,1},{5,0},{6,3},{7,2},{8,13},{9,12},{10,... | collective-permute-start | bytes 49160 | tf_op jit(solution)/shard_map/ppermute | solution.py:340
  30.9 1.1 %collective-permute-done.12.refs_1_ = bf16[32,256]{1,0:T(8,128)(2,1)S(1)} collective-permute-done((bf16[32,256]{1,0:T(8,128)(2,1)S(1)}, bf16[32,256]{1,0:T(8,128)(2,1)S(1)}, u32[]{:S(2)}, u32[]{:S(2)}) %collective-permute-start.12) | collective-permute-done | bytes 16416 | tf_op jit(solution)/shard_map/ppermute | solution.py:340
  32.0 1.7 %collective-permute-done.13.refs_2_ = bf16[32,256]{1,0:T(8,128)(2,1)S(1)} collective-permute-done((bf16[32,256]{1,0:T(8,128)(2,1)S(1)}, bf16[32,256]{1,0:T(8,128)(2,1)S(1)}, u32[]{:S(2)}, u32[]{:S(2)}) %collective-permute-start.13) | collective-permute-done | bytes 16416 | tf_op jit(solution)/shard_map/ppermute | solution.py:340
  33.7 0.0 collective-permute-done.14.refs_3_
  33.7 0.8 %shard_map.71 = bf16[8,16,256]{2,1,0:T(8,128)(2,1)} custom-call(bf16[32,256]{1,0:T(8,128)(2,1)S(1)} %get-tuple-element.47.refs_0_, bf16[32,256]{1,0:T(8,128)(2,1)S(1)} %collective-permute-done.12.refs_1_, bf16[32,256]{1,0:T(8,128)(2,1)S(1)} %collective-permute-done.13.refs_2_, bf16[32,256]{1,0:T(8,128)(2,1)S(1)} %collective-permute-done.14.refs_3_, ...), custom_call_target="tpu_custom_call" | custom-call | bytes 655360 | tf_op jit(solution)/shard_map/pallas_call | solution.py:318
  (1 shorter events, 0.0 us)
Async XLA Ops:
  0.0 5.5 %copy-start = (bf16[8,16,256]{2,1,0:T(8,128)(2,1)S(1)}, bf16[8,16,256]{2,1,0:T(8,128)(2,1)}, u32[]{:S(2)}) copy-start(bf16[8,16,256]{2,1,0:T(8,128)(2,1)} %refs_0_.7) | copy-start | bytes 196612
  0.0 5.5 %collective-permute-start = (bf16[8,16,256]{2,1,0:T(8,128)(2,1)}, bf16[8,16,256]{2,1,0:T(8,128)(2,1)S(1)}, u32[]{:S(2)}, u32[]{:S(2)}) collective-permute-start(bf16[8,16,256]{2,1,0:T(8,128)(2,1)} %refs_0_.7), channel_id=1, source_target_pairs={{16,0},{0,16},{17,1},{1,17},{18,2},{2,18},{19,3},{3,19},{20,4},{4,... | collective-permute-start | bytes 196616 | tf_op jit(solution)/shard_map/ppermute | solution.py:351
  2.9 0.7 %copy-start.1 = (bf16[7,7,256]{2,1,0:T(8,128)(2,1)S(1)}, bf16[7,7,256]{2,1,0:T(8,128)(2,1)}, u32[]{:S(2)}) copy-start(bf16[7,7,256]{2,1,0:T(8,128)(2,1)} %refs_0_.4) | copy-start | bytes 75268
  5.6 7.0 %collective-permute-start.1 = (bf16[64,256]{1,0:T(8,128)(2,1)S(1)}, bf16[64,256]{1,0:T(8,128)(2,1)S(1)}, u32[]{:S(2)}, u32[]{:S(2)}) collective-permute-start(bf16[64,256]{1,0:T(8,128)(2,1)S(1)} %get-tuple-element.31), channel_id=1, source_target_pairs={{0,15},{1,2},{2,1},{3,4},{4,3},{5,6},{6,5},{7,8},{8,7},{9,10},{10,... | collective-permute-start | bytes 98312 | tf_op jit(solution)/shard_map/ppermute | solution.py:370
  9.3 3.2 %collective-permute-start.2 = (bf16[64,256]{1,0:T(8,128)(2,1)S(1)}, bf16[64,256]{1,0:T(8,128)(2,1)S(1)}, u32[]{:S(2)}, u32[]{:S(2)}) collective-permute-start(bf16[64,256]{1,0:T(8,128)(2,1)S(1)} %get-tuple-element.32), channel_id=1, source_target_pairs={{0,1},{1,0},{2,3},{3,2},{4,5},{5,4},{6,7},{7,6},{8,9},{9,8},{10,11... | collective-permute-start | bytes 98312 | tf_op jit(solution)/shard_map/ppermute | solution.py:340
  15.2 4.1 %collective-permute-start.3 = (bf16[32,256]{1,0:T(8,128)(2,1)S(1)}, bf16[32,256]{1,0:T(8,128)(2,1)S(1)}, u32[]{:S(2)}, u32[]{:S(2)}) collective-permute-start(bf16[32,256]{1,0:T(8,128)(2,1)S(1)} %get-tuple-element.38), channel_id=1, source_target_pairs={{0,9},{1,8},{2,11},{3,10},{4,13},{5,12},{6,15},{7,14},{8,1},{9,0},... | collective-permute-start | bytes 49160 | tf_op jit(solution)/shard_map/ppermute | solution.py:340
  15.8 5.1 %collective-permute-start.4 = (bf16[32,256]{1,0:T(8,128)(2,1)S(1)}, bf16[32,256]{1,0:T(8,128)(2,1)S(1)}, u32[]{:S(2)}, u32[]{:S(2)}) collective-permute-start(bf16[32,256]{1,0:T(8,128)(2,1)S(1)} %get-tuple-element.39), channel_id=1, source_target_pairs={{0,13},{1,12},{2,15},{3,14},{4,9},{5,8},{6,11},{7,10},{8,5},{9,4},... | collective-permute-start | bytes 49160 | tf_op jit(solution)/shard_map/ppermute | solution.py:340
  17.3 3.6 %collective-permute-start.5 = (bf16[32,256]{1,0:T(8,128)(2,1)S(1)}, bf16[32,256]{1,0:T(8,128)(2,1)S(1)}, u32[]{:S(2)}, u32[]{:S(2)}) collective-permute-start(bf16[32,256]{1,0:T(8,128)(2,1)S(1)} %get-tuple-element.40), channel_id=1, source_target_pairs={{0,5},{1,4},{2,7},{3,6},{4,1},{5,0},{6,3},{7,2},{8,13},{9,12},{10,... | collective-permute-start | bytes 49160 | tf_op jit(solution)/shard_map/ppermute | solution.py:340
  20.9 3.4 %collective-permute-start.6 = (bf16[64,256]{1,0:T(8,128)(2,1)S(1)}, bf16[64,256]{1,0:T(8,128)(2,1)S(1)}, u32[]{:S(2)}, u32[]{:S(2)}) collective-permute-start(bf16[64,256]{1,0:T(8,128)(2,1)S(1)} %get-tuple-element.41.refs_1_), channel_id=1, source_target_pairs={{0,3},{1,2},{2,1},{3,0},{4,7},{5,6},{6,5},{7,4},{8,11},{9,10},{10,... | collective-permute-start | bytes 98312 | tf_op jit(solution)/shard_map/ppermute | solution.py:340
  22.5 3.5 %collective-permute-start.9 = (bf16[64,256]{1,0:T(8,128)(2,1)S(1)}, bf16[64,256]{1,0:T(8,128)(2,1)S(1)}, u32[]{:S(2)}, u32[]{:S(2)}) collective-permute-start(bf16[64,256]{1,0:T(8,128)(2,1)S(1)} %get-tuple-element.46.refs_5_), channel_id=1, source_target_pairs={{0,3},{1,2},{2,1},{3,0},{4,7},{5,6},{6,5},{7,4},{8,11},{9,10},{10,... | collective-permute-start | bytes 98312 | tf_op jit(solution)/shard_map/ppermute | solution.py:340
  22.7 3.4 %collective-permute-start.7 = (bf16[64,256]{1,0:T(8,128)(2,1)S(1)}, bf16[64,256]{1,0:T(8,128)(2,1)S(1)}, u32[]{:S(2)}, u32[]{:S(2)}) collective-permute-start(bf16[64,256]{1,0:T(8,128)(2,1)S(1)} %get-tuple-element.41.refs_1_), channel_id=1, source_target_pairs={{0,1},{1,0},{2,3},{3,2},{4,5},{5,4},{6,7},{7,6},{8,9},{9,8},{10,11... | collective-permute-start | bytes 98312 | tf_op jit(solution)/shard_map/ppermute | solution.py:340
  24.3 1.8 %collective-permute-start.8 = (bf16[64,256]{1,0:T(8,128)(2,1)S(1)}, bf16[64,256]{1,0:T(8,128)(2,1)S(1)}, u32[]{:S(2)}, u32[]{:S(2)}) collective-permute-start(bf16[64,256]{1,0:T(8,128)(2,1)S(1)} %collective-permute-done.6.refs_2_), channel_id=1, source_target_pairs={{0,1},{1,0},{2,3},{3,2},{4,5},{5,4},{6,7},{7,6},{8,9},{9,8},{10,11... | collective-permute-start | bytes 98312 | tf_op jit(solution)/shard_map/ppermute | solution.py:340
  24.8 2.0 %collective-permute-start.10 = (bf16[64,256]{1,0:T(8,128)(2,1)S(1)}, bf16[64,256]{1,0:T(8,128)(2,1)S(1)}, u32[]{:S(2)}, u32[]{:S(2)}) collective-permute-start(bf16[64,256]{1,0:T(8,128)(2,1)S(1)} %get-tuple-element.46.refs_5_), channel_id=1, source_target_pairs={{0,1},{1,0},{2,3},{3,2},{4,5},{5,4},{6,7},{7,6},{8,9},{9,8},{10,11... | collective-permute-start | bytes 98312 | tf_op jit(solution)/shard_map/ppermute | solution.py:340
  26.0 1.2 %collective-permute-start.11 = (bf16[64,256]{1,0:T(8,128)(2,1)S(1)}, bf16[64,256]{1,0:T(8,128)(2,1)S(1)}, u32[]{:S(2)}, u32[]{:S(2)}) collective-permute-start(bf16[64,256]{1,0:T(8,128)(2,1)S(1)} %collective-permute-done.9.refs_6_), channel_id=1, source_target_pairs={{0,1},{1,0},{2,3},{3,2},{4,5},{5,4},{6,7},{7,6},{8,9},{9,8},{10,11... | collective-permute-start | bytes 98312 | tf_op jit(solution)/shard_map/ppermute | solution.py:340
  27.9 4.1 %collective-permute-start.12 = (bf16[32,256]{1,0:T(8,128)(2,1)S(1)}, bf16[32,256]{1,0:T(8,128)(2,1)S(1)}, u32[]{:S(2)}, u32[]{:S(2)}) collective-permute-start(bf16[32,256]{1,0:T(8,128)(2,1)S(1)} %get-tuple-element.48), channel_id=1, source_target_pairs={{0,9},{1,8},{2,11},{3,10},{4,13},{5,12},{6,15},{7,14},{8,1},{9,0},... | collective-permute-start | bytes 49160 | tf_op jit(solution)/shard_map/ppermute | solution.py:340
  28.8 5.0 %collective-permute-start.13 = (bf16[32,256]{1,0:T(8,128)(2,1)S(1)}, bf16[32,256]{1,0:T(8,128)(2,1)S(1)}, u32[]{:S(2)}, u32[]{:S(2)}) collective-permute-start(bf16[32,256]{1,0:T(8,128)(2,1)S(1)} %get-tuple-element.49), channel_id=1, source_target_pairs={{0,13},{1,12},{2,15},{3,14},{4,9},{5,8},{6,11},{7,10},{8,5},{9,4},... | collective-permute-start | bytes 49160 | tf_op jit(solution)/shard_map/ppermute | solution.py:340
  30.2 3.5 %collective-permute-start.14 = (bf16[32,256]{1,0:T(8,128)(2,1)S(1)}, bf16[32,256]{1,0:T(8,128)(2,1)S(1)}, u32[]{:S(2)}, u32[]{:S(2)}) collective-permute-start(bf16[32,256]{1,0:T(8,128)(2,1)S(1)} %get-tuple-element.50), channel_id=1, source_target_pairs={{0,5},{1,4},{2,7},{3,6},{4,1},{5,0},{6,3},{7,2},{8,13},{9,12},{10,... | collective-permute-start | bytes 49160 | tf_op jit(solution)/shard_map/ppermute | solution.py:340

commit v24 on v23

--- a/solution.py
+++ b/solution.py
@@ -284,12 +284,13 @@
 
 def last_kernel(levels, *refs):
     parts = refs[:levels]
-    inner_ref, outer_ref, attn_ref, out_ref = refs[levels:]
+    inner_ref, outer_ref, attn_ref, out_ref, ready, sems = refs[levels:]
     rows, cols, channels = out_ref.shape
     columns = 2 * SIDE
     some = rows // levels
     every = jnp.concatenate([part[...] for part in parts], axis=0)
     change = dot(every, attn_ref[3]).reshape(levels, some, cols, channels)
+    copies = []
     for k in range(levels):
         start = peer(levels, k) * some
 
@@ -302,11 +303,16 @@
             [state(inner_ref, cols - columns), state(outer_ref, columns)], axis=1
         )
         total = pltpu.roll(before + change[k], SIDE, axis=1)
-        out_ref[pl.ds(start, some)] = total.astype(bf16)
+        ready[k] = total.astype(bf16)
+        place = out_ref.at[pl.ds(start, some)]
+        copies.append(pltpu.make_async_copy(ready.at[k], place, sems.at[k]))
+        copies[-1].start()
+    for copy in copies:
+        copy.wait()
 
 
 def call(
-    kernel, outs, operands, scratch=(), any_space=False, flops=0, grant=VMEM_BYTES
+    kernel, outs, operands, scratch=(), any_space=False, far_out=False, flops=0, grant=VMEM_BYTES
 ):
     vmem = pl.BlockSpec(memory_space=pltpu.VMEM)
     given = pl.BlockSpec(memory_space=pl.ANY) if any_space else vmem
@@ -319,7 +325,7 @@
         kernel,
         out_shape=shapes,
         in_specs=[given] * len(operands),
-        out_specs=[vmem] * len(outs),
+        out_specs=[pl.BlockSpec(memory_space=pl.ANY) if far_out else vmem] * len(outs),
         scratch_shapes=list(scratch),
         compiler_params=pltpu.CompilerParams(vmem_limit_bytes=grant),
         cost_estimate=pl.CostEstimate(flops=flops, bytes_accessed=moved, transcendentals=0),
@@ -422,6 +428,11 @@
         functools.partial(last_kernel, levels),
         [(rows, cols, channels)],
         [*mixes, inner_two, outer_two, lon_proj],
+        [
+            pltpu.VMEM((levels, some, cols, channels), bf16),
+            pltpu.SemaphoreType.DMA((levels,)),
+        ],
+        far_out=True,
     )
     return out
 

time: 34.7 us -> 34.8 us (level)
  no operation moved by 1% of the time
where the time goes in v24:
time: 34.8 us; the launch traced here: 34.6 us
  starting transfers between devices  16 us (46%)
  Pallas kernels  9.88 us (28%)
  waiting for transfers between devices  7.79 us (22%)
  local copies, waits for them, and re-layouts  0.75 us (2%)
    pallas_call x8, Pallas kernels, call(): pl.pallas_call(kernel, out_shape=shapes, in_specs=[given] * len(operands)...  9.88 us
    ppermute x13, starting transfers between devices, swap(): return lax.ppermute(piece, 'lon', [(j, j ^ mask) for j in range(nlon)])  9.32 us
    ppermute x13, waiting for transfers between devices, swap(): return lax.ppermute(piece, 'lon', [(j, j ^ mask) for j in range(nlon)])  7.78 us
    ppermute x1, starting transfers between devices, shards(): lax.ppermute(far, 'lon', [(j, (j - 1) % nlon if j % 2 == 0 else (j + 1) %...  3.78 us
    ppermute x1, starting transfers between devices, shards(): lax.ppermute(field, 'lat', [((i + s) % nlat, i) for i in range(nlat)])  2.94 us
    unnamed x4, local copies, waits for them, and re-layouts  0.75 us
  transfers between devices with their start and end apart: 15, of which 7 were waited for; matrix products, arithmetic and copies ran while one was open for 0% of the time, Pallas kernels for 16%

profile of v24, /device:TPU:0, one launch (start us, length us, event | category | flops | bytes accessed | tf_op | source)
XLA Modules:
  0.0 34.6 jit_solution(17248100207862768517)
XLA Ops:
  0.0 0.0 copy-start
  0.0 2.9 %collective-permute-start = (bf16[8,16,256]{2,1,0:T(8,128)(2,1)}, bf16[8,16,256]{2,1,0:T(8,128)(2,1)S(1)}, u32[]{:S(2)}, u32[]{:S(2)}) collective-permute-start(bf16[8,16,256]{2,1,0:T(8,128)(2,1)} %refs_0_.7), channel_id=1, source_target_pairs={{16,0},{0,16},{17,1},{1,17},{18,2},{2,18},{19,3},{3,19},{20,4},{4,... | collective-permute-start | bytes 196616 | tf_op jit(solution)/shard_map/ppermute | solution.py:357
  2.9 0.0 copy-start.1
  2.9 0.7 %copy-done.1 = bf16[7,7,256]{2,1,0:T(8,128)(2,1)S(1)} copy-done((bf16[7,7,256]{2,1,0:T(8,128)(2,1)S(1)}, bf16[7,7,256]{2,1,0:T(8,128)(2,1)}, u32[]{:S(2)}) %copy-start.1) | copy-done | bytes 25112
  3.7 1.8 %shard_map.64 = (bf16[7,7,256]{2,1,0:T(8,128)(2,1)S(1)}, bf16[256,1024]{1,0:T(8,128)(2,1)S(1)}, bf16[1024,256]{1,0:T(8,128)(2,1)S(1)}, bf16[4,256,256]{2,1,0:T(8,128)(2,1)S(1)}, bf16[4,256,256]{2,1,0:T(8,128)(2,1)S(1)}) custom-call(bf16[7,7,256]{2,1,0:T(8,128)(2,1)S(1)} %copy-done.1, bf16[256,1024]{1,0:T(8,128)(2,1)} %refs_1_.1, bf16[1024,256]{1,0:T(8,128)(2,1)} %refs_2_.1, ...), custom_call_target="tpu_custom_call" | custom-call | bytes 2122240 | tf_op jit(solution)/shard_map/pallas_call | solution.py:324
  5.5 0.0 collective-permute-done.refs_1_
  5.5 0.0 copy-done
  5.5 0.1 shard_map.65
  5.6 3.8 %collective-permute-start.1 = (bf16[64,256]{1,0:T(8,128)(2,1)S(1)}, bf16[64,256]{1,0:T(8,128)(2,1)S(1)}, u32[]{:S(2)}, u32[]{:S(2)}) collective-permute-start(bf16[64,256]{1,0:T(8,128)(2,1)S(1)} %get-tuple-element.31), channel_id=1, source_target_pairs={{0,15},{1,2},{2,1},{3,4},{4,3},{5,6},{6,5},{7,8},{8,7},{9,10},{10,... | collective-permute-start | bytes 98312 | tf_op jit(solution)/shard_map/ppermute | solution.py:376
  9.3 0.0 collective-permute-start.2
  9.4 3.2 %shard_map.66 = (bf16[64,256]{1,0:T(8,128)(2,1)S(1)}, bf16[64,256]{1,0:T(8,128)(2,1)S(1)}) custom-call(bf16[8,16,256]{2,1,0:T(8,128)(2,1)S(1)} %copy-done, bf16[8,16,256]{2,1,0:T(8,128)(2,1)S(1)} %collective-permute-done.refs_1_, bf16[7,7,256]{2,1,0:T(8,128)(2,1)S(1)} %get-tuple-element.33.refs_2_.refs_5_, ...), custom_call_target="tpu_custom_call" | custom-call | flops 134217728 | bytes 1729024 | tf_op jit(solution)/shard_map/pallas_call | solution.py:324
  12.6 0.0 collective-permute-done.1.refs_2_
  12.6 0.0 collective-permute-done.2.refs_3_
  12.6 2.6 %shard_map.67 = (bf16[64,256]{1,0:T(8,128)(2,1)S(1)}, bf16[32,256]{1,0:T(8,128)(2,1)S(1)}, bf16[32,256]{1,0:T(8,128)(2,1)S(1)}, bf16[32,256]{1,0:T(8,128)(2,1)S(1)}, bf16[32,256]{1,0:T(8,128)(2,1)S(1)}) custom-call(bf16[8,16,256]{2,1,0:T(8,128)(2,1)S(1)} %copy-done, bf16[8,16,256]{2,1,0:T(8,128)(2,1)S(1)} %collective-permute-done.refs_1_, ...), custom_call_target="tpu_custom_call" | custom-call | flops 134217728 | bytes 1827328 | tf_op jit(solution)/shard_map/pallas_call | solution.py:324
  15.2 0.6 %collective-permute-start.3 = (bf16[32,256]{1,0:T(8,128)(2,1)S(1)}, bf16[32,256]{1,0:T(8,128)(2,1)S(1)}, u32[]{:S(2)}, u32[]{:S(2)}) collective-permute-start(bf16[32,256]{1,0:T(8,128)(2,1)S(1)} %get-tuple-element.38), channel_id=1, source_target_pairs={{0,9},{1,8},{2,11},{3,10},{4,13},{5,12},{6,15},{7,14},{8,1},{9,0},... | collective-permute-start | bytes 49160 | tf_op jit(solution)/shard_map/ppermute | solution.py:346
  15.8 1.5 %collective-permute-start.4 = (bf16[32,256]{1,0:T(8,128)(2,1)S(1)}, bf16[32,256]{1,0:T(8,128)(2,1)S(1)}, u32[]{:S(2)}, u32[]{:S(2)}) collective-permute-start(bf16[32,256]{1,0:T(8,128)(2,1)S(1)} %get-tuple-element.39), channel_id=1, source_target_pairs={{0,13},{1,12},{2,15},{3,14},{4,9},{5,8},{6,11},{7,10},{8,5},{9,4},... | collective-permute-start | bytes 49160 | tf_op jit(solution)/shard_map/ppermute | solution.py:346
  17.3 1.3 %collective-permute-start.5 = (bf16[32,256]{1,0:T(8,128)(2,1)S(1)}, bf16[32,256]{1,0:T(8,128)(2,1)S(1)}, u32[]{:S(2)}, u32[]{:S(2)}) collective-permute-start(bf16[32,256]{1,0:T(8,128)(2,1)S(1)} %get-tuple-element.40), channel_id=1, source_target_pairs={{0,5},{1,4},{2,7},{3,6},{4,1},{5,0},{6,3},{7,2},{8,13},{9,12},{10,... | collective-permute-start | bytes 49160 | tf_op jit(solution)/shard_map/ppermute | solution.py:346
  18.6 0.7 %collective-permute-done.3.refs_1_ = bf16[32,256]{1,0:T(8,128)(2,1)S(1)} collective-permute-done((bf16[32,256]{1,0:T(8,128)(2,1)S(1)}, bf16[32,256]{1,0:T(8,128)(2,1)S(1)}, u32[]{:S(2)}, u32[]{:S(2)}) %collective-permute-start.3) | collective-permute-done | bytes 16416 | tf_op jit(solution)/shard_map/ppermute | solution.py:346
  19.4 1.6 %collective-permute-done.4.refs_2_ = bf16[32,256]{1,0:T(8,128)(2,1)S(1)} collective-permute-done((bf16[32,256]{1,0:T(8,128)(2,1)S(1)}, bf16[32,256]{1,0:T(8,128)(2,1)S(1)}, u32[]{:S(2)}, u32[]{:S(2)}) %collective-permute-start.4) | collective-permute-done | bytes 16416 | tf_op jit(solution)/shard_map/ppermute | solution.py:346
  20.9 0.0 collective-permute-done.5.refs_3_
  20.9 1.6 %collective-permute-start.6 = (bf16[64,256]{1,0:T(8,128)(2,1)S(1)}, bf16[64,256]{1,0:T(8,128)(2,1)S(1)}, u32[]{:S(2)}, u32[]{:S(2)}) collective-permute-start(bf16[64,256]{1,0:T(8,128)(2,1)S(1)} %get-tuple-element.41.refs_1_), channel_id=1, source_target_pairs={{0,3},{1,2},{2,1},{3,0},{4,7},{5,6},{6,5},{7,4},{8,11},{9,10},{10,... | collective-permute-start | bytes 98312 | tf_op jit(solution)/shard_map/ppermute | solution.py:346
  22.5 0.2 collective-permute-start.9
  22.7 0.5 %collective-permute-start.7 = (bf16[64,256]{1,0:T(8,128)(2,1)S(1)}, bf16[64,256]{1,0:T(8,128)(2,1)S(1)}, u32[]{:S(2)}, u32[]{:S(2)}) collective-permute-start(bf16[64,256]{1,0:T(8,128)(2,1)S(1)} %get-tuple-element.41.refs_1_), channel_id=1, source_target_pairs={{0,1},{1,0},{2,3},{3,2},{4,5},{5,4},{6,7},{7,6},{8,9},{9,8},{10,11... | collective-permute-start | bytes 98312 | tf_op jit(solution)/shard_map/ppermute | solution.py:346
  23.2 1.1 %collective-permute-done.6.refs_2_ = bf16[64,256]{1,0:T(8,128)(2,1)S(1)} collective-permute-done((bf16[64,256]{1,0:T(8,128)(2,1)S(1)}, bf16[64,256]{1,0:T(8,128)(2,1)S(1)}, u32[]{:S(2)}, u32[]{:S(2)}) %collective-permute-start.6) | collective-permute-done | bytes 32800 | tf_op jit(solution)/shard_map/ppermute | solution.py:346
  24.3 0.5 %collective-permute-start.8 = (bf16[64,256]{1,0:T(8,128)(2,1)S(1)}, bf16[64,256]{1,0:T(8,128)(2,1)S(1)}, u32[]{:S(2)}, u32[]{:S(2)}) collective-permute-start(bf16[64,256]{1,0:T(8,128)(2,1)S(1)} %collective-permute-done.6.refs_2_), channel_id=1, source_target_pairs={{0,1},{1,0},{2,3},{3,2},{4,5},{5,4},{6,7},{7,6},{8,9},{9,8},{10,11... | collective-permute-start | bytes 98312 | tf_op jit(solution)/shard_map/ppermute | solution.py:346
  24.8 0.1 collective-permute-start.10
  24.8 1.1 %collective-permute-done.9.refs_6_ = bf16[64,256]{1,0:T(8,128)(2,1)S(1)} collective-permute-done((bf16[64,256]{1,0:T(8,128)(2,1)S(1)}, bf16[64,256]{1,0:T(8,128)(2,1)S(1)}, u32[]{:S(2)}, u32[]{:S(2)}) %collective-permute-start.9) | collective-permute-done | bytes 32800 | tf_op jit(solution)/shard_map/ppermute | solution.py:346
  26.0 0.1 collective-permute-start.11
  26.1 0.0 collective-permute-done.7.refs_3_
  26.1 0.0 collective-permute-done.8.refs_4_
  26.1 0.7 %shard_map.69 = (bf16[16,256]{1,0:T(8,128)(2,1)S(1)}, bf16[16,256]{1,0:T(8,128)(2,1)S(1)}, bf16[16,256]{1,0:T(8,128)(2,1)S(1)}, bf16[16,256]{1,0:T(8,128)(2,1)S(1)}) custom-call(bf16[4,256,256]{2,1,0:T(8,128)(2,1)S(1)} %get-tuple-element.29.refs_0_.refs_6_, bf16[64,256]{1,0:T(8,128)(2,1)S(1)} %get-tuple-element.41.refs_1_, ...), custom_call_target="tpu_custom_call" | custom-call | flops 33554432 | bytes 655360 | tf_op jit(solution)/shard_map/pallas_call | solution.py:324
  26.8 0.0 collective-permute-done.10.refs_7_
  26.8 0.4 %collective-permute-done.11.refs_8_ = bf16[64,256]{1,0:T(8,128)(2,1)S(1)} collective-permute-done((bf16[64,256]{1,0:T(8,128)(2,1)S(1)}, bf16[64,256]{1,0:T(8,128)(2,1)S(1)}, u32[]{:S(2)}, u32[]{:S(2)}) %collective-permute-start.11) | collective-permute-done | bytes 32800 | tf_op jit(solution)/shard_map/ppermute | solution.py:346
  27.2 0.7 %shard_map.70 = (bf16[32,256]{1,0:T(8,128)(2,1)S(1)}, bf16[32,256]{1,0:T(8,128)(2,1)S(1)}, bf16[32,256]{1,0:T(8,128)(2,1)S(1)}, bf16[32,256]{1,0:T(8,128)(2,1)S(1)}) custom-call(bf16[4,256,256]{2,1,0:T(8,128)(2,1)S(1)} %get-tuple-element.29.refs_0_.refs_6_, bf16[16,256]{1,0:T(8,128)(2,1)S(1)} %get-tuple-element.42.refs_1_, ...), custom_call_target="tpu_custom_call" | custom-call | flops 33554432 | bytes 688128 | tf_op jit(solution)/shard_map/pallas_call | solution.py:324
  27.9 0.9 %collective-permute-start.12 = (bf16[32,256]{1,0:T(8,128)(2,1)S(1)}, bf16[32,256]{1,0:T(8,128)(2,1)S(1)}, u32[]{:S(2)}, u32[]{:S(2)}) collective-permute-start(bf16[32,256]{1,0:T(8,128)(2,1)S(1)} %get-tuple-element.48), channel_id=1, source_target_pairs={{0,9},{1,8},{2,11},{3,10},{4,13},{5,12},{6,15},{7,14},{8,1},{9,0},... | collective-permute-start | bytes 49160 | tf_op jit(solution)/shard_map/ppermute | solution.py:346
  28.8 1.5 %collective-permute-start.13 = (bf16[32,256]{1,0:T(8,128)(2,1)S(1)}, bf16[32,256]{1,0:T(8,128)(2,1)S(1)}, u32[]{:S(2)}, u32[]{:S(2)}) collective-permute-start(bf16[32,256]{1,0:T(8,128)(2,1)S(1)} %get-tuple-element.49), channel_id=1, source_target_pairs={{0,13},{1,12},{2,15},{3,14},{4,9},{5,8},{6,11},{7,10},{8,5},{9,4},... | collective-permute-start | bytes 49160 | tf_op jit(solution)/shard_map/ppermute | solution.py:346
  30.2 0.7 %collective-permute-start.14 = (bf16[32,256]{1,0:T(8,128)(2,1)S(1)}, bf16[32,256]{1,0:T(8,128)(2,1)S(1)}, u32[]{:S(2)}, u32[]{:S(2)}) collective-permute-start(bf16[32,256]{1,0:T(8,128)(2,1)S(1)} %get-tuple-element.50), channel_id=1, source_target_pairs={{0,5},{1,4},{2,7},{3,6},{4,1},{5,0},{6,3},{7,2},{8,13},{9,12},{10,... | collective-permute-start | bytes 49160 | tf_op jit(solution)/shard_map/ppermute | solution.py:346
  30.9 1.1 %collective-permute-done.12.refs_1_ = bf16[32,256]{1,0:T(8,128)(2,1)S(1)} collective-permute-done((bf16[32,256]{1,0:T(8,128)(2,1)S(1)}, bf16[32,256]{1,0:T(8,128)(2,1)S(1)}, u32[]{:S(2)}, u32[]{:S(2)}) %collective-permute-start.12) | collective-permute-done | bytes 16416 | tf_op jit(solution)/shard_map/ppermute | solution.py:346
  32.0 1.7 %collective-permute-done.13.refs_2_ = bf16[32,256]{1,0:T(8,128)(2,1)S(1)} collective-permute-done((bf16[32,256]{1,0:T(8,128)(2,1)S(1)}, bf16[32,256]{1,0:T(8,128)(2,1)S(1)}, u32[]{:S(2)}, u32[]{:S(2)}) %collective-permute-start.13) | collective-permute-done | bytes 16416 | tf_op jit(solution)/shard_map/ppermute | solution.py:346
  33.7 0.0 collective-permute-done.14.refs_3_
  33.7 0.8 %shard_map.71 = bf16[8,16,256]{2,1,0:T(8,128)(2,1)} custom-call(bf16[32,256]{1,0:T(8,128)(2,1)S(1)} %get-tuple-element.47.refs_0_, bf16[32,256]{1,0:T(8,128)(2,1)S(1)} %collective-permute-done.12.refs_1_, bf16[32,256]{1,0:T(8,128)(2,1)S(1)} %collective-permute-done.13.refs_2_, bf16[32,256]{1,0:T(8,128)(2,1)S(1)} %collective-permute-done.14.refs_3_, ...), custom_call_target="tpu_custom_call" | custom-call | bytes 655360 | tf_op jit(solution)/shard_map/pallas_call | solution.py:324
  (1 shorter events, 0.0 us)
Async XLA Ops:
  0.0 5.5 %copy-start = (bf16[8,16,256]{2,1,0:T(8,128)(2,1)S(1)}, bf16[8,16,256]{2,1,0:T(8,128)(2,1)}, u32[]{:S(2)}) copy-start(bf16[8,16,256]{2,1,0:T(8,128)(2,1)} %refs_0_.7) | copy-start | bytes 196612
  0.0 5.5 %collective-permute-start = (bf16[8,16,256]{2,1,0:T(8,128)(2,1)}, bf16[8,16,256]{2,1,0:T(8,128)(2,1)S(1)}, u32[]{:S(2)}, u32[]{:S(2)}) collective-permute-start(bf16[8,16,256]{2,1,0:T(8,128)(2,1)} %refs_0_.7), channel_id=1, source_target_pairs={{16,0},{0,16},{17,1},{1,17},{18,2},{2,18},{19,3},{3,19},{20,4},{4,... | collective-permute-start | bytes 196616 | tf_op jit(solution)/shard_map/ppermute | solution.py:357
  2.9 0.7 %copy-start.1 = (bf16[7,7,256]{2,1,0:T(8,128)(2,1)S(1)}, bf16[7,7,256]{2,1,0:T(8,128)(2,1)}, u32[]{:S(2)}) copy-start(bf16[7,7,256]{2,1,0:T(8,128)(2,1)} %refs_0_.4) | copy-start | bytes 75268
  5.6 7.0 %collective-permute-start.1 = (bf16[64,256]{1,0:T(8,128)(2,1)S(1)}, bf16[64,256]{1,0:T(8,128)(2,1)S(1)}, u32[]{:S(2)}, u32[]{:S(2)}) collective-permute-start(bf16[64,256]{1,0:T(8,128)(2,1)S(1)} %get-tuple-element.31), channel_id=1, source_target_pairs={{0,15},{1,2},{2,1},{3,4},{4,3},{5,6},{6,5},{7,8},{8,7},{9,10},{10,... | collective-permute-start | bytes 98312 | tf_op jit(solution)/shard_map/ppermute | solution.py:376
  9.3 3.2 %collective-permute-start.2 = (bf16[64,256]{1,0:T(8,128)(2,1)S(1)}, bf16[64,256]{1,0:T(8,128)(2,1)S(1)}, u32[]{:S(2)}, u32[]{:S(2)}) collective-permute-start(bf16[64,256]{1,0:T(8,128)(2,1)S(1)} %get-tuple-element.32), channel_id=1, source_target_pairs={{0,1},{1,0},{2,3},{3,2},{4,5},{5,4},{6,7},{7,6},{8,9},{9,8},{10,11... | collective-permute-start | bytes 98312 | tf_op jit(solution)/shard_map/ppermute | solution.py:346
  15.2 4.1 %collective-permute-start.3 = (bf16[32,256]{1,0:T(8,128)(2,1)S(1)}, bf16[32,256]{1,0:T(8,128)(2,1)S(1)}, u32[]{:S(2)}, u32[]{:S(2)}) collective-permute-start(bf16[32,256]{1,0:T(8,128)(2,1)S(1)} %get-tuple-element.38), channel_id=1, source_target_pairs={{0,9},{1,8},{2,11},{3,10},{4,13},{5,12},{6,15},{7,14},{8,1},{9,0},... | collective-permute-start | bytes 49160 | tf_op jit(solution)/shard_map/ppermute | solution.py:346
  15.8 5.1 %collective-permute-start.4 = (bf16[32,256]{1,0:T(8,128)(2,1)S(1)}, bf16[32,256]{1,0:T(8,128)(2,1)S(1)}, u32[]{:S(2)}, u32[]{:S(2)}) collective-permute-start(bf16[32,256]{1,0:T(8,128)(2,1)S(1)} %get-tuple-element.39), channel_id=1, source_target_pairs={{0,13},{1,12},{2,15},{3,14},{4,9},{5,8},{6,11},{7,10},{8,5},{9,4},... | collective-permute-start | bytes 49160 | tf_op jit(solution)/shard_map/ppermute | solution.py:346
  17.3 3.6 %collective-permute-start.5 = (bf16[32,256]{1,0:T(8,128)(2,1)S(1)}, bf16[32,256]{1,0:T(8,128)(2,1)S(1)}, u32[]{:S(2)}, u32[]{:S(2)}) collective-permute-start(bf16[32,256]{1,0:T(8,128)(2,1)S(1)} %get-tuple-element.40), channel_id=1, source_target_pairs={{0,5},{1,4},{2,7},{3,6},{4,1},{5,0},{6,3},{7,2},{8,13},{9,12},{10,... | collective-permute-start | bytes 49160 | tf_op jit(solution)/shard_map/ppermute | solution.py:346
  20.9 3.4 %collective-permute-start.6 = (bf16[64,256]{1,0:T(8,128)(2,1)S(1)}, bf16[64,256]{1,0:T(8,128)(2,1)S(1)}, u32[]{:S(2)}, u32[]{:S(2)}) collective-permute-start(bf16[64,256]{1,0:T(8,128)(2,1)S(1)} %get-tuple-element.41.refs_1_), channel_id=1, source_target_pairs={{0,3},{1,2},{2,1},{3,0},{4,7},{5,6},{6,5},{7,4},{8,11},{9,10},{10,... | collective-permute-start | bytes 98312 | tf_op jit(solution)/shard_map/ppermute | solution.py:346
  22.5 3.5 %collective-permute-start.9 = (bf16[64,256]{1,0:T(8,128)(2,1)S(1)}, bf16[64,256]{1,0:T(8,128)(2,1)S(1)}, u32[]{:S(2)}, u32[]{:S(2)}) collective-permute-start(bf16[64,256]{1,0:T(8,128)(2,1)S(1)} %get-tuple-element.46.refs_5_), channel_id=1, source_target_pairs={{0,3},{1,2},{2,1},{3,0},{4,7},{5,6},{6,5},{7,4},{8,11},{9,10},{10,... | collective-permute-start | bytes 98312 | tf_op jit(solution)/shard_map/ppermute | solution.py:346
  22.7 3.4 %collective-permute-start.7 = (bf16[64,256]{1,0:T(8,128)(2,1)S(1)}, bf16[64,256]{1,0:T(8,128)(2,1)S(1)}, u32[]{:S(2)}, u32[]{:S(2)}) collective-permute-start(bf16[64,256]{1,0:T(8,128)(2,1)S(1)} %get-tuple-element.41.refs_1_), channel_id=1, source_target_pairs={{0,1},{1,0},{2,3},{3,2},{4,5},{5,4},{6,7},{7,6},{8,9},{9,8},{10,11... | collective-permute-start | bytes 98312 | tf_op jit(solution)/shard_map/ppermute | solution.py:346
  24.3 1.8 %collective-permute-start.8 = (bf16[64,256]{1,0:T(8,128)(2,1)S(1)}, bf16[64,256]{1,0:T(8,128)(2,1)S(1)}, u32[]{:S(2)}, u32[]{:S(2)}) collective-permute-start(bf16[64,256]{1,0:T(8,128)(2,1)S(1)} %collective-permute-done.6.refs_2_), channel_id=1, source_target_pairs={{0,1},{1,0},{2,3},{3,2},{4,5},{5,4},{6,7},{7,6},{8,9},{9,8},{10,11... | collective-permute-start | bytes 98312 | tf_op jit(solution)/shard_map/ppermute | solution.py:346
  24.8 2.0 %collective-permute-start.10 = (bf16[64,256]{1,0:T(8,128)(2,1)S(1)}, bf16[64,256]{1,0:T(8,128)(2,1)S(1)}, u32[]{:S(2)}, u32[]{:S(2)}) collective-permute-start(bf16[64,256]{1,0:T(8,128)(2,1)S(1)} %get-tuple-element.46.refs_5_), channel_id=1, source_target_pairs={{0,1},{1,0},{2,3},{3,2},{4,5},{5,4},{6,7},{7,6},{8,9},{9,8},{10,11... | collective-permute-start | bytes 98312 | tf_op jit(solution)/shard_map/ppermute | solution.py:346
  26.0 1.2 %collective-permute-start.11 = (bf16[64,256]{1,0:T(8,128)(2,1)S(1)}, bf16[64,256]{1,0:T(8,128)(2,1)S(1)}, u32[]{:S(2)}, u32[]{:S(2)}) collective-permute-start(bf16[64,256]{1,0:T(8,128)(2,1)S(1)} %collective-permute-done.9.refs_6_), channel_id=1, source_target_pairs={{0,1},{1,0},{2,3},{3,2},{4,5},{5,4},{6,7},{7,6},{8,9},{9,8},{10,11... | collective-permute-start | bytes 98312 | tf_op jit(solution)/shard_map/ppermute | solution.py:346
  27.9 4.1 %collective-permute-start.12 = (bf16[32,256]{1,0:T(8,128)(2,1)S(1)}, bf16[32,256]{1,0:T(8,128)(2,1)S(1)}, u32[]{:S(2)}, u32[]{:S(2)}) collective-permute-start(bf16[32,256]{1,0:T(8,128)(2,1)S(1)} %get-tuple-element.48), channel_id=1, source_target_pairs={{0,9},{1,8},{2,11},{3,10},{4,13},{5,12},{6,15},{7,14},{8,1},{9,0},... | collective-permute-start | bytes 49160 | tf_op jit(solution)/shard_map/ppermute | solution.py:346
  28.8 5.0 %collective-permute-start.13 = (bf16[32,256]{1,0:T(8,128)(2,1)S(1)}, bf16[32,256]{1,0:T(8,128)(2,1)S(1)}, u32[]{:S(2)}, u32[]{:S(2)}) collective-permute-start(bf16[32,256]{1,0:T(8,128)(2,1)S(1)} %get-tuple-element.49), channel_id=1, source_target_pairs={{0,13},{1,12},{2,15},{3,14},{4,9},{5,8},{6,11},{7,10},{8,5},{9,4},... | collective-permute-start | bytes 49160 | tf_op jit(solution)/shard_map/ppermute | solution.py:346
  30.2 3.5 %collective-permute-start.14 = (bf16[32,256]{1,0:T(8,128)(2,1)S(1)}, bf16[32,256]{1,0:T(8,128)(2,1)S(1)}, u32[]{:S(2)}, u32[]{:S(2)}) collective-permute-start(bf16[32,256]{1,0:T(8,128)(2,1)S(1)} %get-tuple-element.50), channel_id=1, source_target_pairs={{0,5},{1,4},{2,7},{3,6},{4,1},{5,0},{6,3},{7,2},{8,13},{9,12},{10,... | collective-permute-start | bytes 49160 | tf_op jit(solution)/shard_map/ppermute | solution.py:346

commit v25 on v23

--- a/solution.py
+++ b/solution.py
@@ -258,11 +258,12 @@
 
 
 def join_kernel(levels, some, *refs):
-    parts, joined = refs[:levels], refs[levels:]
+    parts, whole_ref = refs[:levels], refs[levels]
     cols = parts[0].shape[0] // some
     for r in range(some):
         for k in range(levels):
-            joined[r][k * cols : (k + 1) * cols] = parts[k][r * cols : (r + 1) * cols]
+            start = (r * levels + k) * cols
+            whole_ref[start : start + cols] = parts[k][r * cols : (r + 1) * cols]
 
 
 def circle_kernel(levels, before, *refs):
@@ -398,15 +399,18 @@
     )
 
     parts = exchange(parts)
-    joined = call(
-        functools.partial(join_kernel, levels, some), [(levels * cols, channels)] * some, parts
-    )
-    circles = [[part] for part in joined]
+    block = levels * cols
+    wholes = list(call(
+        functools.partial(join_kernel, levels, some), [(some * block, channels)], parts
+    ))
     mask = column // 2
-    while mask:
-        for circle in circles:
-            circle += [swap(part, mask + mask // 2) for part in circle]
+    while mask > 1:
+        wholes = wholes + [swap(part, mask + mask // 2) for part in wholes]
         mask //= 2
+    circles = []
+    for r in range(some):
+        circle = [whole[r * block : (r + 1) * block] for whole in wholes]
+        circles.append(circle + ([swap(part, 1) for part in circle] if mask else []))
     done = []
     for r, circle in enumerate(circles):
         last_one = r == some - 1

time: 34.7 us -> 34.8 us (level)
    ppermute x13 -> x12, waiting for transfers between devices: 7.78 us -> 8.02 us  [swap(): return lax.ppermute(piece, 'lon', [(j, j ^ mask) for j in range(nlon)])]
    ppermute x13 -> x12, starting transfers between devices: 9.32 us -> 9.13 us  [swap(): return lax.ppermute(piece, 'lon', [(j, j ^ mask) for j in range(nlon)])]
  transfers between devices with their start and end apart: 15 -> 14, of which waited for: 7 -> 6; matrix products, arithmetic and copies ran while one was open for 0% -> 0% of each run, Pallas kernels for 16% -> 16%
where the time goes in v25:
time: 34.8 us; the launch traced here: 34.6 us
  starting transfers between devices  15.9 us (46%)
  Pallas kernels  9.87 us (28%)
  waiting for transfers between devices  8.03 us (23%)
  local copies, waits for them, and re-layouts  0.76 us (2%)
    pallas_call x8, Pallas kernels, call(): pl.pallas_call(kernel, out_shape=shapes, in_specs=[given] * len(operands)...  9.87 us
    ppermute x12, starting transfers between devices, swap(): return lax.ppermute(piece, 'lon', [(j, j ^ mask) for j in range(nlon)])  9.13 us
    ppermute x12, waiting for transfers between devices, swap(): return lax.ppermute(piece, 'lon', [(j, j ^ mask) for j in range(nlon)])  8.02 us
    ppermute x1, starting transfers between devices, shards(): lax.ppermute(far, 'lon', [(j, (j - 1) % nlon if j % 2 == 0 else (j + 1) %...  3.78 us
    ppermute x1, starting transfers between devices, shards(): lax.ppermute(field, 'lat', [((i + s) % nlat, i) for i in range(nlat)])  2.94 us
    unnamed x4, local copies, waits for them, and re-layouts  0.75 us
  transfers between devices with their start and end apart: 14, of which 6 were waited for; matrix products, arithmetic and copies ran while one was open for 0% of the time, Pallas kernels for 16%

profile of v25, /device:TPU:0, one launch (start us, length us, event | category | flops | bytes accessed | tf_op | source)
XLA Modules:
  0.0 34.6 jit_solution(3461809143414548161)
XLA Ops:
  0.0 0.0 copy-start
  0.0 2.9 %collective-permute-start = (bf16[8,16,256]{2,1,0:T(8,128)(2,1)}, bf16[8,16,256]{2,1,0:T(8,128)(2,1)S(1)}, u32[]{:S(2)}, u32[]{:S(2)}) collective-permute-start(bf16[8,16,256]{2,1,0:T(8,128)(2,1)} %refs_0_.7), channel_id=1, source_target_pairs={{16,0},{0,16},{17,1},{1,17},{18,2},{2,18},{19,3},{3,19},{20,4},{4,... | collective-permute-start | bytes 196616 | tf_op jit(solution)/shard_map/ppermute | solution.py:352
  2.9 0.0 copy-start.1
  2.9 0.7 %copy-done.1 = bf16[7,7,256]{2,1,0:T(8,128)(2,1)S(1)} copy-done((bf16[7,7,256]{2,1,0:T(8,128)(2,1)S(1)}, bf16[7,7,256]{2,1,0:T(8,128)(2,1)}, u32[]{:S(2)}) %copy-start.1) | copy-done | bytes 25112
  3.7 1.8 %shard_map.64 = (bf16[7,7,256]{2,1,0:T(8,128)(2,1)S(1)}, bf16[256,1024]{1,0:T(8,128)(2,1)S(1)}, bf16[1024,256]{1,0:T(8,128)(2,1)S(1)}, bf16[4,256,256]{2,1,0:T(8,128)(2,1)S(1)}, bf16[4,256,256]{2,1,0:T(8,128)(2,1)S(1)}) custom-call(bf16[7,7,256]{2,1,0:T(8,128)(2,1)S(1)} %copy-done.1, bf16[256,1024]{1,0:T(8,128)(2,1)} %refs_1_.1, bf16[1024,256]{1,0:T(8,128)(2,1)} %refs_2_.1, ...), custom_call_target="tpu_custom_call" | custom-call | bytes 2122240 | tf_op jit(solution)/shard_map/pallas_call | solution.py:319
  5.5 0.0 collective-permute-done.refs_1_
  5.5 0.0 copy-done
  5.5 0.1 shard_map.65
  5.6 3.8 %collective-permute-start.1 = (bf16[64,256]{1,0:T(8,128)(2,1)S(1)}, bf16[64,256]{1,0:T(8,128)(2,1)S(1)}, u32[]{:S(2)}, u32[]{:S(2)}) collective-permute-start(bf16[64,256]{1,0:T(8,128)(2,1)S(1)} %get-tuple-element.29), channel_id=1, source_target_pairs={{0,15},{1,2},{2,1},{3,4},{4,3},{5,6},{6,5},{7,8},{8,7},{9,10},{10,... | collective-permute-start | bytes 98312 | tf_op jit(solution)/shard_map/ppermute | solution.py:371
  9.3 0.0 collective-permute-start.2
  9.4 3.2 %shard_map.66 = (bf16[64,256]{1,0:T(8,128)(2,1)S(1)}, bf16[64,256]{1,0:T(8,128)(2,1)S(1)}) custom-call(bf16[8,16,256]{2,1,0:T(8,128)(2,1)S(1)} %copy-done, bf16[8,16,256]{2,1,0:T(8,128)(2,1)S(1)} %collective-permute-done.refs_1_, bf16[7,7,256]{2,1,0:T(8,128)(2,1)S(1)} %get-tuple-element.31.refs_2_.refs_5_, ...), custom_call_target="tpu_custom_call" | custom-call | flops 134217728 | bytes 1729024 | tf_op jit(solution)/shard_map/pallas_call | solution.py:319
  12.6 0.0 collective-permute-done.1.refs_2_
  12.6 0.0 collective-permute-done.2.refs_3_
  12.6 2.6 %shard_map.67 = (bf16[64,256]{1,0:T(8,128)(2,1)S(1)}, bf16[32,256]{1,0:T(8,128)(2,1)S(1)}, bf16[32,256]{1,0:T(8,128)(2,1)S(1)}, bf16[32,256]{1,0:T(8,128)(2,1)S(1)}, bf16[32,256]{1,0:T(8,128)(2,1)S(1)}) custom-call(bf16[8,16,256]{2,1,0:T(8,128)(2,1)S(1)} %copy-done, bf16[8,16,256]{2,1,0:T(8,128)(2,1)S(1)} %collective-permute-done.refs_1_, ...), custom_call_target="tpu_custom_call" | custom-call | flops 134217728 | bytes 1827328 | tf_op jit(solution)/shard_map/pallas_call | solution.py:319
  15.2 0.6 %collective-permute-start.3 = (bf16[32,256]{1,0:T(8,128)(2,1)S(1)}, bf16[32,256]{1,0:T(8,128)(2,1)S(1)}, u32[]{:S(2)}, u32[]{:S(2)}) collective-permute-start(bf16[32,256]{1,0:T(8,128)(2,1)S(1)} %get-tuple-element.36), channel_id=1, source_target_pairs={{0,9},{1,8},{2,11},{3,10},{4,13},{5,12},{6,15},{7,14},{8,1},{9,0},... | collective-permute-start | bytes 49160 | tf_op jit(solution)/shard_map/ppermute | solution.py:341
  15.8 1.5 %collective-permute-start.4 = (bf16[32,256]{1,0:T(8,128)(2,1)S(1)}, bf16[32,256]{1,0:T(8,128)(2,1)S(1)}, u32[]{:S(2)}, u32[]{:S(2)}) collective-permute-start(bf16[32,256]{1,0:T(8,128)(2,1)S(1)} %get-tuple-element.37), channel_id=1, source_target_pairs={{0,13},{1,12},{2,15},{3,14},{4,9},{5,8},{6,11},{7,10},{8,5},{9,4},... | collective-permute-start | bytes 49160 | tf_op jit(solution)/shard_map/ppermute | solution.py:341
  17.3 1.3 %collective-permute-start.5 = (bf16[32,256]{1,0:T(8,128)(2,1)S(1)}, bf16[32,256]{1,0:T(8,128)(2,1)S(1)}, u32[]{:S(2)}, u32[]{:S(2)}) collective-permute-start(bf16[32,256]{1,0:T(8,128)(2,1)S(1)} %get-tuple-element.38), channel_id=1, source_target_pairs={{0,5},{1,4},{2,7},{3,6},{4,1},{5,0},{6,3},{7,2},{8,13},{9,12},{10,... | collective-permute-start | bytes 49160 | tf_op jit(solution)/shard_map/ppermute | solution.py:341
  18.6 0.7 %collective-permute-done.3.refs_1_ = bf16[32,256]{1,0:T(8,128)(2,1)S(1)} collective-permute-done((bf16[32,256]{1,0:T(8,128)(2,1)S(1)}, bf16[32,256]{1,0:T(8,128)(2,1)S(1)}, u32[]{:S(2)}, u32[]{:S(2)}) %collective-permute-start.3) | collective-permute-done | bytes 16416 | tf_op jit(solution)/shard_map/ppermute | solution.py:341
  19.4 1.6 %collective-permute-done.4.refs_2_ = bf16[32,256]{1,0:T(8,128)(2,1)S(1)} collective-permute-done((bf16[32,256]{1,0:T(8,128)(2,1)S(1)}, bf16[32,256]{1,0:T(8,128)(2,1)S(1)}, u32[]{:S(2)}, u32[]{:S(2)}) %collective-permute-start.4) | collective-permute-done | bytes 16416 | tf_op jit(solution)/shard_map/ppermute | solution.py:341
  20.9 0.0 collective-permute-done.5.refs_3_
  20.9 1.6 %collective-permute-start.6 = (bf16[128,256]{1,0:T(8,128)(2,1)S(1)}, bf16[128,256]{1,0:T(8,128)(2,1)S(1)}, u32[]{:S(2)}, u32[]{:S(2)}) collective-permute-start(bf16[128,256]{1,0:T(8,128)(2,1)S(1)} %shard_map.68), channel_id=1, source_target_pairs={{0,3},{1,2},{2,1},{3,0},{4,7},{5,6},{6,5},{7,4},{8,11},{9,10},{10,... | collective-permute-start | bytes 196616 | tf_op jit(solution)/shard_map/ppermute | solution.py:341
  22.5 0.0 collective-permute-start.7
  22.5 2.3 %collective-permute-done.6 = bf16[128,256]{1,0:T(8,128)(2,1)S(1)} collective-permute-done((bf16[128,256]{1,0:T(8,128)(2,1)S(1)}, bf16[128,256]{1,0:T(8,128)(2,1)S(1)}, u32[]{:S(2)}, u32[]{:S(2)}) %collective-permute-start.6) | collective-permute-done | bytes 65568 | tf_op jit(solution)/shard_map/ppermute | solution.py:341
  24.8 0.4 %collective-permute-start.8 = (bf16[64,256]{1,0:T(8,128)(2,1)S(1)}, bf16[64,256]{1,0:T(8,128)(2,1)S(1)}, u32[]{:S(2)}, u32[]{:S(2)}) collective-permute-start(bf16[64,256]{1,0:T(8,128)(2,1)S(1)} %get-tuple-element.50.refs_2_), channel_id=1, source_target_pairs={{0,1},{1,0},{2,3},{3,2},{4,5},{5,4},{6,7},{7,6},{8,9},{9,8},{10,11... | collective-permute-start | bytes 98312 | tf_op jit(solution)/shard_map/ppermute | solution.py:341
  25.2 0.1 collective-permute-start.9
  25.3 0.4 %collective-permute-start.10 = (bf16[64,256]{1,0:T(8,128)(2,1)S(1)}, bf16[64,256]{1,0:T(8,128)(2,1)S(1)}, u32[]{:S(2)}, u32[]{:S(2)}) collective-permute-start(bf16[64,256]{1,0:T(8,128)(2,1)S(1)} %get-tuple-element.49.refs_6_), channel_id=1, source_target_pairs={{0,1},{1,0},{2,3},{3,2},{4,5},{5,4},{6,7},{7,6},{8,9},{9,8},{10,11... | collective-permute-start | bytes 98312 | tf_op jit(solution)/shard_map/ppermute | solution.py:341
  25.7 0.0 collective-permute-done.7.refs_3_
  25.7 0.3 collective-permute-done.8.refs_4_
  26.1 0.7 %shard_map.69 = (bf16[16,256]{1,0:T(8,128)(2,1)S(1)}, bf16[16,256]{1,0:T(8,128)(2,1)S(1)}, bf16[16,256]{1,0:T(8,128)(2,1)S(1)}, bf16[16,256]{1,0:T(8,128)(2,1)S(1)}) custom-call(bf16[4,256,256]{2,1,0:T(8,128)(2,1)S(1)} %get-tuple-element.27.refs_0_.refs_6_, bf16[64,256]{1,0:T(8,128)(2,1)S(1)} %get-tuple-element.52.refs_1_, ...), custom_call_target="tpu_custom_call" | custom-call | flops 33554432 | bytes 655360 | tf_op jit(solution)/shard_map/pallas_call | solution.py:319
  26.8 0.0 collective-permute-done.9.refs_7_
  26.8 0.0 collective-permute-done.10.refs_8_
  26.8 0.7 %shard_map.70 = (bf16[32,256]{1,0:T(8,128)(2,1)S(1)}, bf16[32,256]{1,0:T(8,128)(2,1)S(1)}, bf16[32,256]{1,0:T(8,128)(2,1)S(1)}, bf16[32,256]{1,0:T(8,128)(2,1)S(1)}) custom-call(bf16[4,256,256]{2,1,0:T(8,128)(2,1)S(1)} %get-tuple-element.27.refs_0_.refs_6_, bf16[16,256]{1,0:T(8,128)(2,1)S(1)} %get-tuple-element.39.refs_1_, ...), custom_call_target="tpu_custom_call" | custom-call | flops 33554432 | bytes 688128 | tf_op jit(solution)/shard_map/pallas_call | solution.py:319
  27.5 1.4 %collective-permute-start.11 = (bf16[32,256]{1,0:T(8,128)(2,1)S(1)}, bf16[32,256]{1,0:T(8,128)(2,1)S(1)}, u32[]{:S(2)}, u32[]{:S(2)}) collective-permute-start(bf16[32,256]{1,0:T(8,128)(2,1)S(1)} %get-tuple-element.44), channel_id=1, source_target_pairs={{0,9},{1,8},{2,11},{3,10},{4,13},{5,12},{6,15},{7,14},{8,1},{9,0},... | collective-permute-start | bytes 49160 | tf_op jit(solution)/shard_map/ppermute | solution.py:341
  28.9 1.5 %collective-permute-start.12 = (bf16[32,256]{1,0:T(8,128)(2,1)S(1)}, bf16[32,256]{1,0:T(8,128)(2,1)S(1)}, u32[]{:S(2)}, u32[]{:S(2)}) collective-permute-start(bf16[32,256]{1,0:T(8,128)(2,1)S(1)} %get-tuple-element.45), channel_id=1, source_target_pairs={{0,13},{1,12},{2,15},{3,14},{4,9},{5,8},{6,11},{7,10},{8,5},{9,4},... | collective-permute-start | bytes 49160 | tf_op jit(solution)/shard_map/ppermute | solution.py:341
  30.3 0.4 %collective-permute-start.13 = (bf16[32,256]{1,0:T(8,128)(2,1)S(1)}, bf16[32,256]{1,0:T(8,128)(2,1)S(1)}, u32[]{:S(2)}, u32[]{:S(2)}) collective-permute-start(bf16[32,256]{1,0:T(8,128)(2,1)S(1)} %get-tuple-element.46), channel_id=1, source_target_pairs={{0,5},{1,4},{2,7},{3,6},{4,1},{5,0},{6,3},{7,2},{8,13},{9,12},{10,... | collective-permute-start | bytes 49160 | tf_op jit(solution)/shard_map/ppermute | solution.py:341
  30.7 0.9 %collective-permute-done.11.refs_1_ = bf16[32,256]{1,0:T(8,128)(2,1)S(1)} collective-permute-done((bf16[32,256]{1,0:T(8,128)(2,1)S(1)}, bf16[32,256]{1,0:T(8,128)(2,1)S(1)}, u32[]{:S(2)}, u32[]{:S(2)}) %collective-permute-start.11) | collective-permute-done | bytes 16416 | tf_op jit(solution)/shard_map/ppermute | solution.py:341
  31.6 2.2 %collective-permute-done.12.refs_2_ = bf16[32,256]{1,0:T(8,128)(2,1)S(1)} collective-permute-done((bf16[32,256]{1,0:T(8,128)(2,1)S(1)}, bf16[32,256]{1,0:T(8,128)(2,1)S(1)}, u32[]{:S(2)}, u32[]{:S(2)}) %collective-permute-start.12) | collective-permute-done | bytes 16416 | tf_op jit(solution)/shard_map/ppermute | solution.py:341
  33.8 0.0 collective-permute-done.13.refs_3_
  33.8 0.8 %shard_map.71 = bf16[8,16,256]{2,1,0:T(8,128)(2,1)} custom-call(bf16[32,256]{1,0:T(8,128)(2,1)S(1)} %get-tuple-element.43.refs_0_, bf16[32,256]{1,0:T(8,128)(2,1)S(1)} %collective-permute-done.11.refs_1_, bf16[32,256]{1,0:T(8,128)(2,1)S(1)} %collective-permute-done.12.refs_2_, bf16[32,256]{1,0:T(8,128)(2,1)S(1)} %collective-permute-done.13.refs_3_, ...), custom_call_target="tpu_custom_call" | custom-call | bytes 655360 | tf_op jit(solution)/shard_map/pallas_call | solution.py:319
  (3 shorter events, 0.0 us)
Async XLA Ops:
  0.0 5.5 %copy-start = (bf16[8,16,256]{2,1,0:T(8,128)(2,1)S(1)}, bf16[8,16,256]{2,1,0:T(8,128)(2,1)}, u32[]{:S(2)}) copy-start(bf16[8,16,256]{2,1,0:T(8,128)(2,1)} %refs_0_.7) | copy-start | bytes 196612
  0.0 5.5 %collective-permute-start = (bf16[8,16,256]{2,1,0:T(8,128)(2,1)}, bf16[8,16,256]{2,1,0:T(8,128)(2,1)S(1)}, u32[]{:S(2)}, u32[]{:S(2)}) collective-permute-start(bf16[8,16,256]{2,1,0:T(8,128)(2,1)} %refs_0_.7), channel_id=1, source_target_pairs={{16,0},{0,16},{17,1},{1,17},{18,2},{2,18},{19,3},{3,19},{20,4},{4,... | collective-permute-start | bytes 196616 | tf_op jit(solution)/shard_map/ppermute | solution.py:352
  2.9 0.7 %copy-start.1 = (bf16[7,7,256]{2,1,0:T(8,128)(2,1)S(1)}, bf16[7,7,256]{2,1,0:T(8,128)(2,1)}, u32[]{:S(2)}) copy-start(bf16[7,7,256]{2,1,0:T(8,128)(2,1)} %refs_0_.4) | copy-start | bytes 75268
  5.6 7.0 %collective-permute-start.1 = (bf16[64,256]{1,0:T(8,128)(2,1)S(1)}, bf16[64,256]{1,0:T(8,128)(2,1)S(1)}, u32[]{:S(2)}, u32[]{:S(2)}) collective-permute-start(bf16[64,256]{1,0:T(8,128)(2,1)S(1)} %get-tuple-element.29), channel_id=1, source_target_pairs={{0,15},{1,2},{2,1},{3,4},{4,3},{5,6},{6,5},{7,8},{8,7},{9,10},{10,... | collective-permute-start | bytes 98312 | tf_op jit(solution)/shard_map/ppermute | solution.py:371
  9.3 3.2 %collective-permute-start.2 = (bf16[64,256]{1,0:T(8,128)(2,1)S(1)}, bf16[64,256]{1,0:T(8,128)(2,1)S(1)}, u32[]{:S(2)}, u32[]{:S(2)}) collective-permute-start(bf16[64,256]{1,0:T(8,128)(2,1)S(1)} %get-tuple-element.30), channel_id=1, source_target_pairs={{0,1},{1,0},{2,3},{3,2},{4,5},{5,4},{6,7},{7,6},{8,9},{9,8},{10,11... | collective-permute-start | bytes 98312 | tf_op jit(solution)/shard_map/ppermute | solution.py:341
  15.2 4.1 %collective-permute-start.3 = (bf16[32,256]{1,0:T(8,128)(2,1)S(1)}, bf16[32,256]{1,0:T(8,128)(2,1)S(1)}, u32[]{:S(2)}, u32[]{:S(2)}) collective-permute-start(bf16[32,256]{1,0:T(8,128)(2,1)S(1)} %get-tuple-element.36), channel_id=1, source_target_pairs={{0,9},{1,8},{2,11},{3,10},{4,13},{5,12},{6,15},{7,14},{8,1},{9,0},... | collective-permute-start | bytes 49160 | tf_op jit(solution)/shard_map/ppermute | solution.py:341
  15.8 5.1 %collective-permute-start.4 = (bf16[32,256]{1,0:T(8,128)(2,1)S(1)}, bf16[32,256]{1,0:T(8,128)(2,1)S(1)}, u32[]{:S(2)}, u32[]{:S(2)}) collective-permute-start(bf16[32,256]{1,0:T(8,128)(2,1)S(1)} %get-tuple-element.37), channel_id=1, source_target_pairs={{0,13},{1,12},{2,15},{3,14},{4,9},{5,8},{6,11},{7,10},{8,5},{9,4},... | collective-permute-start | bytes 49160 | tf_op jit(solution)/shard_map/ppermute | solution.py:341
  17.3 3.6 %collective-permute-start.5 = (bf16[32,256]{1,0:T(8,128)(2,1)S(1)}, bf16[32,256]{1,0:T(8,128)(2,1)S(1)}, u32[]{:S(2)}, u32[]{:S(2)}) collective-permute-start(bf16[32,256]{1,0:T(8,128)(2,1)S(1)} %get-tuple-element.38), channel_id=1, source_target_pairs={{0,5},{1,4},{2,7},{3,6},{4,1},{5,0},{6,3},{7,2},{8,13},{9,12},{10,... | collective-permute-start | bytes 49160 | tf_op jit(solution)/shard_map/ppermute | solution.py:341
  20.9 3.9 %collective-permute-start.6 = (bf16[128,256]{1,0:T(8,128)(2,1)S(1)}, bf16[128,256]{1,0:T(8,128)(2,1)S(1)}, u32[]{:S(2)}, u32[]{:S(2)}) collective-permute-start(bf16[128,256]{1,0:T(8,128)(2,1)S(1)} %shard_map.68), channel_id=1, source_target_pairs={{0,3},{1,2},{2,1},{3,0},{4,7},{5,6},{6,5},{7,4},{8,11},{9,10},{10,... | collective-permute-start | bytes 196616 | tf_op jit(solution)/shard_map/ppermute | solution.py:341
  22.5 3.2 %collective-permute-start.7 = (bf16[64,256]{1,0:T(8,128)(2,1)S(1)}, bf16[64,256]{1,0:T(8,128)(2,1)S(1)}, u32[]{:S(2)}, u32[]{:S(2)}) collective-permute-start(bf16[64,256]{1,0:T(8,128)(2,1)S(1)} %get-tuple-element.52.refs_1_), channel_id=1, source_target_pairs={{0,1},{1,0},{2,3},{3,2},{4,5},{5,4},{6,7},{7,6},{8,9},{9,8},{10,11... | collective-permute-start | bytes 98312 | tf_op jit(solution)/shard_map/ppermute | solution.py:341
  24.8 1.3 %collective-permute-start.8 = (bf16[64,256]{1,0:T(8,128)(2,1)S(1)}, bf16[64,256]{1,0:T(8,128)(2,1)S(1)}, u32[]{:S(2)}, u32[]{:S(2)}) collective-permute-start(bf16[64,256]{1,0:T(8,128)(2,1)S(1)} %get-tuple-element.50.refs_2_), channel_id=1, source_target_pairs={{0,1},{1,0},{2,3},{3,2},{4,5},{5,4},{6,7},{7,6},{8,9},{9,8},{10,11... | collective-permute-start | bytes 98312 | tf_op jit(solution)/shard_map/ppermute | solution.py:341
  25.2 1.6 %collective-permute-start.9 = (bf16[64,256]{1,0:T(8,128)(2,1)S(1)}, bf16[64,256]{1,0:T(8,128)(2,1)S(1)}, u32[]{:S(2)}, u32[]{:S(2)}) collective-permute-start(bf16[64,256]{1,0:T(8,128)(2,1)S(1)} %get-tuple-element.51.refs_5_), channel_id=1, source_target_pairs={{0,1},{1,0},{2,3},{3,2},{4,5},{5,4},{6,7},{7,6},{8,9},{9,8},{10,11... | collective-permute-start | bytes 98312 | tf_op jit(solution)/shard_map/ppermute | solution.py:341
  25.3 1.5 %collective-permute-start.10 = (bf16[64,256]{1,0:T(8,128)(2,1)S(1)}, bf16[64,256]{1,0:T(8,128)(2,1)S(1)}, u32[]{:S(2)}, u32[]{:S(2)}) collective-permute-start(bf16[64,256]{1,0:T(8,128)(2,1)S(1)} %get-tuple-element.49.refs_6_), channel_id=1, source_target_pairs={{0,1},{1,0},{2,3},{3,2},{4,5},{5,4},{6,7},{7,6},{8,9},{9,8},{10,11... | collective-permute-start | bytes 98312 | tf_op jit(solution)/shard_map/ppermute | solution.py:341
  27.5 4.1 %collective-permute-start.11 = (bf16[32,256]{1,0:T(8,128)(2,1)S(1)}, bf16[32,256]{1,0:T(8,128)(2,1)S(1)}, u32[]{:S(2)}, u32[]{:S(2)}) collective-permute-start(bf16[32,256]{1,0:T(8,128)(2,1)S(1)} %get-tuple-element.44), channel_id=1, source_target_pairs={{0,9},{1,8},{2,11},{3,10},{4,13},{5,12},{6,15},{7,14},{8,1},{9,0},... | collective-permute-start | bytes 49160 | tf_op jit(solution)/shard_map/ppermute | solution.py:341
  28.9 5.0 %collective-permute-start.12 = (bf16[32,256]{1,0:T(8,128)(2,1)S(1)}, bf16[32,256]{1,0:T(8,128)(2,1)S(1)}, u32[]{:S(2)}, u32[]{:S(2)}) collective-permute-start(bf16[32,256]{1,0:T(8,128)(2,1)S(1)} %get-tuple-element.45), channel_id=1, source_target_pairs={{0,13},{1,12},{2,15},{3,14},{4,9},{5,8},{6,11},{7,10},{8,5},{9,4},... | collective-permute-start | bytes 49160 | tf_op jit(solution)/shard_map/ppermute | solution.py:341
  30.3 3.5 %collective-permute-start.13 = (bf16[32,256]{1,0:T(8,128)(2,1)S(1)}, bf16[32,256]{1,0:T(8,128)(2,1)S(1)}, u32[]{:S(2)}, u32[]{:S(2)}) collective-permute-start(bf16[32,256]{1,0:T(8,128)(2,1)S(1)} %get-tuple-element.46), channel_id=1, source_target_pairs={{0,5},{1,4},{2,7},{3,6},{4,1},{5,0},{6,3},{7,2},{8,13},{9,12},{10,... | collective-permute-start | bytes 49160 | tf_op jit(solution)/shard_map/ppermute | solution.py:341
